TPU v7x, 32 devices: a whole 2x2x4 slice. The times are simulated.
32 devices in a mesh: dp: 8 (over y, x, core), shard: 4 (over z).
Axes of the slice: x: 2, y: 2, z: 4, core: 2. Of those that a mesh axis runs over, the one named last changes fastest.
Arguments:
- tokens: bfloat16 [2, 8192, 1024], P(None, ('dp', 'shard')), may hold values from -6 to 6
- positions: int32 [2, 8192], P(None, ('dp', 'shard')), may hold values from -1 to 255, as said below
- cotangent: bfloat16 [2, 8192, 1024], P(None, ('dp', 'shard')), may hold values from -6 to 6
- norm_gain: bfloat16 [1024], P(('dp', 'shard')), may hold values from 0.099609375 to 1.8984375
- in_weight: bfloat16 [1024, 3072], P(('dp', 'shard')), may hold values from -0.1875 to 0.1875
- conv_weight: bfloat16 [3, 1024], P(None, ('dp', 'shard')), may hold values from -3 to 3
- out_weight: bfloat16 [1024, 1024], P(('dp', 'shard')), may hold values from -0.1875 to 0.1875
- ffn_gain: bfloat16 [1024], P(('dp', 'shard')), may hold values from 0.099609375 to 1.8984375
- gate_weight: bfloat16 [1024, 4608], P(('dp', 'shard')), may hold values from -0.1875 to 0.1875
- up_weight: bfloat16 [1024, 4608], P(('dp', 'shard')), may hold values from -0.1875 to 0.1875
- down_weight: bfloat16 [4608, 1024], P(('dp', 'shard')), may hold values from -0.125 to 0.125
Outputs:
- block_out: bfloat16 [2, 8192, 1024], P(None, ('dp', 'shard'))
- input_grad: bfloat16 [2, 8192, 1024], P(None, ('dp', 'shard'))
- grad_norm_gain: float32 [1024], P(('dp', 'shard'))
- grad_in_weight: float32 [1024, 3072], P(('dp', 'shard'))
- grad_conv_weight: float32 [3, 1024], P(None, ('dp', 'shard'))
- grad_out_weight: float32 [1024, 1024], P(('dp', 'shard'))
- grad_ffn_gain: float32 [1024], P(('dp', 'shard'))
- grad_gate_weight: float32 [1024, 4608], P(('dp', 'shard'))
- grad_up_weight: float32 [1024, 4608], P(('dp', 'shard'))
- grad_down_weight: float32 [4608, 1024], P(('dp', 'shard'))
Inputs may be any that keep to these rules, and one draw needn't show every extreme that they name: `positions`: each device's 256 rows of a micro-batch hold whole sequences one after another, each starting at a block boundary with place 0 and taking whole blocks of 128 rows, its last block padded with -1; padding blocks follow the sequences. In every micro-batch some device holds one sequence of exactly 256 rows.
All inputs are finite; a program needn't handle non-finite values.
Results may differ from a plain program's by a relative error of at most 0.0096.
Values may be sent and summed in bfloat16 or wider, within the bound.
No kernel may reach another device: no remote copies, remote signals or barrier semaphores. Data moves between devices by JAX's collectives and lax.ppermute only.
A program may use at most 256 MiB of HBM per device.

v0:
```python
from functools import reduce

import jax
import jax.numpy as jnp
from jax import lax
from jax.sharding import PartitionSpec as P

EPSILON = 1e-05
SMALL_COLUMNS = 128


def normed(values, scales):
    return values * lax.rsqrt(jnp.mean(values * values, axis=-1, keepdims=True) + EPSILON) * scales


def causal_conv(mixed_rows, kernel, places):
    zero_row = jnp.zeros((1, mixed_rows.shape[1]), mixed_rows.dtype)
    earlier = jnp.concatenate([zero_row, mixed_rows[:-1]], axis=0)
    earliest = jnp.concatenate([zero_row, zero_row, mixed_rows[:-2]], axis=0)
    first_mask = (places >= 1).astype(mixed_rows.dtype)[:, None]
    second_mask = (places >= 2).astype(mixed_rows.dtype)[:, None]
    return (
        kernel[0] * mixed_rows
        + kernel[1] * earlier * first_mask
        + kernel[2] * earliest * second_mask
    )


def gated(gate_value, up_value):
    return jax.nn.silu(gate_value) * up_value


def forward_dot(left_side, right_side):
    return jnp.dot(left_side, right_side, preferred_element_type=jnp.float32)


def rows_dot(left_side, right_side):
    return lax.dot_general(
        left_side, right_side, (((0,), (0,)), ((), ())), preferred_element_type=jnp.float32
    )


def back_dot(left_side, right_side):
    return lax.dot_general(
        left_side, right_side, (((1,), (1,)), ((), ())), preferred_element_type=jnp.float32
    )


def forward(tokens_rows, places, weights):
    norm_gain, in_weight, conv_weight, out_weight, ffn_gain, gate_weight, up_weight, down_weight = (
        weights
    )
    features = tokens_rows.shape[1]
    inputs = tokens_rows.astype(jnp.float32)
    live_rows = (places >= 0).astype(jnp.float32)[:, None]
    first_normed = normed(inputs, norm_gain.astype(jnp.float32)).astype(jnp.bfloat16)
    projected = forward_dot(first_normed, in_weight)
    b_part = projected[:, :features]
    c_part = projected[:, features : 2 * features]
    x_part = projected[:, 2 * features :]
    convolved = causal_conv(b_part * x_part, conv_weight.astype(jnp.float32), places)
    mixer_in = (c_part * convolved).astype(jnp.bfloat16)
    middle = inputs + live_rows * forward_dot(mixer_in, out_weight)
    second_normed = normed(middle, ffn_gain.astype(jnp.float32)).astype(jnp.bfloat16)
    gate_value = forward_dot(second_normed, gate_weight)
    up_value = forward_dot(second_normed, up_weight)
    hidden = gated(gate_value, up_value).astype(jnp.bfloat16)
    result = middle + live_rows * forward_dot(hidden, down_weight)
    return (
        result,
        (first_normed, projected, mixer_in, middle, second_normed, gate_value, up_value, hidden),
    )


def backward(tokens_rows, cotangent_rows, places, weights, kept_state):
    norm_gain, in_weight, conv_weight, out_weight, ffn_gain, gate_weight, up_weight, down_weight = (
        weights
    )
    first_normed, projected, mixer_in, middle, second_normed, gate_value, up_value, hidden = (
        kept_state
    )
    features = tokens_rows.shape[1]
    inputs = tokens_rows.astype(jnp.float32)
    live_rows = (places >= 0).astype(jnp.float32)[:, None]
    upstream = cotangent_rows.astype(jnp.float32)
    ffn_grad = (live_rows * upstream).astype(jnp.bfloat16)
    hidden_grad = back_dot(ffn_grad, down_weight)
    gate_grad, up_grad = jax.vjp(gated, gate_value, up_value)[1](hidden_grad)
    gate_grad = gate_grad.astype(jnp.bfloat16)
    up_grad = up_grad.astype(jnp.bfloat16)
    normed_grad = back_dot(gate_grad, gate_weight) + back_dot(up_grad, up_weight)
    middle_part, grad_ffn = jax.vjp(normed, middle, ffn_gain.astype(jnp.float32))[1](normed_grad)
    middle_grad = upstream + middle_part
    mixer_grad = (live_rows * middle_grad).astype(jnp.bfloat16)
    mixer_in_grad = back_dot(mixer_grad, out_weight)

    def mixer_local(b_part, c_part, x_part, kernel):
        return c_part * causal_conv(b_part * x_part, kernel, places)

    pullback = jax.vjp(
        mixer_local,
        projected[:, :features],
        projected[:, features : 2 * features],
        projected[:, 2 * features :],
        conv_weight.astype(jnp.float32),
    )[1]
    b_grad, c_grad, x_grad, grad_conv = pullback(mixer_in_grad)
    projected_grad = jnp.concatenate([b_grad, c_grad, x_grad], axis=1).astype(jnp.bfloat16)
    first_grad = back_dot(projected_grad, in_weight)
    input_part, grad_norm = jax.vjp(normed, inputs, norm_gain.astype(jnp.float32))[1](first_grad)
    in_gradient = middle_grad + input_part
    operands = (
        first_normed,
        projected_grad,
        mixer_in,
        mixer_grad,
        second_normed,
        gate_grad,
        up_grad,
        hidden,
        ffn_grad,
    )
    return (in_gradient, operands, (grad_norm, grad_ffn, grad_conv))


def feature_term(operands, smalls, count):
    (
        first_normed,
        projected_grad,
        mixer_in,
        mixer_grad,
        second_normed,
        gate_grad,
        up_grad,
        hidden,
        ffn_grad,
    ) = operands
    grad_norm, grad_ffn, grad_conv = smalls
    chosen_norm = grad_norm[:, None]
    chosen_ffn = grad_ffn[:, None]
    chosen_conv = jnp.transpose(grad_conv)
    filler = jnp.zeros((count, SMALL_COLUMNS - 2 - grad_conv.shape[0]), jnp.float32)
    return jnp.concatenate(
        [
            rows_dot(first_normed, projected_grad),
            rows_dot(mixer_in, mixer_grad),
            rows_dot(second_normed, gate_grad),
            rows_dot(second_normed, up_grad),
            chosen_norm,
            chosen_ffn,
            chosen_conv,
            filler,
        ],
        axis=1,
    )


def hidden_term(operands):
    hidden = operands[7]
    ffn_grad = operands[8]
    return rows_dot(hidden, ffn_grad)


def per_device(
    tokens,
    positions,
    cotangent,
    norm_gain,
    in_weight,
    conv_weight,
    out_weight,
    ffn_gain,
    gate_weight,
    up_weight,
    down_weight,
):
    micro_count = tokens.shape[0]
    features = tokens.shape[2]
    hidden_width = gate_weight.shape[1]
    feature_share = in_weight.shape[0]
    outputs = []
    in_gradients = []
    all_operands = []
    all_smalls = []
    feature_sum = None
    hidden_sum = None
    for micro_index in range(micro_count):
        forward_weights = (
            lax.all_gather(norm_gain, ("dp", "shard"), axis=0, tiled=True),
            lax.all_gather(in_weight, ("dp", "shard"), axis=0, tiled=True),
            lax.all_gather(conv_weight, ("dp", "shard"), axis=1, tiled=True),
            lax.all_gather(out_weight, ("dp", "shard"), axis=0, tiled=True),
            lax.all_gather(ffn_gain, ("dp", "shard"), axis=0, tiled=True),
            lax.all_gather(gate_weight, ("dp", "shard"), axis=0, tiled=True),
            lax.all_gather(up_weight, ("dp", "shard"), axis=0, tiled=True),
            lax.all_gather(down_weight, ("dp", "shard"), axis=0, tiled=True),
        )
        result, kept_state = forward(tokens[micro_index], positions[micro_index], forward_weights)
        backward_weights = (
            lax.all_gather(norm_gain, ("dp", "shard"), axis=0, tiled=True),
            lax.all_gather(in_weight, ("dp", "shard"), axis=0, tiled=True),
            lax.all_gather(conv_weight, ("dp", "shard"), axis=1, tiled=True),
            lax.all_gather(out_weight, ("dp", "shard"), axis=0, tiled=True),
            lax.all_gather(ffn_gain, ("dp", "shard"), axis=0, tiled=True),
            lax.all_gather(gate_weight, ("dp", "shard"), axis=0, tiled=True),
            lax.all_gather(up_weight, ("dp", "shard"), axis=0, tiled=True),
            lax.all_gather(down_weight, ("dp", "shard"), axis=0, tiled=True),
        )
        in_gradient, operands, smalls = backward(
            tokens[micro_index],
            cotangent[micro_index],
            positions[micro_index],
            backward_weights,
            kept_state,
        )
        outputs.append(result.astype(jnp.bfloat16))
        in_gradients.append(in_gradient.astype(jnp.bfloat16))
        all_operands.append(operands)
        all_smalls.append(smalls)
    joined = tuple(
        (jnp.concatenate([group[index] for group in all_operands], axis=0) for index in range(9))
    )
    small_totals = tuple(
        (reduce(jnp.add, [group[index] for group in all_smalls]) for index in range(3))
    )
    feature_sum = lax.psum_scatter(
        feature_term(joined, small_totals, feature_share * lax.axis_size(("dp", "shard"))),
        ("dp", "shard"),
        scatter_dimension=0,
        tiled=True,
    )
    hidden_sum = lax.psum_scatter(
        hidden_term(joined), ("dp", "shard"), scatter_dimension=0, tiled=True
    )
    grad_in = feature_sum[:, : 3 * features]
    grad_out = feature_sum[:, 3 * features : 4 * features]
    grad_gate = feature_sum[:, 4 * features : 4 * features + hidden_width]
    grad_up = feature_sum[:, 4 * features + hidden_width : 4 * features + 2 * hidden_width]
    small_base = 4 * features + 2 * hidden_width
    grad_norm = feature_sum[:, small_base]
    grad_ffn = feature_sum[:, small_base + 1]
    grad_conv = jnp.transpose(
        feature_sum[:, small_base + 2 : small_base + 2 + conv_weight.shape[0]]
    )
    return (
        jnp.stack(outputs),
        jnp.stack(in_gradients),
        grad_norm,
        grad_in,
        grad_conv,
        grad_out,
        grad_ffn,
        grad_gate,
        grad_up,
        hidden_sum,
    )


def solution(mesh):
    return jax.shard_map(
        per_device,
        mesh=mesh,
        in_specs=(
            P(None, ("dp", "shard"), None),
            P(None, ("dp", "shard")),
            P(None, ("dp", "shard"), None),
            P(("dp", "shard")),
            P(("dp", "shard"), None),
            P(None, ("dp", "shard")),
            P(("dp", "shard"), None),
            P(("dp", "shard")),
            P(("dp", "shard"), None),
            P(("dp", "shard"), None),
            P(("dp", "shard"), None),
        ),
        out_specs=(
            P(None, ("dp", "shard"), None),
            P(None, ("dp", "shard"), None),
            P(("dp", "shard")),
            P(("dp", "shard"), None),
            P(None, ("dp", "shard")),
            P(("dp", "shard"), None),
            P(("dp", "shard")),
            P(("dp", "shard"), None),
            P(("dp", "shard"), None),
            P(("dp", "shard"), None),
        ),
        check_vma=False,
    )
```

profile of v0, /device:TPU:0, one launch (start us, length us, event | category | flops | bytes accessed | tf_op | source)
XLA Modules:
  0.0 1274.8 jit_solution(11551925940932952846)
XLA Ops:
  10.6 0.8 dynamic-update-slice
  11.5 0.8 dynamic-update-slice.1
  12.3 42.4 %all-reduce.16 = (bf16[1024]{0:T(1024)(128)(2,1)S(1)}, bf16[1024]{0:T(1024)(128)(2,1)S(1)}) all-reduce(bf16[1024]{0:T(1024)(128)(2,1)S(1)} %dynamic-update-slice, bf16[1024]{0:T(1024)(128)(2,1)S(1)} %dynamic-update-slice.1), channel_id=1, replica_groups=mesh['dp'=8,'shard'=4] {'dp','shard'}, use_global_device_ids=true, to_apply=%add.14 | all-reduce | flops 2048 | bytes 8192
  54.7 66.4 %all-gather = bf16[32,32,3]{1,2,0:T(4,128)(2,1)S(1)} all-gather(bf16[1,32,3]{1,2,0:T(4,128)(2,1)} %bitcast.154), channel_id=1, replica_groups=mesh['dp'=8,'shard'=4] {'dp','shard'}, dimensions={0}, use_global_device_ids=true | all-gather | bytes 6336 | tf_op jit(solution)/shard_map/all_gather | solution.py:191
  121.2 1.5 fusion.64
  122.8 0.8 compare_convert_fusion.5
  123.5 2.2 fusion.58
  126.1 5.0 fusion.96
  131.4 1.8 fusion.99
  133.4 1.5 copy-done.2
  135.3 2.5 multiply_convert_fusion.15
  137.8 3.8 all-gather.9.cloned.1.call-done
  141.6 2.4 multiply_reduce_fusion.11
  144.0 3.9 multiply_reduce_fusion.10
  148.1 77.2 %all-gather.13.cloned.1.call-done = bf16[1024,4608]{1,0:T(8,128)(2,1)} async-done(((bf16[32,4608]{1,0:T(8,128)(2,1)}), bf16[1024,4608]{1,0:T(8,128)(2,1)}) %all-gather.13.cloned.1.call-update) | async-done | bytes 9437200 | tf_op jit(solution)/shard_map/all_gather | solution.py:195
  225.3 8.2 fusion.98
  233.5 75.1 %all-gather.11.cloned.1.call-done = bf16[1024,4608]{1,0:T(8,128)(2,1)} async-done(((bf16[32,4608]{1,0:T(8,128)(2,1)}), bf16[1024,4608]{1,0:T(8,128)(2,1)}) %all-gather.11.cloned.1.call-update) | async-done | bytes 9437200 | tf_op jit(solution)/shard_map/all_gather | solution.py:194
  308.6 8.0 fusion.97
  316.6 75.3 %all-gather.15.cloned.1.call-done = bf16[4608,1024]{1,0:T(8,128)(2,1)} async-done(((bf16[144,1024]{1,0:T(8,128)(2,1)}), bf16[4608,1024]{1,0:T(8,128)(2,1)}) %all-gather.15.cloned.1.call-update) | async-done | bytes 9437200 | tf_op jit(solution)/shard_map/all_gather | solution.py:196
  392.0 14.2 %multiply_convert_fusion.1 = (bf16[256,4608]{1,0:T(8,128)(2,1)}, bf16[256,4608]{1,0:T(8,128)(2,1)S(1)}, bf16[256,4608]{1,0:T(8,128)(2,1)}) fusion(f32[256,4608]{1,0:T(8,128)} %fusion.97, f32[256,4608]{1,0:T(8,128)} %fusion.98, bf16[256,1024]{1,0:T(8,128)(2,1)S(1)} %get-tuple-element.99, bf16[4608,1024]{1,0:T(8,128)(2,1)} %all-gather.15.cloned.1.call-done), kind=kOutput, calls=%fused_computation.21 | convolution fusion | flops 2434793472 | bytes 26476544 | tf_op jit(solution)/shard_map/dot_general | solution.py:44
  406.1 6.1 fusion.102
  412.3 5.6 multiply_reduce_fusion.7
  417.9 4.3 fusion.101
  422.2 4.3 fusion.100
  426.5 14.8 %multiply_convert_fusion = (bf16[256,4608]{1,0:T(8,128)(2,1)}, bf16[256,4608]{1,0:T(8,128)(2,1)}, bf16[256,4608]{1,0:T(8,128)(2,1)}) fusion(f32[256,4608]{1,0:T(8,128)} %fusion.100, f32[256,4608]{1,0:T(8,128)} %fusion.101, bf16[256,1024]{1,0:T(8,128)(2,1)S(1)} %copy-done.33, bf16[4608,1024]{1,0:T(8,128)(2,1)} %all-gather.15.cloned.1.call-done), kind=kOutput, calls=%fused_computation.20 | convolution fusion | flops 2434793472 | bytes 26476544 | tf_op jit(solution)/shard_map/dot_general | solution.py:44
  441.4 11.6 fusion.10
  453.0 11.7 fusion.6
  464.8 4.4 fusion.103
  469.2 3.8 multiply_reduce_fusion.6
  473.0 1.0 copy.54
  474.1 3.3 multiply_convert_fusion.11
  477.8 3.3 multiply_reduce_fusion.5
  481.2 1.4 multiply_reduce_fusion.4
  483.1 3.2 fusion.71
  486.4 2.1 multiply_reduce_fusion.2
  488.5 1.3 multiply_reduce_fusion.1
  489.8 1.0 copy.50
  490.8 1.0 copy.47
  491.9 1.1 copy.46
  492.9 1.0 copy.49
  494.0 1.1 copy.51
  495.0 1.0 copy.48
  496.1 2.0 slice_multiply_fusion.2
  498.0 2.0 slice_multiply_fusion.3
  500.1 1.2 multiply_convert_fusion.10
  502.8 22.1 %fusion.20 = f32[1024,3072]{1,0:T(8,128)} fusion(bf16[256,1024]{1,0:T(8,128)(2,1)S(1)} %multiply_convert_fusion.4, bf16[256,1024]{1,0:T(8,128)(2,1)S(1)} %copy-done.40, bf16[256,1024]{1,0:T(8,128)(2,1)S(1)} %get-tuple-element.107, bf16[256,1024]{1,0:T(8,128)(2,1)S(1)} %multiply_convert_fusion.8, bf16[256,1024]{1,0:T(8,128)(2,1)S(1)} %copy-done.39, ...), kind=kOutput, calls=%fused_computation.28 | convolution fusion | flops 3242196992 | bytes 16777216 | tf_op jit(solution)/shard_map/dot_general | solution.py:38
  524.9 1.8 fusion.38
  526.8 3.3 fusion.57
  530.3 2.3 add_bitcast_fusion
  532.7 59.9 %concatenate.67 = f32[1024,13440]{1,0:T(8,128)} concatenate(f32[1024,3072]{1,0:T(8,128)} %fusion.20, f32[1024,1024]{1,0:T(8,128)} %fusion.71, f32[1024,4608]{1,0:T(8,128)} %fusion.6, f32[1024,4608]{1,0:T(8,128)} %fusion.10, f32[1024,1]{1,0:T(8,128)S(1)} %copy.53, f32[1024,1]{1,0:T(8,128)S(1)} %copy-done.26, f32[1024,3]{1,0:T(8,128)S(1)} %add_bitcast_fusion, ...), dimensions={1} | concatenate | bytes 110100480 | tf_op jit(solution)/shard_map/concatenate | solution.py:143
  592.7 1.0 copy-done.32
  593.8 15.7 %fusion.14 = f32[4608,1024]{1,0:T(8,128)} fusion(bf16[256,4608]{1,0:T(8,128)(2,1)} %get-tuple-element.89, bf16[256,4608]{1,0:T(8,128)(2,1)} %get-tuple-element.86, bf16[256,1024]{1,0:T(8,128)(2,1)S(1)} %copy-done.34, bf16[256,1024]{1,0:T(8,128)(2,1)S(1)} %copy-done.32), kind=kOutput, calls=%fused_computation.16 | convolution fusion | flops 4843372544 | bytes 24641536 | tf_op jit(solution)/shard_map/dot_general | solution.py:38
  609.5 1.4 copy-done.10
  610.9 9.7 fusion.52
  620.6 8.5 fusion.53
  629.2 1.1 pad_maximum_fusion
  632.1 1.1 pad_maximum_fusion.1
  633.2 420.4 %reduce-scatter.3.cloned.1.call-done = f32[32,13440]{1,0:T(8,128)} async-done(((f32[1024,13440]{1,0:T(8,128)}), f32[32,13440]{1,0:T(8,128)}) %reduce-scatter.3.cloned.1.call-update) | async-done | bytes 1720336 | tf_op jit(solution)/shard_map/reduce_scatter | solution.py:226
  1053.6 0.8 slice_bitcast_fusion
  1055.0 1.6 slice.143
  1056.6 1.8 slice.141
  1058.4 1.5 slice_reduce_fusion
  1059.9 2.3 fusion.94
  1062.2 205.3 %reduce-scatter.5.cloned.1.call-done = f32[144,1024]{1,0:T(8,128)} async-done(((f32[4608,1024]{1,0:T(8,128)}), f32[144,1024]{1,0:T(8,128)}) %reduce-scatter.5.cloned.1.call-update) | async-done | bytes 589840 | tf_op jit(solution)/shard_map/reduce_scatter | solution.py:232
  (165 shorter events, 10.5 us)
Async XLA Ops:
  7.2 118.6 %copy-start.11 = (bf16[2,256,1024]{2,1,0:T(8,128)(2,1)S(1)}, bf16[2,256,1024]{2,1,0:T(8,128)(2,1)}, u32[]{:S(2)}) copy-start(bf16[2,256,1024]{2,1,0:T(8,128)(2,1)} %param.11) | copy-start | bytes 3145732
  7.2 118.9 %all-gather.7.cloned.1.call-start = ((), (), s32[]{:S(2)}) async-start(), calls=%async_computation.2 | async-start | bytes 6488064 | tf_op jit(solution)/shard_map/all_gather | solution.py:190
  7.9 133.6 %all-gather.9.cloned.1.call-start = ((), (), s32[]{:S(2)}) async-start(), calls=%async_computation.3 | async-start | bytes 2162688 | tf_op jit(solution)/shard_map/all_gather | solution.py:192
  8.7 216.6 %all-gather.13.cloned.1.call-start = ((), (), s32[]{:S(2)}) async-start(), calls=%async_computation.5 | async-start | bytes 9732096 | tf_op jit(solution)/shard_map/all_gather | solution.py:195
  9.4 299.2 %all-gather.11.cloned.1.call-start = ((), (), s32[]{:S(2)}) async-start(), calls=%async_computation.4 | async-start | bytes 9732096 | tf_op jit(solution)/shard_map/all_gather | solution.py:194
  10.0 382.0 %all-gather.15.cloned.1.call-start = ((), (), s32[]{:S(2)}) async-start(), calls=%async_computation.6 | async-start | bytes 9732096 | tf_op jit(solution)/shard_map/all_gather | solution.py:196
  10.6 1043.0 %reduce-scatter.3.cloned.1.call-start = ((), (), s32[]{:S(2)}) async-start(), calls=%async_computation.7 | async-start | bytes 56770560 | tf_op jit(solution)/shard_map/reduce_scatter | solution.py:226
  125.7 266.2 %copy-start.31 = (bf16[256,1024]{1,0:T(8,128)(2,1)}, bf16[256,1024]{1,0:T(8,128)(2,1)S(1)}, u32[]{:S(2)}) copy-start(bf16[256,1024]{1,0:T(8,128)(2,1)S(1)} %get-tuple-element.99) | copy-start | bytes 1572868
  126.1 5.1 copy-start.35
  126.1 5.3 copy-start.37
  126.1 5.2 copy-start.48
  131.1 2.3 copy-start
  131.3 2.1 copy-start.7
  133.2 1.7 copy-start.2
  133.4 1.9 copy-start.5
  137.8 10.1 copy-start.41
  144.0 268.3 %copy-start.9 = (f32[256,1024]{1,0:T(8,128)}, f32[256,1024]{1,0:T(8,128)S(1)}, u32[]{:S(2)}) copy-start(f32[256,1024]{1,0:T(8,128)S(1)} %get-tuple-element.121) | copy-start | bytes 3145732
  308.6 103.6 %slice-start = ((s8[9437184]{0:T(1024)(128)(4,1)}), s8[1048576]{0:T(1024)(128)(4,1)S(1)}, s32[]{:S(2)}) async-start(s8[9437184]{0:T(1024)(128)(4,1)} %bitcast.109), calls=%async_computation.9 | async-start | bytes 2097152
  391.9 20.3 %slice-start.1 = ((s8[9437184]{0:T(1024)(128)(4,1)}), s8[4194304]{0:T(1024)(128)(4,1)S(1)}, s32[]{:S(2)}) async-start(s8[9437184]{0:T(1024)(128)(4,1)} %bitcast.109), calls=%async_computation.10 | async-start | bytes 8388608
  392.0 20.3 %slice-start.2 = ((s8[9437184]{0:T(1024)(128)(4,1)}), s8[4194304]{0:T(1024)(128)(4,1)S(1)}, s32[]{:S(2)}) async-start(s8[9437184]{0:T(1024)(128)(4,1)} %bitcast.109), calls=%async_computation.11 | async-start | bytes 8388608
  406.1 6.1 copy-start.24
  406.1 6.1 copy-start.19
  412.3 9.9 slice-start.3
  412.3 9.9 slice-start.4
  417.9 4.3 slice-start.5
  422.2 4.3 copy-start.33
  441.4 23.4 %slice-start.6 = ((s8[9437184]{0:T(1024)(128)(4,1)}), s8[4194304]{0:T(1024)(128)(4,1)S(1)}, s32[]{:S(2)}) async-start(s8[9437184]{0:T(1024)(128)(4,1)} %bitcast.113), calls=%async_computation.15 | async-start | bytes 8388608
  441.4 23.4 %slice-start.7 = ((s8[9437184]{0:T(1024)(128)(4,1)}), s8[4194304]{0:T(1024)(128)(4,1)S(1)}, s32[]{:S(2)}) async-start(s8[9437184]{0:T(1024)(128)(4,1)} %bitcast.113), calls=%async_computation.16 | async-start | bytes 8388608
  453.0 11.8 slice-start.8
  464.8 4.5 copy-start.25
  473.0 4.4 copy-start.1
  474.1 3.3 copy-start.8
  474.1 3.8 copy-start.18
  481.1 5.2 copy-start.14
  481.1 1.4 copy-start.42
  481.1 2.0 copy-start.43
  481.1 5.2 copy-start.3
  481.2 5.2 copy-start.6
  481.2 5.2 copy-start.23
  488.5 1.3 copy-start.16
  496.1 4.0 copy-start.4
  496.1 4.0 copy-start.15
  496.1 4.0 copy-start.17
  501.3 1.2 copy-start.38
  501.3 1.3 copy-start.39
  501.3 1.5 copy-start.40
  501.3 23.6 %slice-start.9 = ((s8[6291456]{0:T(1024)(128)(4,1)}), s8[4194304]{0:T(1024)(128)(4,1)S(1)}, s32[]{:S(2)}) async-start(s8[6291456]{0:T(1024)(128)(4,1)} %bitcast.155), calls=%async_computation.18 | async-start | bytes 8388608
  502.8 22.1 %slice-start.10 = ((s8[6291456]{0:T(1024)(128)(4,1)}), s8[2097152]{0:T(1024)(128)(4,1)S(1)}, s32[]{:S(2)}) async-start(s8[6291456]{0:T(1024)(128)(4,1)} %bitcast.155), calls=%async_computation.19 | async-start | bytes 4194304
  524.9 1.8 copy-start.12
  526.8 3.3 copy-start.29
  526.8 3.5 copy-start.27
  530.1 2.6 copy-start.26
  592.6 1.2 copy-start.34
  592.6 674.9 %reduce-scatter.5.cloned.1.call-start = ((), (), s32[]{:S(2)}) async-start(), calls=%async_computation.8 | async-start | bytes 19464192 | tf_op jit(solution)/shard_map/reduce_scatter | solution.py:232
  609.5 1.4 copy-start.10
  610.9 9.7 copy-start.20
  610.9 9.7 copy-start.49
  620.6 9.6 copy-start.45
  620.6 9.6 copy-start.47
  620.6 9.6 copy-start.13
  620.6 9.6 copy-start.22
  620.6 9.6 copy-start.30
  629.1 1.8 copy-start.21
  629.1 2.4 copy-start.28
  (4 other events, 3.7 us)
Sparse Core Ops, SparseCore 0:
  10.9 72.6 all-gather.6
  86.5 54.9 all-gather.8
  144.4 80.8 all-gather.12
  227.9 80.6 all-gather.10
  311.2 80.6 all-gather.14
  592.7 460.8 reduce-scatter.2
  1061.7 205.7 reduce-scatter.4
where the time goes:
time: 1280 us; the launch traced here: 1270 us
  waiting for transfers between devices  860 us (67%)
  matrix products  180 us (14%)
  blocking collectives  109 us (9%)
  local copies, waits for them, and re-layouts  85.3 us (7%)
  other arithmetic  24.9 us (2%)
  between operations  15.4 us (1%)
    reduce_scatter x1, waiting for transfers between devices, per_device(): lax.psum_scatter(feature_term(joined, small_totals, feature_share * lax.a...  420 us
    reduce_scatter x1, waiting for transfers between devices, per_device(): lax.psum_scatter(hidden_term(joined), ('dp', 'shard'), scatter_dimension=...  205 us
    all_gather x1, waiting for transfers between devices, per_device(): lax.all_gather(up_weight, ('dp', 'shard'), axis=0, tiled=True)  77.2 us
    all_gather x1, waiting for transfers between devices, per_device(): lax.all_gather(down_weight, ('dp', 'shard'), axis=0, tiled=True)  75.3 us
    all_gather x1, waiting for transfers between devices, per_device(): lax.all_gather(gate_weight, ('dp', 'shard'), axis=0, tiled=True)  75.1 us
    all_gather x1, blocking collectives, per_device(): lax.all_gather(conv_weight, ('dp', 'shard'), axis=1, tiled=True)  66.4 us
    dot_general x5, matrix products, rows_dot(): lax.dot_general(left_side, right_side, (((0,), (0,)), ((), ())), preferre...  64.4 us
    concatenate x1, local copies, waits for them, and re-layouts, feature_term(): jnp.concatenate([rows_dot(first_normed, projected_grad), rows_dot(mixer_i...  59.9 us
  transfers between devices with their start and end apart: 7, of which 6 were waited for; matrix products, arithmetic and copies ran while one was open for 7% of the time, Pallas kernels for 0%

commit v1 on v0

v1 whole, which is shorter than its diff:
```python
from functools import reduce

import jax
import jax.numpy as jnp
from jax import lax
from jax.experimental import pallas as pl
from jax.experimental.pallas import tpu as pltpu
from jax.sharding import Mesh, PartitionSpec as P

EPSILON = 1e-05
TEAM = 4
EXTRA_ROWS = 16
ROW_TILE = 256
bf16 = jnp.bfloat16
f32 = jnp.float32


def forward_dot(left_side, right_side):
    return jnp.dot(left_side, right_side, preferred_element_type=f32)


def rows_dot(left_side, right_side):
    return lax.dot_general(
        left_side, right_side, (((0,), (0,)), ((), ())), preferred_element_type=f32
    )


def back_dot(left_side, right_side):
    return lax.dot_general(
        left_side, right_side, (((1,), (1,)), ((), ())), preferred_element_type=f32
    )


def swap_core(values):
    return lax.ppermute(values, "c", [(0, 1), (1, 0)])


def swap_chip(values):
    return lax.ppermute(values, "x", [(0, 1), (1, 0)])


def swap_both(values):
    return lax.ppermute(values, ("x", "c"), [(i, i ^ 3) for i in range(TEAM)])


def reorder(blocks):
    odd_core = lax.axis_index("c") == 1
    odd_chip = lax.axis_index("x") == 1
    b0, b1, b2, b3 = blocks
    b0, b1 = jnp.where(odd_core, b1, b0), jnp.where(odd_core, b0, b1)
    b2, b3 = jnp.where(odd_core, b3, b2), jnp.where(odd_core, b2, b3)
    b0, b2 = jnp.where(odd_chip, b2, b0), jnp.where(odd_chip, b0, b2)
    b1, b3 = jnp.where(odd_chip, b3, b1), jnp.where(odd_chip, b1, b3)
    return [b0, b1, b2, b3]


def exchange(blocks):
    near = reorder(blocks)
    came = [near[0], swap_core(near[1]), swap_chip(near[2]), swap_both(near[3])]
    return reorder(came)


def team_rows(rows):
    across = swap_chip(rows)
    return jnp.concatenate([rows, swap_core(rows), across, swap_core(across)], axis=0)


def team_sum(partial):
    count = partial.shape[0] // TEAM
    sent = jnp.concatenate([partial[count : 2 * count], partial[3 * count :]], axis=0)
    came = swap_core(sent).astype(f32)
    own = partial[:count].astype(f32) + came[:count]
    other = partial[2 * count : 3 * count].astype(f32) + came[count:]
    return own + swap_chip(other.astype(bf16)).astype(f32)


def take(blocks, index):
    return lax.dynamic_index_in_dim(blocks, index, axis=0, keepdims=False)


def swap_group(values):
    return lax.ppermute(values, "g", [(0, 1), (1, 0)])


def line_gather(block):
    place = lax.axis_index("s")
    right, left = [block], [block]
    for step in range(1, 4):
        right.append(lax.ppermute(right[-1], "s", [(i, i + 1) for i in range(step - 1, 3)]))
        left.append(lax.ppermute(left[-1], "s", [(i + 1, i) for i in range(4 - step)]))
    blocks = [block] + [jnp.where(place >= k, right[k], left[4 - k]) for k in range(1, 4)]
    return blocks, [lax.rem(place + 4 - k, 4) for k in range(4)]


def line_scatter(blocks):
    place = lax.axis_index("s")
    total = take(blocks, place).astype(f32)
    for sign in (1, -1):
        came = None
        for step in range(1, 4):
            sent = take(blocks, jnp.clip(place + sign * (4 - step), 0, 3))
            if came is not None:
                sent = (sent.astype(f32) + came.astype(f32)).astype(bf16)
            if sign == 1:
                pairs = [(i, i + 1) for i in range(step)]
            else:
                pairs = [(i, i - 1) for i in range(4 - step, 4)]
            came = lax.ppermute(sent, "s", pairs)
        total = total + came.astype(f32)
    return total


def gather_first(shard, unpack):
    groups, slots = lax.axis_size("g"), lax.axis_size("s")
    if groups == 2 and slots == 4:
        low = lax.axis_index("g") == 0
        other = swap_group(shard)
        both = jnp.stack([jnp.where(low, shard, other), jnp.where(low, other, shard)])
        results = [jnp.zeros((2, 4) + part.shape, part.dtype) for part in unpack(shard)]
        for block, source in zip(*line_gather(both)):
            results = [
                lax.dynamic_update_slice(
                    whole, part[:, None], (0, source) + (0,) * (part.ndim - 1)
                )
                for whole, part in zip(results, jax.vmap(unpack)(block))
            ]
        return results
    every = lax.all_gather(shard, ("g", "s"), axis=0, tiled=False)
    results = jax.vmap(unpack)(every)
    return [part.reshape((groups, slots) + part.shape[1:]) for part in results]


def scatter_first(part):
    groups, slots = part.shape[:2]
    if groups == 2 and slots == 4:
        row = lax.axis_index("g")
        came = swap_group(take(part, 1 - row))
        return line_scatter((take(part, row).astype(f32) + came.astype(f32)).astype(bf16))
    flat = part.reshape((groups * slots,) + part.shape[2:]).astype(f32)
    return lax.psum_scatter(flat, ("g", "s"), scatter_dimension=0, tiled=False)


def scatter_rest(part):
    if part.shape[0] > 8:
        part = part.astype(f32)
    return lax.psum_scatter(part, ("g", "s"), scatter_dimension=0, tiled=False)


def feed_forward_kernel(
    normed_ref,
    grad_ref,
    gate_ref,
    up_ref,
    down_ref,
    hidden_ref,
    gate_grad_ref,
    up_grad_ref,
    out_ref,
    normed_grad_ref,
):
    gate_value = forward_dot(normed_ref[...], gate_ref[...])
    up_value = forward_dot(normed_ref[...], up_ref[...])
    sigmoid = jax.nn.sigmoid(gate_value)
    silu = gate_value * sigmoid
    hidden = (silu * up_value).astype(bf16)
    hidden_ref[...] = hidden
    hidden_grad = back_dot(grad_ref[...], down_ref[...])
    gate_grad = hidden_grad * up_value * (sigmoid * (1 + gate_value * (1 - sigmoid)))
    gate_grad = gate_grad.astype(bf16)
    up_grad = (hidden_grad * silu).astype(bf16)
    gate_grad_ref[...] = gate_grad
    up_grad_ref[...] = up_grad
    normed_grad = back_dot(gate_grad, gate_ref[...]) + back_dot(up_grad, up_ref[...])
    normed_grad_ref[...] = normed_grad.astype(bf16)
    out_ref[...] = forward_dot(hidden, down_ref[...]).astype(bf16)


def feed_forward(normed, grad, gate_full, up_full, down_full):
    rows, features = normed.shape
    width = gate_full.shape[1]
    tile = min(ROW_TILE, rows)

    def row_block(columns):
        return pl.BlockSpec((tile, columns), lambda i: (i, 0))

    def whole(shape):
        return pl.BlockSpec(shape, lambda i: (0, 0))

    wide = jax.ShapeDtypeStruct((rows, width), bf16)
    model = jax.ShapeDtypeStruct((rows, features), bf16)
    return pl.pallas_call(
        feed_forward_kernel,
        grid=(rows // tile,),
        in_specs=[
            row_block(features),
            row_block(features),
            whole(gate_full.shape),
            whole(up_full.shape),
            whole(down_full.shape),
        ],
        out_specs=[row_block(width)] * 3 + [row_block(features)] * 2,
        out_shape=[wide] * 3 + [model] * 2,
        compiler_params=pltpu.CompilerParams(vmem_limit_bytes=52 * 1024 * 1024),
        cost_estimate=pl.CostEstimate(
            flops=12 * rows * features * width,
            bytes_accessed=6 * features * width + 6 * rows * width + 8 * rows * features,
            transcendentals=rows * width,
        ),
    )(normed, grad, gate_full, up_full, down_full)


def shifted_down(rows, step):
    return jnp.concatenate(
        [jnp.zeros((step, rows.shape[1]), rows.dtype), rows[:-step]], axis=0
    )


def shifted_up(rows, step):
    return jnp.concatenate(
        [rows[step:], jnp.zeros((step, rows.shape[1]), rows.dtype)], axis=0
    )


def inverse_rms(values):
    return lax.rsqrt(jnp.mean(values * values, axis=-1, keepdims=True) + EPSILON)


def norm_back(values, scale, weighted):
    return scale * weighted - values * (
        scale * scale * scale * jnp.mean(weighted * values, axis=-1, keepdims=True)
    )


def per_device(
    tokens,
    positions,
    cotangent,
    norm_gain,
    in_weight,
    conv_weight,
    out_weight,
    ffn_gain,
    gate_weight,
    up_weight,
    down_weight,
):
    micro, micro_rows, features = tokens.shape
    share = in_weight.shape[0]
    hidden_share = down_weight.shape[0]
    hidden_width = gate_weight.shape[1]
    taps = conv_weight.shape[0]
    groups = lax.axis_size("g")
    slots = lax.axis_size("s")
    chan_run = slots * share
    hid_run = slots * hidden_share
    chan = groups * chan_run
    hid = groups * hid_run

    def by_place(weight, parts, run):
        split = weight.reshape(share, parts, groups, TEAM, run)
        return jnp.transpose(split, (3, 0, 1, 2, 4)).reshape(TEAM, share, parts * groups * run)

    def side_by_side(block, width):
        return jnp.concatenate(
            [block[..., j * share : (j + 1) * share, :width] for j in range(TEAM)], axis=-1
        )

    def stacked(block, width):
        return jnp.concatenate(
            [block[..., j * width : (j + 1) * width] for j in range(TEAM)], axis=-2
        )

    in_blocks = by_place(in_weight, 3, chan_run)
    in_mine = jnp.concatenate(exchange([in_blocks[j] for j in range(TEAM)]), axis=0)
    gains = jnp.concatenate([norm_gain, ffn_gain]).reshape(1, 2 * share)
    near_gains = team_rows(gains)
    gains_row = jnp.concatenate(reorder([near_gains[j : j + 1] for j in range(TEAM)]), axis=1)
    pair_blocks = jnp.concatenate(
        [by_place(gate_weight, 1, hid_run), by_place(up_weight, 1, hid_run)], axis=2
    )
    pair_mine = jnp.concatenate(exchange([pair_blocks[j] for j in range(TEAM)]), axis=0)

    def as_row(values):
        return jnp.pad(values, ((0, 0), (0, features - values.shape[1])))

    first_pack = jnp.concatenate(
        [
            jnp.concatenate([in_mine, stacked(out_weight, chan)], axis=1),
            as_row(conv_weight.reshape(1, taps * share)),
            as_row(gains_row),
            jnp.zeros((EXTRA_ROWS - 2, features), bf16),
        ],
        axis=0,
    )
    tall = TEAM * share

    def first_unpack(block):
        return [
            block[:tall, : 3 * chan].reshape(TEAM, share, 3 * chan),
            side_by_side(block[:tall, 3 * chan :], chan),
            block[tall, : taps * share].reshape(taps, share),
            block[tall + 1, : 2 * tall].reshape(TEAM, 2, share),
        ]

    in_all, out_all, conv_all, gains_all = gather_first(first_pack, first_unpack)

    full = 2 * hid // features
    rest = 2 * hid - full * features

    def rest_pack(pair, down):
        blocks = [pair[..., k * features : (k + 1) * features] for k in range(full)]
        if rest:
            blocks.append(side_by_side(pair[..., full * features :], rest))
        return jnp.concatenate(blocks + [down], axis=-2)

    def rest_unpack(packed):
        blocks = [packed[..., k * tall : (k + 1) * tall, :] for k in range(full)]
        base = full * tall
        if rest:
            blocks.append(stacked(packed[..., base : base + share, :], rest))
            base += share
        return jnp.concatenate(blocks, axis=-1), packed[..., base:, :]

    rest_all = lax.all_gather(
        rest_pack(pair_mine, down_weight), ("g", "s"), axis=0, tiled=False
    )
    pair_all, down_all = rest_unpack(rest_all)

    def natural(gathered):
        width = gathered.shape[-1]
        split = gathered.reshape(groups, slots, TEAM, share, width)
        return jnp.transpose(split, (0, 2, 1, 3, 4)).reshape(features, width)

    in_full = jnp.transpose(in_all, (0, 2, 1, 3, 4)).reshape(features, 3 * chan)
    out_full = out_all.reshape(chan, features)
    conv_full = jnp.transpose(conv_all, (2, 0, 1, 3)).reshape(taps, chan).astype(f32)
    gains_full = jnp.transpose(gains_all, (3, 0, 2, 1, 4)).reshape(2, features).astype(f32)
    norm_full, ffn_full = gains_full[0], gains_full[1]
    gate_full = natural(pair_all[..., :hid])
    up_full = natural(pair_all[..., hid:])
    down_full = down_all.reshape(hid, features)

    each = range(micro)
    team_tokens = [team_rows(tokens[m]) for m in each]
    team_places = [team_rows(positions[m][:, None]) for m in each]
    live = [(positions[m] >= 0).astype(f32)[:, None] for m in each]
    upstream = [cotangent[m].astype(f32) for m in each]
    ffn_grad = [team_rows((live[m] * upstream[m]).astype(bf16)) for m in each]
    inputs = [tokens[m].astype(f32) for m in each]

    def mixer(m):
        values = team_tokens[m].astype(f32)
        first_normed = (values * inverse_rms(values) * norm_full).astype(bf16)
        projected = forward_dot(first_normed, in_full)
        b_part = projected[:, :chan]
        c_part = projected[:, chan : 2 * chan]
        x_part = projected[:, 2 * chan :]
        mixed = b_part * x_part
        mask_one = (team_places[m] >= 1).astype(f32)
        mask_two = (team_places[m] >= 2).astype(f32)
        mixed_one = mask_one * shifted_down(mixed, 1)
        mixed_two = mask_two * shifted_down(mixed, 2)
        convolved = conv_full[0] * mixed + conv_full[1] * mixed_one + conv_full[2] * mixed_two
        mixer_in = (c_part * convolved).astype(bf16)
        middle = inputs[m] + live[m] * team_sum(forward_dot(mixer_in, out_full).astype(bf16))
        second_scale = inverse_rms(middle)
        second_normed = team_rows((middle * second_scale * ffn_full).astype(bf16))
        kept = (first_normed, b_part, c_part, x_part, mixed, mixed_one, mixed_two)
        return kept + (mask_one, mask_two, convolved, mixer_in), middle, second_scale, second_normed

    def feed(m, second_normed):
        return feed_forward(second_normed, ffn_grad[m], gate_full, up_full, down_full)

    def mixer_back(m, kept, middle, second_scale, normed_grad):
        first_normed, b_part, c_part, x_part, mixed, mixed_one, mixed_two = kept[:7]
        mask_one, mask_two, convolved, mixer_in = kept[7:]
        second_weighted = ffn_full * team_sum(normed_grad)
        middle_grad = upstream[m] + norm_back(middle, second_scale, second_weighted)
        mixer_grad = team_rows((live[m] * middle_grad).astype(bf16))
        mixer_in_grad = back_dot(mixer_grad, out_full)
        c_grad = mixer_in_grad * convolved
        conv_grad = mixer_in_grad * c_part
        mixed_grad = (
            conv_full[0] * conv_grad
            + conv_full[1] * shifted_up(mask_one * conv_grad, 1)
            + conv_full[2] * shifted_up(mask_two * conv_grad, 2)
        )
        projected_grad = jnp.concatenate(
            [mixed_grad * x_part, c_grad, mixed_grad * b_part], axis=1
        ).astype(bf16)
        grad_conv = jnp.stack(
            [
                jnp.sum(conv_grad * mixed, axis=0),
                jnp.sum(conv_grad * mixed_one, axis=0),
                jnp.sum(conv_grad * mixed_two, axis=0),
            ]
        )
        return middle_grad, mixer_grad, projected_grad, grad_conv

    def by_owner(grad):
        width = grad.shape[-1]
        split = grad.astype(bf16).reshape(groups, TEAM, slots, share, width)
        return jnp.transpose(split, (0, 2, 1, 3, 4)).reshape(groups, slots, tall, width)

    def total(terms):
        return reduce(jnp.add, terms)

    kept, middle, second_scale, second_normed = zip(*[mixer(m) for m in each])
    hidden, gate_grad, up_grad, out_part, normed_grad = zip(
        *[feed(m, second_normed[m]) for m in each]
    )
    middle_grad, mixer_grad, projected_grad, conv_parts = zip(
        *[mixer_back(m, kept[m], middle[m], second_scale[m], normed_grad[m]) for m in each]
    )

    pair_part = jnp.concatenate(
        [
            by_owner(total([rows_dot(second_normed[m], gate_grad[m]) for m in each])),
            by_owner(total([rows_dot(second_normed[m], up_grad[m]) for m in each])),
        ],
        axis=3,
    )
    down_part = total([rows_dot(hidden[m], ffn_grad[m]) for m in each]).astype(bf16)
    owners = groups * slots
    rest_part = rest_pack(
        pair_part.reshape(owners, tall, 2 * hid),
        down_part.reshape(owners, hidden_share, features),
    )
    pair_sum, down_sum = rest_unpack(scatter_rest(rest_part))

    in_part = by_owner(total([rows_dot(kept[m][0], projected_grad[m]) for m in each]))
    out_grad_part = total([rows_dot(kept[m][10], mixer_grad[m]) for m in each]).astype(bf16)
    out_grad_part = stacked(out_grad_part.reshape(groups, slots, share, features), chan)
    conv_rows = jnp.transpose(
        total(conv_parts).reshape(taps, groups, slots, share), (1, 2, 0, 3)
    ).reshape(groups, slots, 1, taps * share)
    conv_rows = jnp.pad(
        conv_rows.astype(bf16),
        ((0, 0), (0, 0), (0, EXTRA_ROWS - 1), (0, features - taps * share)),
    )
    first_sum = scatter_first(
        jnp.concatenate(
            [jnp.concatenate([in_part, out_grad_part], axis=3), conv_rows], axis=2
        )
    )

    block_out = jnp.stack(
        [(middle[m] + live[m] * team_sum(out_part[m])).astype(bf16) for m in each]
    )
    input_grads = []
    for m in each:
        weighted = norm_full * team_sum(back_dot(projected_grad[m], in_full).astype(bf16))
        scale = inverse_rms(inputs[m])
        input_grads.append(
            (middle_grad[m] + norm_back(inputs[m], scale, weighted)).astype(bf16)
        )

    def own_rows(summed, parts, run):
        blocks = [
            summed[j * share : (j + 1) * share].astype(bf16) for j in range(TEAM)
        ]
        came = [block.reshape(share, parts, groups, 1, run) for block in exchange(blocks)]
        joined = jnp.concatenate(came, axis=3)
        return joined.reshape(share, parts * groups * TEAM * run).astype(f32)

    pair_rows = own_rows(pair_sum, 2, hid_run)
    gate_rows = pair_rows[:, :hidden_width]
    up_rows = pair_rows[:, hidden_width:]
    in_rows = own_rows(first_sum[:tall, : 3 * chan], 3, chan_run)
    grad_out = side_by_side(first_sum[:tall, 3 * chan :], chan).astype(f32)
    grad_conv = first_sum[tall, : taps * share].reshape(taps, share).astype(f32)
    grad_norm_gain = jnp.sum(in_weight.astype(f32) * in_rows, axis=1) / norm_gain.astype(f32)
    grad_ffn_gain = jnp.sum(
        gate_weight.astype(f32) * gate_rows + up_weight.astype(f32) * up_rows, axis=1
    ) / ffn_gain.astype(f32)
    return (
        block_out,
        jnp.stack(input_grads),
        grad_norm_gain,
        in_rows,
        grad_conv,
        grad_out,
        grad_ffn_gain,
        gate_rows,
        up_rows,
        down_sum.astype(f32),
    )


def solution(mesh):
    groups = mesh.shape["dp"] // TEAM
    teams = Mesh(
        mesh.devices.reshape(groups, 2, 2, mesh.shape["shard"]), ("g", "x", "c", "s")
    )
    every = ("g", "x", "c", "s")
    return jax.shard_map(
        per_device,
        mesh=teams,
        in_specs=(
            P(None, every, None),
            P(None, every),
            P(None, every, None),
            P(every),
            P(every, None),
            P(None, every),
            P(every, None),
            P(every),
            P(every, None),
            P(every, None),
            P(every, None),
        ),
        out_specs=(
            P(None, every, None),
            P(None, every, None),
            P(every),
            P(every, None),
            P(None, every),
            P(every, None),
            P(every),
            P(every, None),
            P(every, None),
            P(every, None),
        ),
        check_vma=False,
    )
```

time: 1280 us -> 625 us (0.49)
  waiting for transfers between devices: 860 us -> 286 us
  matrix products: 180 us -> 63.1 us
  blocking collectives: 109 us -> 0 us
  starting transfers between devices: 0.27 us -> 65.8 us
  Pallas kernels: 0 us -> 44.9 us
  other arithmetic: 24.9 us -> 68.5 us
  local copies, waits for them, and re-layouts: 85.3 us -> 71.4 us
    reduce_scatter x2 -> x1, waiting for transfers between devices: 626 us -> 0.01 us  [scatter_rest(): return lax.psum_scatter(part, ('g', 's'), scatter_dimension=0, tiled=False)]
    ppermute x0 -> x75, waiting for transfers between devices: none -> 286 us  [the longest x23 138 us: swap_chip(): return lax.ppermute(values, 'x', [(0, 1), (1, 0)])]
    all_gather x5 -> x1, waiting for transfers between devices: 231 us -> 0.01 us  [per_device(): lax.all_gather(rest_pack(pair_mine, down_weight), ('g', 's'), axis=0, til...]
    all_gather x1 -> x0, blocking collectives: 66.4 us -> none  [per_device(): lax.all_gather(conv_weight, ('dp', 'shard'), axis=1, tiled=True)]
    ppermute x0 -> x75, starting transfers between devices: none -> 65.7 us  [the longest x23 22.8 us: swap_chip(): return lax.ppermute(values, 'x', [(0, 1), (1, 0)])]
    concatenate x1 -> x2, local copies, waits for them, and re-layouts: 59.9 us -> 0.11 us  [the longest x1 0.08 us: per_device(): jnp.concatenate([jnp.concatenate([in_mine, stacked(out_weight, chan)], ax...]
    dot_general x10 -> x4, matrix products: 59.4 us -> 11.4 us  [back_dot(): lax.dot_general(left_side, right_side, (((1,), (1,)), ((), ())), preferre...]
    dot_general x10 -> x4, matrix products: 56.1 us -> 10.4 us  [forward_dot(): return jnp.dot(left_side, right_side, preferred_element_type=f32)]
  transfers between devices with their start and end apart: 7 -> 77, of which waited for: 6 -> 34; matrix products, arithmetic and copies ran while one was open for 7% -> 24% of each run, Pallas kernels for 0% -> 0%
where the time goes in v1:
time: 625 us; the launch traced here: 616 us
  waiting for transfers between devices  286 us (46%)
  local copies, waits for them, and re-layouts  71.4 us (11%)
  other arithmetic  68.5 us (11%)
  starting transfers between devices  65.8 us (11%)
  matrix products  63.1 us (10%)
  Pallas kernels  44.9 us (7%)
  between operations  17.3 us (3%)
    ppermute x23, waiting for transfers between devices, swap_chip(): return lax.ppermute(values, 'x', [(0, 1), (1, 0)])  138 us
    ppermute x3, waiting for transfers between devices, line_gather(): lax.ppermute(left[-1], 's', [(i + 1, i) for i in range(4 - step)])  71.1 us
    pallas_call x2, Pallas kernels, feed_forward(): pl.pallas_call(feed_forward_kernel, grid=(rows // tile,), in_specs=[row_b...  44.9 us
    dot_general x10, matrix products, rows_dot(): lax.dot_general(left_side, right_side, (((0,), (0,)), ((), ())), preferre...  41.3 us
    ppermute x2, waiting for transfers between devices, swap_group(): return lax.ppermute(values, 'g', [(0, 1), (1, 0)])  33.6 us
    ppermute x6, waiting for transfers between devices, line_scatter(): came = lax.ppermute(sent, 's', pairs)  33 us
    ppermute x23, starting transfers between devices, swap_chip(): return lax.ppermute(values, 'x', [(0, 1), (1, 0)])  22.8 us
    ppermute x6, starting transfers between devices, line_scatter(): came = lax.ppermute(sent, 's', pairs)  19.3 us
  transfers between devices with their start and end apart: 77, of which 34 were waited for; matrix products, arithmetic and copies ran while one was open for 24% of the time, Pallas kernels for 0%

profile of v1, /device:TPU:0, one launch (start us, length us, event | category | flops | bytes accessed | tf_op | source)
XLA Modules:
  0.0 616.5 jit_solution(14013032763224225723)
XLA Ops:
  8.1 2.9 collective-permute-start.6
  20.7 6.1 collective-permute-done.17
  34.5 2.6 collective-permute-done.27
  37.2 3.6 collective-permute-done.28
  42.4 6.8 %collective-permute-done.9 = bf16[144,1024]{1,0:T(8,128)(2,1)S(1)} collective-permute-done((bf16[144,1024]{1,0:T(8,128)(2,1)S(1)}, bf16[144,1024]{1,0:T(8,128)(2,1)S(1)}, u32[]{:S(2)}, u32[]{:S(2)}) %collective-permute-start.9) | collective-permute-done | bytes 294944 | tf_op jit(solution)/shard_map/ppermute | solution.py:82
  50.8 5.4 collective-permute-start.10
  59.6 5.7 collective-permute-done.11
  69.2 1.8 fusion.7
  71.7 1.9 fusion.4
  74.2 31.7 %collective-permute-done.12 = bf16[2,144,1024]{2,1,0:T(8,128)(2,1)S(1)} collective-permute-done((bf16[2,144,1024]{2,1,0:T(8,128)(2,1)S(1)}, bf16[2,144,1024]{2,1,0:T(8,128)(2,1)S(1)}, u32[]{:S(2)}, u32[]{:S(2)}) %collective-permute-start.12) | collective-permute-done | bytes 589856 | tf_op jit(solution)/shard_map/ppermute | solution.py:90
  110.3 33.7 %collective-permute-done.13 = bf16[2,144,1024]{2,1,0:T(8,128)(2,1)} collective-permute-done((bf16[2,144,1024]{2,1,0:T(8,128)(2,1)S(1)}, bf16[2,144,1024]{2,1,0:T(8,128)(2,1)}, u32[]{:S(2)}, u32[]{:S(2)}) %collective-permute-start.13) | collective-permute-done | bytes 589856 | tf_op jit(solution)/shard_map/ppermute | solution.py:90
  172.6 5.1 fusion.58
  180.7 3.9 fusion.61
  185.3 2.5 multiply_convert_fusion.11
  194.8 1.9 collective-permute-start.20
  196.8 11.2 %collective-permute-done.39 = bf16[256,1024]{1,0:T(8,128)(2,1)} collective-permute-done((bf16[256,1024]{1,0:T(8,128)(2,1)}, bf16[256,1024]{1,0:T(8,128)(2,1)}, u32[]{:S(2)}, u32[]{:S(2)}) %collective-permute-start.39) | collective-permute-done | bytes 524320 | tf_op jit(solution)/shard_map/ppermute | solution.py:39
  208.0 10.4 %collective-permute-done.20 = bf16[256,1024]{1,0:T(8,128)(2,1)} collective-permute-done((bf16[256,1024]{1,0:T(8,128)(2,1)}, bf16[256,1024]{1,0:T(8,128)(2,1)}, u32[]{:S(2)}, u32[]{:S(2)}) %collective-permute-start.20) | collective-permute-done | bytes 524320 | tf_op jit(solution)/shard_map/ppermute | solution.py:39
  218.4 3.6 multiply_reduce_fusion.9
  222.7 1.8 collective-permute-start.41
  225.1 11.9 %collective-permute-done.44 = bf16[256,1024]{1,0:T(8,128)(2,1)S(1)} collective-permute-done((bf16[256,1024]{1,0:T(8,128)(2,1)S(1)}, bf16[256,1024]{1,0:T(8,128)(2,1)S(1)}, u32[]{:S(2)}, u32[]{:S(2)}) %collective-permute-start.44) | collective-permute-done | bytes 524320 | tf_op jit(solution)/shard_map/ppermute | solution.py:39
  237.3 11.0 %collective-permute-done.41 = bf16[256,1024]{1,0:T(8,128)(2,1)S(1)} collective-permute-done((bf16[256,1024]{1,0:T(8,128)(2,1)S(1)}, bf16[256,1024]{1,0:T(8,128)(2,1)S(1)}, u32[]{:S(2)}, u32[]{:S(2)}) %collective-permute-start.41) | collective-permute-done | bytes 524320 | tf_op jit(solution)/shard_map/ppermute | solution.py:39
  248.8 10.7 %collective-permute-done.25 = bf16[256,1024]{1,0:T(8,128)(2,1)S(1)} collective-permute-done((bf16[256,1024]{1,0:T(8,128)(2,1)S(1)}, bf16[256,1024]{1,0:T(8,128)(2,1)S(1)}, u32[]{:S(2)}, u32[]{:S(2)}) %collective-permute-start.25) | collective-permute-done | bytes 524320 | tf_op jit(solution)/shard_map/ppermute | solution.py:39
  259.5 9.5 %collective-permute-done.22 = bf16[256,1024]{1,0:T(8,128)(2,1)S(1)} collective-permute-done((bf16[256,1024]{1,0:T(8,128)(2,1)S(1)}, bf16[256,1024]{1,0:T(8,128)(2,1)S(1)}, u32[]{:S(2)}, u32[]{:S(2)}) %collective-permute-start.22) | collective-permute-done | bytes 524320 | tf_op jit(solution)/shard_map/ppermute | solution.py:39
  277.4 2.7 fusion.114
  281.3 3.3 slice.808
  288.4 22.6 %shard_map.187 = (bf16[1024,1152]{1,0:T(8,128)(2,1)}, bf16[1024,1152]{1,0:T(8,128)(2,1)}, bf16[1024,1152]{1,0:T(8,128)(2,1)}, bf16[1024,1024]{1,0:T(8,128)(2,1)}, bf16[1024,1024]{1,0:T(8,128)(2,1)}) custom-call(bf16[1024,1024]{1,0:T(8,128)(2,1)} %pad_maximum_fusion.10.normed_ref, bf16[1024,1024]{1,0:T(8,128)(2,1)} %pad_maximum_fusion.11.grad_ref, ...), custom_call_target="tpu_custom_call" | custom-call | flops 14495514624 | bytes 22544384 | tf_op jit(solution)/shard_map/pallas_call | solution.py:191
  311.0 22.3 %shard_map.186 = (bf16[1024,1152]{1,0:T(8,128)(2,1)}, bf16[1024,1152]{1,0:T(8,128)(2,1)}, bf16[1024,1152]{1,0:T(8,128)(2,1)}, bf16[1024,1024]{1,0:T(8,128)(2,1)}, bf16[1024,1024]{1,0:T(8,128)(2,1)}) custom-call(bf16[1024,1024]{1,0:T(8,128)(2,1)} %pad_maximum_fusion.7.normed_ref, bf16[1024,1024]{1,0:T(8,128)(2,1)} %pad_maximum_fusion.8.grad_ref, ...), custom_call_target="tpu_custom_call" | custom-call | flops 14495514624 | bytes 22544384 | tf_op jit(solution)/shard_map/pallas_call | solution.py:191
  333.4 4.9 fusion.110
  338.3 3.4 add_convert_fusion.2
  348.3 4.6 fusion.109
  352.9 5.0 add_convert_fusion.1
  358.0 6.0 fusion.108
  370.3 6.2 %add_convert_fusion = bf16[1152,1024]{1,0:T(8,128)(2,1)S(1)} fusion(f32[1152,1024]{1,0:T(8,128)} %fusion.108, bf16[1024,1152]{1,0:T(8,128)(2,1)} %get-tuple-element.28, bf16[256,1024]{1,0:T(8,128)(2,1)} %copy-done.81, bf16[256,1024]{1,0:T(8,128)(2,1)S(1)} %copy-done.79, bf16[256,1024]{1,0:T(8,128)(2,1)} %copy-done.80, bf16[256,1024]{1,0:T(8,128)(2,1)S(1)} %copy-done.42), kind=kOutput, calls=%fused_computation.9 | convolution fusion | flops 2426667008 | bytes 11534336 | tf_op jit(solution)/shard_map/dot_general | solution.py:23
  376.5 3.1 collective-permute-done.31
  379.6 11.2 %collective-permute-done.47 = bf16[256,1024]{1,0:T(8,128)(2,1)S(1)} collective-permute-done((bf16[256,1024]{1,0:T(8,128)(2,1)S(1)}, bf16[256,1024]{1,0:T(8,128)(2,1)S(1)}, u32[]{:S(2)}, u32[]{:S(2)}) %collective-permute-start.47) | collective-permute-done | bytes 524320 | tf_op jit(solution)/shard_map/ppermute | solution.py:39
  390.8 11.2 %collective-permute-done.56 = bf16[256,1024]{1,0:T(8,128)(2,1)S(1)} collective-permute-done((bf16[256,1024]{1,0:T(8,128)(2,1)S(1)}, bf16[256,1024]{1,0:T(8,128)(2,1)S(1)}, u32[]{:S(2)}, u32[]{:S(2)}) %collective-permute-start.56) | collective-permute-done | bytes 524320 | tf_op jit(solution)/shard_map/ppermute | solution.py:39
  402.0 10.4 %collective-permute-done.49 = bf16[256,1024]{1,0:T(8,128)(2,1)S(1)} collective-permute-done((bf16[256,1024]{1,0:T(8,128)(2,1)S(1)}, bf16[256,1024]{1,0:T(8,128)(2,1)S(1)}, u32[]{:S(2)}, u32[]{:S(2)}) %collective-permute-start.49) | collective-permute-done | bytes 524320 | tf_op jit(solution)/shard_map/ppermute | solution.py:39
  412.4 3.3 multiply_reduce_fusion.7
  415.7 2.5 multiply_convert_fusion.7
  418.8 3.6 fusion.2
  423.9 9.4 %collective-permute-done.58 = bf16[256,1024]{1,0:T(8,128)(2,1)} collective-permute-done((bf16[256,1024]{1,0:T(8,128)(2,1)}, bf16[256,1024]{1,0:T(8,128)(2,1)}, u32[]{:S(2)}, u32[]{:S(2)}) %collective-permute-start.58) | collective-permute-done | bytes 524320 | tf_op jit(solution)/shard_map/ppermute | solution.py:39
  434.1 8.6 %collective-permute-done.51 = bf16[256,1024]{1,0:T(8,128)(2,1)} collective-permute-done((bf16[256,1024]{1,0:T(8,128)(2,1)}, bf16[256,1024]{1,0:T(8,128)(2,1)}, u32[]{:S(2)}, u32[]{:S(2)}) %collective-permute-start.51) | collective-permute-done | bytes 524320 | tf_op jit(solution)/shard_map/ppermute | solution.py:39
  442.8 4.9 multiply_reduce_fusion.2
  450.1 2.9 multiply_reduce_fusion.5
  457.3 3.6 fusion.56
  461.0 3.3 add_convert_fusion.3
  465.4 2.4 fusion.75
  473.3 1.8 convolution_convert_fusion.3
  477.3 1.8 convolution_convert_fusion.2
  483.5 2.1 fusion.31
  487.3 26.8 %collective-permute-done.62 = bf16[4,144,1024]{2,1,0:T(8,128)(2,1)} collective-permute-done((bf16[4,144,1024]{2,1,0:T(8,128)(2,1)S(1)}, bf16[4,144,1024]{2,1,0:T(8,128)(2,1)}, u32[]{:S(2)}, u32[]{:S(2)}) %collective-permute-start.62) | collective-permute-done | bytes 1179680 | tf_op jit(solution)/shard_map/ppermute | solution.py:82
  516.7 2.1 collective-permute-start.63
  518.9 2.0 fusion.25
  522.4 2.5 pad_maximum_fusion.21
  526.6 4.1 collective-permute-start.64
  530.7 3.7 collective-permute-done.61
  534.4 2.3 fusion.15
  537.8 10.0 %collective-permute-start.65 = (bf16[144,1024]{1,0:T(8,128)(2,1)S(1)}, bf16[144,1024]{1,0:T(8,128)(2,1)S(1)}, u32[]{:S(2)}, u32[]{:S(2)}) collective-permute-start(bf16[144,1024]{1,0:T(8,128)(2,1)S(1)} %get-tuple-element.104), channel_id=1, source_target_pairs={{0,1},{1,2},{2,3},{4,5},{5,6},{6,7},{8,9},{9,10},{10,11},{12,13},{... | collective-permute-start | bytes 884744 | tf_op jit(solution)/shard_map/ppermute | solution.py:108
  549.6 2.3 fusion.73
  552.9 7.8 %collective-permute-done.65 = bf16[144,1024]{1,0:T(8,128)(2,1)S(1)} collective-permute-done((bf16[144,1024]{1,0:T(8,128)(2,1)S(1)}, bf16[144,1024]{1,0:T(8,128)(2,1)S(1)}, u32[]{:S(2)}, u32[]{:S(2)}) %collective-permute-start.65) | collective-permute-done | bytes 294944 | tf_op jit(solution)/shard_map/ppermute | solution.py:108
  560.7 25.2 %collective-permute-done.68 = bf16[144,1024]{1,0:T(8,128)(2,1)S(1)} collective-permute-done((bf16[144,1024]{1,0:T(8,128)(2,1)S(1)}, bf16[144,1024]{1,0:T(8,128)(2,1)S(1)}, u32[]{:S(2)}, u32[]{:S(2)}) %collective-permute-start.68) | collective-permute-done | bytes 294944 | tf_op jit(solution)/shard_map/ppermute | solution.py:108
  596.8 1.8 fusion.81
  598.7 2.2 collective-permute-done.72
  600.9 3.4 collective-permute-done.73
  (626 shorter events, 150.0 us)
Async XLA Ops:
  7.2 270.2 %all-gather.3.cloned.1.call-start = ((), (), s32[]{:S(2)}) async-start(), calls=%async_computation.2 | async-start | bytes 7962624 | tf_op jit(solution)/shard_map/all_gather | solution.py:324
  8.1 11.1 %collective-permute-start.6 = (bf16[1,64]{1,0:T(2,128)(2,1)S(1)}, bf16[1,64]{1,0:T(2,128)(2,1)S(1)}, u32[]{:S(2)}, u32[]{:S(2)}) collective-permute-start(bf16[1,64]{1,0:T(2,128)(2,1)S(1)} %maximum_bitcast_fusion.4), channel_id=1, source_target_pairs={{0,8},{8,0},{1,9},{9,1},{2,10},{10,2},{3,11},{11,3},{4,12},{12,4},... | collective-permute-start | bytes 392 | tf_op jit(solution)/shard_map/ppermute | solution.py:39
  11.0 8.2 %collective-permute-start.8 = (bf16[1,64]{1,0:T(2,128)(2,1)S(1)}, bf16[1,64]{1,0:T(2,128)(2,1)S(1)}, u32[]{:S(2)}, u32[]{:S(2)}) collective-permute-start(bf16[1,64]{1,0:T(2,128)(2,1)S(1)} %maximum_bitcast_fusion.4), channel_id=1, source_target_pairs={{0,4},{4,0},{1,5},{5,1},{2,6},{6,2},{3,7},{7,3},{8,12},{12,8},{9,1... | collective-permute-start | bytes 392 | tf_op jit(solution)/shard_map/ppermute | solution.py:35
  12.3 43.9 %collective-permute-start.33 = (bf16[256,1024]{1,0:T(8,128)(2,1)S(1)}, bf16[256,1024]{1,0:T(8,128)(2,1)}, u32[]{:S(2)}, u32[]{:S(2)}) collective-permute-start(bf16[256,1024]{1,0:T(8,128)(2,1)S(1)} %get-tuple-element.121), channel_id=1, source_target_pairs={{0,8},{8,0},{1,9},{9,1},{2,10},{10,2},{3,11},{11,3},{4,12},{12,4},... | collective-permute-start | bytes 1572872 | tf_op jit(solution)/shard_map/ppermute | solution.py:39
  12.4 46.1 %collective-permute-start.32 = (bf16[256,1024]{1,0:T(8,128)(2,1)S(1)}, bf16[256,1024]{1,0:T(8,128)(2,1)}, u32[]{:S(2)}, u32[]{:S(2)}) collective-permute-start(bf16[256,1024]{1,0:T(8,128)(2,1)S(1)} %get-tuple-element.121), channel_id=1, source_target_pairs={{0,4},{4,0},{1,5},{5,1},{2,6},{6,2},{3,7},{7,3},{8,12},{12,8},{9,1... | collective-permute-start | bytes 1572872 | tf_op jit(solution)/shard_map/ppermute | solution.py:35
  13.7 13.1 %collective-permute-start.17 = (s32[256,1]{0,1:T(1,128)S(1)}, s32[256,1]{0,1:T(1,128)S(1)}, u32[]{:S(2)}, u32[]{:S(2)}) collective-permute-start(s32[256,1]{0,1:T(1,128)S(1)} %get-tuple-element.208), channel_id=1, source_target_pairs={{0,8},{8,0},{1,9},{9,1},{2,10},{10,2},{3,11},{11,3},{4,12},{12,4},... | collective-permute-start | bytes 3080 | tf_op jit(solution)/shard_map/ppermute | solution.py:39
  19.2 7.7 %collective-permute-start.16 = (s32[256,1]{0,1:T(1,128)S(1)}, s32[256,1]{0,1:T(1,128)S(1)}, u32[]{:S(2)}, u32[]{:S(2)}) collective-permute-start(s32[256,1]{0,1:T(1,128)S(1)} %get-tuple-element.208), channel_id=1, source_target_pairs={{0,4},{4,0},{1,5},{5,1},{2,6},{6,2},{3,7},{7,3},{8,12},{12,8},{9,1... | collective-permute-start | bytes 3080 | tf_op jit(solution)/shard_map/ppermute | solution.py:35
  20.3 7.2 %collective-permute-start.36 = (s32[256,1]{0,1:T(1,128)S(1)}, s32[256,1]{0,1:T(1,128)S(1)}, u32[]{:S(2)}, u32[]{:S(2)}) collective-permute-start(s32[256,1]{0,1:T(1,128)S(1)} %get-tuple-element.209), channel_id=1, source_target_pairs={{0,8},{8,0},{1,9},{9,1},{2,10},{10,2},{3,11},{11,3},{4,12},{12,4},... | collective-permute-start | bytes 3080 | tf_op jit(solution)/shard_map/ppermute | solution.py:39
  31.2 5.9 collective-permute-start.27
  32.9 7.9 %collective-permute-start.28 = (bf16[32,2304]{1,0:T(8,128)(2,1)S(1)}, bf16[32,2304]{1,0:T(8,128)(2,1)S(1)}, u32[]{:S(2)}, u32[]{:S(2)}) collective-permute-start(bf16[32,2304]{1,0:T(8,128)(2,1)S(1)} %get-tuple-element.69), channel_id=1, source_target_pairs={{0,8},{8,0},{1,9},{9,1},{2,10},{10,2},{3,11},{11,3},{4,12},{12,4},... | collective-permute-start | bytes 442376 | tf_op jit(solution)/shard_map/ppermute | solution.py:39
  34.3 8.0 %collective-permute-start.29 = (bf16[32,2304]{1,0:T(8,128)(2,1)S(1)}, bf16[32,2304]{1,0:T(8,128)(2,1)S(1)}, u32[]{:S(2)}, u32[]{:S(2)}) collective-permute-start(bf16[32,2304]{1,0:T(8,128)(2,1)S(1)} %get-tuple-element.141), channel_id=1, source_target_pairs={{0,4},{4,0},{1,5},{5,1},{2,6},{6,2},{3,7},{7,3},{8,12},{12,8},{9,1... | collective-permute-start | bytes 442376 | tf_op jit(solution)/shard_map/ppermute | solution.py:35
  37.1 22.0 %collective-permute-start.1 = (bf16[256,1024]{1,0:T(8,128)(2,1)S(1)}, bf16[256,1024]{1,0:T(8,128)(2,1)}, u32[]{:S(2)}, u32[]{:S(2)}) collective-permute-start(bf16[256,1024]{1,0:T(8,128)(2,1)S(1)} %get-tuple-element.120), channel_id=1, source_target_pairs={{0,8},{8,0},{1,9},{9,1},{2,10},{10,2},{3,11},{11,3},{4,12},{12,4},... | collective-permute-start | bytes 1572872 | tf_op jit(solution)/shard_map/ppermute | solution.py:39
  40.8 8.4 %collective-permute-start.9 = (bf16[144,1024]{1,0:T(8,128)(2,1)S(1)}, bf16[144,1024]{1,0:T(8,128)(2,1)S(1)}, u32[]{:S(2)}, u32[]{:S(2)}) collective-permute-start(bf16[144,1024]{1,0:T(8,128)(2,1)S(1)} %fusion.80), channel_id=1, source_target_pairs={{0,16},{16,0},{1,17},{17,1},{2,18},{18,2},{3,19},{19,3},{4,20},{20... | collective-permute-start | bytes 884744 | tf_op jit(solution)/shard_map/ppermute | solution.py:82
  49.5 15.8 %collective-permute-start.11 = (bf16[2,144,1024]{2,1,0:T(8,128)(2,1)S(1)}, bf16[2,144,1024]{2,1,0:T(8,128)(2,1)S(1)}, u32[]{:S(2)}, u32[]{:S(2)}) collective-permute-start(bf16[2,144,1024]{2,1,0:T(8,128)(2,1)S(1)} %pad_maximum_fusion.16), channel_id=1, source_target_pairs={{1,0},{2,1},{3,2},{5,4},{6,5},{7,6},{9,8},{10,9},{11,10},{13,12},{... | collective-permute-start | bytes 1769480 | tf_op jit(solution)/shard_map/ppermute | solution.py:90
  50.8 17.0 %collective-permute-start.10 = (bf16[2,144,1024]{2,1,0:T(8,128)(2,1)S(1)}, bf16[2,144,1024]{2,1,0:T(8,128)(2,1)}, u32[]{:S(2)}, u32[]{:S(2)}) collective-permute-start(bf16[2,144,1024]{2,1,0:T(8,128)(2,1)S(1)} %pad_maximum_fusion.16), channel_id=1, source_target_pairs={{0,1},{1,2},{2,3},{4,5},{5,6},{6,7},{8,9},{9,10},{10,11},{12,13},{... | collective-permute-start | bytes 1769480 | tf_op jit(solution)/shard_map/ppermute | solution.py:89
  56.2 13.0 %collective-permute-start.34 = (bf16[256,1024]{1,0:T(8,128)(2,1)}, bf16[256,1024]{1,0:T(8,128)(2,1)}, u32[]{:S(2)}, u32[]{:S(2)}) collective-permute-start(bf16[256,1024]{1,0:T(8,128)(2,1)} %collective-permute-done.33), channel_id=1, source_target_pairs={{0,4},{4,0},{1,5},{5,1},{2,6},{6,2},{3,7},{7,3},{8,12},{12,8},{9,1... | collective-permute-start | bytes 1572872 | tf_op jit(solution)/shard_map/ppermute | solution.py:35
  57.8 535.1 %reduce-scatter.2.cloned.1.call-start = ((), (), s32[]{:S(2)}) async-start(), calls=%async_computation.1 | async-start | bytes 7962624 | tf_op jit(solution)/shard_map/reduce_scatter | solution.py:146
  58.5 13.2 %collective-permute-start = (bf16[256,1024]{1,0:T(8,128)(2,1)S(1)}, bf16[256,1024]{1,0:T(8,128)(2,1)S(1)}, u32[]{:S(2)}, u32[]{:S(2)}) collective-permute-start(bf16[256,1024]{1,0:T(8,128)(2,1)S(1)} %get-tuple-element.120), channel_id=1, source_target_pairs={{0,4},{4,0},{1,5},{5,1},{2,6},{6,2},{3,7},{7,3},{8,12},{12,8},{9,1... | collective-permute-start | bytes 1572872 | tf_op jit(solution)/shard_map/ppermute | solution.py:35
  59.0 12.7 %collective-permute-start.2 = (bf16[256,1024]{1,0:T(8,128)(2,1)}, bf16[256,1024]{1,0:T(8,128)(2,1)S(1)}, u32[]{:S(2)}, u32[]{:S(2)}) collective-permute-start(bf16[256,1024]{1,0:T(8,128)(2,1)} %collective-permute-done.1), channel_id=1, source_target_pairs={{0,4},{4,0},{1,5},{5,1},{2,6},{6,2},{3,7},{7,3},{8,12},{12,8},{9,1... | collective-permute-start | bytes 1572872 | tf_op jit(solution)/shard_map/ppermute | solution.py:35
  65.4 40.5 %collective-permute-start.12 = (bf16[2,144,1024]{2,1,0:T(8,128)(2,1)S(1)}, bf16[2,144,1024]{2,1,0:T(8,128)(2,1)S(1)}, u32[]{:S(2)}, u32[]{:S(2)}) collective-permute-start(bf16[2,144,1024]{2,1,0:T(8,128)(2,1)S(1)} %collective-permute-done.11), channel_id=1, source_target_pairs={{1,0},{2,1},{5,4},{6,5},{9,8},{10,9},{13,12},{14,13},{17,16},{18,1... | collective-permute-start | bytes 1769480 | tf_op jit(solution)/shard_map/ppermute | solution.py:90
  67.8 39.4 %collective-permute-start.14 = (bf16[2,144,1024]{2,1,0:T(8,128)(2,1)}, bf16[2,144,1024]{2,1,0:T(8,128)(2,1)}, u32[]{:S(2)}, u32[]{:S(2)}) collective-permute-start(bf16[2,144,1024]{2,1,0:T(8,128)(2,1)} %collective-permute-done.10), channel_id=1, source_target_pairs={{1,2},{2,3},{5,6},{6,7},{9,10},{10,11},{13,14},{14,15},{17,18},{18... | collective-permute-start | bytes 1769480 | tf_op jit(solution)/shard_map/ppermute | solution.py:89
  105.9 38.1 %collective-permute-start.13 = (bf16[2,144,1024]{2,1,0:T(8,128)(2,1)S(1)}, bf16[2,144,1024]{2,1,0:T(8,128)(2,1)}, u32[]{:S(2)}, u32[]{:S(2)}) collective-permute-start(bf16[2,144,1024]{2,1,0:T(8,128)(2,1)S(1)} %collective-permute-done.12), channel_id=1, source_target_pairs={{1,0},{5,4},{9,8},{13,12},{17,16},{21,20},{25,24},{29,28}} | collective-permute-start | bytes 1769480 | tf_op jit(solution)/shard_map/ppermute | solution.py:90
  108.8 37.1 %collective-permute-start.15 = (bf16[2,144,1024]{2,1,0:T(8,128)(2,1)}, bf16[2,144,1024]{2,1,0:T(8,128)(2,1)}, u32[]{:S(2)}, u32[]{:S(2)}) collective-permute-start(bf16[2,144,1024]{2,1,0:T(8,128)(2,1)} %collective-permute-done.14), channel_id=1, source_target_pairs={{2,3},{6,7},{10,11},{14,15},{18,19},{22,23},{26,27},{30,31}} | collective-permute-start | bytes 1769480 | tf_op jit(solution)/shard_map/ppermute | solution.py:89
  192.9 15.1 %collective-permute-start.39 = (bf16[256,1024]{1,0:T(8,128)(2,1)}, bf16[256,1024]{1,0:T(8,128)(2,1)}, u32[]{:S(2)}, u32[]{:S(2)}) collective-permute-start(bf16[256,1024]{1,0:T(8,128)(2,1)} %fusion.42), channel_id=1, source_target_pairs={{0,8},{8,0},{1,9},{9,1},{2,10},{10,2},{3,11},{11,3},{4,12},{12,4},... | collective-permute-start | bytes 1572872 | tf_op jit(solution)/shard_map/ppermute | solution.py:39
  194.8 23.6 %collective-permute-start.20 = (bf16[256,1024]{1,0:T(8,128)(2,1)}, bf16[256,1024]{1,0:T(8,128)(2,1)}, u32[]{:S(2)}, u32[]{:S(2)}) collective-permute-start(bf16[256,1024]{1,0:T(8,128)(2,1)} %fusion.50), channel_id=1, source_target_pairs={{0,8},{8,0},{1,9},{9,1},{2,10},{10,2},{3,11},{11,3},{4,12},{12,4},... | collective-permute-start | bytes 1572872 | tf_op jit(solution)/shard_map/ppermute | solution.py:39
  222.1 14.9 %collective-permute-start.44 = (bf16[256,1024]{1,0:T(8,128)(2,1)S(1)}, bf16[256,1024]{1,0:T(8,128)(2,1)S(1)}, u32[]{:S(2)}, u32[]{:S(2)}) collective-permute-start(bf16[256,1024]{1,0:T(8,128)(2,1)S(1)} %get-tuple-element.205), channel_id=1, source_target_pairs={{0,8},{8,0},{1,9},{9,1},{2,10},{10,2},{3,11},{11,3},{4,12},{12,4},... | collective-permute-start | bytes 1572872 | tf_op jit(solution)/shard_map/ppermute | solution.py:39
  222.4 14.8 %collective-permute-start.43 = (bf16[256,1024]{1,0:T(8,128)(2,1)S(1)}, bf16[256,1024]{1,0:T(8,128)(2,1)S(1)}, u32[]{:S(2)}, u32[]{:S(2)}) collective-permute-start(bf16[256,1024]{1,0:T(8,128)(2,1)S(1)} %get-tuple-element.205), channel_id=1, source_target_pairs={{0,4},{4,0},{1,5},{5,1},{2,6},{6,2},{3,7},{7,3},{8,12},{12,8},{9,1... | collective-permute-start | bytes 1572872 | tf_op jit(solution)/shard_map/ppermute | solution.py:35
  222.7 25.5 %collective-permute-start.41 = (bf16[256,1024]{1,0:T(8,128)(2,1)S(1)}, bf16[256,1024]{1,0:T(8,128)(2,1)S(1)}, u32[]{:S(2)}, u32[]{:S(2)}) collective-permute-start(bf16[256,1024]{1,0:T(8,128)(2,1)S(1)} %get-tuple-element.196), channel_id=1, source_target_pairs={{0,8},{8,0},{1,9},{9,1},{2,10},{10,2},{3,11},{11,3},{4,12},{12,4},... | collective-permute-start | bytes 1572872 | tf_op jit(solution)/shard_map/ppermute | solution.py:39
  224.5 23.7 %collective-permute-start.40 = (bf16[256,1024]{1,0:T(8,128)(2,1)S(1)}, bf16[256,1024]{1,0:T(8,128)(2,1)S(1)}, u32[]{:S(2)}, u32[]{:S(2)}) collective-permute-start(bf16[256,1024]{1,0:T(8,128)(2,1)S(1)} %get-tuple-element.196), channel_id=1, source_target_pairs={{0,4},{4,0},{1,5},{5,1},{2,6},{6,2},{3,7},{7,3},{8,12},{12,8},{9,1... | collective-permute-start | bytes 1572872 | tf_op jit(solution)/shard_map/ppermute | solution.py:35
  224.8 34.7 %collective-permute-start.25 = (bf16[256,1024]{1,0:T(8,128)(2,1)S(1)}, bf16[256,1024]{1,0:T(8,128)(2,1)S(1)}, u32[]{:S(2)}, u32[]{:S(2)}) collective-permute-start(bf16[256,1024]{1,0:T(8,128)(2,1)S(1)} %get-tuple-element.206), channel_id=1, source_target_pairs={{0,8},{8,0},{1,9},{9,1},{2,10},{10,2},{3,11},{11,3},{4,12},{12,4},... | collective-permute-start | bytes 1572872 | tf_op jit(solution)/shard_map/ppermute | solution.py:39
  237.0 32.0 %collective-permute-start.22 = (bf16[256,1024]{1,0:T(8,128)(2,1)S(1)}, bf16[256,1024]{1,0:T(8,128)(2,1)S(1)}, u32[]{:S(2)}, u32[]{:S(2)}) collective-permute-start(bf16[256,1024]{1,0:T(8,128)(2,1)S(1)} %get-tuple-element.195), channel_id=1, source_target_pairs={{0,8},{8,0},{1,9},{9,1},{2,10},{10,2},{3,11},{11,3},{4,12},{12,4},... | collective-permute-start | bytes 1572872 | tf_op jit(solution)/shard_map/ppermute | solution.py:39
  237.3 31.7 %collective-permute-start.45 = (bf16[256,1024]{1,0:T(8,128)(2,1)S(1)}, bf16[256,1024]{1,0:T(8,128)(2,1)S(1)}, u32[]{:S(2)}, u32[]{:S(2)}) collective-permute-start(bf16[256,1024]{1,0:T(8,128)(2,1)S(1)} %collective-permute-done.44), channel_id=1, source_target_pairs={{0,4},{4,0},{1,5},{5,1},{2,6},{6,2},{3,7},{7,3},{8,12},{12,8},{9,1... | collective-permute-start | bytes 1572872 | tf_op jit(solution)/shard_map/ppermute | solution.py:35
  248.3 22.8 %collective-permute-start.42 = (bf16[256,1024]{1,0:T(8,128)(2,1)S(1)}, bf16[256,1024]{1,0:T(8,128)(2,1)S(1)}, u32[]{:S(2)}, u32[]{:S(2)}) collective-permute-start(bf16[256,1024]{1,0:T(8,128)(2,1)S(1)} %collective-permute-done.41), channel_id=1, source_target_pairs={{0,4},{4,0},{1,5},{5,1},{2,6},{6,2},{3,7},{7,3},{8,12},{12,8},{9,1... | collective-permute-start | bytes 1572872 | tf_op jit(solution)/shard_map/ppermute | solution.py:35
  248.3 24.4 %collective-permute-start.24 = (bf16[256,1024]{1,0:T(8,128)(2,1)S(1)}, bf16[256,1024]{1,0:T(8,128)(2,1)S(1)}, u32[]{:S(2)}, u32[]{:S(2)}) collective-permute-start(bf16[256,1024]{1,0:T(8,128)(2,1)S(1)} %get-tuple-element.206), channel_id=1, source_target_pairs={{0,4},{4,0},{1,5},{5,1},{2,6},{6,2},{3,7},{7,3},{8,12},{12,8},{9,1... | collective-permute-start | bytes 1572872 | tf_op jit(solution)/shard_map/ppermute | solution.py:35
  259.5 13.2 %collective-permute-start.26 = (bf16[256,1024]{1,0:T(8,128)(2,1)S(1)}, bf16[256,1024]{1,0:T(8,128)(2,1)S(1)}, u32[]{:S(2)}, u32[]{:S(2)}) collective-permute-start(bf16[256,1024]{1,0:T(8,128)(2,1)S(1)} %collective-permute-done.25), channel_id=1, source_target_pairs={{0,4},{4,0},{1,5},{5,1},{2,6},{6,2},{3,7},{7,3},{8,12},{12,8},{9,1... | collective-permute-start | bytes 1572872 | tf_op jit(solution)/shard_map/ppermute | solution.py:35
  269.0 5.3 collective-permute-start.21
  269.0 5.3 collective-permute-start.23
  343.7 20.6 %collective-permute-start.30 = (bf16[512,1024]{1,0:T(8,128)(2,1)S(1)}, bf16[512,1024]{1,0:T(8,128)(2,1)S(1)}, u32[]{:S(2)}, u32[]{:S(2)}) collective-permute-start(bf16[512,1024]{1,0:T(8,128)(2,1)S(1)} %pad_maximum_fusion.18), channel_id=1, source_target_pairs={{0,4},{4,0},{1,5},{5,1},{2,6},{6,2},{3,7},{7,3},{8,12},{12,8},{9,1... | collective-permute-start | bytes 3145736 | tf_op jit(solution)/shard_map/ppermute | solution.py:35
  344.4 20.9 %collective-permute-start.46 = (bf16[512,1024]{1,0:T(8,128)(2,1)S(1)}, bf16[512,1024]{1,0:T(8,128)(2,1)S(1)}, u32[]{:S(2)}, u32[]{:S(2)}) collective-permute-start(bf16[512,1024]{1,0:T(8,128)(2,1)S(1)} %pad_maximum_fusion.20), channel_id=1, source_target_pairs={{0,4},{4,0},{1,5},{5,1},{2,6},{6,2},{3,7},{7,3},{8,12},{12,8},{9,1... | collective-permute-start | bytes 3145736 | tf_op jit(solution)/shard_map/ppermute | solution.py:35
  345.7 21.6 %collective-permute-start.55 = (bf16[512,1024]{1,0:T(8,128)(2,1)S(1)}, bf16[512,1024]{1,0:T(8,128)(2,1)S(1)}, u32[]{:S(2)}, u32[]{:S(2)}) collective-permute-start(bf16[512,1024]{1,0:T(8,128)(2,1)S(1)} %pad_maximum_fusion.24), channel_id=1, source_target_pairs={{0,4},{4,0},{1,5},{5,1},{2,6},{6,2},{3,7},{7,3},{8,12},{12,8},{9,1... | collective-permute-start | bytes 3145736 | tf_op jit(solution)/shard_map/ppermute | solution.py:35
  347.3 21.0 %collective-permute-start.48 = (bf16[512,1024]{1,0:T(8,128)(2,1)}, bf16[512,1024]{1,0:T(8,128)(2,1)S(1)}, u32[]{:S(2)}, u32[]{:S(2)}) collective-permute-start(bf16[512,1024]{1,0:T(8,128)(2,1)} %pad_maximum_fusion.22), channel_id=1, source_target_pairs={{0,4},{4,0},{1,5},{5,1},{2,6},{6,2},{3,7},{7,3},{8,12},{12,8},{9,1... | collective-permute-start | bytes 3145736 | tf_op jit(solution)/shard_map/ppermute | solution.py:35
  364.7 14.8 %collective-permute-start.31 = (bf16[256,1024]{1,0:T(8,128)(2,1)S(1)}, bf16[256,1024]{1,0:T(8,128)(2,1)S(1)}, u32[]{:S(2)}, u32[]{:S(2)}) collective-permute-start(bf16[256,1024]{1,0:T(8,128)(2,1)S(1)} %fusion.45), channel_id=1, source_target_pairs={{0,8},{8,0},{1,9},{9,1},{2,10},{10,2},{3,11},{11,3},{4,12},{12,4},... | collective-permute-start | bytes 1572872 | tf_op jit(solution)/shard_map/ppermute | solution.py:39
  365.8 25.0 %collective-permute-start.47 = (bf16[256,1024]{1,0:T(8,128)(2,1)S(1)}, bf16[256,1024]{1,0:T(8,128)(2,1)S(1)}, u32[]{:S(2)}, u32[]{:S(2)}) collective-permute-start(bf16[256,1024]{1,0:T(8,128)(2,1)S(1)} %fusion.37), channel_id=1, source_target_pairs={{0,8},{8,0},{1,9},{9,1},{2,10},{10,2},{3,11},{11,3},{4,12},{12,4},... | collective-permute-start | bytes 1572872 | tf_op jit(solution)/shard_map/ppermute | solution.py:39
  367.7 34.3 %collective-permute-start.56 = (bf16[256,1024]{1,0:T(8,128)(2,1)S(1)}, bf16[256,1024]{1,0:T(8,128)(2,1)S(1)}, u32[]{:S(2)}, u32[]{:S(2)}) collective-permute-start(bf16[256,1024]{1,0:T(8,128)(2,1)S(1)} %fusion.28), channel_id=1, source_target_pairs={{0,8},{8,0},{1,9},{9,1},{2,10},{10,2},{3,11},{11,3},{4,12},{12,4},... | collective-permute-start | bytes 1572872 | tf_op jit(solution)/shard_map/ppermute | solution.py:39
  368.8 43.6 %collective-permute-start.49 = (bf16[256,1024]{1,0:T(8,128)(2,1)S(1)}, bf16[256,1024]{1,0:T(8,128)(2,1)S(1)}, u32[]{:S(2)}, u32[]{:S(2)}) collective-permute-start(bf16[256,1024]{1,0:T(8,128)(2,1)S(1)} %fusion.34), channel_id=1, source_target_pairs={{0,8},{8,0},{1,9},{9,1},{2,10},{10,2},{3,11},{11,3},{4,12},{12,4},... | collective-permute-start | bytes 1572872 | tf_op jit(solution)/shard_map/ppermute | solution.py:39
  418.2 15.2 %collective-permute-start.58 = (bf16[256,1024]{1,0:T(8,128)(2,1)}, bf16[256,1024]{1,0:T(8,128)(2,1)}, u32[]{:S(2)}, u32[]{:S(2)}) collective-permute-start(bf16[256,1024]{1,0:T(8,128)(2,1)} %get-tuple-element.110), channel_id=1, source_target_pairs={{0,8},{8,0},{1,9},{9,1},{2,10},{10,2},{3,11},{11,3},{4,12},{12,4},... | collective-permute-start | bytes 1572872 | tf_op jit(solution)/shard_map/ppermute | solution.py:39
  422.4 20.3 %collective-permute-start.51 = (bf16[256,1024]{1,0:T(8,128)(2,1)}, bf16[256,1024]{1,0:T(8,128)(2,1)}, u32[]{:S(2)}, u32[]{:S(2)}) collective-permute-start(bf16[256,1024]{1,0:T(8,128)(2,1)} %get-tuple-element.59), channel_id=1, source_target_pairs={{0,8},{8,0},{1,9},{9,1},{2,10},{10,2},{3,11},{11,3},{4,12},{12,4},... | collective-permute-start | bytes 1572872 | tf_op jit(solution)/shard_map/ppermute | solution.py:39
  423.9 18.9 %collective-permute-start.57 = (bf16[256,1024]{1,0:T(8,128)(2,1)}, bf16[256,1024]{1,0:T(8,128)(2,1)}, u32[]{:S(2)}, u32[]{:S(2)}) collective-permute-start(bf16[256,1024]{1,0:T(8,128)(2,1)} %get-tuple-element.110), channel_id=1, source_target_pairs={{0,4},{4,0},{1,5},{5,1},{2,6},{6,2},{3,7},{7,3},{8,12},{12,8},{9,1... | collective-permute-start | bytes 1572872 | tf_op jit(solution)/shard_map/ppermute | solution.py:35
  433.3 9.5 %collective-permute-start.59 = (bf16[256,1024]{1,0:T(8,128)(2,1)}, bf16[256,1024]{1,0:T(8,128)(2,1)}, u32[]{:S(2)}, u32[]{:S(2)}) collective-permute-start(bf16[256,1024]{1,0:T(8,128)(2,1)} %collective-permute-done.58), channel_id=1, source_target_pairs={{0,4},{4,0},{1,5},{5,1},{2,6},{6,2},{3,7},{7,3},{8,12},{12,8},{9,1... | collective-permute-start | bytes 1572872 | tf_op jit(solution)/shard_map/ppermute | solution.py:35
  433.6 14.5 %collective-permute-start.50 = (bf16[256,1024]{1,0:T(8,128)(2,1)}, bf16[256,1024]{1,0:T(8,128)(2,1)S(1)}, u32[]{:S(2)}, u32[]{:S(2)}) collective-permute-start(bf16[256,1024]{1,0:T(8,128)(2,1)} %get-tuple-element.59), channel_id=1, source_target_pairs={{0,4},{4,0},{1,5},{5,1},{2,6},{6,2},{3,7},{7,3},{8,12},{12,8},{9,1... | collective-permute-start | bytes 1572872 | tf_op jit(solution)/shard_map/ppermute | solution.py:35
  442.8 5.4 collective-permute-start.52
  471.8 42.2 %collective-permute-start.62 = (bf16[4,144,1024]{2,1,0:T(8,128)(2,1)S(1)}, bf16[4,144,1024]{2,1,0:T(8,128)(2,1)}, u32[]{:S(2)}, u32[]{:S(2)}) collective-permute-start(bf16[4,144,1024]{2,1,0:T(8,128)(2,1)S(1)} %dynamic-slice_bitcast_fusion), channel_id=1, source_target_pairs={{0,16},{16,0},{1,17},{17,1},{2,18},{18,2},{3,19},{19,3},{4,20},{20... | collective-permute-start | bytes 3538952 | tf_op jit(solution)/shard_map/ppermute | solution.py:82
  475.3 6.7 %collective-permute-start.53 = (bf16[512,1024]{1,0:T(8,128)(2,1)S(1)}, bf16[512,1024]{1,0:T(8,128)(2,1)}, u32[]{:S(2)}, u32[]{:S(2)}) collective-permute-start(bf16[512,1024]{1,0:T(8,128)(2,1)S(1)} %pad_maximum_fusion.23), channel_id=1, source_target_pairs={{0,4},{4,0},{1,5},{5,1},{2,6},{6,2},{3,7},{7,3},{8,12},{12,8},{9,1... | collective-permute-start | bytes 3145736 | tf_op jit(solution)/shard_map/ppermute | solution.py:35
  485.6 45.1 %collective-permute-start.54 = (bf16[256,1024]{1,0:T(8,128)(2,1)}, bf16[256,1024]{1,0:T(8,128)(2,1)}, u32[]{:S(2)}, u32[]{:S(2)}) collective-permute-start(bf16[256,1024]{1,0:T(8,128)(2,1)} %fusion.31), channel_id=1, source_target_pairs={{0,8},{8,0},{1,9},{9,1},{2,10},{10,2},{3,11},{11,3},{4,12},{12,4},... | collective-permute-start | bytes 1572872 | tf_op jit(solution)/shard_map/ppermute | solution.py:39
  516.7 8.8 %collective-permute-start.63 = (bf16[144,1024]{1,0:T(8,128)(2,1)}, bf16[144,1024]{1,0:T(8,128)(2,1)S(1)}, u32[]{:S(2)}, u32[]{:S(2)}) collective-permute-start(bf16[144,1024]{1,0:T(8,128)(2,1)} %get-tuple-element.106), channel_id=1, source_target_pairs={{0,1},{4,5},{8,9},{12,13},{16,17},{20,21},{24,25},{28,29}} | collective-permute-start | bytes 884744 | tf_op jit(solution)/shard_map/ppermute | solution.py:108
  520.9 13.5 %collective-permute-start.61 = (bf16[256,1024]{1,0:T(8,128)(2,1)}, bf16[256,1024]{1,0:T(8,128)(2,1)}, u32[]{:S(2)}, u32[]{:S(2)}) collective-permute-start(bf16[256,1024]{1,0:T(8,128)(2,1)} %fusion.25), channel_id=1, source_target_pairs={{0,8},{8,0},{1,9},{9,1},{2,10},{10,2},{3,11},{11,3},{4,12},{12,4},... | collective-permute-start | bytes 1572872 | tf_op jit(solution)/shard_map/ppermute | solution.py:39
  524.9 11.9 %collective-permute-start.66 = (bf16[144,1024]{1,0:T(8,128)(2,1)}, bf16[144,1024]{1,0:T(8,128)(2,1)S(1)}, u32[]{:S(2)}, u32[]{:S(2)}) collective-permute-start(bf16[144,1024]{1,0:T(8,128)(2,1)} %get-tuple-element.107), channel_id=1, source_target_pairs={{3,2},{7,6},{11,10},{15,14},{19,18},{23,22},{27,26},{31,30}} | collective-permute-start | bytes 884744 | tf_op jit(solution)/shard_map/ppermute | solution.py:108
  526.6 10.1 %collective-permute-start.64 = (bf16[144,1024]{1,0:T(8,128)(2,1)S(1)}, bf16[144,1024]{1,0:T(8,128)(2,1)S(1)}, u32[]{:S(2)}, u32[]{:S(2)}) collective-permute-start(bf16[144,1024]{1,0:T(8,128)(2,1)S(1)} %fusion.65), channel_id=1, source_target_pairs={{0,1},{1,2},{4,5},{5,6},{8,9},{9,10},{12,13},{13,14},{16,17},{17,1... | collective-permute-start | bytes 884744 | tf_op jit(solution)/shard_map/ppermute | solution.py:108
  537.0 10.9 %collective-permute-start.67 = (bf16[144,1024]{1,0:T(8,128)(2,1)S(1)}, bf16[144,1024]{1,0:T(8,128)(2,1)S(1)}, u32[]{:S(2)}, u32[]{:S(2)}) collective-permute-start(bf16[144,1024]{1,0:T(8,128)(2,1)S(1)} %get-tuple-element.105), channel_id=1, source_target_pairs={{2,1},{3,2},{6,5},{7,6},{10,9},{11,10},{14,13},{15,14},{18,17},{19... | collective-permute-start | bytes 884744 | tf_op jit(solution)/shard_map/ppermute | solution.py:108
  537.8 22.9 %collective-permute-start.65 = (bf16[144,1024]{1,0:T(8,128)(2,1)S(1)}, bf16[144,1024]{1,0:T(8,128)(2,1)S(1)}, u32[]{:S(2)}, u32[]{:S(2)}) collective-permute-start(bf16[144,1024]{1,0:T(8,128)(2,1)S(1)} %get-tuple-element.104), channel_id=1, source_target_pairs={{0,1},{1,2},{2,3},{4,5},{5,6},{6,7},{8,9},{9,10},{10,11},{12,13},{... | collective-permute-start | bytes 884744 | tf_op jit(solution)/shard_map/ppermute | solution.py:108
  548.0 37.9 %collective-permute-start.68 = (bf16[144,1024]{1,0:T(8,128)(2,1)S(1)}, bf16[144,1024]{1,0:T(8,128)(2,1)S(1)}, u32[]{:S(2)}, u32[]{:S(2)}) collective-permute-start(bf16[144,1024]{1,0:T(8,128)(2,1)S(1)} %fusion.64), channel_id=1, source_target_pairs={{1,0},{2,1},{3,2},{5,4},{6,5},{7,6},{9,8},{10,9},{11,10},{13,12},{... | collective-permute-start | bytes 884744 | tf_op jit(solution)/shard_map/ppermute | solution.py:108
  594.9 6.0 collective-permute-start.72
  595.6 8.7 %collective-permute-start.73 = (bf16[32,2304]{1,0:T(8,128)(2,1)S(1)}, bf16[32,2304]{1,0:T(8,128)(2,1)S(1)}, u32[]{:S(2)}, u32[]{:S(2)}) collective-permute-start(bf16[32,2304]{1,0:T(8,128)(2,1)S(1)} %get-tuple-element.134), channel_id=1, source_target_pairs={{0,8},{8,0},{1,9},{9,1},{2,10},{10,2},{3,11},{11,3},{4,12},{12,4},... | collective-permute-start | bytes 442376 | tf_op jit(solution)/shard_map/ppermute | solution.py:39
  596.7 7.6 %collective-permute-start.74 = (bf16[32,2304]{1,0:T(8,128)(2,1)S(1)}, bf16[32,2304]{1,0:T(8,128)(2,1)S(1)}, u32[]{:S(2)}, u32[]{:S(2)}) collective-permute-start(bf16[32,2304]{1,0:T(8,128)(2,1)S(1)} %get-tuple-element.132), channel_id=1, source_target_pairs={{0,4},{4,0},{1,5},{5,1},{2,6},{6,2},{3,7},{7,3},{8,12},{12,8},{9,1... | collective-permute-start | bytes 442376 | tf_op jit(solution)/shard_map/ppermute | solution.py:35
  (151 other events, 1557.7 us)
Sparse Core Ops, SparseCore 0:
  57.9 121.9 all-gather.2
  422.6 163.1 reduce-scatter.1

commit v2 on v1

--- a/solution.py
+++ b/solution.py
@@ -1,4 +1,4 @@
-from functools import reduce
+from functools import partial, reduce
 
 import jax
 import jax.numpy as jnp
@@ -9,8 +9,9 @@
 
 EPSILON = 1e-05
 TEAM = 4
+CREW = 8
 EXTRA_ROWS = 16
-ROW_TILE = 256
+ROW_TILE = 512
 bf16 = jnp.bfloat16
 f32 = jnp.float32
 
@@ -39,25 +40,30 @@
     return lax.ppermute(values, "x", [(0, 1), (1, 0)])
 
 
-def swap_both(values):
-    return lax.ppermute(values, ("x", "c"), [(i, i ^ 3) for i in range(TEAM)])
+def swap_row(values):
+    return lax.ppermute(values, "y", [(0, 1), (1, 0)])
+
+
+def swap_far(values, distance):
+    axes = ("y", "x", "c")
+    return lax.ppermute(values, axes, [(i, i ^ distance) for i in range(CREW)])
+
+
+def after(values, token):
+    return values + (token.ravel()[0] * 0).astype(values.dtype)
 
 
 def reorder(blocks):
-    odd_core = lax.axis_index("c") == 1
-    odd_chip = lax.axis_index("x") == 1
-    b0, b1, b2, b3 = blocks
-    b0, b1 = jnp.where(odd_core, b1, b0), jnp.where(odd_core, b0, b1)
-    b2, b3 = jnp.where(odd_core, b3, b2), jnp.where(odd_core, b2, b3)
-    b0, b2 = jnp.where(odd_chip, b2, b0), jnp.where(odd_chip, b0, b2)
-    b1, b3 = jnp.where(odd_chip, b3, b1), jnp.where(odd_chip, b1, b3)
-    return [b0, b1, b2, b3]
+    blocks = list(blocks)
+    for bit, axis in ((1, "c"), (2, "x"), (4, "y"))[: len(blocks).bit_length() - 1]:
+        odd = lax.axis_index(axis) == 1
+        blocks = [jnp.where(odd, blocks[j ^ bit], blocks[j]) for j in range(len(blocks))]
+    return blocks
 
 
 def exchange(blocks):
     near = reorder(blocks)
-    came = [near[0], swap_core(near[1]), swap_chip(near[2]), swap_both(near[3])]
-    return reorder(came)
+    return reorder(near[:1] + [swap_far(near[j], j) for j in range(1, len(near))])
 
 
 def team_rows(rows):
@@ -65,12 +71,12 @@
     return jnp.concatenate([rows, swap_core(rows), across, swap_core(across)], axis=0)
 
 
-def team_sum(partial):
-    count = partial.shape[0] // TEAM
-    sent = jnp.concatenate([partial[count : 2 * count], partial[3 * count :]], axis=0)
+def team_sum(terms):
+    count = terms.shape[0] // TEAM
+    sent = jnp.concatenate([terms[count : 2 * count], terms[3 * count :]], axis=0)
     came = swap_core(sent).astype(f32)
-    own = partial[:count].astype(f32) + came[:count]
-    other = partial[2 * count : 3 * count].astype(f32) + came[count:]
+    own = terms[:count].astype(f32) + came[:count]
+    other = terms[2 * count : 3 * count].astype(f32) + came[count:]
     return own + swap_chip(other.astype(bf16)).astype(f32)
 
 
@@ -78,72 +84,23 @@
     return lax.dynamic_index_in_dim(blocks, index, axis=0, keepdims=False)
 
 
-def swap_group(values):
-    return lax.ppermute(values, "g", [(0, 1), (1, 0)])
-
-
-def line_gather(block):
-    place = lax.axis_index("s")
-    right, left = [block], [block]
-    for step in range(1, 4):
-        right.append(lax.ppermute(right[-1], "s", [(i, i + 1) for i in range(step - 1, 3)]))
-        left.append(lax.ppermute(left[-1], "s", [(i + 1, i) for i in range(4 - step)]))
-    blocks = [block] + [jnp.where(place >= k, right[k], left[4 - k]) for k in range(1, 4)]
-    return blocks, [lax.rem(place + 4 - k, 4) for k in range(4)]
-
-
-def line_scatter(blocks):
-    place = lax.axis_index("s")
-    total = take(blocks, place).astype(f32)
-    for sign in (1, -1):
-        came = None
-        for step in range(1, 4):
-            sent = take(blocks, jnp.clip(place + sign * (4 - step), 0, 3))
-            if came is not None:
-                sent = (sent.astype(f32) + came.astype(f32)).astype(bf16)
-            if sign == 1:
-                pairs = [(i, i + 1) for i in range(step)]
-            else:
-                pairs = [(i, i - 1) for i in range(4 - step, 4)]
-            came = lax.ppermute(sent, "s", pairs)
-        total = total + came.astype(f32)
-    return total
-
-
-def gather_first(shard, unpack):
-    groups, slots = lax.axis_size("g"), lax.axis_size("s")
-    if groups == 2 and slots == 4:
-        low = lax.axis_index("g") == 0
-        other = swap_group(shard)
-        both = jnp.stack([jnp.where(low, shard, other), jnp.where(low, other, shard)])
-        results = [jnp.zeros((2, 4) + part.shape, part.dtype) for part in unpack(shard)]
-        for block, source in zip(*line_gather(both)):
-            results = [
-                lax.dynamic_update_slice(
-                    whole, part[:, None], (0, source) + (0,) * (part.ndim - 1)
-                )
-                for whole, part in zip(results, jax.vmap(unpack)(block))
-            ]
-        return results
-    every = lax.all_gather(shard, ("g", "s"), axis=0, tiled=False)
-    results = jax.vmap(unpack)(every)
-    return [part.reshape((groups, slots) + part.shape[1:]) for part in results]
-
-
 def scatter_first(part):
     groups, slots = part.shape[:2]
-    if groups == 2 and slots == 4:
-        row = lax.axis_index("g")
-        came = swap_group(take(part, 1 - row))
-        return line_scatter((take(part, row).astype(f32) + came.astype(f32)).astype(bf16))
+    if groups == 2:
+        row = lax.axis_index("y")
+        came = swap_row(take(part, 1 - row))
+        summed = (take(part, row).astype(f32) + came.astype(f32)).astype(bf16)
+        return lax.psum_scatter(summed, "s", scatter_dimension=0, tiled=False)
     flat = part.reshape((groups * slots,) + part.shape[2:]).astype(f32)
-    return lax.psum_scatter(flat, ("g", "s"), scatter_dimension=0, tiled=False)
+    return lax.psum_scatter(flat, ("g", "y", "s"), scatter_dimension=0, tiled=False)
 
 
 def scatter_rest(part):
-    if part.shape[0] > 8:
-        part = part.astype(f32)
-    return lax.psum_scatter(part, ("g", "s"), scatter_dimension=0, tiled=False)
+    if lax.axis_size("g") > 1:
+        return lax.psum_scatter(
+            part.astype(f32), ("g", "s"), scatter_dimension=0, tiled=False
+        )
+    return lax.psum_scatter(part, "s", scatter_dimension=0, tiled=False)
 
 
 def feed_forward_kernel(
@@ -209,6 +166,102 @@
     )(normed, grad, gate_full, up_full, down_full)
 
 
+def crew_rows(rows):
+    half = rows.shape[1] // 2
+    left, right = rows[:, :half], rows[:, half:]
+    left_x = swap_chip(left)
+    right_y = swap_row(right)
+    left_y = swap_row(jnp.concatenate([left, left_x], axis=0))
+    right_x = swap_chip(jnp.concatenate([right, right_y], axis=0))
+    count = rows.shape[0]
+    core = jnp.concatenate(
+        [
+            rows,
+            jnp.concatenate([left_x, right_x[:count]], axis=1),
+            jnp.concatenate([left_y[:count], right_y], axis=1),
+            jnp.concatenate([left_y[count:], right_x[count:]], axis=1),
+        ],
+        axis=0,
+    )
+    return jnp.concatenate([core, swap_core(core)], axis=0)
+
+
+def crew_sum(terms):
+    count = terms.shape[0] // CREW
+    half = terms.shape[1] // 2
+    came = swap_core(terms[4 * count :])
+    both = terms[: 4 * count].astype(f32) + came.astype(f32)
+    own, x_rows, y_rows, xy_rows = [both[k * count : (k + 1) * count] for k in range(4)]
+    sent_y = jnp.concatenate([y_rows[:, :half], xy_rows[:, :half]], axis=0).astype(bf16)
+    sent_x = jnp.concatenate([x_rows[:, half:], xy_rows[:, half:]], axis=0).astype(bf16)
+    came_y = swap_row(sent_y).astype(f32)
+    came_x = swap_chip(sent_x).astype(f32)
+    last_x = swap_chip((x_rows[:, :half] + came_y[count:]).astype(bf16)).astype(f32)
+    last_y = swap_row((y_rows[:, half:] + came_x[count:]).astype(bf16)).astype(f32)
+    left = own[:, :half] + came_y[:count] + last_x
+    right = own[:, half:] + came_x[:count] + last_y
+    return jnp.concatenate([left, right], axis=1), sent_y
+
+
+def weight_grad_kernel(steps, count, *refs):
+    token_ref, operands, outs, sums = refs[0], refs[1:-6], refs[-6:-3], refs[-3:]
+    del token_ref
+    step = pl.program_id(0)
+
+    @pl.when(step == 0)
+    def _():
+        for total in sums:
+            total[...] = jnp.zeros_like(total)
+
+    for m in range(count):
+        normed, grad, hidden, gate_grad, up_grad = operands[5 * m : 5 * m + 5]
+
+        @pl.when(step // steps == m)
+        def _():
+            sums[0][...] += rows_dot(normed[...], gate_grad[...])
+            sums[1][...] += rows_dot(normed[...], up_grad[...])
+            sums[2][...] += rows_dot(hidden[...], grad[...])
+
+    @pl.when(step == count * steps - 1)
+    def _():
+        for out, total in zip(outs, sums):
+            out[...] = total[...].astype(out.dtype)
+
+
+def weight_grads(token, operands):
+    count = len(operands)
+    rows, features = operands[0][0].shape
+    width = operands[0][2].shape[1]
+    tile = min(ROW_TILE, rows)
+    steps = rows // tile
+
+    def row_block(m, columns):
+        return pl.BlockSpec(
+            (tile, columns), lambda i: (jnp.clip(i - m * steps, 0, steps - 1), 0)
+        )
+
+    def whole(shape):
+        return pl.BlockSpec(shape, lambda i: (0, 0))
+
+    shapes = [(features, width), (features, width), (width, features)]
+    columns = (features, features, width, width, width)
+    return pl.pallas_call(
+        partial(weight_grad_kernel, steps, count),
+        grid=(count * steps,),
+        in_specs=[whole(token.shape)]
+        + [row_block(m, size) for m in range(count) for size in columns],
+        out_specs=[whole(shape) for shape in shapes],
+        out_shape=[jax.ShapeDtypeStruct(shape, bf16) for shape in shapes],
+        scratch_shapes=[pltpu.VMEM(shape, f32) for shape in shapes],
+        compiler_params=pltpu.CompilerParams(vmem_limit_bytes=52 * 1024 * 1024),
+        cost_estimate=pl.CostEstimate(
+            flops=6 * count * rows * features * width,
+            bytes_accessed=count * rows * (4 * features + 6 * width) + 6 * features * width,
+            transcendentals=0,
+        ),
+    )(token, *[value for group in operands for value in group])
+
+
 def shifted_down(rows, step):
     return jnp.concatenate(
         [jnp.zeros((step, rows.shape[1]), rows.dtype), rows[:-step]], axis=0
@@ -249,36 +302,39 @@
     hidden_share = down_weight.shape[0]
     hidden_width = gate_weight.shape[1]
     taps = conv_weight.shape[0]
-    groups = lax.axis_size("g")
+    outer = lax.axis_size("g")
+    groups = outer * lax.axis_size("y")
     slots = lax.axis_size("s")
     chan_run = slots * share
     hid_run = slots * hidden_share
     chan = groups * chan_run
-    hid = groups * hid_run
-
-    def by_place(weight, parts, run):
-        split = weight.reshape(share, parts, groups, TEAM, run)
-        return jnp.transpose(split, (3, 0, 1, 2, 4)).reshape(TEAM, share, parts * groups * run)
+    hid = outer * hid_run
+
+    def by_place(weight, parts, team, run):
+        count = weight.shape[1] // (parts * team * run)
+        split = weight.reshape(share, parts, count, team, run)
+        return jnp.transpose(split, (3, 0, 1, 2, 4)).reshape(team, share, parts * count * run)
 
     def side_by_side(block, width):
         return jnp.concatenate(
-            [block[..., j * share : (j + 1) * share, :width] for j in range(TEAM)], axis=-1
+            [block[..., j * share : (j + 1) * share, :width] for j in range(features // width)],
+            axis=-1,
         )
 
     def stacked(block, width):
         return jnp.concatenate(
-            [block[..., j * width : (j + 1) * width] for j in range(TEAM)], axis=-2
-        )
-
-    in_blocks = by_place(in_weight, 3, chan_run)
+            [block[..., j * width : (j + 1) * width] for j in range(features // width)], axis=-2
+        )
+
+    in_blocks = by_place(in_weight, 3, TEAM, chan_run)
     in_mine = jnp.concatenate(exchange([in_blocks[j] for j in range(TEAM)]), axis=0)
     gains = jnp.concatenate([norm_gain, ffn_gain]).reshape(1, 2 * share)
     near_gains = team_rows(gains)
     gains_row = jnp.concatenate(reorder([near_gains[j : j + 1] for j in range(TEAM)]), axis=1)
     pair_blocks = jnp.concatenate(
-        [by_place(gate_weight, 1, hid_run), by_place(up_weight, 1, hid_run)], axis=2
-    )
-    pair_mine = jnp.concatenate(exchange([pair_blocks[j] for j in range(TEAM)]), axis=0)
+        [by_place(gate_weight, 1, CREW, hid_run), by_place(up_weight, 1, CREW, hid_run)], axis=2
+    )
+    pair_mine = jnp.concatenate(exchange([pair_blocks[j] for j in range(CREW)]), axis=0)
 
     def as_row(values):
         return jnp.pad(values, ((0, 0), (0, features - values.shape[1])))
@@ -302,10 +358,14 @@
             block[tall + 1, : 2 * tall].reshape(TEAM, 2, share),
         ]
 
-    in_all, out_all, conv_all, gains_all = gather_first(first_pack, first_unpack)
+    first_all = lax.all_gather(first_pack, ("g", "y", "s"), axis=0, tiled=False)
+    in_all, out_all, conv_all, gains_all = [
+        part.reshape((groups, slots) + part.shape[1:]) for part in jax.vmap(first_unpack)(first_all)
+    ]
 
     full = 2 * hid // features
     rest = 2 * hid - full * features
+    rest_tall = CREW * share
 
     def rest_pack(pair, down):
         blocks = [pair[..., k * features : (k + 1) * features] for k in range(full)]
@@ -314,8 +374,8 @@
         return jnp.concatenate(blocks + [down], axis=-2)
 
     def rest_unpack(packed):
-        blocks = [packed[..., k * tall : (k + 1) * tall, :] for k in range(full)]
-        base = full * tall
+        blocks = [packed[..., k * rest_tall : (k + 1) * rest_tall, :] for k in range(full)]
+        base = full * rest_tall
         if rest:
             blocks.append(stacked(packed[..., base : base + share, :], rest))
             base += share
@@ -328,7 +388,7 @@
 
     def natural(gathered):
         width = gathered.shape[-1]
-        split = gathered.reshape(groups, slots, TEAM, share, width)
+        split = gathered.reshape(outer, slots, CREW, share, width)
         return jnp.transpose(split, (0, 2, 1, 3, 4)).reshape(features, width)
 
     in_full = jnp.transpose(in_all, (0, 2, 1, 3, 4)).reshape(features, 3 * chan)
@@ -345,7 +405,7 @@
     team_places = [team_rows(positions[m][:, None]) for m in each]
     live = [(positions[m] >= 0).astype(f32)[:, None] for m in each]
     upstream = [cotangent[m].astype(f32) for m in each]
-    ffn_grad = [team_rows((live[m] * upstream[m]).astype(bf16)) for m in each]
+    ffn_grad = [crew_rows((live[m] * upstream[m]).astype(bf16)) for m in each]
     inputs = [tokens[m].astype(f32) for m in each]
 
     def mixer(m):
@@ -356,7 +416,7 @@
         c_part = projected[:, chan : 2 * chan]
         x_part = projected[:, 2 * chan :]
         mixed = b_part * x_part
-        mask_one = (team_places[m] >= 1).astype(f32)
+        mask_one = after((team_places[m] >= 1).astype(f32), ffn_grad[m][-1:])
         mask_two = (team_places[m] >= 2).astype(f32)
         mixed_one = mask_one * shifted_down(mixed, 1)
         mixed_two = mask_two * shifted_down(mixed, 2)
@@ -364,17 +424,17 @@
         mixer_in = (c_part * convolved).astype(bf16)
         middle = inputs[m] + live[m] * team_sum(forward_dot(mixer_in, out_full).astype(bf16))
         second_scale = inverse_rms(middle)
-        second_normed = team_rows((middle * second_scale * ffn_full).astype(bf16))
+        second_normed = crew_rows((middle * second_scale * ffn_full).astype(bf16))
         kept = (first_normed, b_part, c_part, x_part, mixed, mixed_one, mixed_two)
         return kept + (mask_one, mask_two, convolved, mixer_in), middle, second_scale, second_normed
 
     def feed(m, second_normed):
         return feed_forward(second_normed, ffn_grad[m], gate_full, up_full, down_full)
 
-    def mixer_back(m, kept, middle, second_scale, normed_grad):
+    def mixer_back(m, kept, middle, second_scale, normed_sum):
         first_normed, b_part, c_part, x_part, mixed, mixed_one, mixed_two = kept[:7]
         mask_one, mask_two, convolved, mixer_in = kept[7:]
-        second_weighted = ffn_full * team_sum(normed_grad)
+        second_weighted = ffn_full * normed_sum
         middle_grad = upstream[m] + norm_back(middle, second_scale, second_weighted)
         mixer_grad = team_rows((live[m] * middle_grad).astype(bf16))
         mixer_in_grad = back_dot(mixer_grad, out_full)
@@ -397,10 +457,11 @@
         )
         return middle_grad, mixer_grad, projected_grad, grad_conv
 
-    def by_owner(grad):
+    def by_owner(grad, team):
         width = grad.shape[-1]
-        split = grad.astype(bf16).reshape(groups, TEAM, slots, share, width)
-        return jnp.transpose(split, (0, 2, 1, 3, 4)).reshape(groups, slots, tall, width)
+        count = features // (team * slots * share)
+        split = grad.astype(bf16).reshape(count, team, slots, share, width)
+        return jnp.transpose(split, (0, 2, 1, 3, 4)).reshape(count, slots, team * share, width)
 
     def total(terms):
         return reduce(jnp.add, terms)
@@ -409,26 +470,27 @@
     hidden, gate_grad, up_grad, out_part, normed_grad = zip(
         *[feed(m, second_normed[m]) for m in each]
     )
+    normed_sum, sent = zip(*[crew_sum(normed_grad[m]) for m in each])
+
+    gate_part, up_part, down_part = weight_grads(
+        sum([sent[m][:16, :128] for m in each]),
+        [
+            (second_normed[m], ffn_grad[m], hidden[m], gate_grad[m], up_grad[m])
+            for m in each
+        ],
+    )
+    pair_part = jnp.concatenate([by_owner(gate_part, CREW), by_owner(up_part, CREW)], axis=3)
+    owners = outer * slots
+    rest_part = rest_pack(
+        pair_part.reshape(owners, rest_tall, 2 * hid),
+        down_part.reshape(owners, hidden_share, features),
+    )
     middle_grad, mixer_grad, projected_grad, conv_parts = zip(
-        *[mixer_back(m, kept[m], middle[m], second_scale[m], normed_grad[m]) for m in each]
-    )
-
-    pair_part = jnp.concatenate(
-        [
-            by_owner(total([rows_dot(second_normed[m], gate_grad[m]) for m in each])),
-            by_owner(total([rows_dot(second_normed[m], up_grad[m]) for m in each])),
-        ],
-        axis=3,
-    )
-    down_part = total([rows_dot(hidden[m], ffn_grad[m]) for m in each]).astype(bf16)
-    owners = groups * slots
-    rest_part = rest_pack(
-        pair_part.reshape(owners, tall, 2 * hid),
-        down_part.reshape(owners, hidden_share, features),
+        *[mixer_back(m, kept[m], middle[m], second_scale[m], normed_sum[m]) for m in each]
     )
     pair_sum, down_sum = rest_unpack(scatter_rest(rest_part))
 
-    in_part = by_owner(total([rows_dot(kept[m][0], projected_grad[m]) for m in each]))
+    in_part = by_owner(total([rows_dot(kept[m][0], projected_grad[m]) for m in each]), TEAM)
     out_grad_part = total([rows_dot(kept[m][10], mixer_grad[m]) for m in each]).astype(bf16)
     out_grad_part = stacked(out_grad_part.reshape(groups, slots, share, features), chan)
     conv_rows = jnp.transpose(
@@ -445,7 +507,12 @@
     )
 
     block_out = jnp.stack(
-        [(middle[m] + live[m] * team_sum(out_part[m])).astype(bf16) for m in each]
+        [
+            (
+                middle[m] + live[m] * crew_sum(after(out_part[m], mixer_grad[-1][-1:]))[0]
+            ).astype(bf16)
+            for m in each
+        ]
     )
     input_grads = []
     for m in each:
@@ -455,18 +522,16 @@
             (middle_grad[m] + norm_back(inputs[m], scale, weighted)).astype(bf16)
         )
 
-    def own_rows(summed, parts, run):
-        blocks = [
-            summed[j * share : (j + 1) * share].astype(bf16) for j in range(TEAM)
-        ]
-        came = [block.reshape(share, parts, groups, 1, run) for block in exchange(blocks)]
+    def own_rows(summed, parts, team, run):
+        blocks = [summed[j * share : (j + 1) * share].astype(bf16) for j in range(team)]
+        came = [block.reshape(share, parts, -1, 1, run) for block in exchange(blocks)]
         joined = jnp.concatenate(came, axis=3)
-        return joined.reshape(share, parts * groups * TEAM * run).astype(f32)
-
-    pair_rows = own_rows(pair_sum, 2, hid_run)
+        return joined.reshape(share, -1).astype(f32)
+
+    pair_rows = own_rows(pair_sum, 2, CREW, hid_run)
     gate_rows = pair_rows[:, :hidden_width]
     up_rows = pair_rows[:, hidden_width:]
-    in_rows = own_rows(first_sum[:tall, : 3 * chan], 3, chan_run)
+    in_rows = own_rows(first_sum[:tall, : 3 * chan], 3, TEAM, chan_run)
     grad_out = side_by_side(first_sum[:tall, 3 * chan :], chan).astype(f32)
     grad_conv = first_sum[tall, : taps * share].reshape(taps, share).astype(f32)
     grad_norm_gain = jnp.sum(in_weight.astype(f32) * in_rows, axis=1) / norm_gain.astype(f32)
@@ -488,11 +553,9 @@
 
 
 def solution(mesh):
-    groups = mesh.shape["dp"] // TEAM
-    teams = Mesh(
-        mesh.devices.reshape(groups, 2, 2, mesh.shape["shard"]), ("g", "x", "c", "s")
-    )
-    every = ("g", "x", "c", "s")
+    every = ("g", "y", "x", "c", "s")
+    outer = mesh.shape["dp"] // CREW
+    teams = Mesh(mesh.devices.reshape(outer, 2, 2, 2, mesh.shape["shard"]), every)
     return jax.shard_map(
         per_device,
         mesh=teams,

time: 625 us -> 616 us (0.986)
  waiting for transfers between devices: 286 us -> 177 us
  other arithmetic: 68.5 us -> 133 us
  Pallas kernels: 44.9 us -> 79.3 us
  matrix products: 63.1 us -> 35.1 us
  local copies, waits for them, and re-layouts: 71.4 us -> 88 us
  starting transfers between devices: 65.8 us -> 74.1 us
    ppermute x18 -> x37, waiting for transfers between devices: 145 us -> 61.9 us  [the longest x17 58.2 us: swap_row(): return lax.ppermute(values, 'y', [(0, 1), (1, 0)])]
    concatenate x12 -> x21, other arithmetic: 8.7 us -> 54.8 us  [the longest x4 46.1 us: crew_rows(): jnp.concatenate([rows, jnp.concatenate([left_x, right_x[:count]], axis=1)...]
    ppermute x23 -> x27, waiting for transfers between devices: 138 us -> 99.1 us  [swap_chip(): return lax.ppermute(values, 'x', [(0, 1), (1, 0)])]
    dot_general x10 -> x4, matrix products: 41.3 us -> 11.8 us  [rows_dot(): lax.dot_general(left_side, right_side, (((0,), (0,)), ((), ())), preferre...]
    pallas_call x0 -> x1, Pallas kernels: none -> 26.1 us  [weight_grads(): pl.pallas_call(partial(weight_grad_kernel, steps, count), grid=(count * s...]
    all_gather x1, waiting for transfers between devices: 0.01 us -> 15.4 us  [per_device(): lax.all_gather(rest_pack(pair_mine, down_weight), ('g', 's'), axis=0, til...]
    concatenate x1 -> x13, local copies, waits for them, and re-layouts: 0.03 us -> 10.6 us  [the longest x4 6.75 us: crew_rows(): return jnp.concatenate([core, swap_core(core)], axis=0)]
    squeeze x16 -> x0, local copies, waits for them, and re-layouts: 10.1 us -> none  [gather_first(): part[:, None]]
  transfers between devices with their start and end apart: 77 -> 94, of which waited for: 34 -> 38; matrix products, arithmetic and copies ran while one was open for 24% -> 32% of each run, Pallas kernels for 0% -> 13%
where the time goes in v2:
time: 616 us; the launch traced here: 606 us
  waiting for transfers between devices  177 us (29%)
  other arithmetic  133 us (22%)
  local copies, waits for them, and re-layouts  88 us (14%)
  Pallas kernels  79.3 us (13%)
  starting transfers between devices  74.1 us (12%)
  matrix products  35.1 us (6%)
  between operations  19.1 us (3%)
    ppermute x27, waiting for transfers between devices, swap_chip(): return lax.ppermute(values, 'x', [(0, 1), (1, 0)])  99.1 us
    ppermute x17, waiting for transfers between devices, swap_row(): return lax.ppermute(values, 'y', [(0, 1), (1, 0)])  58.2 us
    pallas_call x2, Pallas kernels, feed_forward(): pl.pallas_call(feed_forward_kernel, grid=(rows // tile,), in_specs=[row_b...  53.2 us
    concatenate x4, other arithmetic, crew_rows(): jnp.concatenate([rows, jnp.concatenate([left_x, right_x[:count]], axis=1)...  46.1 us
    ppermute x27, starting transfers between devices, swap_chip(): return lax.ppermute(values, 'x', [(0, 1), (1, 0)])  28.9 us
    unnamed x313, local copies, waits for them, and re-layouts  26.3 us
    pallas_call x1, Pallas kernels, weight_grads(): pl.pallas_call(partial(weight_grad_kernel, steps, count), grid=(count * s...  26.1 us
    ppermute x17, starting transfers between devices, swap_row(): return lax.ppermute(values, 'y', [(0, 1), (1, 0)])  21.6 us
  transfers between devices with their start and end apart: 94, of which 38 were waited for; matrix products, arithmetic and copies ran while one was open for 32% of the time, Pallas kernels for 13%

profile of v2, /device:TPU:0, one launch (start us, length us, event | category | flops | bytes accessed | tf_op | source)
XLA Modules:
  0.0 606.1 jit_solution(15730433627476710500)
XLA Ops:
  8.5 2.5 collective-permute-start.6
  20.5 3.1 broadcast_select_fusion.16
  31.4 1.8 collective-permute-start.4
  49.9 4.9 collective-permute-done.13
  56.4 7.4 %collective-permute-done.12 = bf16[256,512]{1,0:T(8,128)(2,1)S(1)} collective-permute-done((bf16[256,512]{1,0:T(8,128)(2,1)}, bf16[256,512]{1,0:T(8,128)(2,1)S(1)}, u32[]{:S(2)}, u32[]{:S(2)}) %collective-permute-start.12) | collective-permute-done | bytes 262176 | tf_op jit(solution)/shard_map/ppermute | solution.py:40
  66.2 3.2 collective-permute-done.37
  72.2 8.4 %collective-permute-done.14 = bf16[512,512]{1,0:T(8,128)(2,1)S(1)} collective-permute-done((bf16[512,512]{1,0:T(8,128)(2,1)S(1)}, bf16[512,512]{1,0:T(8,128)(2,1)S(1)}, u32[]{:S(2)}, u32[]{:S(2)}) %collective-permute-start.14) | collective-permute-done | bytes 524320 | tf_op jit(solution)/shard_map/ppermute | solution.py:40
  83.3 12.1 %maximum_maximum_fusion = bf16[1024,1024]{1,0:T(8,128)(2,1)} fusion(bf16[256,512]{1,0:T(8,128)(2,1)S(1)} %get-tuple-element.236, bf16[256,512]{1,0:T(8,128)(2,1)S(1)} %get-tuple-element.238, bf16[256,512]{1,0:T(8,128)(2,1)S(1)} %collective-permute-done.13, bf16[256,512]{1,0:T(8,128)(2,1)S(1)} %get-tuple-element.237, ...), kind=kLoop, calls=%fused_computation.23 | loop fusion | flops 14680064 | bytes 4194304 | tf_op jit(solution)/shard_map/concatenate | solution.py:177
  95.4 7.4 %collective-permute-done.39 = bf16[512,512]{1,0:T(8,128)(2,1)S(1)} collective-permute-done((bf16[512,512]{1,0:T(8,128)(2,1)S(1)}, bf16[512,512]{1,0:T(8,128)(2,1)S(1)}, u32[]{:S(2)}, u32[]{:S(2)}) %collective-permute-start.39) | collective-permute-done | bytes 524320 | tf_op jit(solution)/shard_map/ppermute | solution.py:40
  102.9 11.8 %maximum_maximum_fusion.2 = bf16[1024,1024]{1,0:T(8,128)(2,1)} fusion(bf16[256,512]{1,0:T(8,128)(2,1)S(1)} %get-tuple-element.248, bf16[256,512]{1,0:T(8,128)(2,1)S(1)} %get-tuple-element.250, bf16[256,512]{1,0:T(8,128)(2,1)S(1)} %collective-permute-done.38, bf16[256,512]{1,0:T(8,128)(2,1)S(1)} %get-tuple-element.249, ...), kind=kLoop, calls=%fused_computation.26 | loop fusion | flops 14680064 | bytes 4194304 | tf_op jit(solution)/shard_map/concatenate | solution.py:177
  117.0 1.9 maximum_dynamic-update-slice_fusion.11
  120.4 2.0 fusion.1
  122.4 2.1 fusion.4
  134.1 4.8 fusion.40
  139.1 4.7 fusion.43
  144.5 2.5 multiply_convert_fusion.11
  154.3 1.8 constant_dynamic-update-slice_fusion.2.grad_ref.refs_2_
  156.1 3.3 constant_dynamic-update-slice_fusion.30.grad_ref.refs_7_
  159.4 1.9 copy-done.90
  166.1 2.8 convert_element_type.444
  171.5 15.4 %all-gather.7.cloned.1.call-done = bf16[1728,1024]{1,0:T(8,128)(2,1)} async-done(((bf16[432,1024]{1,0:T(8,128)(2,1)}), bf16[1728,1024]{1,0:T(8,128)(2,1)}) %all-gather.7.cloned.1.call-update) | async-done | bytes 3538960 | tf_op jit(solution)/shard_map/all_gather | solution.py:384
  190.8 2.9 multiply_reduce_fusion.9
  197.1 5.3 collective-permute-done.45
  206.9 6.1 %collective-permute-done.20 = bf16[256,512]{1,0:T(8,128)(2,1)S(1)} collective-permute-done((bf16[256,512]{1,0:T(8,128)(2,1)S(1)}, bf16[256,512]{1,0:T(8,128)(2,1)S(1)}, u32[]{:S(2)}, u32[]{:S(2)}) %collective-permute-start.20) | collective-permute-done | bytes 262176 | tf_op jit(solution)/shard_map/ppermute | solution.py:44
  214.0 3.4 collective-permute-done.46
  217.4 4.2 collective-permute-done.47
  221.6 11.1 %maximum_maximum_fusion.3 = bf16[1024,1024]{1,0:T(8,128)(2,1)S(1)} fusion(bf16[256,512]{1,0:T(8,128)(2,1)S(1)} %get-tuple-element.243, bf16[256,512]{1,0:T(8,128)(2,1)S(1)} %get-tuple-element.241, bf16[256,512]{1,0:T(8,128)(2,1)S(1)} %collective-permute-done.45, bf16[256,512]{1,0:T(8,128)(2,1)S(1)} %get-tuple-element.242, ...), kind=kLoop, calls=%fused_computation.27 | loop fusion | flops 14680064 | bytes 4194304 | tf_op jit(solution)/shard_map/concatenate | solution.py:177
  238.3 9.4 %collective-permute-done.22 = bf16[512,512]{1,0:T(8,128)(2,1)S(1)} collective-permute-done((bf16[512,512]{1,0:T(8,128)(2,1)S(1)}, bf16[512,512]{1,0:T(8,128)(2,1)S(1)}, u32[]{:S(2)}, u32[]{:S(2)}) %collective-permute-start.22) | collective-permute-done | bytes 524320 | tf_op jit(solution)/shard_map/ppermute | solution.py:44
  247.7 11.1 %maximum_maximum_fusion.1 = bf16[1024,1024]{1,0:T(8,128)(2,1)S(1)} fusion(bf16[256,512]{1,0:T(8,128)(2,1)S(1)} %get-tuple-element.231, bf16[256,512]{1,0:T(8,128)(2,1)S(1)} %get-tuple-element.229, bf16[256,512]{1,0:T(8,128)(2,1)S(1)} %collective-permute-done.20, bf16[256,512]{1,0:T(8,128)(2,1)S(1)} %get-tuple-element.230, ...), kind=kLoop, calls=%fused_computation.24 | loop fusion | flops 14680064 | bytes 4194304 | tf_op jit(solution)/shard_map/concatenate | solution.py:177
  261.9 1.9 copy-done.86
  263.8 26.4 %shard_map.187 = (bf16[2048,576]{1,0:T(8,128)(2,1)}, bf16[2048,576]{1,0:T(8,128)(2,1)}, bf16[2048,576]{1,0:T(8,128)(2,1)}, bf16[2048,1024]{1,0:T(8,128)(2,1)}, bf16[2048,1024]{1,0:T(8,128)(2,1)}) custom-call(bf16[2048,1024]{1,0:T(8,128)(2,1)} %copy-done.86, bf16[2048,1024]{1,0:T(8,128)(2,1)} %copy-done.90, bf16[1024,576]{1,0:T(8,128)(2,1)} %bitcast.210, ...), custom_call_target="tpu_custom_call" | custom-call | flops 14495514624 | bytes 27394048 | tf_op jit(solution)/shard_map/pallas_call | solution.py:148
  290.2 3.1 slice.908
  295.3 26.8 %shard_map.186 = (bf16[2048,576]{1,0:T(8,128)(2,1)}, bf16[2048,576]{1,0:T(8,128)(2,1)}, bf16[2048,576]{1,0:T(8,128)(2,1)}, bf16[2048,1024]{1,0:T(8,128)(2,1)}, bf16[2048,1024]{1,0:T(8,128)(2,1)}) custom-call(bf16[2048,1024]{1,0:T(8,128)(2,1)} %constant_dynamic-update-slice_fusion.normed_ref.refs_1_, bf16[2048,1024]{1,0:T(8,128)(2,1)} %copy-done.88, ...), custom_call_target="tpu_custom_call" | custom-call | flops 14495514624 | bytes 27394048 | tf_op jit(solution)/shard_map/pallas_call | solution.py:148
  322.1 1.9 slice.945
  331.8 9.1 %collective-permute-done.52 = bf16[512,512]{1,0:T(8,128)(2,1)S(1)} collective-permute-done((bf16[512,512]{1,0:T(8,128)(2,1)S(1)}, bf16[512,512]{1,0:T(8,128)(2,1)S(1)}, u32[]{:S(2)}, u32[]{:S(2)}) %collective-permute-start.52) | collective-permute-done | bytes 524320 | tf_op jit(solution)/shard_map/ppermute | solution.py:40
  345.2 7.0 %collective-permute-done.69 = bf16[512,512]{1,0:T(8,128)(2,1)S(1)} collective-permute-done((bf16[512,512]{1,0:T(8,128)(2,1)S(1)}, bf16[512,512]{1,0:T(8,128)(2,1)S(1)}, u32[]{:S(2)}, u32[]{:S(2)}) %collective-permute-start.69) | collective-permute-done | bytes 524320 | tf_op jit(solution)/shard_map/ppermute | solution.py:40
  358.9 3.7 collective-permute-done.68
  363.6 2.3 multiply_convert_fusion.6
  371.3 9.8 %collective-permute-done.72 = bf16[256,1024]{1,0:T(8,128)(2,1)} collective-permute-done((bf16[256,1024]{1,0:T(8,128)(2,1)}, bf16[256,1024]{1,0:T(8,128)(2,1)}, u32[]{:S(2)}, u32[]{:S(2)}) %collective-permute-start.72) | collective-permute-done | bytes 524320 | tf_op jit(solution)/shard_map/ppermute | solution.py:40
  381.1 26.1 %shard_map.188 = (bf16[1024,576]{1,0:T(8,128)(2,1)}, bf16[1024,576]{1,0:T(8,128)(2,1)}, bf16[576,1024]{1,0:T(8,128)(2,1)S(1)}) custom-call(bf16[16,128]{1,0:T(8,128)(2,1)S(1)} %slice_add_fusion.24.refs_0_, bf16[2048,1024]{1,0:T(8,128)(2,1)} %constant_dynamic-update-slice_fusion.normed_ref.refs_1_, bf16[2048,1024]{1,0:T(8,128)(2,1)} %copy-done.88, ...), custom_call_target="tpu_custom_call" | custom-call | flops 14495514624 | bytes 34471936 | tf_op jit(solution)/shard_map/pallas_call | solution.py:248
  407.2 2.7 copy.333
  409.9 2.5 copy.334
  413.0 4.1 multiply_reduce_fusion.5
  419.1 2.5 fusion.67
  421.7 2.1 fusion.9
  424.6 4.6 multiply_reduce_fusion.2
  442.3 3.4 fusion.38
  445.8 3.7 add_convert_fusion
  452.5 2.2 maximum_bitcast_fusion
  458.6 20.7 %collective-permute-done.79 = bf16[4,144,1024]{2,1,0:T(8,128)(2,1)S(1)} collective-permute-done((bf16[4,144,1024]{2,1,0:T(8,128)(2,1)S(1)}, bf16[4,144,1024]{2,1,0:T(8,128)(2,1)S(1)}, u32[]{:S(2)}, u32[]{:S(2)}) %collective-permute-start.79) | collective-permute-done | bytes 1179680 | tf_op jit(solution)/shard_map/ppermute | solution.py:44
  481.9 3.1 slice.1197
  486.6 1.8 convolution_convert_fusion.3
  490.9 1.8 convolution_convert_fusion.2
  495.2 3.3 pad_maximum_fusion
  500.4 2.5 broadcast_add_fusion
  511.4 8.8 %collective-permute-done.75 = bf16[256,1024]{1,0:T(8,128)(2,1)S(1)} collective-permute-done((bf16[256,1024]{1,0:T(8,128)(2,1)S(1)}, bf16[256,1024]{1,0:T(8,128)(2,1)S(1)}, u32[]{:S(2)}, u32[]{:S(2)}) %collective-permute-start.75) | collective-permute-done | bytes 524320 | tf_op jit(solution)/shard_map/ppermute | solution.py:40
  520.1 10.5 %collective-permute-done.78 = bf16[256,1024]{1,0:T(8,128)(2,1)S(1)} collective-permute-done((bf16[256,1024]{1,0:T(8,128)(2,1)S(1)}, bf16[256,1024]{1,0:T(8,128)(2,1)S(1)}, u32[]{:S(2)}, u32[]{:S(2)}) %collective-permute-start.78) | collective-permute-done | bytes 524320 | tf_op jit(solution)/shard_map/ppermute | solution.py:40
  540.2 7.4 %collective-permute-done.64 = bf16[512,512]{1,0:T(8,128)(2,1)S(1)} collective-permute-done((bf16[512,512]{1,0:T(8,128)(2,1)S(1)}, bf16[512,512]{1,0:T(8,128)(2,1)S(1)}, u32[]{:S(2)}, u32[]{:S(2)}) %collective-permute-start.64) | collective-permute-done | bytes 524320 | tf_op jit(solution)/shard_map/ppermute | solution.py:40
  551.6 7.2 %collective-permute-done.59 = bf16[512,512]{1,0:T(8,128)(2,1)S(1)} collective-permute-done((bf16[512,512]{1,0:T(8,128)(2,1)S(1)}, bf16[512,512]{1,0:T(8,128)(2,1)S(1)}, u32[]{:S(2)}, u32[]{:S(2)}) %collective-permute-start.59) | collective-permute-done | bytes 524320 | tf_op jit(solution)/shard_map/ppermute | solution.py:40
  566.3 2.1 collective-permute-done.58
  580.9 2.4 collective-permute-start.83
  588.1 1.8 fusion.73
  589.9 2.6 collective-permute-done.84
  593.9 2.9 concatenate.385
  (713 shorter events, 202.8 us)
Async XLA Ops:
  7.2 121.2 %all-gather.5.cloned.1.call-start = ((), (), s32[]{:S(2)}) async-start(), calls=%async_computation.4 | async-start | bytes 2654208 | tf_op jit(solution)/shard_map/all_gather | solution.py:361
  8.1 21.8 %collective-permute-start.8 = (bf16[1,64]{1,0:T(2,128)(2,1)S(1)}, bf16[1,64]{1,0:T(2,128)(2,1)S(1)}, u32[]{:S(2)}, u32[]{:S(2)}) collective-permute-start(bf16[1,64]{1,0:T(2,128)(2,1)S(1)} %maximum_bitcast_fusion.1), channel_id=1, source_target_pairs={{0,4},{4,0},{1,5},{5,1},{2,6},{6,2},{3,7},{7,3},{8,12},{12,8},{9,1... | collective-permute-start | bytes 392 | tf_op jit(solution)/shard_map/ppermute | solution.py:36
  8.5 21.1 %collective-permute-start.6 = (bf16[1,64]{1,0:T(2,128)(2,1)S(1)}, bf16[1,64]{1,0:T(2,128)(2,1)S(1)}, u32[]{:S(2)}, u32[]{:S(2)}) collective-permute-start(bf16[1,64]{1,0:T(2,128)(2,1)S(1)} %maximum_bitcast_fusion.1), channel_id=1, source_target_pairs={{0,8},{8,0},{1,9},{9,1},{2,10},{10,2},{3,11},{11,3},{4,12},{12,4},... | collective-permute-start | bytes 392 | tf_op jit(solution)/shard_map/ppermute | solution.py:40
  11.8 19.2 %collective-permute-start.10 = (s32[256,1]{0,1:T(1,128)S(1)}, s32[256,1]{0,1:T(1,128)S(1)}, u32[]{:S(2)}, u32[]{:S(2)}) collective-permute-start(s32[256,1]{0,1:T(1,128)S(1)} %get-tuple-element.297), channel_id=1, source_target_pairs={{0,8},{8,0},{1,9},{9,1},{2,10},{10,2},{3,11},{11,3},{4,12},{12,4},... | collective-permute-start | bytes 3080 | tf_op jit(solution)/shard_map/ppermute | solution.py:40
  11.9 19.4 %collective-permute-start.9 = (s32[256,1]{0,1:T(1,128)S(1)}, s32[256,1]{0,1:T(1,128)S(1)}, u32[]{:S(2)}, u32[]{:S(2)}) collective-permute-start(s32[256,1]{0,1:T(1,128)S(1)} %get-tuple-element.297), channel_id=1, source_target_pairs={{0,4},{4,0},{1,5},{5,1},{2,6},{6,2},{3,7},{7,3},{8,12},{12,8},{9,1... | collective-permute-start | bytes 3080 | tf_op jit(solution)/shard_map/ppermute | solution.py:36
  12.1 21.1 %collective-permute-start.35 = (s32[256,1]{0,1:T(1,128)S(1)}, s32[256,1]{0,1:T(1,128)S(1)}, u32[]{:S(2)}, u32[]{:S(2)}) collective-permute-start(s32[256,1]{0,1:T(1,128)S(1)} %get-tuple-element.298), channel_id=1, source_target_pairs={{0,8},{8,0},{1,9},{9,1},{2,10},{10,2},{3,11},{11,3},{4,12},{12,4},... | collective-permute-start | bytes 3080 | tf_op jit(solution)/shard_map/ppermute | solution.py:40
  43.1 143.8 %all-gather.7.cloned.1.call-start = ((), (), s32[]{:S(2)}) async-start(), calls=%async_computation.5 | async-start | bytes 4423680 | tf_op jit(solution)/shard_map/all_gather | solution.py:384
  43.2 72.2 %collective-permute-start.1 = (bf16[256,1024]{1,0:T(8,128)(2,1)}, bf16[256,1024]{1,0:T(8,128)(2,1)}, u32[]{:S(2)}, u32[]{:S(2)}) collective-permute-start(bf16[256,1024]{1,0:T(8,128)(2,1)} %get-tuple-element.212), channel_id=1, source_target_pairs={{0,8},{8,0},{1,9},{9,1},{2,10},{10,2},{3,11},{11,3},{4,12},{12,4},... | collective-permute-start | bytes 1572872 | tf_op jit(solution)/shard_map/ppermute | solution.py:40
  43.8 20.0 %collective-permute-start.12 = (bf16[256,512]{1,0:T(8,128)(2,1)}, bf16[256,512]{1,0:T(8,128)(2,1)S(1)}, u32[]{:S(2)}, u32[]{:S(2)}) collective-permute-start(bf16[256,512]{1,0:T(8,128)(2,1)} %get-tuple-element.239), channel_id=1, source_target_pairs={{0,8},{8,0},{1,9},{9,1},{2,10},{10,2},{3,11},{11,3},{4,12},{12,4},... | collective-permute-start | bytes 786440 | tf_op jit(solution)/shard_map/ppermute | solution.py:40
  45.3 9.4 %collective-permute-start.13 = (bf16[256,512]{1,0:T(8,128)(2,1)}, bf16[256,512]{1,0:T(8,128)(2,1)S(1)}, u32[]{:S(2)}, u32[]{:S(2)}) collective-permute-start(bf16[256,512]{1,0:T(8,128)(2,1)} %get-tuple-element.240), channel_id=1, source_target_pairs={{0,16},{16,0},{1,17},{17,1},{2,18},{18,2},{3,19},{19,3},{4,20},{20... | collective-permute-start | bytes 786440 | tf_op jit(solution)/shard_map/ppermute | solution.py:44
  46.6 22.8 %collective-permute-start.37 = (bf16[256,512]{1,0:T(8,128)(2,1)}, bf16[256,512]{1,0:T(8,128)(2,1)S(1)}, u32[]{:S(2)}, u32[]{:S(2)}) collective-permute-start(bf16[256,512]{1,0:T(8,128)(2,1)} %get-tuple-element.251), channel_id=1, source_target_pairs={{0,8},{8,0},{1,9},{9,1},{2,10},{10,2},{3,11},{11,3},{4,12},{12,4},... | collective-permute-start | bytes 786440 | tf_op jit(solution)/shard_map/ppermute | solution.py:40
  47.6 22.9 %collective-permute-start.38 = (bf16[256,512]{1,0:T(8,128)(2,1)}, bf16[256,512]{1,0:T(8,128)(2,1)S(1)}, u32[]{:S(2)}, u32[]{:S(2)}) collective-permute-start(bf16[256,512]{1,0:T(8,128)(2,1)} %get-tuple-element.252), channel_id=1, source_target_pairs={{0,16},{16,0},{1,17},{17,1},{2,18},{18,2},{3,19},{19,3},{4,20},{20... | collective-permute-start | bytes 786440 | tf_op jit(solution)/shard_map/ppermute | solution.py:44
  55.8 24.8 %collective-permute-start.14 = (bf16[512,512]{1,0:T(8,128)(2,1)S(1)}, bf16[512,512]{1,0:T(8,128)(2,1)S(1)}, u32[]{:S(2)}, u32[]{:S(2)}) collective-permute-start(bf16[512,512]{1,0:T(8,128)(2,1)S(1)} %pad_maximum_fusion.19), channel_id=1, source_target_pairs={{0,8},{8,0},{1,9},{9,1},{2,10},{10,2},{3,11},{11,3},{4,12},{12,4},... | collective-permute-start | bytes 1572872 | tf_op jit(solution)/shard_map/ppermute | solution.py:40
  64.8 17.0 %collective-permute-start.15 = (bf16[512,512]{1,0:T(8,128)(2,1)S(1)}, bf16[512,512]{1,0:T(8,128)(2,1)S(1)}, u32[]{:S(2)}, u32[]{:S(2)}) collective-permute-start(bf16[512,512]{1,0:T(8,128)(2,1)S(1)} %pad_maximum_fusion.20), channel_id=1, source_target_pairs={{0,16},{16,0},{1,17},{17,1},{2,18},{18,2},{3,19},{19,3},{4,20},{20... | collective-permute-start | bytes 1572872 | tf_op jit(solution)/shard_map/ppermute | solution.py:44
  69.4 49.5 %collective-permute-start = (bf16[256,1024]{1,0:T(8,128)(2,1)}, bf16[256,1024]{1,0:T(8,128)(2,1)}, u32[]{:S(2)}, u32[]{:S(2)}) collective-permute-start(bf16[256,1024]{1,0:T(8,128)(2,1)} %get-tuple-element.212), channel_id=1, source_target_pairs={{0,4},{4,0},{1,5},{5,1},{2,6},{6,2},{3,7},{7,3},{8,12},{12,8},{9,1... | collective-permute-start | bytes 1572872 | tf_op jit(solution)/shard_map/ppermute | solution.py:36
  70.5 48.9 %collective-permute-start.32 = (bf16[256,1024]{1,0:T(8,128)(2,1)}, bf16[256,1024]{1,0:T(8,128)(2,1)}, u32[]{:S(2)}, u32[]{:S(2)}) collective-permute-start(bf16[256,1024]{1,0:T(8,128)(2,1)} %get-tuple-element.213), channel_id=1, source_target_pairs={{0,8},{8,0},{1,9},{9,1},{2,10},{10,2},{3,11},{11,3},{4,12},{12,4},... | collective-permute-start | bytes 1572872 | tf_op jit(solution)/shard_map/ppermute | solution.py:40
  80.7 22.1 %collective-permute-start.39 = (bf16[512,512]{1,0:T(8,128)(2,1)S(1)}, bf16[512,512]{1,0:T(8,128)(2,1)S(1)}, u32[]{:S(2)}, u32[]{:S(2)}) collective-permute-start(bf16[512,512]{1,0:T(8,128)(2,1)S(1)} %pad_maximum_fusion.24), channel_id=1, source_target_pairs={{0,8},{8,0},{1,9},{9,1},{2,10},{10,2},{3,11},{11,3},{4,12},{12,4},... | collective-permute-start | bytes 1572872 | tf_op jit(solution)/shard_map/ppermute | solution.py:40
  81.8 21.1 %collective-permute-start.40 = (bf16[512,512]{1,0:T(8,128)(2,1)S(1)}, bf16[512,512]{1,0:T(8,128)(2,1)S(1)}, u32[]{:S(2)}, u32[]{:S(2)}) collective-permute-start(bf16[512,512]{1,0:T(8,128)(2,1)S(1)} %pad_maximum_fusion.25), channel_id=1, source_target_pairs={{0,16},{16,0},{1,17},{17,1},{2,18},{18,2},{3,19},{19,3},{4,20},{20... | collective-permute-start | bytes 1572872 | tf_op jit(solution)/shard_map/ppermute | solution.py:44
  102.7 21.8 %collective-permute-start.16 = (bf16[1024,1024]{1,0:T(8,128)(2,1)}, bf16[1024,1024]{1,0:T(8,128)(2,1)}, u32[]{:S(2)}, u32[]{:S(2)}) collective-permute-start(bf16[1024,1024]{1,0:T(8,128)(2,1)} %maximum_maximum_fusion), channel_id=1, source_target_pairs={{0,4},{4,0},{1,5},{5,1},{2,6},{6,2},{3,7},{7,3},{8,12},{12,8},{9,1... | collective-permute-start | bytes 6291464 | tf_op jit(solution)/shard_map/ppermute | solution.py:36
  114.8 11.7 %collective-permute-start.41 = (bf16[1024,1024]{1,0:T(8,128)(2,1)}, bf16[1024,1024]{1,0:T(8,128)(2,1)}, u32[]{:S(2)}, u32[]{:S(2)}) collective-permute-start(bf16[1024,1024]{1,0:T(8,128)(2,1)} %maximum_maximum_fusion.2), channel_id=1, source_target_pairs={{0,4},{4,0},{1,5},{5,1},{2,6},{6,2},{3,7},{7,3},{8,12},{12,8},{9,1... | collective-permute-start | bytes 6291464 | tf_op jit(solution)/shard_map/ppermute | solution.py:36
  116.5 454.6 %reduce-scatter.3.cloned.1.call-start = ((), (), s32[]{:S(2)}) async-start(), calls=%async_computation.2 | async-start | bytes 1474560 | tf_op jit(solution)/shard_map/reduce_scatter | solution.py:93
  148.9 12.4 %collective-permute-start.17 = (bf16[512,1024]{1,0:T(8,128)(2,1)}, bf16[512,1024]{1,0:T(8,128)(2,1)}, u32[]{:S(2)}, u32[]{:S(2)}) collective-permute-start(bf16[512,1024]{1,0:T(8,128)(2,1)} %pad_maximum_fusion.8), channel_id=1, source_target_pairs={{0,4},{4,0},{1,5},{5,1},{2,6},{6,2},{3,7},{7,3},{8,12},{12,8},{9,1... | collective-permute-start | bytes 3145736 | tf_op jit(solution)/shard_map/ppermute | solution.py:36
  151.3 14.8 %collective-permute-start.42 = (bf16[512,1024]{1,0:T(8,128)(2,1)}, bf16[512,1024]{1,0:T(8,128)(2,1)}, u32[]{:S(2)}, u32[]{:S(2)}) collective-permute-start(bf16[512,1024]{1,0:T(8,128)(2,1)} %pad_maximum_fusion.9), channel_id=1, source_target_pairs={{0,4},{4,0},{1,5},{5,1},{2,6},{6,2},{3,7},{7,3},{8,12},{12,8},{9,1... | collective-permute-start | bytes 3145736 | tf_op jit(solution)/shard_map/ppermute | solution.py:36
  165.2 24.1 %collective-permute-start.18 = (bf16[256,1024]{1,0:T(8,128)(2,1)}, bf16[256,1024]{1,0:T(8,128)(2,1)S(1)}, u32[]{:S(2)}, u32[]{:S(2)}) collective-permute-start(bf16[256,1024]{1,0:T(8,128)(2,1)} %fusion.31), channel_id=1, source_target_pairs={{0,8},{8,0},{1,9},{9,1},{2,10},{10,2},{3,11},{11,3},{4,12},{12,4},... | collective-permute-start | bytes 1572872 | tf_op jit(solution)/shard_map/ppermute | solution.py:40
  170.4 20.4 %collective-permute-start.43 = (bf16[256,1024]{1,0:T(8,128)(2,1)S(1)}, bf16[256,1024]{1,0:T(8,128)(2,1)}, u32[]{:S(2)}, u32[]{:S(2)}) collective-permute-start(bf16[256,1024]{1,0:T(8,128)(2,1)S(1)} %fusion.28), channel_id=1, source_target_pairs={{0,8},{8,0},{1,9},{9,1},{2,10},{10,2},{3,11},{11,3},{4,12},{12,4},... | collective-permute-start | bytes 1572872 | tf_op jit(solution)/shard_map/ppermute | solution.py:40
  194.7 7.7 %collective-permute-start.45 = (bf16[256,512]{1,0:T(8,128)(2,1)S(1)}, bf16[256,512]{1,0:T(8,128)(2,1)S(1)}, u32[]{:S(2)}, u32[]{:S(2)}) collective-permute-start(bf16[256,512]{1,0:T(8,128)(2,1)S(1)} %get-tuple-element.246), channel_id=1, source_target_pairs={{0,16},{16,0},{1,17},{17,1},{2,18},{18,2},{3,19},{19,3},{4,20},{20... | collective-permute-start | bytes 786440 | tf_op jit(solution)/shard_map/ppermute | solution.py:44
  195.9 9.4 %collective-permute-start.44 = (bf16[256,512]{1,0:T(8,128)(2,1)S(1)}, bf16[256,512]{1,0:T(8,128)(2,1)S(1)}, u32[]{:S(2)}, u32[]{:S(2)}) collective-permute-start(bf16[256,512]{1,0:T(8,128)(2,1)S(1)} %get-tuple-element.245), channel_id=1, source_target_pairs={{0,8},{8,0},{1,9},{9,1},{2,10},{10,2},{3,11},{11,3},{4,12},{12,4},... | collective-permute-start | bytes 786440 | tf_op jit(solution)/shard_map/ppermute | solution.py:40
  202.5 14.9 %collective-permute-start.46 = (bf16[512,512]{1,0:T(8,128)(2,1)S(1)}, bf16[512,512]{1,0:T(8,128)(2,1)S(1)}, u32[]{:S(2)}, u32[]{:S(2)}) collective-permute-start(bf16[512,512]{1,0:T(8,128)(2,1)S(1)} %pad_maximum_fusion.26), channel_id=1, source_target_pairs={{0,8},{8,0},{1,9},{9,1},{2,10},{10,2},{3,11},{11,3},{4,12},{12,4},... | collective-permute-start | bytes 1572872 | tf_op jit(solution)/shard_map/ppermute | solution.py:40
  203.7 9.3 %collective-permute-start.20 = (bf16[256,512]{1,0:T(8,128)(2,1)S(1)}, bf16[256,512]{1,0:T(8,128)(2,1)S(1)}, u32[]{:S(2)}, u32[]{:S(2)}) collective-permute-start(bf16[256,512]{1,0:T(8,128)(2,1)S(1)} %get-tuple-element.234), channel_id=1, source_target_pairs={{0,16},{16,0},{1,17},{17,1},{2,18},{18,2},{3,19},{19,3},{4,20},{20... | collective-permute-start | bytes 786440 | tf_op jit(solution)/shard_map/ppermute | solution.py:44
  205.3 16.4 %collective-permute-start.47 = (bf16[512,512]{1,0:T(8,128)(2,1)S(1)}, bf16[512,512]{1,0:T(8,128)(2,1)S(1)}, u32[]{:S(2)}, u32[]{:S(2)}) collective-permute-start(bf16[512,512]{1,0:T(8,128)(2,1)S(1)} %pad_maximum_fusion.27), channel_id=1, source_target_pairs={{0,16},{16,0},{1,17},{17,1},{2,18},{18,2},{3,19},{19,3},{4,20},{20... | collective-permute-start | bytes 1572872 | tf_op jit(solution)/shard_map/ppermute | solution.py:44
  205.9 27.4 %collective-permute-start.19 = (bf16[256,512]{1,0:T(8,128)(2,1)S(1)}, bf16[256,512]{1,0:T(8,128)(2,1)S(1)}, u32[]{:S(2)}, u32[]{:S(2)}) collective-permute-start(bf16[256,512]{1,0:T(8,128)(2,1)S(1)} %get-tuple-element.233), channel_id=1, source_target_pairs={{0,8},{8,0},{1,9},{9,1},{2,10},{10,2},{3,11},{11,3},{4,12},{12,4},... | collective-permute-start | bytes 786440 | tf_op jit(solution)/shard_map/ppermute | solution.py:40
  213.0 25.2 %collective-permute-start.21 = (bf16[512,512]{1,0:T(8,128)(2,1)S(1)}, bf16[512,512]{1,0:T(8,128)(2,1)S(1)}, u32[]{:S(2)}, u32[]{:S(2)}) collective-permute-start(bf16[512,512]{1,0:T(8,128)(2,1)S(1)} %pad_maximum_fusion.22), channel_id=1, source_target_pairs={{0,8},{8,0},{1,9},{9,1},{2,10},{10,2},{3,11},{11,3},{4,12},{12,4},... | collective-permute-start | bytes 1572872 | tf_op jit(solution)/shard_map/ppermute | solution.py:40
  232.7 29.0 %collective-permute-start.48 = (bf16[1024,1024]{1,0:T(8,128)(2,1)S(1)}, bf16[1024,1024]{1,0:T(8,128)(2,1)S(1)}, u32[]{:S(2)}, u32[]{:S(2)}) collective-permute-start(bf16[1024,1024]{1,0:T(8,128)(2,1)S(1)} %maximum_maximum_fusion.3), channel_id=1, source_target_pairs={{0,4},{4,0},{1,5},{5,1},{2,6},{6,2},{3,7},{7,3},{8,12},{12,8},{9,1... | collective-permute-start | bytes 6291464 | tf_op jit(solution)/shard_map/ppermute | solution.py:36
  233.3 14.4 %collective-permute-start.22 = (bf16[512,512]{1,0:T(8,128)(2,1)S(1)}, bf16[512,512]{1,0:T(8,128)(2,1)S(1)}, u32[]{:S(2)}, u32[]{:S(2)}) collective-permute-start(bf16[512,512]{1,0:T(8,128)(2,1)S(1)} %pad_maximum_fusion.23), channel_id=1, source_target_pairs={{0,16},{16,0},{1,17},{17,1},{2,18},{18,2},{3,19},{19,3},{4,20},{20... | collective-permute-start | bytes 1572872 | tf_op jit(solution)/shard_map/ppermute | solution.py:44
  258.8 35.0 %collective-permute-start.23 = (bf16[1024,1024]{1,0:T(8,128)(2,1)S(1)}, bf16[1024,1024]{1,0:T(8,128)(2,1)S(1)}, u32[]{:S(2)}, u32[]{:S(2)}) collective-permute-start(bf16[1024,1024]{1,0:T(8,128)(2,1)S(1)} %maximum_maximum_fusion.1), channel_id=1, source_target_pairs={{0,4},{4,0},{1,5},{5,1},{2,6},{6,2},{3,7},{7,3},{8,12},{12,8},{9,1... | collective-permute-start | bytes 6291464 | tf_op jit(solution)/shard_map/ppermute | solution.py:36
  293.3 30.8 %collective-permute-start.49 = (bf16[1024,1024]{1,0:T(8,128)(2,1)}, bf16[1024,1024]{1,0:T(8,128)(2,1)S(1)}, u32[]{:S(2)}, u32[]{:S(2)}) collective-permute-start(bf16[1024,1024]{1,0:T(8,128)(2,1)} %slice.908), channel_id=1, source_target_pairs={{0,4},{4,0},{1,5},{5,1},{2,6},{6,2},{3,7},{7,3},{8,12},{12,8},{9,1... | collective-permute-start | bytes 6291464 | tf_op jit(solution)/shard_map/ppermute | solution.py:36
  326.1 14.8 %collective-permute-start.52 = (bf16[512,512]{1,0:T(8,128)(2,1)S(1)}, bf16[512,512]{1,0:T(8,128)(2,1)S(1)}, u32[]{:S(2)}, u32[]{:S(2)}) collective-permute-start(bf16[512,512]{1,0:T(8,128)(2,1)S(1)} %pad_maximum_fusion.28), channel_id=1, source_target_pairs={{0,8},{8,0},{1,9},{9,1},{2,10},{10,2},{3,11},{11,3},{4,12},{12,4},... | collective-permute-start | bytes 1572872 | tf_op jit(solution)/shard_map/ppermute | solution.py:40
  326.9 14.8 %collective-permute-start.50 = (bf16[512,512]{1,0:T(8,128)(2,1)S(1)}, bf16[512,512]{1,0:T(8,128)(2,1)S(1)}, u32[]{:S(2)}, u32[]{:S(2)}) collective-permute-start(bf16[512,512]{1,0:T(8,128)(2,1)S(1)} %concatenate.386), channel_id=1, source_target_pairs={{0,16},{16,0},{1,17},{17,1},{2,18},{18,2},{3,19},{19,3},{4,20},{20... | collective-permute-start | bytes 1572872 | tf_op jit(solution)/shard_map/ppermute | solution.py:44
  329.6 22.6 %collective-permute-start.69 = (bf16[512,512]{1,0:T(8,128)(2,1)S(1)}, bf16[512,512]{1,0:T(8,128)(2,1)S(1)}, u32[]{:S(2)}, u32[]{:S(2)}) collective-permute-start(bf16[512,512]{1,0:T(8,128)(2,1)S(1)} %pad_maximum_fusion.31), channel_id=1, source_target_pairs={{0,8},{8,0},{1,9},{9,1},{2,10},{10,2},{3,11},{11,3},{4,12},{12,4},... | collective-permute-start | bytes 1572872 | tf_op jit(solution)/shard_map/ppermute | solution.py:40
  331.2 21.8 %collective-permute-start.67 = (bf16[512,512]{1,0:T(8,128)(2,1)S(1)}, bf16[512,512]{1,0:T(8,128)(2,1)S(1)}, u32[]{:S(2)}, u32[]{:S(2)}) collective-permute-start(bf16[512,512]{1,0:T(8,128)(2,1)S(1)} %concatenate.389), channel_id=1, source_target_pairs={{0,16},{16,0},{1,17},{17,1},{2,18},{18,2},{3,19},{19,3},{4,20},{20... | collective-permute-start | bytes 1572872 | tf_op jit(solution)/shard_map/ppermute | solution.py:44
  342.1 15.7 %collective-permute-start.51 = (bf16[256,512]{1,0:T(8,128)(2,1)S(1)}, bf16[256,512]{1,0:T(8,128)(2,1)S(1)}, u32[]{:S(2)}, u32[]{:S(2)}) collective-permute-start(bf16[256,512]{1,0:T(8,128)(2,1)S(1)} %get-tuple-element.176), channel_id=1, source_target_pairs={{0,8},{8,0},{1,9},{9,1},{2,10},{10,2},{3,11},{11,3},{4,12},{12,4},... | collective-permute-start | bytes 786440 | tf_op jit(solution)/shard_map/ppermute | solution.py:40
  343.5 15.1 %collective-permute-start.53 = (bf16[256,512]{1,0:T(8,128)(2,1)S(1)}, bf16[256,512]{1,0:T(8,128)(2,1)S(1)}, u32[]{:S(2)}, u32[]{:S(2)}) collective-permute-start(bf16[256,512]{1,0:T(8,128)(2,1)S(1)} %get-tuple-element.177), channel_id=1, source_target_pairs={{0,16},{16,0},{1,17},{17,1},{2,18},{18,2},{3,19},{19,3},{4,20},{20... | collective-permute-start | bytes 786440 | tf_op jit(solution)/shard_map/ppermute | solution.py:44
  353.3 9.2 %collective-permute-start.68 = (bf16[256,512]{1,0:T(8,128)(2,1)S(1)}, bf16[256,512]{1,0:T(8,128)(2,1)S(1)}, u32[]{:S(2)}, u32[]{:S(2)}) collective-permute-start(bf16[256,512]{1,0:T(8,128)(2,1)S(1)} %get-tuple-element.180), channel_id=1, source_target_pairs={{0,8},{8,0},{1,9},{9,1},{2,10},{10,2},{3,11},{11,3},{4,12},{12,4},... | collective-permute-start | bytes 786440 | tf_op jit(solution)/shard_map/ppermute | solution.py:40
  354.7 8.2 %collective-permute-start.70 = (bf16[256,512]{1,0:T(8,128)(2,1)S(1)}, bf16[256,512]{1,0:T(8,128)(2,1)S(1)}, u32[]{:S(2)}, u32[]{:S(2)}) collective-permute-start(bf16[256,512]{1,0:T(8,128)(2,1)S(1)} %get-tuple-element.181), channel_id=1, source_target_pairs={{0,16},{16,0},{1,17},{17,1},{2,18},{18,2},{3,19},{19,3},{4,20},{20... | collective-permute-start | bytes 786440 | tf_op jit(solution)/shard_map/ppermute | solution.py:44
  365.9 15.2 %collective-permute-start.72 = (bf16[256,1024]{1,0:T(8,128)(2,1)}, bf16[256,1024]{1,0:T(8,128)(2,1)}, u32[]{:S(2)}, u32[]{:S(2)}) collective-permute-start(bf16[256,1024]{1,0:T(8,128)(2,1)} %get-tuple-element.94), channel_id=1, source_target_pairs={{0,8},{8,0},{1,9},{9,1},{2,10},{10,2},{3,11},{11,3},{4,12},{12,4},... | collective-permute-start | bytes 1572872 | tf_op jit(solution)/shard_map/ppermute | solution.py:40
  370.6 42.4 %collective-permute-start.71 = (bf16[256,1024]{1,0:T(8,128)(2,1)}, bf16[256,1024]{1,0:T(8,128)(2,1)S(1)}, u32[]{:S(2)}, u32[]{:S(2)}) collective-permute-start(bf16[256,1024]{1,0:T(8,128)(2,1)} %get-tuple-element.94), channel_id=1, source_target_pairs={{0,4},{4,0},{1,5},{5,1},{2,6},{6,2},{3,7},{7,3},{8,12},{12,8},{9,1... | collective-permute-start | bytes 1572872 | tf_op jit(solution)/shard_map/ppermute | solution.py:36
  370.6 42.4 %collective-permute-start.54 = (bf16[256,1024]{1,0:T(8,128)(2,1)}, bf16[256,1024]{1,0:T(8,128)(2,1)}, u32[]{:S(2)}, u32[]{:S(2)}) collective-permute-start(bf16[256,1024]{1,0:T(8,128)(2,1)} %get-tuple-element.204), channel_id=1, source_target_pairs={{0,8},{8,0},{1,9},{9,1},{2,10},{10,2},{3,11},{11,3},{4,12},{12,4},... | collective-permute-start | bytes 1572872 | tf_op jit(solution)/shard_map/ppermute | solution.py:40
  381.1 31.9 %collective-permute-start.73 = (bf16[256,1024]{1,0:T(8,128)(2,1)}, bf16[256,1024]{1,0:T(8,128)(2,1)S(1)}, u32[]{:S(2)}, u32[]{:S(2)}) collective-permute-start(bf16[256,1024]{1,0:T(8,128)(2,1)} %collective-permute-done.72), channel_id=1, source_target_pairs={{0,4},{4,0},{1,5},{5,1},{2,6},{6,2},{3,7},{7,3},{8,12},{12,8},{9,1... | collective-permute-start | bytes 1572872 | tf_op jit(solution)/shard_map/ppermute | solution.py:36
  450.9 28.4 %collective-permute-start.79 = (bf16[4,144,1024]{2,1,0:T(8,128)(2,1)S(1)}, bf16[4,144,1024]{2,1,0:T(8,128)(2,1)S(1)}, u32[]{:S(2)}, u32[]{:S(2)}) collective-permute-start(bf16[4,144,1024]{2,1,0:T(8,128)(2,1)S(1)} %dynamic-slice_bitcast_fusion), channel_id=1, source_target_pairs={{0,16},{16,0},{1,17},{17,1},{2,18},{18,2},{3,19},{19,3},{4,20},{20... | collective-permute-start | bytes 3538952 | tf_op jit(solution)/shard_map/ppermute | solution.py:44
  480.9 97.7 %reduce-scatter.5.cloned.1.call-start = ((), (), s32[]{:S(2)}) async-start(), calls=%async_computation.3 | async-start | bytes 4423680 | tf_op jit(solution)/shard_map/reduce_scatter | solution.py:103
  489.6 14.1 %collective-permute-start.74 = (bf16[512,1024]{1,0:T(8,128)(2,1)}, bf16[512,1024]{1,0:T(8,128)(2,1)}, u32[]{:S(2)}, u32[]{:S(2)}) collective-permute-start(bf16[512,1024]{1,0:T(8,128)(2,1)} %pad_maximum_fusion.11), channel_id=1, source_target_pairs={{0,4},{4,0},{1,5},{5,1},{2,6},{6,2},{3,7},{7,3},{8,12},{12,8},{9,1... | collective-permute-start | bytes 3145736 | tf_op jit(solution)/shard_map/ppermute | solution.py:36
  495.2 11.5 %collective-permute-start.77 = (bf16[512,1024]{1,0:T(8,128)(2,1)}, bf16[512,1024]{1,0:T(8,128)(2,1)}, u32[]{:S(2)}, u32[]{:S(2)}) collective-permute-start(bf16[512,1024]{1,0:T(8,128)(2,1)} %pad_maximum_fusion.12), channel_id=1, source_target_pairs={{0,4},{4,0},{1,5},{5,1},{2,6},{6,2},{3,7},{7,3},{8,12},{12,8},{9,1... | collective-permute-start | bytes 3145736 | tf_op jit(solution)/shard_map/ppermute | solution.py:36
  503.1 28.4 %collective-permute-start.61 = (bf16[1024,1024]{1,0:T(8,128)(2,1)S(1)}, bf16[1024,1024]{1,0:T(8,128)(2,1)S(1)}, u32[]{:S(2)}, u32[]{:S(2)}) collective-permute-start(bf16[1024,1024]{1,0:T(8,128)(2,1)S(1)} %slice.1141), channel_id=1, source_target_pairs={{0,4},{4,0},{1,5},{5,1},{2,6},{6,2},{3,7},{7,3},{8,12},{12,8},{9,1... | collective-permute-start | bytes 6291464 | tf_op jit(solution)/shard_map/ppermute | solution.py:36
  505.3 14.8 %collective-permute-start.75 = (bf16[256,1024]{1,0:T(8,128)(2,1)S(1)}, bf16[256,1024]{1,0:T(8,128)(2,1)S(1)}, u32[]{:S(2)}, u32[]{:S(2)}) collective-permute-start(bf16[256,1024]{1,0:T(8,128)(2,1)S(1)} %fusion.25), channel_id=1, source_target_pairs={{0,8},{8,0},{1,9},{9,1},{2,10},{10,2},{3,11},{11,3},{4,12},{12,4},... | collective-permute-start | bytes 1572872 | tf_op jit(solution)/shard_map/ppermute | solution.py:40
  508.6 21.9 %collective-permute-start.78 = (bf16[256,1024]{1,0:T(8,128)(2,1)S(1)}, bf16[256,1024]{1,0:T(8,128)(2,1)S(1)}, u32[]{:S(2)}, u32[]{:S(2)}) collective-permute-start(bf16[256,1024]{1,0:T(8,128)(2,1)S(1)} %fusion.22), channel_id=1, source_target_pairs={{0,8},{8,0},{1,9},{9,1},{2,10},{10,2},{3,11},{11,3},{4,12},{12,4},... | collective-permute-start | bytes 1572872 | tf_op jit(solution)/shard_map/ppermute | solution.py:40
  511.4 24.3 %collective-permute-start.56 = (bf16[1024,1024]{1,0:T(8,128)(2,1)}, bf16[1024,1024]{1,0:T(8,128)(2,1)S(1)}, u32[]{:S(2)}, u32[]{:S(2)}) collective-permute-start(bf16[1024,1024]{1,0:T(8,128)(2,1)} %slice.1129), channel_id=1, source_target_pairs={{0,4},{4,0},{1,5},{5,1},{2,6},{6,2},{3,7},{7,3},{8,12},{12,8},{9,1... | collective-permute-start | bytes 6291464 | tf_op jit(solution)/shard_map/ppermute | solution.py:36
  532.6 14.9 %collective-permute-start.64 = (bf16[512,512]{1,0:T(8,128)(2,1)S(1)}, bf16[512,512]{1,0:T(8,128)(2,1)S(1)}, u32[]{:S(2)}, u32[]{:S(2)}) collective-permute-start(bf16[512,512]{1,0:T(8,128)(2,1)S(1)} %pad_maximum_fusion.30), channel_id=1, source_target_pairs={{0,8},{8,0},{1,9},{9,1},{2,10},{10,2},{3,11},{11,3},{4,12},{12,4},... | collective-permute-start | bytes 1572872 | tf_op jit(solution)/shard_map/ppermute | solution.py:40
  534.0 14.9 %collective-permute-start.62 = (bf16[512,512]{1,0:T(8,128)(2,1)S(1)}, bf16[512,512]{1,0:T(8,128)(2,1)S(1)}, u32[]{:S(2)}, u32[]{:S(2)}) collective-permute-start(bf16[512,512]{1,0:T(8,128)(2,1)S(1)} %concatenate.388), channel_id=1, source_target_pairs={{0,16},{16,0},{1,17},{17,1},{2,18},{18,2},{3,19},{19,3},{4,20},{20... | collective-permute-start | bytes 1572872 | tf_op jit(solution)/shard_map/ppermute | solution.py:44
  537.0 21.8 %collective-permute-start.59 = (bf16[512,512]{1,0:T(8,128)(2,1)S(1)}, bf16[512,512]{1,0:T(8,128)(2,1)S(1)}, u32[]{:S(2)}, u32[]{:S(2)}) collective-permute-start(bf16[512,512]{1,0:T(8,128)(2,1)S(1)} %pad_maximum_fusion.29), channel_id=1, source_target_pairs={{0,8},{8,0},{1,9},{9,1},{2,10},{10,2},{3,11},{11,3},{4,12},{12,4},... | collective-permute-start | bytes 1572872 | tf_op jit(solution)/shard_map/ppermute | solution.py:40
  537.6 22.5 %collective-permute-start.57 = (bf16[512,512]{1,0:T(8,128)(2,1)S(1)}, bf16[512,512]{1,0:T(8,128)(2,1)S(1)}, u32[]{:S(2)}, u32[]{:S(2)}) collective-permute-start(bf16[512,512]{1,0:T(8,128)(2,1)S(1)} %concatenate.387), channel_id=1, source_target_pairs={{0,16},{16,0},{1,17},{17,1},{2,18},{18,2},{3,19},{19,3},{4,20},{20... | collective-permute-start | bytes 1572872 | tf_op jit(solution)/shard_map/ppermute | solution.py:44
  549.3 15.1 %collective-permute-start.63 = (bf16[256,512]{1,0:T(8,128)(2,1)S(1)}, bf16[256,512]{1,0:T(8,128)(2,1)S(1)}, u32[]{:S(2)}, u32[]{:S(2)}) collective-permute-start(bf16[256,512]{1,0:T(8,128)(2,1)S(1)} %get-tuple-element.172), channel_id=1, source_target_pairs={{0,8},{8,0},{1,9},{9,1},{2,10},{10,2},{3,11},{11,3},{4,12},{12,4},... | collective-permute-start | bytes 786440 | tf_op jit(solution)/shard_map/ppermute | solution.py:40
  550.0 15.7 %collective-permute-start.65 = (bf16[256,512]{1,0:T(8,128)(2,1)S(1)}, bf16[256,512]{1,0:T(8,128)(2,1)S(1)}, u32[]{:S(2)}, u32[]{:S(2)}) collective-permute-start(bf16[256,512]{1,0:T(8,128)(2,1)S(1)} %get-tuple-element.173), channel_id=1, source_target_pairs={{0,16},{16,0},{1,17},{17,1},{2,18},{18,2},{3,19},{19,3},{4,20},{20... | collective-permute-start | bytes 786440 | tf_op jit(solution)/shard_map/ppermute | solution.py:44
  560.5 7.9 %collective-permute-start.58 = (bf16[256,512]{1,0:T(8,128)(2,1)S(1)}, bf16[256,512]{1,0:T(8,128)(2,1)S(1)}, u32[]{:S(2)}, u32[]{:S(2)}) collective-permute-start(bf16[256,512]{1,0:T(8,128)(2,1)S(1)} %get-tuple-element.168), channel_id=1, source_target_pairs={{0,8},{8,0},{1,9},{9,1},{2,10},{10,2},{3,11},{11,3},{4,12},{12,4},... | collective-permute-start | bytes 786440 | tf_op jit(solution)/shard_map/ppermute | solution.py:40
  561.3 8.2 %collective-permute-start.60 = (bf16[256,512]{1,0:T(8,128)(2,1)S(1)}, bf16[256,512]{1,0:T(8,128)(2,1)S(1)}, u32[]{:S(2)}, u32[]{:S(2)}) collective-permute-start(bf16[256,512]{1,0:T(8,128)(2,1)S(1)} %get-tuple-element.169), channel_id=1, source_target_pairs={{0,16},{16,0},{1,17},{17,1},{2,18},{18,2},{3,19},{19,3},{4,20},{20... | collective-permute-start | bytes 786440 | tf_op jit(solution)/shard_map/ppermute | solution.py:44
  (169 other events, 1098.6 us)
Sparse Core Ops, SparseCore 0:
  43.2 64.2 all-gather.4
  116.6 70.2 all-gather.6
  481.0 29.3 reduce-scatter.2
  512.6 65.0 reduce-scatter.4

commit v3 on v2

--- a/solution.py
+++ b/solution.py
@@ -1,4 +1,4 @@
-from functools import partial, reduce
+from functools import partial
 
 import jax
 import jax.numpy as jnp
@@ -90,9 +90,10 @@
         row = lax.axis_index("y")
         came = swap_row(take(part, 1 - row))
         summed = (take(part, row).astype(f32) + came.astype(f32)).astype(bf16)
-        return lax.psum_scatter(summed, "s", scatter_dimension=0, tiled=False)
+        return lax.psum_scatter(summed, "s", scatter_dimension=0, tiled=False), summed[0, :1]
     flat = part.reshape((groups * slots,) + part.shape[2:]).astype(f32)
-    return lax.psum_scatter(flat, ("g", "y", "s"), scatter_dimension=0, tiled=False)
+    total = lax.psum_scatter(flat, ("g", "y", "s"), scatter_dimension=0, tiled=False)
+    return total, total[:1]
 
 
 def scatter_rest(part):
@@ -103,18 +104,36 @@
     return lax.psum_scatter(part, "s", scatter_dimension=0, tiled=False)
 
 
-def feed_forward_kernel(
-    normed_ref,
-    grad_ref,
-    gate_ref,
-    up_ref,
-    down_ref,
-    hidden_ref,
-    gate_grad_ref,
-    up_grad_ref,
-    out_ref,
-    normed_grad_ref,
-):
+def feed_forward_kernel(*refs):
+    pieces, (gate_ref, up_ref, down_ref) = refs[:10], refs[10:13]
+    hidden_ref, gate_grad_ref, up_grad_ref, out_ref, normed_grad_ref = refs[13:18]
+    step = pl.program_id(0)
+    half = gate_ref.shape[0] // 2
+    for target, (own, left_x, right_y, left_y, right_x) in zip(
+        refs[18:], (pieces[:5], pieces[5:])
+    ):
+        count = own.shape[0]
+
+        @pl.when(step == 0)
+        def _():
+            target[...] = own[...]
+
+        @pl.when(step == 1)
+        def _():
+            target[:, :half] = left_x[...]
+            target[:, half:] = right_x[:count, :]
+
+        @pl.when(step == 2)
+        def _():
+            target[:, :half] = left_y[:count, :]
+            target[:, half:] = right_y[...]
+
+        @pl.when(step == 3)
+        def _():
+            target[:, :half] = left_y[count:, :]
+            target[:, half:] = right_x[count:, :]
+
+    normed_ref, grad_ref = refs[18:]
     gate_value = forward_dot(normed_ref[...], gate_ref[...])
     up_value = forward_dot(normed_ref[...], up_ref[...])
     sigmoid = jax.nn.sigmoid(gate_value)
@@ -133,79 +152,64 @@
 
 
 def feed_forward(normed, grad, gate_full, up_full, down_full):
-    rows, features = normed.shape
+    count, features = normed[0].shape
     width = gate_full.shape[1]
-    tile = min(ROW_TILE, rows)
 
     def row_block(columns):
-        return pl.BlockSpec((tile, columns), lambda i: (i, 0))
-
-    def whole(shape):
-        return pl.BlockSpec(shape, lambda i: (0, 0))
-
-    wide = jax.ShapeDtypeStruct((rows, width), bf16)
-    model = jax.ShapeDtypeStruct((rows, features), bf16)
+        return pl.BlockSpec((count, columns), lambda i: (i, 0))
+
+    def whole(values):
+        return pl.BlockSpec(values.shape, lambda i: (0, 0), pipeline_mode=pl.Buffered(1))
+
+    wide = jax.ShapeDtypeStruct((4 * count, width), bf16)
+    model = jax.ShapeDtypeStruct((4 * count, features), bf16)
+    operands = [*normed, *grad, gate_full, up_full, down_full]
     return pl.pallas_call(
         feed_forward_kernel,
-        grid=(rows // tile,),
-        in_specs=[
-            row_block(features),
-            row_block(features),
-            whole(gate_full.shape),
-            whole(up_full.shape),
-            whole(down_full.shape),
-        ],
-        out_specs=[row_block(width)] * 3 + [row_block(features)] * 2,
-        out_shape=[wide] * 3 + [model] * 2,
-        compiler_params=pltpu.CompilerParams(vmem_limit_bytes=52 * 1024 * 1024),
+        grid=(4,),
+        in_specs=[whole(values) for values in operands],
+        out_specs=[row_block(width)] * 3 + [row_block(features)] * 4,
+        out_shape=[wide] * 3 + [model] * 4,
+        compiler_params=pltpu.CompilerParams(vmem_limit_bytes=56 * 1024 * 1024),
         cost_estimate=pl.CostEstimate(
-            flops=12 * rows * features * width,
-            bytes_accessed=6 * features * width + 6 * rows * width + 8 * rows * features,
-            transcendentals=rows * width,
+            flops=48 * count * features * width,
+            bytes_accessed=6 * features * width + 24 * count * width + 48 * count * features,
+            transcendentals=4 * count * width,
         ),
-    )(normed, grad, gate_full, up_full, down_full)
-
-
-def crew_rows(rows):
+    )(*operands)
+
+
+def crew_pieces(rows):
     half = rows.shape[1] // 2
     left, right = rows[:, :half], rows[:, half:]
     left_x = swap_chip(left)
     right_y = swap_row(right)
     left_y = swap_row(jnp.concatenate([left, left_x], axis=0))
     right_x = swap_chip(jnp.concatenate([right, right_y], axis=0))
-    count = rows.shape[0]
-    core = jnp.concatenate(
-        [
-            rows,
-            jnp.concatenate([left_x, right_x[:count]], axis=1),
-            jnp.concatenate([left_y[:count], right_y], axis=1),
-            jnp.concatenate([left_y[count:], right_x[count:]], axis=1),
-        ],
-        axis=0,
-    )
-    return jnp.concatenate([core, swap_core(core)], axis=0)
-
-
-def crew_sum(terms):
-    count = terms.shape[0] // CREW
-    half = terms.shape[1] // 2
-    came = swap_core(terms[4 * count :])
-    both = terms[: 4 * count].astype(f32) + came.astype(f32)
+    return [rows, left_x, right_y, left_y, right_x]
+
+
+def crew_sum(mine, theirs, beside):
+    count = mine.shape[0] // 4
+    half = mine.shape[1] // 2
+    both = mine.astype(f32) + swap_core(theirs).astype(f32)
     own, x_rows, y_rows, xy_rows = [both[k * count : (k + 1) * count] for k in range(4)]
     sent_y = jnp.concatenate([y_rows[:, :half], xy_rows[:, :half]], axis=0).astype(bf16)
     sent_x = jnp.concatenate([x_rows[:, half:], xy_rows[:, half:]], axis=0).astype(bf16)
     came_y = swap_row(sent_y).astype(f32)
     came_x = swap_chip(sent_x).astype(f32)
+    token, made = beside(sent_y[:16, :128])
+    if token is not None:
+        came_y, came_x = after(came_y, token), after(came_x, token)
     last_x = swap_chip((x_rows[:, :half] + came_y[count:]).astype(bf16)).astype(f32)
     last_y = swap_row((y_rows[:, half:] + came_x[count:]).astype(bf16)).astype(f32)
     left = own[:, :half] + came_y[:count] + last_x
     right = own[:, half:] + came_x[:count] + last_y
-    return jnp.concatenate([left, right], axis=1), sent_y
-
-
-def weight_grad_kernel(steps, count, *refs):
-    token_ref, operands, outs, sums = refs[0], refs[1:-6], refs[-6:-3], refs[-3:]
-    del token_ref
+    return jnp.concatenate([left, right], axis=1), made
+
+
+def weight_grad_kernel(steps, count, share, *refs):
+    operands, outs, sums = refs[1 : 1 + 5 * count], refs[1 + 5 * count : -3], refs[-3:]
     step = pl.program_id(0)
 
     @pl.when(step == 0)
@@ -224,11 +228,30 @@
 
     @pl.when(step == count * steps - 1)
     def _():
-        for out, total in zip(outs, sums):
-            out[...] = total[...].astype(out.dtype)
-
-
-def weight_grads(token, operands):
+        if len(outs) == 3:
+            for out, total in zip(outs, sums):
+                out[...] = total[...].astype(bf16)
+            return
+        (out,) = outs
+        gate, up, down = sums
+        features, width = gate.shape
+        slots = out.shape[0]
+        hidden_share = width // slots
+        tall = CREW * share
+        rest = 2 * width - features
+        for s in range(slots):
+            for place in range(CREW):
+                rows = pl.ds((place * slots + s) * share, share)
+                at = pl.ds(place * share, share)
+                out[s, at, :width] = gate[rows, :].astype(bf16)
+                out[s, at, width:] = up[rows, : features - width].astype(bf16)
+                out[s, pl.ds(tall, share), place * rest : (place + 1) * rest] = up[
+                    rows, features - width :
+                ].astype(bf16)
+            out[s, tall + share :, :] = down[pl.ds(s * hidden_share, hidden_share), :].astype(bf16)
+
+
+def weight_grads(token, operands, share, slots, packed):
     count = len(operands)
     rows, features = operands[0][0].shape
     width = operands[0][2].shape[1]
@@ -240,19 +263,17 @@
             (tile, columns), lambda i: (jnp.clip(i - m * steps, 0, steps - 1), 0)
         )
 
-    def whole(shape):
-        return pl.BlockSpec(shape, lambda i: (0, 0))
-
-    shapes = [(features, width), (features, width), (width, features)]
+    sums = [(features, width), (features, width), (width, features)]
     columns = (features, features, width, width, width)
+    shapes = [(slots, CREW * share + share + width // slots, features)] if packed else sums
     return pl.pallas_call(
-        partial(weight_grad_kernel, steps, count),
+        partial(weight_grad_kernel, steps, count, share),
         grid=(count * steps,),
-        in_specs=[whole(token.shape)]
+        in_specs=[pl.BlockSpec(token.shape, lambda i: (0, 0))]
         + [row_block(m, size) for m in range(count) for size in columns],
-        out_specs=[whole(shape) for shape in shapes],
+        out_specs=[pl.BlockSpec(shape, lambda i, r=len(shape): (0,) * r) for shape in shapes],
         out_shape=[jax.ShapeDtypeStruct(shape, bf16) for shape in shapes],
-        scratch_shapes=[pltpu.VMEM(shape, f32) for shape in shapes],
+        scratch_shapes=[pltpu.VMEM(size, f32) for size in sums],
         compiler_params=pltpu.CompilerParams(vmem_limit_bytes=52 * 1024 * 1024),
         cost_estimate=pl.CostEstimate(
             flops=6 * count * rows * features * width,
@@ -297,7 +318,9 @@
     up_weight,
     down_weight,
 ):
-    micro, micro_rows, features = tokens.shape
+    shape = tokens.shape
+    features = shape[2]
+    rows = shape[0] * shape[1]
     share = in_weight.shape[0]
     hidden_share = down_weight.shape[0]
     hidden_width = gate_weight.shape[1]
@@ -331,11 +354,6 @@
     gains = jnp.concatenate([norm_gain, ffn_gain]).reshape(1, 2 * share)
     near_gains = team_rows(gains)
     gains_row = jnp.concatenate(reorder([near_gains[j : j + 1] for j in range(TEAM)]), axis=1)
-    pair_blocks = jnp.concatenate(
-        [by_place(gate_weight, 1, CREW, hid_run), by_place(up_weight, 1, CREW, hid_run)], axis=2
-    )
-    pair_mine = jnp.concatenate(exchange([pair_blocks[j] for j in range(CREW)]), axis=0)
-
     def as_row(values):
         return jnp.pad(values, ((0, 0), (0, features - values.shape[1])))
 
@@ -358,6 +376,12 @@
             block[tall + 1, : 2 * tall].reshape(TEAM, 2, share),
         ]
 
+    pair_blocks = jnp.concatenate(
+        [by_place(gate_weight, 1, CREW, hid_run), by_place(up_weight, 1, CREW, hid_run)], axis=2
+    )
+    pair_blocks = after(pair_blocks, first_pack[:1])
+    pair_mine = jnp.concatenate(exchange([pair_blocks[j] for j in range(CREW)]), axis=0)
+
     first_all = lax.all_gather(first_pack, ("g", "y", "s"), axis=0, tiled=False)
     in_all, out_all, conv_all, gains_all = [
         part.reshape((groups, slots) + part.shape[1:]) for part in jax.vmap(first_unpack)(first_all)
@@ -400,62 +424,41 @@
     up_full = natural(pair_all[..., hid:])
     down_full = down_all.reshape(hid, features)
 
-    each = range(micro)
-    team_tokens = [team_rows(tokens[m]) for m in each]
-    team_places = [team_rows(positions[m][:, None]) for m in each]
-    live = [(positions[m] >= 0).astype(f32)[:, None] for m in each]
-    upstream = [cotangent[m].astype(f32) for m in each]
-    ffn_grad = [crew_rows((live[m] * upstream[m]).astype(bf16)) for m in each]
-    inputs = [tokens[m].astype(f32) for m in each]
-
-    def mixer(m):
-        values = team_tokens[m].astype(f32)
-        first_normed = (values * inverse_rms(values) * norm_full).astype(bf16)
-        projected = forward_dot(first_normed, in_full)
-        b_part = projected[:, :chan]
-        c_part = projected[:, chan : 2 * chan]
-        x_part = projected[:, 2 * chan :]
-        mixed = b_part * x_part
-        mask_one = after((team_places[m] >= 1).astype(f32), ffn_grad[m][-1:])
-        mask_two = (team_places[m] >= 2).astype(f32)
-        mixed_one = mask_one * shifted_down(mixed, 1)
-        mixed_two = mask_two * shifted_down(mixed, 2)
-        convolved = conv_full[0] * mixed + conv_full[1] * mixed_one + conv_full[2] * mixed_two
-        mixer_in = (c_part * convolved).astype(bf16)
-        middle = inputs[m] + live[m] * team_sum(forward_dot(mixer_in, out_full).astype(bf16))
-        second_scale = inverse_rms(middle)
-        second_normed = crew_rows((middle * second_scale * ffn_full).astype(bf16))
-        kept = (first_normed, b_part, c_part, x_part, mixed, mixed_one, mixed_two)
-        return kept + (mask_one, mask_two, convolved, mixer_in), middle, second_scale, second_normed
-
-    def feed(m, second_normed):
-        return feed_forward(second_normed, ffn_grad[m], gate_full, up_full, down_full)
-
-    def mixer_back(m, kept, middle, second_scale, normed_sum):
-        first_normed, b_part, c_part, x_part, mixed, mixed_one, mixed_two = kept[:7]
-        mask_one, mask_two, convolved, mixer_in = kept[7:]
-        second_weighted = ffn_full * normed_sum
-        middle_grad = upstream[m] + norm_back(middle, second_scale, second_weighted)
-        mixer_grad = team_rows((live[m] * middle_grad).astype(bf16))
-        mixer_in_grad = back_dot(mixer_grad, out_full)
-        c_grad = mixer_in_grad * convolved
-        conv_grad = mixer_in_grad * c_part
-        mixed_grad = (
-            conv_full[0] * conv_grad
-            + conv_full[1] * shifted_up(mask_one * conv_grad, 1)
-            + conv_full[2] * shifted_up(mask_two * conv_grad, 2)
-        )
-        projected_grad = jnp.concatenate(
-            [mixed_grad * x_part, c_grad, mixed_grad * b_part], axis=1
-        ).astype(bf16)
-        grad_conv = jnp.stack(
-            [
-                jnp.sum(conv_grad * mixed, axis=0),
-                jnp.sum(conv_grad * mixed_one, axis=0),
-                jnp.sum(conv_grad * mixed_two, axis=0),
-            ]
-        )
-        return middle_grad, mixer_grad, projected_grad, grad_conv
+    own_tokens = after(tokens.reshape(rows, features), first_pack[:1])
+    places = positions.reshape(rows, 1)
+    team_tokens = team_rows(own_tokens)
+    team_places = team_rows(places)
+    live = (places >= 0).astype(f32)
+    upstream = cotangent.reshape(rows, features).astype(f32)
+    ffn_pieces = crew_pieces((after(live, own_tokens[:1]) * upstream).astype(bf16))
+    inputs = tokens.reshape(rows, features).astype(f32)
+
+    values = team_tokens.astype(f32)
+    first_normed = (values * inverse_rms(values) * norm_full).astype(bf16)
+    projected = forward_dot(first_normed, in_full)
+    b_part = projected[:, :chan]
+    c_part = projected[:, chan : 2 * chan]
+    x_part = projected[:, 2 * chan :]
+    mixed = b_part * x_part
+    mask_one = (team_places >= 1).astype(f32)
+    mask_two = (team_places >= 2).astype(f32)
+    mixed_one = mask_one * shifted_down(mixed, 1)
+    mixed_two = mask_two * shifted_down(mixed, 2)
+    convolved = conv_full[0] * mixed + conv_full[1] * mixed_one + conv_full[2] * mixed_two
+    mixer_in = (c_part * convolved).astype(bf16)
+    mixer_out = team_sum(forward_dot(mixer_in, out_full).astype(bf16))
+    middle = inputs + after(live, ffn_pieces[3][-1:]) * mixer_out
+    second_scale = inverse_rms(middle)
+    second_pieces = crew_pieces((middle * second_scale * ffn_full).astype(bf16))
+
+    runs = []
+    for normed, grad in (
+        (second_pieces, ffn_pieces),
+        ([swap_core(v) for v in second_pieces], [swap_core(v) for v in ffn_pieces]),
+    ):
+        runs.append(feed_forward(normed, grad, gate_full, up_full, down_full))
+    (_, _, _, out_mine, normed_mine, _, _), (_, _, _, out_theirs, normed_theirs, _, _) = runs
+    owners = outer * slots
 
     def by_owner(grad, team):
         width = grad.shape[-1]
@@ -463,64 +466,65 @@
         split = grad.astype(bf16).reshape(count, team, slots, share, width)
         return jnp.transpose(split, (0, 2, 1, 3, 4)).reshape(count, slots, team * share, width)
 
-    def total(terms):
-        return reduce(jnp.add, terms)
-
-    kept, middle, second_scale, second_normed = zip(*[mixer(m) for m in each])
-    hidden, gate_grad, up_grad, out_part, normed_grad = zip(
-        *[feed(m, second_normed[m]) for m in each]
-    )
-    normed_sum, sent = zip(*[crew_sum(normed_grad[m]) for m in each])
-
-    gate_part, up_part, down_part = weight_grads(
-        sum([sent[m][:16, :128] for m in each]),
+    def rest_grads(token):
+        groups_of = [(run[5], run[6], run[0], run[1], run[2]) for run in runs]
+        if outer == 1 and share % 16 == 0 and hidden_share % 16 == 0:
+            (packed,) = weight_grads(token, groups_of, share, owners, True)
+            return packed[0, :1, :128], packed
+        gate_part, up_part, down_part = weight_grads(token, groups_of, share, owners, False)
+        pair_part = jnp.concatenate([by_owner(gate_part, CREW), by_owner(up_part, CREW)], axis=3)
+        packed = rest_pack(
+            pair_part.reshape(owners, rest_tall, 2 * hid),
+            down_part.reshape(owners, hidden_share, features),
+        )
+        return packed[0, :1], packed
+
+    normed_sum, rest_part = crew_sum(normed_mine, normed_theirs, rest_grads)
+    second_weighted = ffn_full * normed_sum
+    middle_grad = upstream + norm_back(middle, second_scale, second_weighted)
+
+    mixer_grad = team_rows((live * middle_grad).astype(bf16))
+    mixer_in_grad = back_dot(mixer_grad, out_full)
+    c_grad = mixer_in_grad * convolved
+    conv_grad = mixer_in_grad * c_part
+    mixed_grad = (
+        conv_full[0] * conv_grad
+        + conv_full[1] * shifted_up(mask_one * conv_grad, 1)
+        + conv_full[2] * shifted_up(mask_two * conv_grad, 2)
+    )
+    projected_grad = jnp.concatenate(
+        [mixed_grad * x_part, c_grad, mixed_grad * b_part], axis=1
+    ).astype(bf16)
+    grad_conv_part = jnp.stack(
         [
-            (second_normed[m], ffn_grad[m], hidden[m], gate_grad[m], up_grad[m])
-            for m in each
-        ],
-    )
-    pair_part = jnp.concatenate([by_owner(gate_part, CREW), by_owner(up_part, CREW)], axis=3)
-    owners = outer * slots
-    rest_part = rest_pack(
-        pair_part.reshape(owners, rest_tall, 2 * hid),
-        down_part.reshape(owners, hidden_share, features),
-    )
-    middle_grad, mixer_grad, projected_grad, conv_parts = zip(
-        *[mixer_back(m, kept[m], middle[m], second_scale[m], normed_sum[m]) for m in each]
+            jnp.sum(conv_grad * mixed, axis=0),
+            jnp.sum(conv_grad * mixed_one, axis=0),
+            jnp.sum(conv_grad * mixed_two, axis=0),
+        ]
     )
     pair_sum, down_sum = rest_unpack(scatter_rest(rest_part))
 
-    in_part = by_owner(total([rows_dot(kept[m][0], projected_grad[m]) for m in each]), TEAM)
-    out_grad_part = total([rows_dot(kept[m][10], mixer_grad[m]) for m in each]).astype(bf16)
+    in_part = by_owner(rows_dot(first_normed, projected_grad), TEAM)
+    out_grad_part = rows_dot(mixer_in, mixer_grad).astype(bf16)
     out_grad_part = stacked(out_grad_part.reshape(groups, slots, share, features), chan)
     conv_rows = jnp.transpose(
-        total(conv_parts).reshape(taps, groups, slots, share), (1, 2, 0, 3)
+        grad_conv_part.reshape(taps, groups, slots, share), (1, 2, 0, 3)
     ).reshape(groups, slots, 1, taps * share)
     conv_rows = jnp.pad(
         conv_rows.astype(bf16),
         ((0, 0), (0, 0), (0, EXTRA_ROWS - 1), (0, features - taps * share)),
     )
-    first_sum = scatter_first(
+    first_sum, token = scatter_first(
         jnp.concatenate(
             [jnp.concatenate([in_part, out_grad_part], axis=3), conv_rows], axis=2
         )
     )
 
-    block_out = jnp.stack(
-        [
-            (
-                middle[m] + live[m] * crew_sum(after(out_part[m], mixer_grad[-1][-1:]))[0]
-            ).astype(bf16)
-            for m in each
-        ]
-    )
-    input_grads = []
-    for m in each:
-        weighted = norm_full * team_sum(back_dot(projected_grad[m], in_full).astype(bf16))
-        scale = inverse_rms(inputs[m])
-        input_grads.append(
-            (middle_grad[m] + norm_back(inputs[m], scale, weighted)).astype(bf16)
-        )
+    first_weighted = norm_full * team_sum(back_dot(projected_grad, in_full).astype(bf16))
+    input_grad = middle_grad + norm_back(inputs, inverse_rms(inputs), first_weighted)
+    input_grad = input_grad.astype(bf16)
+    out_sum, _ = crew_sum(after(out_mine, token), out_theirs, lambda sent: (None, None))
+    block_out = (middle + live * out_sum).astype(bf16)
 
     def own_rows(summed, parts, team, run):
         blocks = [summed[j * share : (j + 1) * share].astype(bf16) for j in range(team)]
@@ -539,8 +543,8 @@
         gate_weight.astype(f32) * gate_rows + up_weight.astype(f32) * up_rows, axis=1
     ) / ffn_gain.astype(f32)
     return (
-        block_out,
-        jnp.stack(input_grads),
+        block_out.reshape(shape),
+        input_grad.reshape(shape),
         grad_norm_gain,
         in_rows,
         grad_conv,

time: 616 us -> 589 us (0.956)
  waiting for transfers between devices: 177 us -> 233 us
  other arithmetic: 133 us -> 94 us
  starting transfers between devices: 74.1 us -> 47.2 us
  local copies, waits for them, and re-layouts: 88 us -> 66.5 us
    ppermute x27 -> x14, waiting for transfers between devices: 99.1 us -> 150 us  [swap_chip(): return lax.ppermute(values, 'x', [(0, 1), (1, 0)])]
    concatenate x12 -> x4, other arithmetic: 50.4 us -> 4.52 us  [the longest x2 3.4 us: crew_pieces(): right_x = swap_chip(jnp.concatenate([right, right_y], axis=0))]
    all_gather x1, waiting for transfers between devices: 0.02 us -> 22.6 us  [per_device(): first_all = lax.all_gather(first_pack, ('g', 'y', 's'), axis=0, tiled=False)]
    all_gather x1, waiting for transfers between devices: 15.4 us -> 0.01 us  [per_device(): lax.all_gather(rest_pack(pair_mine, down_weight), ('g', 's'), axis=0, til...]
    ppermute x27 -> x14, starting transfers between devices: 28.9 us -> 16.1 us  [swap_chip(): return lax.ppermute(values, 'x', [(0, 1), (1, 0)])]
    ppermute x17 -> x9, starting transfers between devices: 21.6 us -> 9.58 us  [swap_row(): return lax.ppermute(values, 'y', [(0, 1), (1, 0)])]
    ppermute x17 -> x9, waiting for transfers between devices: 58.2 us -> 47.7 us  [swap_row(): return lax.ppermute(values, 'y', [(0, 1), (1, 0)])]
    unnamed x313 -> x176, local copies, waits for them, and re-layouts: 26.3 us -> 16.2 us
  transfers between devices with their start and end apart: 94 -> 69, of which waited for: 38 -> 27; matrix products, arithmetic and copies ran while one was open for 32% -> 21% of each run, Pallas kernels for 13% -> 10%
where the time goes in v3:
time: 589 us; the launch traced here: 579 us
  waiting for transfers between devices  233 us (40%)
  other arithmetic  94 us (16%)
  Pallas kernels  85.4 us (14%)
  local copies, waits for them, and re-layouts  66.5 us (11%)
  starting transfers between devices  47.2 us (8%)
  matrix products  31.9 us (5%)
  between operations  21 us (4%)
    ppermute x14, waiting for transfers between devices, swap_chip(): return lax.ppermute(values, 'x', [(0, 1), (1, 0)])  150 us
    pallas_call x2, Pallas kernels, feed_forward(): pl.pallas_call(feed_forward_kernel, grid=(4,), in_specs=[whole(values) fo...  59 us
    ppermute x9, waiting for transfers between devices, swap_row(): return lax.ppermute(values, 'y', [(0, 1), (1, 0)])  47.7 us
    pallas_call x1, Pallas kernels, weight_grads(): pl.pallas_call(partial(weight_grad_kernel, steps, count, share), grid=(co...  26.4 us
    all_gather x1, waiting for transfers between devices, per_device(): first_all = lax.all_gather(first_pack, ('g', 'y', 's'), axis=0, tiled=False)  22.6 us
    ppermute x20, starting transfers between devices, swap_far(): return lax.ppermute(values, axes, [(i, i ^ distance) for i in range(CREW)])  17 us
    unnamed x176, local copies, waits for them, and re-layouts  16.2 us
    ppermute x14, starting transfers between devices, swap_chip(): return lax.ppermute(values, 'x', [(0, 1), (1, 0)])  16.1 us
  transfers between devices with their start and end apart: 69, of which 27 were waited for; matrix products, arithmetic and copies ran while one was open for 21% of the time, Pallas kernels for 10%

profile of v3, /device:TPU:0, one launch (start us, length us, event | category | flops | bytes accessed | tf_op | source)
XLA Modules:
  0.0 579.0 jit_solution(11263011944597765035)
XLA Ops:
  8.9 2.9 collective-permute-start.8
  14.5 1.7 collective-permute-start
  20.8 1.7 collective-permute-done.1
  24.7 1.6 collective-permute-start.23
  28.1 2.0 collective-permute-start.24
  33.1 1.6 collective-permute-start.6
  34.9 1.7 collective-permute-done.27
  40.6 18.4 %collective-permute-done.6 = bf16[512,1024]{1,0:T(8,128)(2,1)S(1)} collective-permute-done((bf16[512,1024]{1,0:T(8,128)(2,1)S(1)}, bf16[512,1024]{1,0:T(8,128)(2,1)S(1)}, u32[]{:S(2)}, u32[]{:S(2)}) %collective-permute-start.6) | collective-permute-done | bytes 1048608 | tf_op jit(solution)/shard_map/ppermute | solution.py:40
  59.7 1.9 collective-permute-done.7
  63.2 22.6 %all-gather.5.cloned.1.call-done = bf16[1152,1024]{1,0:T(8,128)(2,1)} async-done(((bf16[144,1024]{1,0:T(8,128)(2,1)}), bf16[1152,1024]{1,0:T(8,128)(2,1)}) %all-gather.5.cloned.1.call-update) | async-done | bytes 2359312 | tf_op jit(solution)/shard_map/all_gather | solution.py:385
  90.0 1.8 fusion.69
  97.9 7.7 %fusion.22 = f32[2048,768]{1,0:T(8,128)S(1)} fusion(bf16[1024,768]{1,0:T(8,128)(2,1)} %bitcast.161, f32[1024]{0:T(1024)} %mul.322, f32[2048]{0:T(1024)} %add_rsqrt_fusion, bf16[512,1024]{1,0:T(8,128)(2,1)} %copy-done.39, bf16[512,1024]{1,0:T(8,128)(2,1)S(1)} %collective-permute-done.6, bf16[512,1024]{1,0:T(8,128)(2,1)} %copy-done.37, ...), kind=kOutput, calls=%fused_computation.76 | convolution fusion | flops 3244294144 | bytes 12070912 | tf_op jit(solution)/shard_map/dot_general | solution.py:20
  105.7 2.6 copy-done
  116.3 4.7 multiply_convert_fusion.5
  122.5 1.9 copy-done.1
  131.2 2.1 fusion.70
  134.7 12.8 %collective-permute-done.3.refs_6_ = bf16[512,512]{1,0:T(8,128)(2,1)S(1)} collective-permute-done((bf16[512,512]{1,0:T(8,128)(2,1)S(1)}, bf16[512,512]{1,0:T(8,128)(2,1)S(1)}, u32[]{:S(2)}, u32[]{:S(2)}) %collective-permute-start.3) | collective-permute-done | bytes 524320 | tf_op jit(solution)/shard_map/ppermute | solution.py:40
  148.3 2.0 convert_element_type.301
  150.4 2.5 fusion.10
  152.9 1.5 collective-permute-start.15
  155.8 18.0 %collective-permute-done.4.refs_8_ = bf16[1024,512]{1,0:T(8,128)(2,1)S(1)} collective-permute-done((bf16[1024,512]{1,0:T(8,128)(2,1)S(1)}, bf16[1024,512]{1,0:T(8,128)(2,1)S(1)}, u32[]{:S(2)}, u32[]{:S(2)}) %collective-permute-start.4) | collective-permute-done | bytes 1048608 | tf_op jit(solution)/shard_map/ppermute | solution.py:44
  175.1 2.8 collective-permute-done.15
  177.9 2.9 multiply_reduce_fusion.4
  182.3 2.5 collective-permute-done.20.refs_7_
  184.8 2.2 pad_maximum_fusion.11
  189.6 5.4 collective-permute-done.17.refs_2_
  196.1 25.5 %collective-permute-done.16.refs_1_ = bf16[512,512]{1,0:T(8,128)(2,1)S(1)} collective-permute-done((bf16[512,512]{1,0:T(8,128)(2,1)S(1)}, bf16[512,512]{1,0:T(8,128)(2,1)S(1)}, u32[]{:S(2)}, u32[]{:S(2)}) %collective-permute-start.16) | collective-permute-done | bytes 524320 | tf_op jit(solution)/shard_map/ppermute | solution.py:40
  225.4 1.9 slice.700
  230.1 13.9 %collective-permute-done.19.refs_4_ = bf16[1024,512]{1,0:T(8,128)(2,1)} collective-permute-done((bf16[1024,512]{1,0:T(8,128)(2,1)}, bf16[1024,512]{1,0:T(8,128)(2,1)}, u32[]{:S(2)}, u32[]{:S(2)}) %collective-permute-start.19) | collective-permute-done | bytes 1048608 | tf_op jit(solution)/shard_map/ppermute | solution.py:40
  244.0 2.9 collective-permute-done.18.refs_3_
  252.7 29.5 %shard_map.187 = (bf16[2048,576]{1,0:T(8,128)(2,1)}, bf16[2048,576]{1,0:T(8,128)(2,1)}, bf16[2048,576]{1,0:T(8,128)(2,1)}, bf16[2048,1024]{1,0:T(8,128)(2,1)}, b...) custom-call(bf16[512,1024]{1,0:T(8,128)(2,1)} %copy-done.69, ...), custom_call_target="tpu_custom_call" | custom-call | flops 14495514624 | bytes 35782656 | tf_op jit(solution)/shard_map/pallas_call | solution.py:167
  282.7 29.5 %shard_map.186 = (bf16[2048,576]{1,0:T(8,128)(2,1)}, bf16[2048,576]{1,0:T(8,128)(2,1)}, bf16[2048,576]{1,0:T(8,128)(2,1)}, bf16[2048,1024]{1,0:T(8,128)(2,1)}, b...) custom-call(bf16[512,1024]{1,0:T(8,128)(2,1)} %copy-done.23, ...), custom_call_target="tpu_custom_call" | custom-call | flops 14495514624 | bytes 35782656 | tf_op jit(solution)/shard_map/pallas_call | solution.py:167
  312.3 7.7 %convert_add_fusion.1 = (f32[2048,1024]{1,0:T(8,128)}, bf16[2048,1024]{1,0:T(8,128)(2,1)S(1)}) fusion(bf16[2048,1024]{1,0:T(8,128)(2,1)S(1)} %collective-permute-done.39, bf16[2048,1024]{1,0:T(8,128)(2,1)} %get-tuple-element.25), kind=kLoop, calls=%fused_computation.6 | loop fusion | flops 8388608 | bytes 20971520 | tf_op jit(solution)/shard_map/add | solution.py:195
  323.5 26.4 %shard_map.188 = bf16[4,432,1024]{2,1,0:T(8,128)(2,1)} custom-call(bf16[16,128]{1,0:T(8,128)(2,1)S(1)} %slice.711.refs_0_, bf16[2048,1024]{1,0:T(8,128)(2,1)} %get-tuple-element.27.refs_1_, bf16[2048,1024]{1,0:T(8,128)(2,1)} %get-tuple-element.28.refs_2_, bf16[2048,576]{1,0:T(8,128)(2,1)} %get-tuple-element.29.refs_3_, ...), custom_call_target="tpu_custom_call" | custom-call | flops 14495514624 | bytes 34471936 | tf_op jit(solution)/shard_map/pallas_call | solution.py:269
  354.8 1.9 fusion.30
  359.6 10.5 %collective-permute-done.41 = bf16[512,512]{1,0:T(8,128)(2,1)S(1)} collective-permute-done((bf16[512,512]{1,0:T(8,128)(2,1)S(1)}, bf16[512,512]{1,0:T(8,128)(2,1)S(1)}, u32[]{:S(2)}, u32[]{:S(2)}) %collective-permute-start.41) | collective-permute-done | bytes 524320 | tf_op jit(solution)/shard_map/ppermute | solution.py:40
  371.3 2.2 fusion.31
  375.5 1.6 multiply_convert_fusion.3
  377.7 23.1 %collective-permute-done.45 = bf16[512,1024]{1,0:T(8,128)(2,1)} collective-permute-done((bf16[512,1024]{1,0:T(8,128)(2,1)}, bf16[512,1024]{1,0:T(8,128)(2,1)}, u32[]{:S(2)}, u32[]{:S(2)}) %collective-permute-start.45) | collective-permute-done | bytes 1048608 | tf_op jit(solution)/shard_map/ppermute | solution.py:40
  401.5 2.3 collective-permute-done.46
  403.8 9.3 %multiply_reduce_fusion.2 = (bf16[256]{0:T(256)(128)(2,1)S(1)}, bf16[256]{0:T(256)(128)(2,1)S(1)}, bf16[256]{0:T(256)(128)(2,1)S(1)}, f32[2048,256]{1,0:T(8,128)S(1)}, bf16[2048,256]{1,0:T(8,128)(2,1)S(1)}) fusion(f32[2048,256]{1,0:T(8,128)} %copy-done.6, f32[2046,256]{1,0:T(8,128)} %bitcast.132, f32[2048]{0:T(1024)S(1)} %get-tuple-element.212, ...), kind=kOutput, calls=%fused_computation.49 | convolution fusion | flops 1096285440 | bytes 18364928 | tf_op jit(solution)/shard_map/dot_general | solution.py:30
  414.1 2.5 multiply_convert_fusion.2
  416.7 2.3 multiply_convert_fusion
  420.0 3.8 convolution_convert_fusion.2
  425.4 3.9 convolution_convert_fusion.3
  433.9 5.9 %convolution_convert_fusion.1 = bf16[2048,1024]{1,0:T(8,128)(2,1)S(1)} fusion(bf16[1024,768]{1,0:T(8,128)(2,1)} %bitcast.162, bf16[2048,256]{1,0:T(8,128)(2,1)} %copy-done.34, bf16[2048,256]{1,0:T(8,128)(2,1)} %copy-done.75, bf16[2048,256]{1,0:T(8,128)(2,1)} %copy-done.33), kind=kOutput, calls=%fused_computation.12 | convolution fusion | flops 3232759808 | bytes 8912896 | tf_op jit(solution)/shard_map/dot_general | solution.py:30
  440.0 1.9 copy-done.21
  441.9 1.6 pad_maximum_fusion.4
  443.5 17.4 %collective-permute-done.47 = bf16[4,144,1024]{2,1,0:T(8,128)(2,1)} collective-permute-done((bf16[4,144,1024]{2,1,0:T(8,128)(2,1)}, bf16[4,144,1024]{2,1,0:T(8,128)(2,1)}, u32[]{:S(2)}, u32[]{:S(2)}) %collective-permute-start.47) | collective-permute-done | bytes 1179680 | tf_op jit(solution)/shard_map/ppermute | solution.py:44
  460.9 2.8 fusion.5
  465.6 7.8 %fusion.63 = (bf16[2048,1024]{1,0:T(8,128)(2,1)}, f32[2048,1024]{1,0:T(8,128)S(1)}) fusion(bf16[2048,1024]{1,0:T(8,128)(2,1)} %collective-permute-done.48, bf16[2048,1024]{1,0:T(8,128)(2,1)} %get-tuple-element.24, bf16[]{:T(256)} %bitcast.49), kind=kLoop, calls=%fused_computation.341 | loop fusion | flops 10485760 | bytes 20971522 | tf_op jit(solution)/shard_map/convert.18
  473.4 2.0 fusion.66
  476.1 1.7 concatenate.189
  479.3 2.0 convert_element_type.337
  481.3 3.4 fusion.7
  485.7 16.0 %collective-permute-done.51 = bf16[1024,512]{1,0:T(8,128)(2,1)S(1)} collective-permute-done((bf16[1024,512]{1,0:T(8,128)(2,1)S(1)}, bf16[1024,512]{1,0:T(8,128)(2,1)S(1)}, u32[]{:S(2)}, u32[]{:S(2)}) %collective-permute-start.51) | collective-permute-done | bytes 1048608 | tf_op jit(solution)/shard_map/ppermute | solution.py:40
  502.6 1.6 fusion.26
  506.6 27.1 %collective-permute-done.50 = bf16[512,512]{1,0:T(8,128)(2,1)} collective-permute-done((bf16[512,512]{1,0:T(8,128)(2,1)}, bf16[512,512]{1,0:T(8,128)(2,1)}, u32[]{:S(2)}, u32[]{:S(2)}) %collective-permute-start.50) | collective-permute-done | bytes 524320 | tf_op jit(solution)/shard_map/ppermute | solution.py:40
  533.7 3.1 fusion.27
  536.9 2.3 fusion.17
  539.3 4.0 fusion.20
  545.6 1.8 collective-permute-start.60
  551.8 1.8 fusion.38
  557.3 2.9 concatenate.187
  (437 shorter events, 120.7 us)
Async XLA Ops:
  8.0 77.7 %all-gather.5.cloned.1.call-start = ((), (), s32[]{:S(2)}) async-start(), calls=%async_computation.4 | async-start | bytes 2654208 | tf_op jit(solution)/shard_map/all_gather | solution.py:385
  8.9 9.3 %collective-permute-start.8 = (bf16[1,64]{1,0:T(2,128)(2,1)S(1)}, bf16[1,64]{1,0:T(2,128)(2,1)S(1)}, u32[]{:S(2)}, u32[]{:S(2)}) collective-permute-start(bf16[1,64]{1,0:T(2,128)(2,1)S(1)} %maximum_bitcast_fusion.1), channel_id=1, source_target_pairs={{0,8},{8,0},{1,9},{9,1},{2,10},{10,2},{3,11},{11,3},{4,12},{12,4},... | collective-permute-start | bytes 392 | tf_op jit(solution)/shard_map/ppermute | solution.py:40
  11.8 6.6 %collective-permute-start.10 = (bf16[1,64]{1,0:T(2,128)(2,1)S(1)}, bf16[1,64]{1,0:T(2,128)(2,1)S(1)}, u32[]{:S(2)}, u32[]{:S(2)}) collective-permute-start(bf16[1,64]{1,0:T(2,128)(2,1)S(1)} %maximum_bitcast_fusion.1), channel_id=1, source_target_pairs={{0,4},{4,0},{1,5},{5,1},{2,6},{6,2},{3,7},{7,3},{8,12},{12,8},{9,1... | collective-permute-start | bytes 392 | tf_op jit(solution)/shard_map/ppermute | solution.py:36
  12.5 7.1 %collective-permute-start.12 = (s32[512,1]{0,1:T(1,128)S(1)}, s32[512,1]{0,1:T(1,128)S(1)}, u32[]{:S(2)}, u32[]{:S(2)}) collective-permute-start(s32[512,1]{0,1:T(1,128)S(1)} %bitcast.192), channel_id=1, source_target_pairs={{0,8},{8,0},{1,9},{9,1},{2,10},{10,2},{3,11},{11,3},{4,12},{12,4},... | collective-permute-start | bytes 6152 | tf_op jit(solution)/shard_map/ppermute | solution.py:40
  12.6 7.4 %collective-permute-start.11 = (s32[512,1]{0,1:T(1,128)S(1)}, s32[512,1]{0,1:T(1,128)S(1)}, u32[]{:S(2)}, u32[]{:S(2)}) collective-permute-start(s32[512,1]{0,1:T(1,128)S(1)} %bitcast.193), channel_id=1, source_target_pairs={{0,4},{4,0},{1,5},{5,1},{2,6},{6,2},{3,7},{7,3},{8,12},{12,8},{9,1... | collective-permute-start | bytes 6152 | tf_op jit(solution)/shard_map/ppermute | solution.py:36
  14.5 6.3 %collective-permute-start = (bf16[32,768]{1,0:T(8,128)(2,1)S(1)}, bf16[32,768]{1,0:T(8,128)(2,1)S(1)}, u32[]{:S(2)}, u32[]{:S(2)}) collective-permute-start(bf16[32,768]{1,0:T(8,128)(2,1)S(1)} %select_n.644), channel_id=1, source_target_pairs={{0,12},{4,8},{8,4},{12,0},{16,28},{20,24},{24,20},{28,16},{1,13},{... | collective-permute-start | bytes 147464 | tf_op jit(solution)/shard_map/ppermute | solution.py:49
  18.4 4.1 collective-permute-start.1
  24.7 5.6 collective-permute-start.23
  26.2 5.6 collective-permute-start.25
  27.2 5.9 %collective-permute-start.22 = (bf16[32,1152]{1,0:T(8,128)(2,1)S(1)}, bf16[32,1152]{1,0:T(8,128)(2,1)S(1)}, u32[]{:S(2)}, u32[]{:S(2)}) collective-permute-start(bf16[32,1152]{1,0:T(8,128)(2,1)S(1)} %get-tuple-element.190), channel_id=1, source_target_pairs={{0,28},{4,24},{8,20},{12,16},{16,12},{20,8},{24,4},{28,0},{1,29},{... | collective-permute-start | bytes 221192 | tf_op jit(solution)/shard_map/ppermute | solution.py:49
  28.1 6.6 %collective-permute-start.24 = (bf16[32,1152]{1,0:T(8,128)(2,1)}, bf16[32,1152]{1,0:T(8,128)(2,1)}, u32[]{:S(2)}, u32[]{:S(2)}) collective-permute-start(bf16[32,1152]{1,0:T(8,128)(2,1)} %get-tuple-element.191), channel_id=1, source_target_pairs={{0,20},{4,16},{8,28},{12,24},{16,4},{20,0},{24,12},{28,8},{1,21},{... | collective-permute-start | bytes 221192 | tf_op jit(solution)/shard_map/ppermute | solution.py:49
  30.1 4.8 collective-permute-start.26
  30.3 6.4 %collective-permute-start.27 = (bf16[32,1152]{1,0:T(8,128)(2,1)}, bf16[32,1152]{1,0:T(8,128)(2,1)}, u32[]{:S(2)}, u32[]{:S(2)}) collective-permute-start(bf16[32,1152]{1,0:T(8,128)(2,1)} %get-tuple-element.115), channel_id=1, source_target_pairs={{0,8},{4,12},{8,0},{12,4},{16,24},{20,28},{24,16},{28,20},{1,9},{5... | collective-permute-start | bytes 221192 | tf_op jit(solution)/shard_map/ppermute | solution.py:49
  31.8 4.8 collective-permute-start.28
  33.0 192.3 %all-gather.7.cloned.1.call-start = ((), (), s32[]{:S(2)}) async-start(), calls=%async_computation.5 | async-start | bytes 4423680 | tf_op jit(solution)/shard_map/all_gather | solution.py:408
  33.1 25.9 %collective-permute-start.6 = (bf16[512,1024]{1,0:T(8,128)(2,1)S(1)}, bf16[512,1024]{1,0:T(8,128)(2,1)S(1)}, u32[]{:S(2)}, u32[]{:S(2)}) collective-permute-start(bf16[512,1024]{1,0:T(8,128)(2,1)S(1)} %bitcast.149), channel_id=1, source_target_pairs={{0,8},{8,0},{1,9},{9,1},{2,10},{10,2},{3,11},{11,3},{4,12},{12,4},... | collective-permute-start | bytes 3145736 | tf_op jit(solution)/shard_map/ppermute | solution.py:40
  34.7 24.3 %collective-permute-start.5 = (bf16[512,1024]{1,0:T(8,128)(2,1)S(1)}, bf16[512,1024]{1,0:T(8,128)(2,1)S(1)}, u32[]{:S(2)}, u32[]{:S(2)}) collective-permute-start(bf16[512,1024]{1,0:T(8,128)(2,1)S(1)} %bitcast.150), channel_id=1, source_target_pairs={{0,4},{4,0},{1,5},{5,1},{2,6},{6,2},{3,7},{7,3},{8,12},{12,8},{9,1... | collective-permute-start | bytes 3145736 | tf_op jit(solution)/shard_map/ppermute | solution.py:36
  125.9 22.5 %collective-permute-start.14 = (bf16[1024,1024]{1,0:T(8,128)(2,1)}, bf16[1024,1024]{1,0:T(8,128)(2,1)}, u32[]{:S(2)}, u32[]{:S(2)}) collective-permute-start(bf16[1024,1024]{1,0:T(8,128)(2,1)} %pad_maximum_fusion.3), channel_id=1, source_target_pairs={{0,4},{4,0},{1,5},{5,1},{2,6},{6,2},{3,7},{7,3},{8,12},{12,8},{9,1... | collective-permute-start | bytes 6291464 | tf_op jit(solution)/shard_map/ppermute | solution.py:36
  127.7 415.7 %reduce-scatter.5.cloned.1.call-start = ((), (), s32[]{:S(2)}) async-start(), calls=%async_computation.3 | async-start | bytes 4423680 | tf_op jit(solution)/shard_map/reduce_scatter | solution.py:104
  133.3 14.3 %collective-permute-start.3 = (bf16[512,512]{1,0:T(8,128)(2,1)S(1)}, bf16[512,512]{1,0:T(8,128)(2,1)S(1)}, u32[]{:S(2)}, u32[]{:S(2)}) collective-permute-start(bf16[512,512]{1,0:T(8,128)(2,1)S(1)} %get-tuple-element.153), channel_id=1, source_target_pairs={{0,8},{8,0},{1,9},{9,1},{2,10},{10,2},{3,11},{11,3},{4,12},{12,4},... | collective-permute-start | bytes 1572872 | tf_op jit(solution)/shard_map/ppermute | solution.py:40
  147.6 26.1 %collective-permute-start.4 = (bf16[1024,512]{1,0:T(8,128)(2,1)S(1)}, bf16[1024,512]{1,0:T(8,128)(2,1)S(1)}, u32[]{:S(2)}, u32[]{:S(2)}) collective-permute-start(bf16[1024,512]{1,0:T(8,128)(2,1)S(1)} %pad_maximum_fusion.8), channel_id=1, source_target_pairs={{0,16},{16,0},{1,17},{17,1},{2,18},{18,2},{3,19},{19,3},{4,20},{20... | collective-permute-start | bytes 3145736 | tf_op jit(solution)/shard_map/ppermute | solution.py:44
  152.9 25.0 %collective-permute-start.15 = (bf16[512,1024]{1,0:T(8,128)(2,1)S(1)}, bf16[512,1024]{1,0:T(8,128)(2,1)}, u32[]{:S(2)}, u32[]{:S(2)}) collective-permute-start(bf16[512,1024]{1,0:T(8,128)(2,1)S(1)} %fusion.10), channel_id=1, source_target_pairs={{0,8},{8,0},{1,9},{9,1},{2,10},{10,2},{3,11},{11,3},{4,12},{12,4},... | collective-permute-start | bytes 3145736 | tf_op jit(solution)/shard_map/ppermute | solution.py:40
  154.4 30.4 %collective-permute-start.20 = (bf16[512,512]{1,0:T(8,128)(2,1)}, bf16[512,512]{1,0:T(8,128)(2,1)}, u32[]{:S(2)}, u32[]{:S(2)}) collective-permute-start(bf16[512,512]{1,0:T(8,128)(2,1)} %get-tuple-element.152), channel_id=1, source_target_pairs={{0,16},{16,0},{1,17},{17,1},{2,18},{18,2},{3,19},{19,3},{4,20},{20... | collective-permute-start | bytes 1572872 | tf_op jit(solution)/shard_map/ppermute | solution.py:44
  181.2 13.8 %collective-permute-start.17 = (bf16[512,512]{1,0:T(8,128)(2,1)S(1)}, bf16[512,512]{1,0:T(8,128)(2,1)S(1)}, u32[]{:S(2)}, u32[]{:S(2)}) collective-permute-start(bf16[512,512]{1,0:T(8,128)(2,1)S(1)} %get-tuple-element.154), channel_id=1, source_target_pairs={{0,16},{16,0},{1,17},{17,1},{2,18},{18,2},{3,19},{19,3},{4,20},{20... | collective-permute-start | bytes 1572872 | tf_op jit(solution)/shard_map/ppermute | solution.py:44
  187.0 42.3 %collective-permute-start.21 = (bf16[1024,512]{1,0:T(8,128)(2,1)}, bf16[1024,512]{1,0:T(8,128)(2,1)}, u32[]{:S(2)}, u32[]{:S(2)}) collective-permute-start(bf16[1024,512]{1,0:T(8,128)(2,1)} %pad_maximum_fusion.11), channel_id=1, source_target_pairs={{0,8},{8,0},{1,9},{9,1},{2,10},{10,2},{3,11},{11,3},{4,12},{12,4},... | collective-permute-start | bytes 3145736 | tf_op jit(solution)/shard_map/ppermute | solution.py:40
  188.5 33.1 %collective-permute-start.16 = (bf16[512,512]{1,0:T(8,128)(2,1)S(1)}, bf16[512,512]{1,0:T(8,128)(2,1)S(1)}, u32[]{:S(2)}, u32[]{:S(2)}) collective-permute-start(bf16[512,512]{1,0:T(8,128)(2,1)S(1)} %get-tuple-element.155), channel_id=1, source_target_pairs={{0,8},{8,0},{1,9},{9,1},{2,10},{10,2},{3,11},{11,3},{4,12},{12,4},... | collective-permute-start | bytes 1572872 | tf_op jit(solution)/shard_map/ppermute | solution.py:40
  189.0 35.1 %collective-permute-start.35 = (bf16[512,512]{1,0:T(8,128)(2,1)S(1)}, bf16[512,512]{1,0:T(8,128)(2,1)S(1)}, u32[]{:S(2)}, u32[]{:S(2)}) collective-permute-start(bf16[512,512]{1,0:T(8,128)(2,1)S(1)} %copy-done.43), channel_id=1, source_target_pairs={{0,4},{4,0},{1,5},{5,1},{2,6},{6,2},{3,7},{7,3},{8,12},{12,8},{9,1... | collective-permute-start | bytes 1572872 | tf_op jit(solution)/shard_map/ppermute | solution.py:36
  189.1 40.9 %collective-permute-start.34 = (bf16[512,1024]{1,0:T(8,128)(2,1)}, bf16[512,1024]{1,0:T(8,128)(2,1)}, u32[]{:S(2)}, u32[]{:S(2)}) collective-permute-start(bf16[512,1024]{1,0:T(8,128)(2,1)} %fusion.6.refs_5_), channel_id=1, source_target_pairs={{0,4},{4,0},{1,5},{5,1},{2,6},{6,2},{3,7},{7,3},{8,12},{12,8},{9,1... | collective-permute-start | bytes 3145736 | tf_op jit(solution)/shard_map/ppermute | solution.py:36
  194.9 34.3 %collective-permute-start.36 = (bf16[512,512]{1,0:T(8,128)(2,1)}, bf16[512,512]{1,0:T(8,128)(2,1)}, u32[]{:S(2)}, u32[]{:S(2)}) collective-permute-start(bf16[512,512]{1,0:T(8,128)(2,1)} %collective-permute-done.20.refs_7_), channel_id=1, source_target_pairs={{0,4},{4,0},{1,5},{5,1},{2,6},{6,2},{3,7},{7,3},{8,12},{12,8},{9,1... | collective-permute-start | bytes 1572872 | tf_op jit(solution)/shard_map/ppermute | solution.py:36
  221.6 22.4 %collective-permute-start.19 = (bf16[1024,512]{1,0:T(8,128)(2,1)}, bf16[1024,512]{1,0:T(8,128)(2,1)}, u32[]{:S(2)}, u32[]{:S(2)}) collective-permute-start(bf16[1024,512]{1,0:T(8,128)(2,1)} %pad_maximum_fusion.10), channel_id=1, source_target_pairs={{0,8},{8,0},{1,9},{9,1},{2,10},{10,2},{3,11},{11,3},{4,12},{12,4},... | collective-permute-start | bytes 3145736 | tf_op jit(solution)/shard_map/ppermute | solution.py:40
  224.9 21.9 %collective-permute-start.18 = (bf16[1024,512]{1,0:T(8,128)(2,1)}, bf16[1024,512]{1,0:T(8,128)(2,1)}, u32[]{:S(2)}, u32[]{:S(2)}) collective-permute-start(bf16[1024,512]{1,0:T(8,128)(2,1)} %pad_maximum_fusion.9), channel_id=1, source_target_pairs={{0,16},{16,0},{1,17},{17,1},{2,18},{18,2},{3,19},{19,3},{4,20},{20... | collective-permute-start | bytes 3145736 | tf_op jit(solution)/shard_map/ppermute | solution.py:44
  229.4 17.6 %collective-permute-start.37 = (bf16[1024,512]{1,0:T(8,128)(2,1)S(1)}, bf16[1024,512]{1,0:T(8,128)(2,1)S(1)}, u32[]{:S(2)}, u32[]{:S(2)}) collective-permute-start(bf16[1024,512]{1,0:T(8,128)(2,1)S(1)} %copy-done.66), channel_id=1, source_target_pairs={{0,4},{4,0},{1,5},{5,1},{2,6},{6,2},{3,7},{7,3},{8,12},{12,8},{9,1... | collective-permute-start | bytes 3145736 | tf_op jit(solution)/shard_map/ppermute | solution.py:36
  229.4 18.2 %collective-permute-start.38 = (bf16[1024,512]{1,0:T(8,128)(2,1)}, bf16[1024,512]{1,0:T(8,128)(2,1)S(1)}, u32[]{:S(2)}, u32[]{:S(2)}) collective-permute-start(bf16[1024,512]{1,0:T(8,128)(2,1)} %collective-permute-done.21.refs_9_), channel_id=1, source_target_pairs={{0,4},{4,0},{1,5},{5,1},{2,6},{6,2},{3,7},{7,3},{8,12},{12,8},{9,1... | collective-permute-start | bytes 3145736 | tf_op jit(solution)/shard_map/ppermute | solution.py:36
  230.0 20.9 %collective-permute-start.29 = (bf16[512,1024]{1,0:T(8,128)(2,1)S(1)}, bf16[512,1024]{1,0:T(8,128)(2,1)S(1)}, u32[]{:S(2)}, u32[]{:S(2)}) collective-permute-start(bf16[512,1024]{1,0:T(8,128)(2,1)S(1)} %copy-done.24), channel_id=1, source_target_pairs={{0,4},{4,0},{1,5},{5,1},{2,6},{6,2},{3,7},{7,3},{8,12},{12,8},{9,1... | collective-permute-start | bytes 3145736 | tf_op jit(solution)/shard_map/ppermute | solution.py:36
  244.0 7.0 %collective-permute-start.33 = (bf16[1024,512]{1,0:T(8,128)(2,1)}, bf16[1024,512]{1,0:T(8,128)(2,1)S(1)}, u32[]{:S(2)}, u32[]{:S(2)}) collective-permute-start(bf16[1024,512]{1,0:T(8,128)(2,1)} %collective-permute-done.19.refs_4_), channel_id=1, source_target_pairs={{0,4},{4,0},{1,5},{5,1},{2,6},{6,2},{3,7},{7,3},{8,12},{12,8},{9,1... | collective-permute-start | bytes 3145736 | tf_op jit(solution)/shard_map/ppermute | solution.py:36
  246.9 4.8 collective-permute-start.32
  247.0 3.9 collective-permute-start.30
  247.5 3.5 collective-permute-start.31
  282.2 30.1 %collective-permute-start.39 = (bf16[2048,1024]{1,0:T(8,128)(2,1)}, bf16[2048,1024]{1,0:T(8,128)(2,1)S(1)}, u32[]{:S(2)}, u32[]{:S(2)}) collective-permute-start(bf16[2048,1024]{1,0:T(8,128)(2,1)} %get-tuple-element.26), channel_id=1, source_target_pairs={{0,4},{4,0},{1,5},{5,1},{2,6},{6,2},{3,7},{7,3},{8,12},{12,8},{9,1... | collective-permute-start | bytes 12582920 | tf_op jit(solution)/shard_map/ppermute | solution.py:36
  322.3 29.5 %collective-permute-start.42 = (bf16[1024,512]{1,0:T(8,128)(2,1)}, bf16[1024,512]{1,0:T(8,128)(2,1)}, u32[]{:S(2)}, u32[]{:S(2)}) collective-permute-start(bf16[1024,512]{1,0:T(8,128)(2,1)} %pad_maximum_fusion.12), channel_id=1, source_target_pairs={{0,8},{8,0},{1,9},{9,1},{2,10},{10,2},{3,11},{11,3},{4,12},{12,4},... | collective-permute-start | bytes 3145736 | tf_op jit(solution)/shard_map/ppermute | solution.py:40
  322.8 30.5 %collective-permute-start.40 = (bf16[1024,512]{1,0:T(8,128)(2,1)}, bf16[1024,512]{1,0:T(8,128)(2,1)}, u32[]{:S(2)}, u32[]{:S(2)}) collective-permute-start(bf16[1024,512]{1,0:T(8,128)(2,1)} %concatenate.188), channel_id=1, source_target_pairs={{0,16},{16,0},{1,17},{17,1},{2,18},{18,2},{3,19},{19,3},{4,20},{20... | collective-permute-start | bytes 3145736 | tf_op jit(solution)/shard_map/ppermute | solution.py:44
  356.7 13.4 %collective-permute-start.41 = (bf16[512,512]{1,0:T(8,128)(2,1)S(1)}, bf16[512,512]{1,0:T(8,128)(2,1)S(1)}, u32[]{:S(2)}, u32[]{:S(2)}) collective-permute-start(bf16[512,512]{1,0:T(8,128)(2,1)S(1)} %get-tuple-element.133), channel_id=1, source_target_pairs={{0,8},{8,0},{1,9},{9,1},{2,10},{10,2},{3,11},{11,3},{4,12},{12,4},... | collective-permute-start | bytes 1572872 | tf_op jit(solution)/shard_map/ppermute | solution.py:40
  358.3 13.0 %collective-permute-start.43 = (bf16[512,512]{1,0:T(8,128)(2,1)S(1)}, bf16[512,512]{1,0:T(8,128)(2,1)S(1)}, u32[]{:S(2)}, u32[]{:S(2)}) collective-permute-start(bf16[512,512]{1,0:T(8,128)(2,1)S(1)} %get-tuple-element.134), channel_id=1, source_target_pairs={{0,16},{16,0},{1,17},{17,1},{2,18},{18,2},{3,19},{19,3},{4,20},{20... | collective-permute-start | bytes 1572872 | tf_op jit(solution)/shard_map/ppermute | solution.py:44
  377.1 23.6 %collective-permute-start.45 = (bf16[512,1024]{1,0:T(8,128)(2,1)}, bf16[512,1024]{1,0:T(8,128)(2,1)}, u32[]{:S(2)}, u32[]{:S(2)}) collective-permute-start(bf16[512,1024]{1,0:T(8,128)(2,1)} %multiply_convert_fusion.3), channel_id=1, source_target_pairs={{0,8},{8,0},{1,9},{9,1},{2,10},{10,2},{3,11},{11,3},{4,12},{12,4},... | collective-permute-start | bytes 3145736 | tf_op jit(solution)/shard_map/ppermute | solution.py:40
  377.7 23.8 %collective-permute-start.44 = (bf16[512,1024]{1,0:T(8,128)(2,1)}, bf16[512,1024]{1,0:T(8,128)(2,1)}, u32[]{:S(2)}, u32[]{:S(2)}) collective-permute-start(bf16[512,1024]{1,0:T(8,128)(2,1)} %multiply_convert_fusion.3), channel_id=1, source_target_pairs={{0,4},{4,0},{1,5},{5,1},{2,6},{6,2},{3,7},{7,3},{8,12},{12,8},{9,1... | collective-permute-start | bytes 3145736 | tf_op jit(solution)/shard_map/ppermute | solution.py:36
  400.9 64.7 %collective-permute-start.48 = (bf16[2048,1024]{1,0:T(8,128)(2,1)}, bf16[2048,1024]{1,0:T(8,128)(2,1)}, u32[]{:S(2)}, u32[]{:S(2)}) collective-permute-start(bf16[2048,1024]{1,0:T(8,128)(2,1)} %get-tuple-element.37), channel_id=1, source_target_pairs={{0,4},{4,0},{1,5},{5,1},{2,6},{6,2},{3,7},{7,3},{8,12},{12,8},{9,1... | collective-permute-start | bytes 12582920 | tf_op jit(solution)/shard_map/ppermute | solution.py:36
  401.4 161.1 %reduce-scatter.3.cloned.1.call-start = ((), (), s32[]{:S(2)}) async-start(), calls=%async_computation.2 | async-start | bytes 1474560 | tf_op jit(solution)/shard_map/reduce_scatter | solution.py:93
  432.6 28.3 %collective-permute-start.47 = (bf16[4,144,1024]{2,1,0:T(8,128)(2,1)}, bf16[4,144,1024]{2,1,0:T(8,128)(2,1)}, u32[]{:S(2)}, u32[]{:S(2)}) collective-permute-start(bf16[4,144,1024]{2,1,0:T(8,128)(2,1)} %dynamic-slice_bitcast_fusion), channel_id=1, source_target_pairs={{0,16},{16,0},{1,17},{17,1},{2,18},{18,2},{3,19},{19,3},{4,20},{20... | collective-permute-start | bytes 3538952 | tf_op jit(solution)/shard_map/ppermute | solution.py:44
  443.5 35.8 %collective-permute-start.53 = (bf16[1024,1024]{1,0:T(8,128)(2,1)}, bf16[1024,1024]{1,0:T(8,128)(2,1)}, u32[]{:S(2)}, u32[]{:S(2)}) collective-permute-start(bf16[1024,1024]{1,0:T(8,128)(2,1)} %pad_maximum_fusion.4), channel_id=1, source_target_pairs={{0,4},{4,0},{1,5},{5,1},{2,6},{6,2},{3,7},{7,3},{8,12},{12,8},{9,1... | collective-permute-start | bytes 6291464 | tf_op jit(solution)/shard_map/ppermute | solution.py:36
  475.5 26.2 %collective-permute-start.51 = (bf16[1024,512]{1,0:T(8,128)(2,1)S(1)}, bf16[1024,512]{1,0:T(8,128)(2,1)S(1)}, u32[]{:S(2)}, u32[]{:S(2)}) collective-permute-start(bf16[1024,512]{1,0:T(8,128)(2,1)S(1)} %pad_maximum_fusion.13), channel_id=1, source_target_pairs={{0,8},{8,0},{1,9},{9,1},{2,10},{10,2},{3,11},{11,3},{4,12},{12,4},... | collective-permute-start | bytes 3145736 | tf_op jit(solution)/shard_map/ppermute | solution.py:40
  477.9 24.4 %collective-permute-start.49 = (bf16[1024,512]{1,0:T(8,128)(2,1)S(1)}, bf16[1024,512]{1,0:T(8,128)(2,1)S(1)}, u32[]{:S(2)}, u32[]{:S(2)}) collective-permute-start(bf16[1024,512]{1,0:T(8,128)(2,1)S(1)} %concatenate.189), channel_id=1, source_target_pairs={{0,16},{16,0},{1,17},{17,1},{2,18},{18,2},{3,19},{19,3},{4,20},{20... | collective-permute-start | bytes 3145736 | tf_op jit(solution)/shard_map/ppermute | solution.py:44
  484.7 52.2 %collective-permute-start.54 = (bf16[512,1024]{1,0:T(8,128)(2,1)}, bf16[512,1024]{1,0:T(8,128)(2,1)}, u32[]{:S(2)}, u32[]{:S(2)}) collective-permute-start(bf16[512,1024]{1,0:T(8,128)(2,1)} %fusion.7), channel_id=1, source_target_pairs={{0,8},{8,0},{1,9},{9,1},{2,10},{10,2},{3,11},{11,3},{4,12},{12,4},... | collective-permute-start | bytes 3145736 | tf_op jit(solution)/shard_map/ppermute | solution.py:40
  504.3 29.5 %collective-permute-start.50 = (bf16[512,512]{1,0:T(8,128)(2,1)}, bf16[512,512]{1,0:T(8,128)(2,1)}, u32[]{:S(2)}, u32[]{:S(2)}) collective-permute-start(bf16[512,512]{1,0:T(8,128)(2,1)} %get-tuple-element.129), channel_id=1, source_target_pairs={{0,8},{8,0},{1,9},{9,1},{2,10},{10,2},{3,11},{11,3},{4,12},{12,4},... | collective-permute-start | bytes 1572872 | tf_op jit(solution)/shard_map/ppermute | solution.py:40
  505.0 28.8 %collective-permute-start.52 = (bf16[512,512]{1,0:T(8,128)(2,1)}, bf16[512,512]{1,0:T(8,128)(2,1)}, u32[]{:S(2)}, u32[]{:S(2)}) collective-permute-start(bf16[512,512]{1,0:T(8,128)(2,1)} %get-tuple-element.130), channel_id=1, source_target_pairs={{0,16},{16,0},{1,17},{17,1},{2,18},{18,2},{3,19},{19,3},{4,20},{20... | collective-permute-start | bytes 1572872 | tf_op jit(solution)/shard_map/ppermute | solution.py:44
  545.6 4.9 collective-permute-start.58
  545.6 6.2 %collective-permute-start.60 = (bf16[32,1152]{1,0:T(8,128)(2,1)S(1)}, bf16[32,1152]{1,0:T(8,128)(2,1)S(1)}, u32[]{:S(2)}, u32[]{:S(2)}) collective-permute-start(bf16[32,1152]{1,0:T(8,128)(2,1)S(1)} %get-tuple-element.178), channel_id=1, source_target_pairs={{0,20},{4,16},{8,28},{12,24},{16,4},{20,0},{24,12},{28,8},{1,21},{... | collective-permute-start | bytes 221192 | tf_op jit(solution)/shard_map/ppermute | solution.py:49
  547.5 6.2 %collective-permute-start.62 = (bf16[32,1152]{1,0:T(8,128)(2,1)S(1)}, bf16[32,1152]{1,0:T(8,128)(2,1)S(1)}, u32[]{:S(2)}, u32[]{:S(2)}) collective-permute-start(bf16[32,1152]{1,0:T(8,128)(2,1)S(1)} %get-tuple-element.179), channel_id=1, source_target_pairs={{0,12},{4,8},{8,4},{12,0},{16,28},{20,24},{24,20},{28,16},{1,13},{... | collective-permute-start | bytes 221192 | tf_op jit(solution)/shard_map/ppermute | solution.py:49
  548.3 6.2 %collective-permute-start.59 = (bf16[32,1152]{1,0:T(8,128)(2,1)S(1)}, bf16[32,1152]{1,0:T(8,128)(2,1)S(1)}, u32[]{:S(2)}, u32[]{:S(2)}) collective-permute-start(bf16[32,1152]{1,0:T(8,128)(2,1)S(1)} %get-tuple-element.176), channel_id=1, source_target_pairs={{0,24},{4,28},{8,16},{12,20},{16,8},{20,12},{24,0},{28,4},{1,25},{... | collective-permute-start | bytes 221192 | tf_op jit(solution)/shard_map/ppermute | solution.py:49
  549.8 6.1 %collective-permute-start.61 = (bf16[32,1152]{1,0:T(8,128)(2,1)S(1)}, bf16[32,1152]{1,0:T(8,128)(2,1)S(1)}, u32[]{:S(2)}, u32[]{:S(2)}) collective-permute-start(bf16[32,1152]{1,0:T(8,128)(2,1)S(1)} %get-tuple-element.75), channel_id=1, source_target_pairs={{0,16},{4,20},{8,24},{12,28},{16,0},{20,4},{24,8},{28,12},{1,17},{... | collective-permute-start | bytes 221192 | tf_op jit(solution)/shard_map/ppermute | solution.py:49
  550.5 5.4 collective-permute-start.63
  551.8 4.1 collective-permute-start.64
  564.3 3.9 collective-permute-start.55
  564.7 4.7 collective-permute-start.56
  566.0 3.4 collective-permute-start.57
  (81 other events, 515.2 us)
Sparse Core Ops, SparseCore 0:
  33.1 52.5 all-gather.4
Sparse Core Ops, SparseCore 1:
  127.8 68.3 all-gather.6
  401.5 64.7 reduce-scatter.4
  506.7 27.7 reduce-scatter.2

commit v4 on v3

v4 whole, which is shorter than its diff:
```python
import jax
import jax.numpy as jnp
from jax import lax
from jax.experimental import pallas as pl
from jax.experimental.pallas import tpu as pltpu
from jax.sharding import Mesh, PartitionSpec as P

EPSILON = 1e-05
TEAM = 4
EXTRA_ROWS = 16
ROW_TILE = 512
bf16 = jnp.bfloat16
f32 = jnp.float32


def forward_dot(left_side, right_side):
    return jnp.dot(left_side, right_side, preferred_element_type=f32)


def rows_dot(left_side, right_side):
    return lax.dot_general(
        left_side, right_side, (((0,), (0,)), ((), ())), preferred_element_type=f32
    )


def back_dot(left_side, right_side):
    return lax.dot_general(
        left_side, right_side, (((1,), (1,)), ((), ())), preferred_element_type=f32
    )


def swap_core(values):
    return lax.ppermute(values, "c", [(0, 1), (1, 0)])


def swap_chip(values):
    return lax.ppermute(values, "x", [(0, 1), (1, 0)])


def swap_row(values):
    return lax.ppermute(values, "y", [(0, 1), (1, 0)])


def swap_far(values, distance):
    return lax.ppermute(values, ("x", "c"), [(i, i ^ distance) for i in range(TEAM)])


def after(values, token):
    return values + (token.ravel()[0] * 0).astype(values.dtype)


def reorder(blocks):
    blocks = list(blocks)
    for bit, axis in ((1, "c"), (2, "x")):
        odd = lax.axis_index(axis) == 1
        blocks = [jnp.where(odd, blocks[j ^ bit], blocks[j]) for j in range(len(blocks))]
    return blocks


def exchange(blocks):
    near = reorder(blocks)
    return reorder(near[:1] + [swap_far(near[j], j) for j in range(1, len(near))])


def team_rows(rows):
    across = swap_chip(rows)
    return jnp.concatenate([rows, swap_core(rows), across, swap_core(across)], axis=0)


def team_sum(terms):
    count = terms.shape[0] // TEAM
    sent = jnp.concatenate([terms[count : 2 * count], terms[3 * count :]], axis=0)
    came = swap_core(sent).astype(f32)
    own = terms[:count].astype(f32) + came[:count]
    other = terms[2 * count : 3 * count].astype(f32) + came[count:]
    return own + swap_chip(other.astype(bf16)).astype(f32)


def take(blocks, index):
    return lax.dynamic_index_in_dim(blocks, index, axis=0, keepdims=False)


def scatter_first(part):
    groups, slots = part.shape[:2]
    if groups == 2:
        row = lax.axis_index("y")
        came = swap_row(take(part, 1 - row))
        summed = (take(part, row).astype(f32) + came.astype(f32)).astype(bf16)
        return lax.psum_scatter(summed, "s", scatter_dimension=0, tiled=False), summed[0, :1]
    flat = part.reshape((groups * slots,) + part.shape[2:]).astype(f32)
    total = lax.psum_scatter(flat, ("g", "y", "s"), scatter_dimension=0, tiled=False)
    return total, total[:1]


def scatter_rest(part):
    wide = part if part.shape[0] <= 8 else part.astype(f32)
    return lax.psum_scatter(wide, ("g", "y", "s"), scatter_dimension=0, tiled=False)


def forward_kernel(normed_ref, pair_ref, hidden_ref, silu_ref, slope_ref):
    width = hidden_ref.shape[1]
    values = forward_dot(normed_ref[...], pair_ref[...])
    gate_value, up_value = values[:, :width], values[:, width:]
    sigmoid = jax.nn.sigmoid(gate_value)
    silu = gate_value * sigmoid
    hidden_ref[...] = (silu * up_value).astype(bf16)
    silu_ref[...] = silu.astype(bf16)
    slope_ref[...] = (up_value * (sigmoid * (1 + gate_value * (1 - sigmoid)))).astype(bf16)


def backward_kernel(
    grad_ref, hidden_ref, silu_ref, slope_ref, pair_ref, down_ref, pair_grad_ref, normed_ref, out_ref
):
    width = hidden_ref.shape[1]
    hidden_grad = back_dot(grad_ref[...], down_ref[...])
    pair_grad_ref[:, :width] = (hidden_grad * slope_ref[...].astype(f32)).astype(bf16)
    pair_grad_ref[:, width:] = (hidden_grad * silu_ref[...].astype(f32)).astype(bf16)
    normed_ref[...] = back_dot(pair_grad_ref[...], pair_ref[...]).astype(bf16)
    out_ref[...] = forward_dot(hidden_ref[...], down_ref[...]).astype(bf16)


def by_rows(kernel, rowed, whole, columns, flops, transcendentals):
    rows = rowed[0].shape[0]
    tile = min(ROW_TILE, rows)

    def row_block(count):
        return pl.BlockSpec((tile, count), lambda i: (i, 0))

    moved = sum(2 * value.size for value in rowed + whole) + 2 * rows * sum(columns)
    return pl.pallas_call(
        kernel,
        grid=(rows // tile,),
        in_specs=[row_block(value.shape[1]) for value in rowed]
        + [
            pl.BlockSpec(value.shape, lambda i: (0, 0), pipeline_mode=pl.Buffered(1))
            for value in whole
        ],
        out_specs=[row_block(count) for count in columns],
        out_shape=[jax.ShapeDtypeStruct((rows, count), bf16) for count in columns],
        compiler_params=pltpu.CompilerParams(vmem_limit_bytes=52 * 1024 * 1024),
        cost_estimate=pl.CostEstimate(
            flops=flops, bytes_accessed=moved, transcendentals=transcendentals
        ),
    )(*rowed, *whole)


def shifted_down(rows, step):
    return jnp.concatenate(
        [jnp.zeros((step, rows.shape[1]), rows.dtype), rows[:-step]], axis=0
    )


def shifted_up(rows, step):
    return jnp.concatenate(
        [rows[step:], jnp.zeros((step, rows.shape[1]), rows.dtype)], axis=0
    )


def inverse_rms(values):
    return lax.rsqrt(jnp.mean(values * values, axis=-1, keepdims=True) + EPSILON)


def norm_back(values, scale, weighted):
    return scale * weighted - values * (
        scale * scale * scale * jnp.mean(weighted * values, axis=-1, keepdims=True)
    )


def per_device(
    tokens,
    positions,
    cotangent,
    norm_gain,
    in_weight,
    conv_weight,
    out_weight,
    ffn_gain,
    gate_weight,
    up_weight,
    down_weight,
):
    shape = tokens.shape
    features = shape[2]
    rows = shape[0] * shape[1]
    share = in_weight.shape[0]
    hidden_share = down_weight.shape[0]
    hidden_width = gate_weight.shape[1]
    taps = conv_weight.shape[0]
    groups = lax.axis_size("g") * lax.axis_size("y")
    slots = lax.axis_size("s")
    chan_run = slots * share
    hid_run = slots * hidden_share
    chan = groups * chan_run
    hid = groups * hid_run

    def by_place(weight, parts, team, run):
        count = weight.shape[1] // (parts * team * run)
        split = weight.reshape(share, parts, count, team, run)
        return jnp.transpose(split, (3, 0, 1, 2, 4)).reshape(team, share, parts * count * run)

    def side_by_side(block, width):
        return jnp.concatenate(
            [block[..., j * share : (j + 1) * share, :width] for j in range(features // width)],
            axis=-1,
        )

    def stacked(block, width):
        return jnp.concatenate(
            [block[..., j * width : (j + 1) * width] for j in range(features // width)], axis=-2
        )

    in_blocks = by_place(in_weight, 3, TEAM, chan_run)
    in_mine = jnp.concatenate(exchange([in_blocks[j] for j in range(TEAM)]), axis=0)
    gains = jnp.concatenate([norm_gain, ffn_gain]).reshape(1, 2 * share)
    near_gains = team_rows(gains)
    gains_row = jnp.concatenate(reorder([near_gains[j : j + 1] for j in range(TEAM)]), axis=1)
    def as_row(values):
        return jnp.pad(values, ((0, 0), (0, features - values.shape[1])))

    first_pack = jnp.concatenate(
        [
            jnp.concatenate([in_mine, stacked(out_weight, chan)], axis=1),
            as_row(conv_weight.reshape(1, taps * share)),
            as_row(gains_row),
            jnp.zeros((EXTRA_ROWS - 2, features), bf16),
        ],
        axis=0,
    )
    tall = TEAM * share

    def first_unpack(block):
        return [
            block[:tall, : 3 * chan].reshape(TEAM, share, 3 * chan),
            side_by_side(block[:tall, 3 * chan :], chan),
            block[tall, : taps * share].reshape(taps, share),
            block[tall + 1, : 2 * tall].reshape(TEAM, 2, share),
        ]

    pair_blocks = jnp.concatenate(
        [by_place(gate_weight, 1, TEAM, hid_run), by_place(up_weight, 1, TEAM, hid_run)], axis=2
    )
    pair_mine = jnp.concatenate(exchange([pair_blocks[j] for j in range(TEAM)]), axis=0)

    first_all = lax.all_gather(first_pack, ("g", "y", "s"), axis=0, tiled=False)
    in_all, out_all, conv_all, gains_all = [
        part.reshape((groups, slots) + part.shape[1:]) for part in jax.vmap(first_unpack)(first_all)
    ]

    pair_all = lax.all_gather(pair_mine, ("g", "y", "s"), axis=0, tiled=False)
    down_full = lax.all_gather(down_weight, ("g", "y", "s"), axis=0, tiled=True)

    in_full = jnp.transpose(in_all, (0, 2, 1, 3, 4)).reshape(features, 3 * chan)
    out_full = out_all.reshape(chan, features)
    conv_full = jnp.transpose(conv_all, (2, 0, 1, 3)).reshape(taps, chan).astype(f32)
    gains_full = jnp.transpose(gains_all, (3, 0, 2, 1, 4)).reshape(2, features).astype(f32)
    norm_full, ffn_full = gains_full[0], gains_full[1]
    pair_full = jnp.transpose(
        pair_all.reshape(groups, slots, TEAM, share, 2 * hid), (0, 2, 1, 3, 4)
    ).reshape(features, 2 * hid)

    own_tokens = tokens.reshape(rows, features)
    places = positions.reshape(rows, 1)
    team_tokens = team_rows(own_tokens)
    team_places = team_rows(places)
    live = (places >= 0).astype(f32)
    upstream = cotangent.reshape(rows, features).astype(f32)
    ffn_grad = team_rows((live * upstream).astype(bf16))
    inputs = tokens.reshape(rows, features).astype(f32)

    values = team_tokens.astype(f32)
    early_full = after(norm_full, ffn_grad[-1:])
    first_normed = (values * inverse_rms(values) * early_full).astype(bf16)
    projected = forward_dot(first_normed, in_full)
    b_part = projected[:, :chan]
    c_part = projected[:, chan : 2 * chan]
    x_part = projected[:, 2 * chan :]
    mixed = b_part * x_part
    mask_one = (team_places >= 1).astype(f32)
    mask_two = (team_places >= 2).astype(f32)
    mixed_one = mask_one * shifted_down(mixed, 1)
    mixed_two = mask_two * shifted_down(mixed, 2)
    convolved = conv_full[0] * mixed + conv_full[1] * mixed_one + conv_full[2] * mixed_two
    mixer_in = (c_part * convolved).astype(bf16)
    mixer_out = team_sum(forward_dot(mixer_in, out_full).astype(bf16))
    middle = inputs + live * mixer_out
    second_scale = inverse_rms(middle)
    second_normed = team_rows((middle * second_scale * ffn_full).astype(bf16))

    team_count = TEAM * rows
    unit = 2 * team_count * features * hid
    hidden, silu, slope = by_rows(
        forward_kernel, [second_normed], [pair_full], [hid] * 3, 2 * unit, team_count * hid
    )
    owners = groups * slots
    down_part = rows_dot(hidden, ffn_grad).astype(bf16)
    grad_down = scatter_rest(down_part.reshape(owners, hidden_share, features))
    pair_grad, normed_part, out_part = by_rows(
        backward_kernel,
        [ffn_grad, hidden, silu, slope],
        [pair_full, down_full],
        [2 * hid, features, features],
        4 * unit,
        0,
    )

    def by_owner(grad, team):
        width = grad.shape[-1]
        count = features // (team * slots * share)
        split = grad.astype(bf16).reshape(count, team, slots, share, width)
        return jnp.transpose(split, (0, 2, 1, 3, 4)).reshape(count, slots, team * share, width)

    pair_part = by_owner(rows_dot(second_normed, pair_grad), TEAM)
    pair_sum = scatter_rest(pair_part.reshape(owners, tall, 2 * hid))
    normed_sum = team_sum(normed_part)
    second_weighted = ffn_full * normed_sum
    middle_grad = upstream + norm_back(middle, second_scale, second_weighted)

    mixer_grad = team_rows((live * middle_grad).astype(bf16))
    mixer_in_grad = back_dot(mixer_grad, out_full)
    c_grad = mixer_in_grad * convolved
    conv_grad = mixer_in_grad * c_part
    mixed_grad = (
        conv_full[0] * conv_grad
        + conv_full[1] * shifted_up(mask_one * conv_grad, 1)
        + conv_full[2] * shifted_up(mask_two * conv_grad, 2)
    )
    projected_grad = jnp.concatenate(
        [mixed_grad * x_part, c_grad, mixed_grad * b_part], axis=1
    ).astype(bf16)
    grad_conv_part = jnp.stack(
        [
            jnp.sum(conv_grad * mixed, axis=0),
            jnp.sum(conv_grad * mixed_one, axis=0),
            jnp.sum(conv_grad * mixed_two, axis=0),
        ]
    )
    in_part = by_owner(rows_dot(first_normed, projected_grad), TEAM)
    out_grad_part = rows_dot(mixer_in, mixer_grad).astype(bf16)
    out_grad_part = stacked(out_grad_part.reshape(groups, slots, share, features), chan)
    conv_rows = jnp.transpose(
        grad_conv_part.reshape(taps, groups, slots, share), (1, 2, 0, 3)
    ).reshape(groups, slots, 1, taps * share)
    conv_rows = jnp.pad(
        conv_rows.astype(bf16),
        ((0, 0), (0, 0), (0, EXTRA_ROWS - 1), (0, features - taps * share)),
    )
    first_sum, token = scatter_first(
        jnp.concatenate(
            [jnp.concatenate([in_part, out_grad_part], axis=3), conv_rows], axis=2
        )
    )

    first_weighted = norm_full * team_sum(back_dot(projected_grad, in_full).astype(bf16))
    input_grad = middle_grad + norm_back(inputs, inverse_rms(inputs), first_weighted)
    input_grad = input_grad.astype(bf16)
    out_sum = team_sum(after(out_part, token))
    block_out = (middle + live * out_sum).astype(bf16)

    def own_rows(summed, parts, team, run):
        blocks = [summed[j * share : (j + 1) * share].astype(bf16) for j in range(team)]
        came = [block.reshape(share, parts, -1, 1, run) for block in exchange(blocks)]
        joined = jnp.concatenate(came, axis=3)
        return joined.reshape(share, -1).astype(f32)

    pair_rows = own_rows(pair_sum, 2, TEAM, hid_run)
    gate_rows = pair_rows[:, :hidden_width]
    up_rows = pair_rows[:, hidden_width:]
    in_rows = own_rows(first_sum[:tall, : 3 * chan], 3, TEAM, chan_run)
    grad_out = side_by_side(first_sum[:tall, 3 * chan :], chan).astype(f32)
    grad_conv = first_sum[tall, : taps * share].reshape(taps, share).astype(f32)
    grad_norm_gain = jnp.sum(in_weight.astype(f32) * in_rows, axis=1) / norm_gain.astype(f32)
    grad_ffn_gain = jnp.sum(
        gate_weight.astype(f32) * gate_rows + up_weight.astype(f32) * up_rows, axis=1
    ) / ffn_gain.astype(f32)
    return (
        block_out.reshape(shape),
        input_grad.reshape(shape),
        grad_norm_gain,
        in_rows,
        grad_conv,
        grad_out,
        grad_ffn_gain,
        gate_rows,
        up_rows,
        grad_down.astype(f32),
    )


def solution(mesh):
    every = ("g", "y", "x", "c", "s")
    outer = mesh.shape["dp"] // (2 * TEAM)
    teams = Mesh(mesh.devices.reshape(outer, 2, 2, 2, mesh.shape["shard"]), every)
    return jax.shard_map(
        per_device,
        mesh=teams,
        in_specs=(
            P(None, every, None),
            P(None, every),
            P(None, every, None),
            P(every),
            P(every, None),
            P(None, every),
            P(every, None),
            P(every),
            P(every, None),
            P(every, None),
            P(every, None),
        ),
        out_specs=(
            P(None, every, None),
            P(None, every, None),
            P(every),
            P(every, None),
            P(None, every),
            P(every, None),
            P(every),
            P(every, None),
            P(every, None),
            P(every, None),
        ),
        check_vma=False,
    )
```

time: 589 us -> 545 us (0.925)
  waiting for transfers between devices: 233 us -> 272 us
  Pallas kernels: 85.4 us -> 53 us
  matrix products: 31.9 us -> 58.3 us
  other arithmetic: 94 us -> 71.1 us
  local copies, waits for them, and re-layouts: 66.5 us -> 43.6 us
  starting transfers between devices: 47.2 us -> 25.4 us
    ppermute x20 -> x12, waiting for transfers between devices: 6.91 us -> 69 us  [swap_far(): lax.ppermute(values, ('x', 'c'), [(i, i ^ distance) for i in range(TEAM)])]
    pallas_call x3 -> x2, Pallas kernels: 85.4 us -> 53 us  [by_rows(): pl.pallas_call(kernel, grid=(rows // tile,), in_specs=[row_block(value.sh...]
    ppermute x14 -> x10, waiting for transfers between devices: 150 us -> 118 us  [swap_chip(): return lax.ppermute(values, 'x', [(0, 1), (1, 0)])]
    reduce_scatter x1 -> x2, waiting for transfers between devices: 0.03 us -> 31.4 us  [scatter_rest(): lax.psum_scatter(wide, ('g', 'y', 's'), scatter_dimension=0, tiled=False)]
    dot_general x2 -> x4, matrix products: 7.69 us -> 33.1 us  [rows_dot(): lax.dot_general(left_side, right_side, (((0,), (0,)), ((), ())), preferre...]
    all_gather x1, waiting for transfers between devices: 22.6 us -> 0.02 us  [per_device(): first_all = lax.all_gather(first_pack, ('g', 'y', 's'), axis=0, tiled=False)]
    add x3 -> x0, other arithmetic: 13 us -> none  [the longest x1 7.73 us: crew_sum(): both = mine.astype(f32) + swap_core(theirs).astype(f32)]
    ppermute x9 -> x1, waiting for transfers between devices: 47.7 us -> 35 us  [swap_row(): return lax.ppermute(values, 'y', [(0, 1), (1, 0)])]
  transfers between devices with their start and end apart: 69 -> 45, of which waited for: 27 -> 19; matrix products, arithmetic and copies ran while one was open for 21% -> 27% of each run, Pallas kernels for 10% -> 3%
where the time goes in v4:
time: 545 us; the launch traced here: 540 us
  waiting for transfers between devices  272 us (50%)
  other arithmetic  71.1 us (13%)
  matrix products  58.3 us (11%)
  Pallas kernels  53 us (10%)
  local copies, waits for them, and re-layouts  43.6 us (8%)
  starting transfers between devices  25.4 us (5%)
  between operations  17 us (3%)
    ppermute x10, waiting for transfers between devices, swap_chip(): return lax.ppermute(values, 'x', [(0, 1), (1, 0)])  118 us
    ppermute x12, waiting for transfers between devices, swap_far(): lax.ppermute(values, ('x', 'c'), [(i, i ^ distance) for i in range(TEAM)])  69 us
    pallas_call x2, Pallas kernels, by_rows(): pl.pallas_call(kernel, grid=(rows // tile,), in_specs=[row_block(value.sh...  53 us
    ppermute x1, waiting for transfers between devices, swap_row(): return lax.ppermute(values, 'y', [(0, 1), (1, 0)])  35 us
    dot_general x4, matrix products, rows_dot(): lax.dot_general(left_side, right_side, (((0,), (0,)), ((), ())), preferre...  33.1 us
    reduce_scatter x2, waiting for transfers between devices, scatter_rest(): lax.psum_scatter(wide, ('g', 'y', 's'), scatter_dimension=0, tiled=False)  31.4 us
    dot_general x2, matrix products, back_dot(): lax.dot_general(left_side, right_side, (((1,), (1,)), ((), ())), preferre...  16.1 us
    unnamed x80, local copies, waits for them, and re-layouts  13.7 us
  transfers between devices with their start and end apart: 45, of which 19 were waited for; matrix products, arithmetic and copies ran while one was open for 27% of the time, Pallas kernels for 3%

profile of v4, /device:TPU:0, one launch (start us, length us, event | category | flops | bytes accessed | tf_op | source)
XLA Modules:
  0.0 540.2 jit_solution(1521875340288037802)
XLA Ops:
  8.5 2.5 collective-permute-start.6
  12.7 1.8 collective-permute-start.4
  20.0 1.8 collective-permute-start.1
  22.7 1.3 reshape.393
  25.0 1.9 collective-permute-start.20
  26.8 44.5 %collective-permute-done.21 = bf16[32,2304]{1,0:T(8,128)(2,1)S(1)} collective-permute-done((bf16[32,2304]{1,0:T(8,128)(2,1)S(1)}, bf16[32,2304]{1,0:T(8,128)(2,1)S(1)}, u32[]{:S(2)}, u32[]{:S(2)}) %collective-permute-start.21) | collective-permute-done | bytes 147488 | tf_op jit(solution)/shard_map/ppermute | solution.py:45
  75.1 3.0 collective-permute-done.12
  81.2 3.6 fusion
  84.8 1.5 slice.348
  88.4 1.3 copy.65
  91.6 7.9 %fusion.26 = f32[2048,768]{1,0:T(8,128)S(1)} fusion(bf16[1024,768]{1,0:T(8,128)(2,1)} %bitcast.146, f32[1024]{0:T(1024)S(1)} %mul.300, f32[2048]{0:T(1024)S(1)} %add_rsqrt_fusion, bf16[512,1024]{1,0:T(8,128)(2,1)} %copy-done.29, bf16[512,1024]{1,0:T(8,128)(2,1)} %collective-permute-done.1, bf16[512,1024]{1,0:T(8,128)(2,1)} %copy-done.27, ...), kind=kOutput, calls=%fused_computation.78 | convolution fusion | flops 3244294144 | bytes 12070912 | tf_op jit(solution)/shard_map/dot_general | solution.py:17
  99.7 2.3 copy-done
  102.0 2.3 multiply_convert_fusion.5
  106.2 4.0 collective-permute-done.14
  111.1 1.7 copy-done.7
  113.7 24.4 %collective-permute-done.15 = bf16[512,1024]{1,0:T(8,128)(2,1)} collective-permute-done((bf16[512,1024]{1,0:T(8,128)(2,1)S(1)}, bf16[512,1024]{1,0:T(8,128)(2,1)}, u32[]{:S(2)}, u32[]{:S(2)}) %collective-permute-start.15) | collective-permute-done | bytes 1048608 | tf_op jit(solution)/shard_map/ppermute | solution.py:37
  138.1 3.1 multiply_reduce_fusion.5
  143.1 23.9 %collective-permute-done.18 = bf16[512,1024]{1,0:T(8,128)(2,1)} collective-permute-done((bf16[512,1024]{1,0:T(8,128)(2,1)}, bf16[512,1024]{1,0:T(8,128)(2,1)}, u32[]{:S(2)}, u32[]{:S(2)}) %collective-permute-start.18) | collective-permute-done | bytes 1048608 | tf_op jit(solution)/shard_map/ppermute | solution.py:37
  168.1 7.7 %pad_maximum_fusion.1.grad_ref = bf16[2048,1024]{1,0:T(8,128)(2,1)} fusion(bf16[512,1024]{1,0:T(8,128)(2,1)} %collective-permute-done.10, bf16[512,1024]{1,0:T(8,128)(2,1)} %collective-permute-done.9, bf16[512,1024]{1,0:T(8,128)(2,1)S(1)} %collective-permute-done.16, bf16[512,1024]{1,0:T(8,128)(2,1)S(1)} %copy-done.19), kind=kLoop, calls=%fused_computation.9 | loop fusion | flops 16777216 | bytes 8388608 | tf_op jit(solution)/shard_map/concatenate | solution.py:67
  175.8 4.9 copy.68
  180.7 3.9 pad_maximum_fusion.2.normed_ref
  184.6 14.9 %shard_map.186 = (bf16[2048,1152]{1,0:T(8,128)(2,1)}, bf16[2048,1152]{1,0:T(8,128)(2,1)}, bf16[2048,1152]{1,0:T(8,128)(2,1)}) custom-call(bf16[2048,1024]{1,0:T(8,128)(2,1)} %pad_maximum_fusion.2.normed_ref, bf16[1024,2304]{1,0:T(8,128)(2,1)} %bitcast.136), custom_call_target="tpu_custom_call" | custom-call | flops 9663676416 | bytes 23068672 | tf_op jit(solution)/shard_map/pallas_call | solution.py:130
  199.4 7.6 %all-gather.6.cloned.1.call-done.down_ref = bf16[1152,1024]{1,0:T(8,128)(2,1)} async-done(((bf16[144,1024]{1,0:T(8,128)(2,1)}), bf16[1152,1024]{1,0:T(8,128)(2,1)}) %all-gather.6.cloned.1.call-update) | async-done | bytes 2359312 | tf_op jit(solution)/shard_map/all_gather | solution.py:250
  207.0 38.2 %shard_map.187 = (bf16[2048,2304]{1,0:T(8,128)(2,1)}, bf16[2048,1024]{1,0:T(8,128)(2,1)}, bf16[2048,1024]{1,0:T(8,128)(2,1)}) custom-call(bf16[2048,1024]{1,0:T(8,128)(2,1)} %pad_maximum_fusion.1.grad_ref, bf16[2048,1152]{1,0:T(8,128)(2,1)} %get-tuple-element.16.hidden_ref, bf16[2048,1152]{1,0:T(8,128)(2,1)} %get-tuple-element.17.silu_ref, ...), custom_call_target="tpu_custom_call" | custom-call | flops 19327352832 | bytes 43253760 | tf_op jit(solution)/shard_map/pallas_call | solution.py:130
  245.2 1.7 fusion.45
  247.2 4.1 collective-permute-done.23
  252.2 1.5 collective-permute-start.24
  253.7 23.7 %collective-permute-done.24 = bf16[512,1024]{1,0:T(8,128)(2,1)S(1)} collective-permute-done((bf16[512,1024]{1,0:T(8,128)(2,1)S(1)}, bf16[512,1024]{1,0:T(8,128)(2,1)S(1)}, u32[]{:S(2)}, u32[]{:S(2)}) %collective-permute-start.24) | collective-permute-done | bytes 1048608 | tf_op jit(solution)/shard_map/ppermute | solution.py:37
  278.1 2.6 multiply_convert_fusion.3
  280.7 1.5 collective-permute-start.26
  282.3 23.1 %collective-permute-done.26 = bf16[512,1024]{1,0:T(8,128)(2,1)} collective-permute-done((bf16[512,1024]{1,0:T(8,128)(2,1)}, bf16[512,1024]{1,0:T(8,128)(2,1)}, u32[]{:S(2)}, u32[]{:S(2)}) %collective-permute-start.26) | collective-permute-done | bytes 1048608 | tf_op jit(solution)/shard_map/ppermute | solution.py:37
  305.4 9.5 %convolution_convert_fusion.1 = bf16[1152,1024]{1,0:T(8,128)(2,1)} fusion(bf16[2048,1152]{1,0:T(8,128)(2,1)} %get-tuple-element.16.hidden_ref, bf16[512,1024]{1,0:T(8,128)(2,1)} %collective-permute-done.10, bf16[512,1024]{1,0:T(8,128)(2,1)} %collective-permute-done.9, bf16[512,1024]{1,0:T(8,128)(2,1)} %copy-done.31, bf16[512,1024]{1,0:T(8,128)(2,1)} %copy-done.18), kind=kOutput, calls=%fused_computation.12 | convolution fusion | flops 4849795072 | bytes 11272192 | tf_op jit(solution)/shard_map/dot_general | solution.py:21
  314.9 10.3 %multiply_reduce_fusion.3 = (bf16[256]{0:T(256)(128)(2,1)S(1)}, bf16[256]{0:T(256)(128)(2,1)S(1)}, bf16[256]{0:T(256)(128)(2,1)S(1)}, f32[2048,256]{1,0:T(8,128)}, bf16[2048,256]{1,0:T(8,128)(2,1)}) fusion(f32[2048,256]{1,0:T(8,128)} %copy-done.6, f32[2046,256]{1,0:T(8,128)} %bitcast.131, f32[2048]{0:T(1024)S(1)} %get-tuple-element.110, ...), kind=kOutput, calls=%fused_computation.61 | convolution fusion | flops 1096285440 | bytes 18364928 | tf_op jit(solution)/shard_map/dot_general | solution.py:27
  325.5 2.1 slice_multiply_fusion
  328.1 2.4 multiply_convert_fusion.2
  330.6 2.3 multiply_convert_fusion
  333.5 5.2 convolution_convert_fusion.4
  340.0 3.5 convolution_convert_fusion.5
  343.9 1.4 copy-done.10
  346.9 35.0 %collective-permute-done.28 = bf16[4,144,1024]{2,1,0:T(8,128)(2,1)} collective-permute-done((bf16[4,144,1024]{2,1,0:T(8,128)(2,1)}, bf16[4,144,1024]{2,1,0:T(8,128)(2,1)}, u32[]{:S(2)}, u32[]{:S(2)}) %collective-permute-start.28) | collective-permute-done | bytes 1179680 | tf_op jit(solution)/shard_map/ppermute | solution.py:41
  381.9 3.1 fusion.5
  385.1 14.9 %convolution_convert_fusion = bf16[1024,2304]{1,0:T(8,128)(2,1)S(1)} fusion(bf16[2048,2304]{1,0:T(8,128)(2,1)} %get-tuple-element.21, bf16[512,1024]{1,0:T(8,128)(2,1)} %collective-permute-done.19, bf16[512,1024]{1,0:T(8,128)(2,1)} %collective-permute-done.18, bf16[512,1024]{1,0:T(8,128)(2,1)} %collective-permute-done.17, ...), kind=kOutput, calls=%fused_computation.5 | convolution fusion | flops 9682812928 | bytes 18350080 | tf_op jit(solution)/shard_map/dot_general | solution.py:21
  400.0 2.6 copy.77
  402.6 5.8 %convolution_convert_fusion.3 = bf16[2048,1024]{1,0:T(8,128)(2,1)S(1)} fusion(bf16[1024,768]{1,0:T(8,128)(2,1)} %bitcast.147, bf16[2048,256]{1,0:T(8,128)(2,1)} %copy-done.26, bf16[2048,256]{1,0:T(8,128)(2,1)} %get-tuple-element.61, bf16[2048,256]{1,0:T(8,128)(2,1)} %copy-done.25), kind=kOutput, calls=%fused_computation.14 | convolution fusion | flops 3232759808 | bytes 8912896 | tf_op jit(solution)/shard_map/dot_general | solution.py:27
  408.9 2.3 slice.383
  414.5 2.0 copy-done.2
  416.5 1.3 fusion.11
  417.8 1.8 collective-permute-start.32
  419.6 1.5 pad_maximum_fusion.7
  421.8 1.8 bitcast_convert_fusion
  423.7 20.2 %collective-permute-done.32 = bf16[512,1024]{1,0:T(8,128)(2,1)} collective-permute-done((bf16[512,1024]{1,0:T(8,128)(2,1)}, bf16[512,1024]{1,0:T(8,128)(2,1)}, u32[]{:S(2)}, u32[]{:S(2)}) %collective-permute-start.32) | collective-permute-done | bytes 1048608 | tf_op jit(solution)/shard_map/ppermute | solution.py:37
  443.8 2.8 fusion.7
  446.7 4.1 fusion.10
  450.8 2.1 convert_element_type.280
  452.9 2.1 copy-done.9
  454.9 2.6 fusion.14
  457.5 1.7 collective-permute-start.30
  460.7 1.7 collective-permute-start.34
  465.2 18.3 %collective-permute-done.33 = bf16[32,768]{1,0:T(8,128)(2,1)S(1)} collective-permute-done((bf16[32,768]{1,0:T(8,128)(2,1)S(1)}, bf16[32,768]{1,0:T(8,128)(2,1)S(1)}, u32[]{:S(2)}, u32[]{:S(2)}) %collective-permute-start.33) | collective-permute-done | bytes 49184 | tf_op jit(solution)/shard_map/ppermute | solution.py:45
  483.5 1.3 collective-permute-done.34
  486.1 31.4 %reduce-scatter.6.cloned.1.call-done = bf16[1,128,2304]{2,1,0:T(8,128)(2,1)} async-done(((bf16[8,128,2304]{2,1,0:T(8,128)(2,1)}), bf16[1,128,2304]{2,1,0:T(8,128)(2,1)}) %reduce-scatter.6.cloned.1.call-update) | async-done | bytes 589840 | tf_op jit(solution)/shard_map/reduce_scatter | solution.py:97
  518.8 1.6 collective-permute-start.36
  520.9 3.6 fusion.18
  524.6 3.6 collective-permute-done.37
  (259 shorter events, 49.4 us)
Async XLA Ops:
  7.2 12.2 %copy-start.34 = (s32[2,256]{1,0:T(2,128)S(1)}, s32[2,256]{1,0:T(2,128)}, u32[]{:S(2)}) copy-start(s32[2,256]{1,0:T(2,128)} %param.12) | copy-start | bytes 6148
  7.2 12.2 %copy-start.15 = (bf16[2,256,1024]{2,1,0:T(8,128)(2,1)S(1)}, bf16[2,256,1024]{2,1,0:T(8,128)(2,1)}, u32[]{:S(2)}) copy-start(bf16[2,256,1024]{2,1,0:T(8,128)(2,1)} %param.13) | copy-start | bytes 3145732
  7.2 77.6 %all-gather.8.cloned.1.call-start = ((), (), s32[]{:S(2)}) async-start(), calls=%async_computation.7 | async-start | bytes 2654208 | tf_op jit(solution)/shard_map/all_gather | solution.py:244
  8.1 8.8 %collective-permute-start.8 = (bf16[1,64]{1,0:T(2,128)(2,1)S(1)}, bf16[1,64]{1,0:T(2,128)(2,1)S(1)}, u32[]{:S(2)}, u32[]{:S(2)}) collective-permute-start(bf16[1,64]{1,0:T(2,128)(2,1)S(1)} %maximum_bitcast_fusion.1), channel_id=1, source_target_pairs={{0,4},{4,0},{1,5},{5,1},{2,6},{6,2},{3,7},{7,3},{8,12},{12,8},{9,1... | collective-permute-start | bytes 392 | tf_op jit(solution)/shard_map/ppermute | solution.py:33
  8.5 7.7 %collective-permute-start.6 = (bf16[1,64]{1,0:T(2,128)(2,1)S(1)}, bf16[1,64]{1,0:T(2,128)(2,1)S(1)}, u32[]{:S(2)}, u32[]{:S(2)}) collective-permute-start(bf16[1,64]{1,0:T(2,128)(2,1)S(1)} %maximum_bitcast_fusion.1), channel_id=1, source_target_pairs={{0,8},{8,0},{1,9},{9,1},{2,10},{10,2},{3,11},{11,3},{4,12},{12,4},... | collective-permute-start | bytes 392 | tf_op jit(solution)/shard_map/ppermute | solution.py:37
  12.1 7.9 %copy-start.4 = (bf16[2,256,1024]{2,1,0:T(8,128)(2,1)S(1)}, bf16[2,256,1024]{2,1,0:T(8,128)(2,1)}, u32[]{:S(2)}) copy-start(bf16[2,256,1024]{2,1,0:T(8,128)(2,1)} %param.11) | copy-start | bytes 3145732
  12.1 9.7 %copy-start.22 = (bf16[32,4608]{1,0:T(8,128)(2,1)S(1)}, bf16[32,4608]{1,0:T(8,128)(2,1)}, u32[]{:S(2)}) copy-start(bf16[32,4608]{1,0:T(8,128)(2,1)} %param.19) | copy-start | bytes 884740
  12.6 5.9 %collective-permute-start.3 = (bf16[32,768]{1,0:T(8,128)(2,1)S(1)}, bf16[32,768]{1,0:T(8,128)(2,1)S(1)}, u32[]{:S(2)}, u32[]{:S(2)}) collective-permute-start(bf16[32,768]{1,0:T(8,128)(2,1)S(1)} %select_n.376), channel_id=1, source_target_pairs={{0,12},{4,8},{8,4},{12,0},{1,13},{5,9},{9,5},{13,1},{2,14},{6,10},... | collective-permute-start | bytes 147464 | tf_op jit(solution)/shard_map/ppermute | solution.py:45
  12.7 5.7 %collective-permute-start.4 = (bf16[32,768]{1,0:T(8,128)(2,1)S(1)}, bf16[32,768]{1,0:T(8,128)(2,1)S(1)}, u32[]{:S(2)}, u32[]{:S(2)}) collective-permute-start(bf16[32,768]{1,0:T(8,128)(2,1)S(1)} %select_n.380), channel_id=1, source_target_pairs={{0,8},{4,12},{8,0},{12,4},{1,9},{5,13},{9,1},{13,5},{2,10},{6,14},... | collective-permute-start | bytes 147464 | tf_op jit(solution)/shard_map/ppermute | solution.py:45
  14.5 3.9 collective-permute-start.5
  16.2 1.3 collective-permute-start.7
  19.3 156.4 %all-gather.10.cloned.1.call-start = ((), (), s32[]{:S(2)}) async-start(), calls=%async_computation.8 | async-start | bytes 5308416 | tf_op jit(solution)/shard_map/all_gather | solution.py:249
  19.7 4.9 copy-start.18
  19.7 51.7 %collective-permute-start.9 = (bf16[512,1024]{1,0:T(8,128)(2,1)S(1)}, bf16[512,1024]{1,0:T(8,128)(2,1)}, u32[]{:S(2)}, u32[]{:S(2)}) collective-permute-start(bf16[512,1024]{1,0:T(8,128)(2,1)S(1)} %fusion.6), channel_id=1, source_target_pairs={{0,8},{8,0},{1,9},{9,1},{2,10},{10,2},{3,11},{11,3},{4,12},{12,4},... | collective-permute-start | bytes 3145736 | tf_op jit(solution)/shard_map/ppermute | solution.py:37
  20.0 51.9 %collective-permute-start.1 = (bf16[512,1024]{1,0:T(8,128)(2,1)S(1)}, bf16[512,1024]{1,0:T(8,128)(2,1)}, u32[]{:S(2)}, u32[]{:S(2)}) collective-permute-start(bf16[512,1024]{1,0:T(8,128)(2,1)S(1)} %bitcast.123), channel_id=1, source_target_pairs={{0,8},{8,0},{1,9},{9,1},{2,10},{10,2},{3,11},{11,3},{4,12},{12,4},... | collective-permute-start | bytes 3145736 | tf_op jit(solution)/shard_map/ppermute | solution.py:37
  24.6 46.8 %collective-permute-start.21 = (bf16[32,2304]{1,0:T(8,128)(2,1)S(1)}, bf16[32,2304]{1,0:T(8,128)(2,1)S(1)}, u32[]{:S(2)}, u32[]{:S(2)}) collective-permute-start(bf16[32,2304]{1,0:T(8,128)(2,1)S(1)} %get-tuple-element.42), channel_id=1, source_target_pairs={{0,8},{4,12},{8,0},{12,4},{1,9},{5,13},{9,1},{13,5},{2,10},{6,14},... | collective-permute-start | bytes 442376 | tf_op jit(solution)/shard_map/ppermute | solution.py:45
  25.0 47.0 %collective-permute-start.22 = (bf16[32,2304]{1,0:T(8,128)(2,1)S(1)}, bf16[32,2304]{1,0:T(8,128)(2,1)S(1)}, u32[]{:S(2)}, u32[]{:S(2)}) collective-permute-start(bf16[32,2304]{1,0:T(8,128)(2,1)S(1)} %get-tuple-element.75), channel_id=1, source_target_pairs={{0,4},{4,0},{8,12},{12,8},{1,5},{5,1},{9,13},{13,9},{2,6},{6,2},{1... | collective-permute-start | bytes 442376 | tf_op jit(solution)/shard_map/ppermute | solution.py:45
  25.0 48.3 %collective-permute-start.20 = (bf16[32,2304]{1,0:T(8,128)(2,1)S(1)}, bf16[32,2304]{1,0:T(8,128)(2,1)S(1)}, u32[]{:S(2)}, u32[]{:S(2)}) collective-permute-start(bf16[32,2304]{1,0:T(8,128)(2,1)S(1)} %get-tuple-element.76), channel_id=1, source_target_pairs={{0,12},{4,8},{8,4},{12,0},{1,13},{5,9},{9,5},{13,1},{2,14},{6,10},... | collective-permute-start | bytes 442376 | tf_op jit(solution)/shard_map/ppermute | solution.py:45
  71.4 9.8 %collective-permute-start = (bf16[512,1024]{1,0:T(8,128)(2,1)S(1)}, bf16[512,1024]{1,0:T(8,128)(2,1)S(1)}, u32[]{:S(2)}, u32[]{:S(2)}) collective-permute-start(bf16[512,1024]{1,0:T(8,128)(2,1)S(1)} %bitcast.124), channel_id=1, source_target_pairs={{0,4},{4,0},{1,5},{5,1},{2,6},{6,2},{3,7},{7,3},{8,12},{12,8},{9,1... | collective-permute-start | bytes 3145736 | tf_op jit(solution)/shard_map/ppermute | solution.py:33
  71.4 7.9 %collective-permute-start.10 = (bf16[512,1024]{1,0:T(8,128)(2,1)}, bf16[512,1024]{1,0:T(8,128)(2,1)}, u32[]{:S(2)}, u32[]{:S(2)}) collective-permute-start(bf16[512,1024]{1,0:T(8,128)(2,1)} %collective-permute-done.9), channel_id=1, source_target_pairs={{0,4},{4,0},{1,5},{5,1},{2,6},{6,2},{3,7},{7,3},{8,12},{12,8},{9,1... | collective-permute-start | bytes 3145736 | tf_op jit(solution)/shard_map/ppermute | solution.py:33
  71.9 9.3 %collective-permute-start.2 = (bf16[512,1024]{1,0:T(8,128)(2,1)}, bf16[512,1024]{1,0:T(8,128)(2,1)S(1)}, u32[]{:S(2)}, u32[]{:S(2)}) collective-permute-start(bf16[512,1024]{1,0:T(8,128)(2,1)} %collective-permute-done.1), channel_id=1, source_target_pairs={{0,4},{4,0},{1,5},{5,1},{2,6},{6,2},{3,7},{7,3},{8,12},{12,8},{9,1... | collective-permute-start | bytes 3145736 | tf_op jit(solution)/shard_map/ppermute | solution.py:33
  74.2 132.9 %all-gather.6.cloned.1.call-start = ((), (), s32[]{:S(2)}) async-start(), calls=%async_computation.3 | async-start | bytes 2654208 | tf_op jit(solution)/shard_map/all_gather | solution.py:250
  74.5 3.7 collective-permute-start.12
  74.9 3.3 collective-permute-start.11
  78.1 1.2 collective-permute-start.13
  81.2 3.6 copy-start.27
  81.2 3.6 copy-start.29
  91.6 12.8 %copy-start.20 = (bf16[8,32,1024]{2,1,0:T(8,128)(2,1)}, bf16[8,32,1024]{2,1,0:T(8,128)(2,1)S(1)}, u32[]{:S(2)}) copy-start(bf16[8,32,1024]{2,1,0:T(8,128)(2,1)S(1)} %pad_maximum_fusion.14) | copy-start | bytes 1572868
  99.7 4.6 copy-start.6
  105.6 5.1 copy-start.1
  106.0 4.2 collective-permute-start.14
  112.7 25.4 %collective-permute-start.15 = (bf16[512,1024]{1,0:T(8,128)(2,1)S(1)}, bf16[512,1024]{1,0:T(8,128)(2,1)}, u32[]{:S(2)}, u32[]{:S(2)}) collective-permute-start(bf16[512,1024]{1,0:T(8,128)(2,1)S(1)} %fusion.22), channel_id=1, source_target_pairs={{0,8},{8,0},{1,9},{9,1},{2,10},{10,2},{3,11},{11,3},{4,12},{12,4},... | collective-permute-start | bytes 3145736 | tf_op jit(solution)/shard_map/ppermute | solution.py:37
  113.2 308.6 %reduce-scatter.8.cloned.1.call-start = ((), (), s32[]{:S(2)}) async-start(), calls=%async_computation.6 | async-start | bytes 2654208 | tf_op jit(solution)/shard_map/reduce_scatter | solution.py:97
  142.4 24.7 %collective-permute-start.18 = (bf16[512,1024]{1,0:T(8,128)(2,1)}, bf16[512,1024]{1,0:T(8,128)(2,1)}, u32[]{:S(2)}, u32[]{:S(2)}) collective-permute-start(bf16[512,1024]{1,0:T(8,128)(2,1)} %multiply_convert_fusion.4), channel_id=1, source_target_pairs={{0,8},{8,0},{1,9},{9,1},{2,10},{10,2},{3,11},{11,3},{4,12},{12,4},... | collective-permute-start | bytes 3145736 | tf_op jit(solution)/shard_map/ppermute | solution.py:37
  142.6 24.4 %collective-permute-start.16 = (bf16[512,1024]{1,0:T(8,128)(2,1)S(1)}, bf16[512,1024]{1,0:T(8,128)(2,1)S(1)}, u32[]{:S(2)}, u32[]{:S(2)}) collective-permute-start(bf16[512,1024]{1,0:T(8,128)(2,1)S(1)} %copy-done.19), channel_id=1, source_target_pairs={{0,4},{4,0},{1,5},{5,1},{2,6},{6,2},{3,7},{7,3},{8,12},{12,8},{9,1... | collective-permute-start | bytes 3145736 | tf_op jit(solution)/shard_map/ppermute | solution.py:33
  142.6 38.0 %collective-permute-start.17 = (bf16[512,1024]{1,0:T(8,128)(2,1)}, bf16[512,1024]{1,0:T(8,128)(2,1)}, u32[]{:S(2)}, u32[]{:S(2)}) collective-permute-start(bf16[512,1024]{1,0:T(8,128)(2,1)} %multiply_convert_fusion.4), channel_id=1, source_target_pairs={{0,4},{4,0},{1,5},{5,1},{2,6},{6,2},{3,7},{7,3},{8,12},{12,8},{9,1... | collective-permute-start | bytes 3145736 | tf_op jit(solution)/shard_map/ppermute | solution.py:33
  167.0 13.6 %collective-permute-start.19 = (bf16[512,1024]{1,0:T(8,128)(2,1)}, bf16[512,1024]{1,0:T(8,128)(2,1)}, u32[]{:S(2)}, u32[]{:S(2)}) collective-permute-start(bf16[512,1024]{1,0:T(8,128)(2,1)} %collective-permute-done.18), channel_id=1, source_target_pairs={{0,4},{4,0},{1,5},{5,1},{2,6},{6,2},{3,7},{7,3},{8,12},{12,8},{9,1... | collective-permute-start | bytes 3145736 | tf_op jit(solution)/shard_map/ppermute | solution.py:33
  247.1 4.7 copy-start.13
  247.1 4.2 collective-permute-start.23
  252.2 25.9 %copy-start.16 = (bf16[2,256,1024]{2,1,0:T(8,128)(2,1)S(1)}, bf16[2,256,1024]{2,1,0:T(8,128)(2,1)}, u32[]{:S(2)}) copy-start(bf16[2,256,1024]{2,1,0:T(8,128)(2,1)} %param.13) | copy-start | bytes 3145732
  252.2 25.3 %collective-permute-start.24 = (bf16[512,1024]{1,0:T(8,128)(2,1)S(1)}, bf16[512,1024]{1,0:T(8,128)(2,1)S(1)}, u32[]{:S(2)}, u32[]{:S(2)}) collective-permute-start(bf16[512,1024]{1,0:T(8,128)(2,1)S(1)} %fusion.19), channel_id=1, source_target_pairs={{0,8},{8,0},{1,9},{9,1},{2,10},{10,2},{3,11},{11,3},{4,12},{12,4},... | collective-permute-start | bytes 3145736 | tf_op jit(solution)/shard_map/ppermute | solution.py:37
  280.7 24.7 %collective-permute-start.26 = (bf16[512,1024]{1,0:T(8,128)(2,1)}, bf16[512,1024]{1,0:T(8,128)(2,1)}, u32[]{:S(2)}, u32[]{:S(2)}) collective-permute-start(bf16[512,1024]{1,0:T(8,128)(2,1)} %get-tuple-element.40), channel_id=1, source_target_pairs={{0,8},{8,0},{1,9},{9,1},{2,10},{10,2},{3,11},{11,3},{4,12},{12,4},... | collective-permute-start | bytes 3145736 | tf_op jit(solution)/shard_map/ppermute | solution.py:37
  282.3 32.6 %collective-permute-start.25 = (bf16[512,1024]{1,0:T(8,128)(2,1)}, bf16[512,1024]{1,0:T(8,128)(2,1)}, u32[]{:S(2)}, u32[]{:S(2)}) collective-permute-start(bf16[512,1024]{1,0:T(8,128)(2,1)} %get-tuple-element.40), channel_id=1, source_target_pairs={{0,4},{4,0},{1,5},{5,1},{2,6},{6,2},{3,7},{7,3},{8,12},{12,8},{9,1... | collective-permute-start | bytes 3145736 | tf_op jit(solution)/shard_map/ppermute | solution.py:33
  305.4 9.5 %collective-permute-start.27 = (bf16[512,1024]{1,0:T(8,128)(2,1)}, bf16[512,1024]{1,0:T(8,128)(2,1)}, u32[]{:S(2)}, u32[]{:S(2)}) collective-permute-start(bf16[512,1024]{1,0:T(8,128)(2,1)} %collective-permute-done.26), channel_id=1, source_target_pairs={{0,4},{4,0},{1,5},{5,1},{2,6},{6,2},{3,7},{7,3},{8,12},{12,8},{9,1... | collective-permute-start | bytes 3145736 | tf_op jit(solution)/shard_map/ppermute | solution.py:33
  314.8 144.4 %reduce-scatter.4.cloned.1.call-start = ((), (), s32[]{:S(2)}) async-start(), calls=%async_computation.4 | async-start | bytes 1474560 | tf_op jit(solution)/shard_map/reduce_scatter | solution.py:89
  332.9 5.8 %copy-start.26 = (bf16[2048,256]{1,0:T(8,128)(2,1)}, bf16[2048,256]{1,0:T(8,128)(2,1)S(1)}, u32[]{:S(2)}) copy-start(bf16[2048,256]{1,0:T(8,128)(2,1)S(1)} %multiply_convert_fusion) | copy-start | bytes 3145732
  346.3 35.5 %collective-permute-start.28 = (bf16[4,144,1024]{2,1,0:T(8,128)(2,1)}, bf16[4,144,1024]{2,1,0:T(8,128)(2,1)}, u32[]{:S(2)}, u32[]{:S(2)}) collective-permute-start(bf16[4,144,1024]{2,1,0:T(8,128)(2,1)} %dynamic-slice_bitcast_fusion), channel_id=1, source_target_pairs={{0,16},{16,0},{1,17},{17,1},{2,18},{18,2},{3,19},{19,3},{4,20},{20... | collective-permute-start | bytes 3538952 | tf_op jit(solution)/shard_map/ppermute | solution.py:41
  385.0 132.5 %reduce-scatter.6.cloned.1.call-start = ((), (), s32[]{:S(2)}) async-start(), calls=%async_computation.5 | async-start | bytes 5308416 | tf_op jit(solution)/shard_map/reduce_scatter | solution.py:97
  408.4 5.1 copy-start.14
  408.6 3.5 copy-start.17
  408.8 4.2 collective-permute-start.31
  417.8 26.1 %collective-permute-start.32 = (bf16[512,1024]{1,0:T(8,128)(2,1)}, bf16[512,1024]{1,0:T(8,128)(2,1)}, u32[]{:S(2)}, u32[]{:S(2)}) collective-permute-start(bf16[512,1024]{1,0:T(8,128)(2,1)} %fusion.11), channel_id=1, source_target_pairs={{0,8},{8,0},{1,9},{9,1},{2,10},{10,2},{3,11},{11,3},{4,12},{12,4},... | collective-permute-start | bytes 3145736 | tf_op jit(solution)/shard_map/ppermute | solution.py:37
  421.1 29.7 %collective-permute-start.29 = (bf16[1024,1024]{1,0:T(8,128)(2,1)}, bf16[1024,1024]{1,0:T(8,128)(2,1)}, u32[]{:S(2)}, u32[]{:S(2)}) collective-permute-start(bf16[1024,1024]{1,0:T(8,128)(2,1)} %pad_maximum_fusion.7), channel_id=1, source_target_pairs={{0,4},{4,0},{1,5},{5,1},{2,6},{6,2},{3,7},{7,3},{8,12},{12,8},{9,1... | collective-permute-start | bytes 6291464 | tf_op jit(solution)/shard_map/ppermute | solution.py:33
  423.6 23.0 %copy-start.3 = (f32[1024,1024]{1,0:T(8,128)S(1)}, f32[1024,1024]{1,0:T(8,128)}, u32[]{:S(2)}) copy-start(f32[1024,1024]{1,0:T(8,128)} %copy-done.2) | copy-start | bytes 12582916
  457.5 27.9 %copy-start.32 = (bf16[32,3072]{1,0:T(8,128)(2,1)S(1)}, bf16[32,3072]{1,0:T(8,128)(2,1)}, u32[]{:S(2)}) copy-start(bf16[32,3072]{1,0:T(8,128)(2,1)} %param.15) | copy-start | bytes 589828
  457.5 63.4 %collective-permute-start.30 = (bf16[512,1024]{1,0:T(8,128)(2,1)}, bf16[512,1024]{1,0:T(8,128)(2,1)}, u32[]{:S(2)}, u32[]{:S(2)}) collective-permute-start(bf16[512,1024]{1,0:T(8,128)(2,1)} %fusion.14), channel_id=1, source_target_pairs={{0,8},{8,0},{1,9},{9,1},{2,10},{10,2},{3,11},{11,3},{4,12},{12,4},... | collective-permute-start | bytes 3145736 | tf_op jit(solution)/shard_map/ppermute | solution.py:37
  459.3 26.4 %copy-start.35 = (bf16[32]{0:T(256)(128)(2,1)S(1)}, bf16[32]{0:T(256)(128)(2,1)}, u32[]{:S(2)}) copy-start(bf16[32]{0:T(256)(128)(2,1)} %param.14) | copy-start | bytes 196
  460.2 5.0 collective-permute-start.35
  460.2 23.2 %collective-permute-start.33 = (bf16[32,768]{1,0:T(8,128)(2,1)S(1)}, bf16[32,768]{1,0:T(8,128)(2,1)S(1)}, u32[]{:S(2)}, u32[]{:S(2)}) collective-permute-start(bf16[32,768]{1,0:T(8,128)(2,1)S(1)} %get-tuple-element.86), channel_id=1, source_target_pairs={{0,12},{4,8},{8,4},{12,0},{1,13},{5,9},{9,5},{13,1},{2,14},{6,10},... | collective-permute-start | bytes 147464 | tf_op jit(solution)/shard_map/ppermute | solution.py:45
  460.7 24.1 %collective-permute-start.34 = (bf16[32,768]{1,0:T(8,128)(2,1)S(1)}, bf16[32,768]{1,0:T(8,128)(2,1)S(1)}, u32[]{:S(2)}, u32[]{:S(2)}) collective-permute-start(bf16[32,768]{1,0:T(8,128)(2,1)S(1)} %get-tuple-element.87), channel_id=1, source_target_pairs={{0,8},{4,12},{8,0},{12,4},{1,9},{5,13},{9,1},{13,5},{2,10},{6,14},... | collective-permute-start | bytes 147464 | tf_op jit(solution)/shard_map/ppermute | solution.py:45
  485.4 39.1 %copy-start.21 = (f32[32,3072]{1,0:T(8,128)}, f32[32,3072]{1,0:T(8,128)S(1)}, u32[]{:S(2)}) copy-start(f32[32,3072]{1,0:T(8,128)S(1)} %reshape.415) | copy-start | bytes 1179652
  518.7 5.8 %collective-permute-start.38 = (bf16[32,2304]{1,0:T(8,128)(2,1)S(1)}, bf16[32,2304]{1,0:T(8,128)(2,1)S(1)}, u32[]{:S(2)}, u32[]{:S(2)}) collective-permute-start(bf16[32,2304]{1,0:T(8,128)(2,1)S(1)} %get-tuple-element.70), channel_id=1, source_target_pairs={{0,4},{4,0},{8,12},{12,8},{1,5},{5,1},{9,13},{13,9},{2,6},{6,2},{1... | collective-permute-start | bytes 442376 | tf_op jit(solution)/shard_map/ppermute | solution.py:45
  518.8 5.8 %collective-permute-start.36 = (bf16[32,2304]{1,0:T(8,128)(2,1)S(1)}, bf16[32,2304]{1,0:T(8,128)(2,1)S(1)}, u32[]{:S(2)}, u32[]{:S(2)}) collective-permute-start(bf16[32,2304]{1,0:T(8,128)(2,1)S(1)} %get-tuple-element.71), channel_id=1, source_target_pairs={{0,12},{4,8},{8,4},{12,0},{1,13},{5,9},{9,5},{13,1},{2,14},{6,10},... | collective-permute-start | bytes 442376 | tf_op jit(solution)/shard_map/ppermute | solution.py:45
  520.4 7.8 %collective-permute-start.37 = (bf16[32,2304]{1,0:T(8,128)(2,1)S(1)}, bf16[32,2304]{1,0:T(8,128)(2,1)S(1)}, u32[]{:S(2)}, u32[]{:S(2)}) collective-permute-start(bf16[32,2304]{1,0:T(8,128)(2,1)S(1)} %get-tuple-element.72), channel_id=1, source_target_pairs={{0,8},{4,12},{8,0},{12,4},{1,9},{5,13},{9,1},{13,5},{2,10},{6,14},... | collective-permute-start | bytes 442376 | tf_op jit(solution)/shard_map/ppermute | solution.py:45
  (19 other events, 38.1 us)
Sparse Core Ops, SparseCore 0:
  19.4 52.3 all-gather.7
  74.5 80.0 all-gather.9
  156.8 50.2 all-gather.5
  315.0 74.6 reduce-scatter.7
  391.8 28.0 reduce-scatter.3
  423.4 94.1 reduce-scatter.5

commit v5 on v4

--- a/solution.py
+++ b/solution.py
@@ -62,18 +62,23 @@
     return reorder(near[:1] + [swap_far(near[j], j) for j in range(1, len(near))])
 
 
+def team_pieces(rows):
+    across = swap_chip(rows)
+    return [rows, swap_core(rows), across, swap_core(across)]
+
+
 def team_rows(rows):
-    across = swap_chip(rows)
-    return jnp.concatenate([rows, swap_core(rows), across, swap_core(across)], axis=0)
-
-
-def team_sum(terms):
+    return jnp.concatenate(team_pieces(rows), axis=0)
+
+
+def team_sum(terms, token=None):
     count = terms.shape[0] // TEAM
     sent = jnp.concatenate([terms[count : 2 * count], terms[3 * count :]], axis=0)
     came = swap_core(sent).astype(f32)
     own = terms[:count].astype(f32) + came[:count]
     other = terms[2 * count : 3 * count].astype(f32) + came[count:]
-    return own + swap_chip(other.astype(bf16)).astype(f32)
+    came = swap_chip(other.astype(bf16)).astype(f32)
+    return own + (came if token is None else after(came, token))
 
 
 def take(blocks, index):
@@ -86,10 +91,9 @@
         row = lax.axis_index("y")
         came = swap_row(take(part, 1 - row))
         summed = (take(part, row).astype(f32) + came.astype(f32)).astype(bf16)
-        return lax.psum_scatter(summed, "s", scatter_dimension=0, tiled=False), summed[0, :1]
+        return lax.psum_scatter(summed, "s", scatter_dimension=0, tiled=False)
     flat = part.reshape((groups * slots,) + part.shape[2:]).astype(f32)
-    total = lax.psum_scatter(flat, ("g", "y", "s"), scatter_dimension=0, tiled=False)
-    return total, total[:1]
+    return lax.psum_scatter(flat, ("g", "y", "s"), scatter_dimension=0, tiled=False)
 
 
 def scatter_rest(part):
@@ -97,7 +101,16 @@
     return lax.psum_scatter(wide, ("g", "y", "s"), scatter_dimension=0, tiled=False)
 
 
-def forward_kernel(normed_ref, pair_ref, hidden_ref, silu_ref, slope_ref):
+def forward_kernel(*refs):
+    pieces, pair_ref = refs[: 2 * TEAM], refs[2 * TEAM]
+    hidden_ref, silu_ref, slope_ref, normed_ref, grad_ref = refs[2 * TEAM + 1 :]
+    for k in range(TEAM):
+
+        @pl.when(pl.program_id(0) == k)
+        def _():
+            normed_ref[...] = pieces[k][...]
+            grad_ref[...] = pieces[TEAM + k][...]
+
     width = hidden_ref.shape[1]
     values = forward_dot(normed_ref[...], pair_ref[...])
     gate_value, up_value = values[:, :width], values[:, width:]
@@ -109,8 +122,18 @@
 
 
 def backward_kernel(
-    grad_ref, hidden_ref, silu_ref, slope_ref, pair_ref, down_ref, pair_grad_ref, normed_ref, out_ref
+    grad_ref,
+    hidden_ref,
+    silu_ref,
+    slope_ref,
+    pair_ref,
+    down_ref,
+    token_ref,
+    pair_grad_ref,
+    normed_ref,
+    out_ref,
 ):
+    del token_ref
     width = hidden_ref.shape[1]
     hidden_grad = back_dot(grad_ref[...], down_ref[...])
     pair_grad_ref[:, :width] = (hidden_grad * slope_ref[...].astype(f32)).astype(bf16)
@@ -119,9 +142,8 @@
     out_ref[...] = forward_dot(hidden_ref[...], down_ref[...]).astype(bf16)
 
 
-def by_rows(kernel, rowed, whole, columns, flops, transcendentals):
-    rows = rowed[0].shape[0]
-    tile = min(ROW_TILE, rows)
+def by_rows(kernel, tile, steps, rowed, whole, tokens, columns, flops, transcendentals):
+    rows = steps * tile
 
     def row_block(count):
         return pl.BlockSpec((tile, count), lambda i: (i, 0))
@@ -129,19 +151,20 @@
     moved = sum(2 * value.size for value in rowed + whole) + 2 * rows * sum(columns)
     return pl.pallas_call(
         kernel,
-        grid=(rows // tile,),
+        grid=(steps,),
         in_specs=[row_block(value.shape[1]) for value in rowed]
         + [
             pl.BlockSpec(value.shape, lambda i: (0, 0), pipeline_mode=pl.Buffered(1))
             for value in whole
-        ],
+        ]
+        + [pl.BlockSpec(memory_space=pl.ANY)] * len(tokens),
         out_specs=[row_block(count) for count in columns],
         out_shape=[jax.ShapeDtypeStruct((rows, count), bf16) for count in columns],
         compiler_params=pltpu.CompilerParams(vmem_limit_bytes=52 * 1024 * 1024),
         cost_estimate=pl.CostEstimate(
             flops=flops, bytes_accessed=moved, transcendentals=transcendentals
         ),
-    )(*rowed, *whole)
+    )(*rowed, *whole, *tokens)
 
 
 def shifted_down(rows, step):
@@ -264,11 +287,11 @@
     team_places = team_rows(places)
     live = (places >= 0).astype(f32)
     upstream = cotangent.reshape(rows, features).astype(f32)
-    ffn_grad = team_rows((live * upstream).astype(bf16))
+    ffn_pieces = team_pieces((live * upstream).astype(bf16))
     inputs = tokens.reshape(rows, features).astype(f32)
 
     values = team_tokens.astype(f32)
-    early_full = after(norm_full, ffn_grad[-1:])
+    early_full = after(norm_full, ffn_pieces[3][-1:])
     first_normed = (values * inverse_rms(values) * early_full).astype(bf16)
     projected = forward_dot(first_normed, in_full)
     b_part = projected[:, :chan]
@@ -284,20 +307,31 @@
     mixer_out = team_sum(forward_dot(mixer_in, out_full).astype(bf16))
     middle = inputs + live * mixer_out
     second_scale = inverse_rms(middle)
-    second_normed = team_rows((middle * second_scale * ffn_full).astype(bf16))
+    second_pieces = team_pieces((middle * second_scale * ffn_full).astype(bf16))
 
     team_count = TEAM * rows
     unit = 2 * team_count * features * hid
-    hidden, silu, slope = by_rows(
-        forward_kernel, [second_normed], [pair_full], [hid] * 3, 2 * unit, team_count * hid
+    hidden, silu, slope, second_normed, ffn_grad = by_rows(
+        forward_kernel,
+        rows,
+        TEAM,
+        [],
+        second_pieces + ffn_pieces + [pair_full],
+        [],
+        [hid] * 3 + [features] * 2,
+        2 * unit,
+        team_count * hid,
     )
     owners = groups * slots
     down_part = rows_dot(hidden, ffn_grad).astype(bf16)
     grad_down = scatter_rest(down_part.reshape(owners, hidden_share, features))
     pair_grad, normed_part, out_part = by_rows(
         backward_kernel,
+        ROW_TILE,
+        team_count // ROW_TILE,
         [ffn_grad, hidden, silu, slope],
         [pair_full, down_full],
+        [down_part],
         [2 * hid, features, features],
         4 * unit,
         0,
@@ -311,7 +345,7 @@
 
     pair_part = by_owner(rows_dot(second_normed, pair_grad), TEAM)
     pair_sum = scatter_rest(pair_part.reshape(owners, tall, 2 * hid))
-    normed_sum = team_sum(normed_part)
+    normed_sum = team_sum(normed_part, pair_part[0, 0, :1])
     second_weighted = ffn_full * normed_sum
     middle_grad = upstream + norm_back(middle, second_scale, second_weighted)
 
@@ -344,7 +378,7 @@
         conv_rows.astype(bf16),
         ((0, 0), (0, 0), (0, EXTRA_ROWS - 1), (0, features - taps * share)),
     )
-    first_sum, token = scatter_first(
+    first_sum = scatter_first(
         jnp.concatenate(
             [jnp.concatenate([in_part, out_grad_part], axis=3), conv_rows], axis=2
         )
@@ -353,7 +387,7 @@
     first_weighted = norm_full * team_sum(back_dot(projected_grad, in_full).astype(bf16))
     input_grad = middle_grad + norm_back(inputs, inverse_rms(inputs), first_weighted)
     input_grad = input_grad.astype(bf16)
-    out_sum = team_sum(after(out_part, token))
+    out_sum = team_sum(after(out_part, mixer_grad[-1:]))
     block_out = (middle + live * out_sum).astype(bf16)
 
     def own_rows(summed, parts, team, run):

time: 545 us -> 535 us (0.982)
  waiting for transfers between devices: 272 us -> 287 us
  other arithmetic: 71.1 us -> 59.8 us
  Pallas kernels: 53 us -> 45.9 us
    reduce_scatter x2, waiting for transfers between devices: 31.4 us -> 55 us  [scatter_rest(): lax.psum_scatter(wide, ('g', 'y', 's'), scatter_dimension=0, tiled=False)]
    ppermute x12, waiting for transfers between devices: 69 us -> 54.4 us  [swap_far(): lax.ppermute(values, ('x', 'c'), [(i, i ^ distance) for i in range(TEAM)])]
    concatenate x2 -> x0, other arithmetic: 11.6 us -> none  [team_rows(): jnp.concatenate([rows, swap_core(rows), across, swap_core(across)], axis=0)]
    pallas_call x2, Pallas kernels: 53 us -> 45.9 us  [by_rows(): pl.pallas_call(kernel, grid=(steps,), in_specs=[row_block(value.shape[1])...]
    all_gather x1, waiting for transfers between devices: 7.6 us -> 13.9 us  [per_device(): down_full = lax.all_gather(down_weight, ('g', 'y', 's'), axis=0, tiled=True)]
    unnamed x80 -> x92, local copies, waits for them, and re-layouts: 13.7 us -> 9.99 us
  transfers between devices with their start and end apart: 45 -> 45, of which waited for: 19 -> 19; matrix products, arithmetic and copies ran while one was open for 27% -> 23% of each run, Pallas kernels for 3% -> 3%
where the time goes in v5:
time: 535 us; the launch traced here: 530 us
  waiting for transfers between devices  287 us (54%)
  other arithmetic  59.8 us (11%)
  matrix products  53.7 us (10%)
  Pallas kernels  45.9 us (9%)
  local copies, waits for them, and re-layouts  38.7 us (7%)
  starting transfers between devices  27 us (5%)
  between operations  17.5 us (3%)
    ppermute x10, waiting for transfers between devices, swap_chip(): return lax.ppermute(values, 'x', [(0, 1), (1, 0)])  116 us
    reduce_scatter x2, waiting for transfers between devices, scatter_rest(): lax.psum_scatter(wide, ('g', 'y', 's'), scatter_dimension=0, tiled=False)  55 us
    ppermute x12, waiting for transfers between devices, swap_far(): lax.ppermute(values, ('x', 'c'), [(i, i ^ distance) for i in range(TEAM)])  54.4 us
    pallas_call x2, Pallas kernels, by_rows(): pl.pallas_call(kernel, grid=(steps,), in_specs=[row_block(value.shape[1])...  45.9 us
    ppermute x1, waiting for transfers between devices, swap_row(): return lax.ppermute(values, 'y', [(0, 1), (1, 0)])  34.6 us
    dot_general x4, matrix products, rows_dot(): lax.dot_general(left_side, right_side, (((0,), (0,)), ((), ())), preferre...  29.7 us
    dot_general x2, matrix products, back_dot(): lax.dot_general(left_side, right_side, (((1,), (1,)), ((), ())), preferre...  15.4 us
    all_gather x1, waiting for transfers between devices, per_device(): down_full = lax.all_gather(down_weight, ('g', 'y', 's'), axis=0, tiled=True)  13.9 us
  transfers between devices with their start and end apart: 45, of which 19 were waited for; matrix products, arithmetic and copies ran while one was open for 23% of the time, Pallas kernels for 3%

profile of v5, /device:TPU:0, one launch (start us, length us, event | category | flops | bytes accessed | tf_op | source)
XLA Modules:
  0.0 529.8 jit_solution(7842571340273629870)
XLA Ops:
  8.1 2.9 collective-permute-start.6
  12.8 2.0 collective-permute-start.4
  20.1 1.2 fusion.6.refs_4_
  21.3 1.7 collective-permute-start.9
  25.3 1.8 collective-permute-start.20
  27.5 44.8 %collective-permute-done.20 = bf16[32,2304]{1,0:T(8,128)(2,1)S(1)} collective-permute-done((bf16[32,2304]{1,0:T(8,128)(2,1)S(1)}, bf16[32,2304]{1,0:T(8,128)(2,1)S(1)}, u32[]{:S(2)}, u32[]{:S(2)}) %collective-permute-start.20) | collective-permute-done | bytes 147488 | tf_op jit(solution)/shard_map/ppermute | solution.py:45
  73.5 2.3 collective-permute-done.21
  76.9 1.5 collective-permute-done.10.refs_7_
  78.4 1.2 slice.354
  80.3 3.5 fusion
  83.9 1.5 slice.355
  87.1 1.3 copy.65
  90.8 7.4 %fusion.26 = f32[2048,768]{1,0:T(8,128)S(1)} fusion(bf16[1024,768]{1,0:T(8,128)(2,1)S(1)} %bitcast.154, f32[1024]{0:T(1024)S(1)} %mul.304, f32[2048]{0:T(1024)S(1)} %add_rsqrt_fusion, bf16[512,1024]{1,0:T(8,128)(2,1)} %copy-done.34, bf16[512,1024]{1,0:T(8,128)(2,1)} %collective-permute-done.1, bf16[512,1024]{1,0:T(8,128)(2,1)} %copy-done.32, ...), kind=kOutput, calls=%fused_computation.76 | convolution fusion | flops 3244294144 | bytes 12070912 | tf_op jit(solution)/shard_map/dot_general | solution.py:17
  98.5 2.3 copy-done
  100.8 2.3 multiply_convert_fusion.5
  103.1 1.3 convolution_convert_fusion.2
  105.0 4.0 collective-permute-done.14
  109.9 1.6 copy-done.10
  111.5 1.6 collective-permute-start.15
  113.2 23.6 %collective-permute-done.15 = bf16[512,1024]{1,0:T(8,128)(2,1)} collective-permute-done((bf16[512,1024]{1,0:T(8,128)(2,1)S(1)}, bf16[512,1024]{1,0:T(8,128)(2,1)}, u32[]{:S(2)}, u32[]{:S(2)}) %collective-permute-start.15) | collective-permute-done | bytes 1048608 | tf_op jit(solution)/shard_map/ppermute | solution.py:37
  136.8 2.9 multiply_reduce_fusion.5
  140.0 1.7 collective-permute-start.17
  142.5 22.0 %collective-permute-done.17.refs_2_ = bf16[512,1024]{1,0:T(8,128)(2,1)} collective-permute-done((bf16[512,1024]{1,0:T(8,128)(2,1)S(1)}, bf16[512,1024]{1,0:T(8,128)(2,1)}, u32[]{:S(2)}, u32[]{:S(2)}) %collective-permute-start.17) | collective-permute-done | bytes 1048608 | tf_op jit(solution)/shard_map/ppermute | solution.py:37
  164.5 5.0 copy.68
  169.6 17.7 %shard_map.186 = (bf16[2048,1152]{1,0:T(8,128)(2,1)}, bf16[2048,1152]{1,0:T(8,128)(2,1)}, bf16[2048,1152]{1,0:T(8,128)(2,1)}, bf16[2048,1024]{1,0:T(8,128)(2,1)}, bf16[2048,1024]{1,0:T(8,128)(2,1)}) custom-call(bf16[512,1024]{1,0:T(8,128)(2,1)S(1)} %multiply_convert_fusion.4.refs_0_, bf16[512,1024]{1,0:T(8,128)(2,1)} %collective-permute-done.16.refs_1_, ...), custom_call_target="tpu_custom_call" | custom-call | flops 9663676416 | bytes 35651584 | tf_op jit(solution)/shard_map/pallas_call | solution.py:152
  187.3 9.4 %convolution_convert_fusion.1.token_ref = bf16[1152,1024]{1,0:T(8,128)(2,1)} fusion(bf16[2048,1152]{1,0:T(8,128)(2,1)} %get-tuple-element.19.hidden_ref, bf16[2048,1024]{1,0:T(8,128)(2,1)} %get-tuple-element.18.grad_ref), kind=kOutput, calls=%fused_computation.10 | convolution fusion | flops 4833017856 | bytes 11272192 | tf_op jit(solution)/shard_map/dot_general | solution.py:21
  196.7 13.9 %all-gather.6.cloned.1.call-done.down_ref = bf16[1152,1024]{1,0:T(8,128)(2,1)} async-done(((bf16[144,1024]{1,0:T(8,128)(2,1)}), bf16[1152,1024]{1,0:T(8,128)(2,1)}) %all-gather.6.cloned.1.call-update) | async-done | bytes 2359312 | tf_op jit(solution)/shard_map/all_gather | solution.py:273
  210.6 28.1 %shard_map.187 = (bf16[2048,2304]{1,0:T(8,128)(2,1)}, bf16[2048,1024]{1,0:T(8,128)(2,1)}, bf16[2048,1024]{1,0:T(8,128)(2,1)}) custom-call(bf16[2048,1024]{1,0:T(8,128)(2,1)} %get-tuple-element.18.grad_ref, bf16[2048,1152]{1,0:T(8,128)(2,1)} %get-tuple-element.19.hidden_ref, bf16[2048,1152]{1,0:T(8,128)(2,1)} %get-tuple-element.20.silu_ref, ...), custom_call_target="tpu_custom_call" | custom-call | flops 19327352832 | bytes 43253760 | tf_op jit(solution)/shard_map/pallas_call | solution.py:152
  238.8 1.7 fusion.45
  240.7 4.1 collective-permute-done.23
  245.4 4.1 fusion.19
  249.4 1.5 collective-permute-start.24
  250.9 11.4 %convolution_convert_fusion = bf16[1024,2304]{1,0:T(8,128)(2,1)S(1)} fusion(bf16[2048,1024]{1,0:T(8,128)(2,1)S(1)} %copy-done.43, bf16[2048,2304]{1,0:T(8,128)(2,1)S(1)} %copy-done.42), kind=kOutput, calls=%fused_computation.5 | convolution fusion | flops 9666035712 | bytes 18350080 | tf_op jit(solution)/shard_map/dot_general | solution.py:21
  262.6 2.1 copy-done.8
  266.0 8.8 %collective-permute-done.24 = bf16[512,1024]{1,0:T(8,128)(2,1)S(1)} collective-permute-done((bf16[512,1024]{1,0:T(8,128)(2,1)}, bf16[512,1024]{1,0:T(8,128)(2,1)S(1)}, u32[]{:S(2)}, u32[]{:S(2)}) %collective-permute-start.24) | collective-permute-done | bytes 1048608 | tf_op jit(solution)/shard_map/ppermute | solution.py:37
  274.8 2.5 multiply_reduce_fusion.4
  277.3 3.8 multiply_convert_fusion.3
  281.1 1.5 collective-permute-start.25
  282.6 23.2 %collective-permute-done.25 = bf16[512,1024]{1,0:T(8,128)(2,1)} collective-permute-done((bf16[512,1024]{1,0:T(8,128)(2,1)}, bf16[512,1024]{1,0:T(8,128)(2,1)}, u32[]{:S(2)}, u32[]{:S(2)}) %collective-permute-start.25) | collective-permute-done | bytes 1048608 | tf_op jit(solution)/shard_map/ppermute | solution.py:37
  306.1 2.8 collective-permute-done.26
  308.8 9.5 %multiply_reduce_fusion.2 = (bf16[256]{0:T(256)(128)(2,1)S(1)}, bf16[256]{0:T(256)(128)(2,1)S(1)}, bf16[256]{0:T(256)(128)(2,1)S(1)}, f32[2048,256]{1,0:T(8,128)S(1)}, bf16[2048,256]{1,0:T(8,128)(2,1)S(1)}) fusion(f32[2048,256]{1,0:T(8,128)} %copy-done.9, f32[2046,256]{1,0:T(8,128)} %bitcast.138, f32[2048]{0:T(1024)S(1)} %get-tuple-element.114, ...), kind=kOutput, calls=%fused_computation.57 | convolution fusion | flops 1096285440 | bytes 18364928 | tf_op jit(solution)/shard_map/dot_general | solution.py:27
  319.0 2.5 multiply_convert_fusion.2
  321.6 2.3 multiply_convert_fusion
  324.5 5.1 convolution_convert_fusion.4
  329.6 1.3 copy.70
  331.2 3.9 convolution_convert_fusion.5
  335.6 1.4 copy-done.14
  338.7 34.6 %collective-permute-done.32 = bf16[4,144,1024]{2,1,0:T(8,128)(2,1)} collective-permute-done((bf16[4,144,1024]{2,1,0:T(8,128)(2,1)}, bf16[4,144,1024]{2,1,0:T(8,128)(2,1)}, u32[]{:S(2)}, u32[]{:S(2)}) %collective-permute-start.32) | collective-permute-done | bytes 1179680 | tf_op jit(solution)/shard_map/ppermute | solution.py:41
  373.2 3.1 fusion.5
  377.0 5.9 %convolution_convert_fusion.3 = bf16[2048,1024]{1,0:T(8,128)(2,1)S(1)} fusion(bf16[1024,768]{1,0:T(8,128)(2,1)} %bitcast.153, bf16[2048,256]{1,0:T(8,128)(2,1)} %copy-done.31, bf16[2048,256]{1,0:T(8,128)(2,1)} %copy-done.41, bf16[2048,256]{1,0:T(8,128)(2,1)} %copy-done.30), kind=kOutput, calls=%fused_computation.12 | convolution fusion | flops 3232759808 | bytes 8912896 | tf_op jit(solution)/shard_map/dot_general | solution.py:27
  383.3 2.3 slice.383
  388.3 1.6 fusion.11
  390.6 1.5 collective-permute-start.31
  392.9 1.6 fusion.14
  396.0 1.8 bitcast_convert_fusion
  397.8 19.1 %collective-permute-done.31 = bf16[512,1024]{1,0:T(8,128)(2,1)} collective-permute-done((bf16[512,1024]{1,0:T(8,128)(2,1)}, bf16[512,1024]{1,0:T(8,128)(2,1)}, u32[]{:S(2)}, u32[]{:S(2)}) %collective-permute-start.31) | collective-permute-done | bytes 1048608 | tf_op jit(solution)/shard_map/ppermute | solution.py:37
  416.9 2.8 fusion.7
  419.8 19.1 %collective-permute-done.28 = bf16[512,1024]{1,0:T(8,128)(2,1)} collective-permute-done((bf16[512,1024]{1,0:T(8,128)(2,1)}, bf16[512,1024]{1,0:T(8,128)(2,1)}, u32[]{:S(2)}, u32[]{:S(2)}) %collective-permute-start.28) | collective-permute-done | bytes 1048608 | tf_op jit(solution)/shard_map/ppermute | solution.py:37
  438.8 3.1 fusion.18
  442.0 3.4 fusion.10
  452.3 55.0 %reduce-scatter.6.cloned.1.call-done = bf16[1,128,2304]{2,1,0:T(8,128)(2,1)} async-done(((bf16[8,128,2304]{2,1,0:T(8,128)(2,1)}), bf16[1,128,2304]{2,1,0:T(8,128)(2,1)}) %reduce-scatter.6.cloned.1.call-update) | async-done | bytes 589840 | tf_op jit(solution)/shard_map/reduce_scatter | solution.py:101
  510.9 3.8 collective-permute-done.36
  514.6 3.2 collective-permute-done.37
  520.9 1.2 add_reduce_fusion
  (270 shorter events, 45.1 us)
Async XLA Ops:
  7.2 12.4 %copy-start.38 = (s32[2,256]{1,0:T(2,128)S(1)}, s32[2,256]{1,0:T(2,128)}, u32[]{:S(2)}) copy-start(s32[2,256]{1,0:T(2,128)} %param.12) | copy-start | bytes 6148
  7.2 12.9 %copy-start.19 = (bf16[2,256,1024]{2,1,0:T(8,128)(2,1)S(1)}, bf16[2,256,1024]{2,1,0:T(8,128)(2,1)}, u32[]{:S(2)}) copy-start(bf16[2,256,1024]{2,1,0:T(8,128)(2,1)} %param.13) | copy-start | bytes 3145732
  7.2 76.7 %all-gather.8.cloned.1.call-start = ((), (), s32[]{:S(2)}) async-start(), calls=%async_computation.7 | async-start | bytes 2654208 | tf_op jit(solution)/shard_map/all_gather | solution.py:267
  8.1 8.4 %collective-permute-start.6 = (bf16[1,64]{1,0:T(2,128)(2,1)S(1)}, bf16[1,64]{1,0:T(2,128)(2,1)S(1)}, u32[]{:S(2)}, u32[]{:S(2)}) collective-permute-start(bf16[1,64]{1,0:T(2,128)(2,1)S(1)} %maximum_bitcast_fusion.1), channel_id=1, source_target_pairs={{0,8},{8,0},{1,9},{9,1},{2,10},{10,2},{3,11},{11,3},{4,12},{12,4},... | collective-permute-start | bytes 392 | tf_op jit(solution)/shard_map/ppermute | solution.py:37
  11.0 6.0 %collective-permute-start.8 = (bf16[1,64]{1,0:T(2,128)(2,1)S(1)}, bf16[1,64]{1,0:T(2,128)(2,1)S(1)}, u32[]{:S(2)}, u32[]{:S(2)}) collective-permute-start(bf16[1,64]{1,0:T(2,128)(2,1)S(1)} %maximum_bitcast_fusion.1), channel_id=1, source_target_pairs={{0,4},{4,0},{1,5},{5,1},{2,6},{6,2},{3,7},{7,3},{8,12},{12,8},{9,1... | collective-permute-start | bytes 392 | tf_op jit(solution)/shard_map/ppermute | solution.py:33
  12.2 10.7 %copy-start.6 = (bf16[2,256,1024]{2,1,0:T(8,128)(2,1)S(1)}, bf16[2,256,1024]{2,1,0:T(8,128)(2,1)}, u32[]{:S(2)}) copy-start(bf16[2,256,1024]{2,1,0:T(8,128)(2,1)} %param.11) | copy-start | bytes 3145732
  12.2 11.1 %copy-start.26 = (bf16[32,4608]{1,0:T(8,128)(2,1)S(1)}, bf16[32,4608]{1,0:T(8,128)(2,1)}, u32[]{:S(2)}) copy-start(bf16[32,4608]{1,0:T(8,128)(2,1)} %param.19) | copy-start | bytes 884740
  12.5 6.1 %collective-permute-start.3 = (bf16[32,768]{1,0:T(8,128)(2,1)S(1)}, bf16[32,768]{1,0:T(8,128)(2,1)S(1)}, u32[]{:S(2)}, u32[]{:S(2)}) collective-permute-start(bf16[32,768]{1,0:T(8,128)(2,1)S(1)} %select_n.376), channel_id=1, source_target_pairs={{0,12},{4,8},{8,4},{12,0},{1,13},{5,9},{9,5},{13,1},{2,14},{6,10},... | collective-permute-start | bytes 147464 | tf_op jit(solution)/shard_map/ppermute | solution.py:45
  12.8 5.9 %collective-permute-start.4 = (bf16[32,768]{1,0:T(8,128)(2,1)S(1)}, bf16[32,768]{1,0:T(8,128)(2,1)S(1)}, u32[]{:S(2)}, u32[]{:S(2)}) collective-permute-start(bf16[32,768]{1,0:T(8,128)(2,1)S(1)} %select_n.380), channel_id=1, source_target_pairs={{0,8},{4,12},{8,0},{12,4},{1,9},{5,13},{9,1},{13,5},{2,10},{6,14},... | collective-permute-start | bytes 147464 | tf_op jit(solution)/shard_map/ppermute | solution.py:45
  14.8 3.8 collective-permute-start.5
  16.5 1.3 collective-permute-start.7
  19.5 145.0 %all-gather.10.cloned.1.call-start = ((), (), s32[]{:S(2)}) async-start(), calls=%async_computation.8 | async-start | bytes 5308416 | tf_op jit(solution)/shard_map/all_gather | solution.py:272
  19.6 5.5 %collective-permute-start.12 = (s32[512,1]{0,1:T(1,128)S(1)}, s32[512,1]{0,1:T(1,128)S(1)}, u32[]{:S(2)}, u32[]{:S(2)}) collective-permute-start(s32[512,1]{0,1:T(1,128)S(1)} %bitcast.176), channel_id=1, source_target_pairs={{0,8},{8,0},{1,9},{9,1},{2,10},{10,2},{3,11},{11,3},{4,12},{12,4},... | collective-permute-start | bytes 6152 | tf_op jit(solution)/shard_map/ppermute | solution.py:37
  19.9 7.2 %collective-permute-start.11 = (s32[512,1]{0,1:T(1,128)S(1)}, s32[512,1]{0,1:T(1,128)S(1)}, u32[]{:S(2)}, u32[]{:S(2)}) collective-permute-start(s32[512,1]{0,1:T(1,128)S(1)} %bitcast.177), channel_id=1, source_target_pairs={{0,4},{4,0},{1,5},{5,1},{2,6},{6,2},{3,7},{7,3},{8,12},{12,8},{9,1... | collective-permute-start | bytes 6152 | tf_op jit(solution)/shard_map/ppermute | solution.py:33
  21.3 51.7 %collective-permute-start.9 = (bf16[512,1024]{1,0:T(8,128)(2,1)}, bf16[512,1024]{1,0:T(8,128)(2,1)}, u32[]{:S(2)}, u32[]{:S(2)}) collective-permute-start(bf16[512,1024]{1,0:T(8,128)(2,1)} %fusion.6.refs_4_), channel_id=1, source_target_pairs={{0,8},{8,0},{1,9},{9,1},{2,10},{10,2},{3,11},{11,3},{4,12},{12,4},... | collective-permute-start | bytes 3145736 | tf_op jit(solution)/shard_map/ppermute | solution.py:37
  23.0 50.0 %collective-permute-start.1 = (bf16[512,1024]{1,0:T(8,128)(2,1)S(1)}, bf16[512,1024]{1,0:T(8,128)(2,1)}, u32[]{:S(2)}, u32[]{:S(2)}) collective-permute-start(bf16[512,1024]{1,0:T(8,128)(2,1)S(1)} %bitcast.129), channel_id=1, source_target_pairs={{0,8},{8,0},{1,9},{9,1},{2,10},{10,2},{3,11},{11,3},{4,12},{12,4},... | collective-permute-start | bytes 3145736 | tf_op jit(solution)/shard_map/ppermute | solution.py:37
  25.2 2.3 collective-permute-start.13
  25.3 47.0 %collective-permute-start.20 = (bf16[32,2304]{1,0:T(8,128)(2,1)S(1)}, bf16[32,2304]{1,0:T(8,128)(2,1)S(1)}, u32[]{:S(2)}, u32[]{:S(2)}) collective-permute-start(bf16[32,2304]{1,0:T(8,128)(2,1)S(1)} %get-tuple-element.80), channel_id=1, source_target_pairs={{0,12},{4,8},{8,4},{12,0},{1,13},{5,9},{9,5},{13,1},{2,14},{6,10},... | collective-permute-start | bytes 442376 | tf_op jit(solution)/shard_map/ppermute | solution.py:45
  27.1 48.7 %collective-permute-start.21 = (bf16[32,2304]{1,0:T(8,128)(2,1)S(1)}, bf16[32,2304]{1,0:T(8,128)(2,1)S(1)}, u32[]{:S(2)}, u32[]{:S(2)}) collective-permute-start(bf16[32,2304]{1,0:T(8,128)(2,1)S(1)} %get-tuple-element.46), channel_id=1, source_target_pairs={{0,8},{4,12},{8,0},{12,4},{1,9},{5,13},{9,1},{13,5},{2,10},{6,14},... | collective-permute-start | bytes 442376 | tf_op jit(solution)/shard_map/ppermute | solution.py:45
  27.5 48.3 %collective-permute-start.22 = (bf16[32,2304]{1,0:T(8,128)(2,1)S(1)}, bf16[32,2304]{1,0:T(8,128)(2,1)S(1)}, u32[]{:S(2)}, u32[]{:S(2)}) collective-permute-start(bf16[32,2304]{1,0:T(8,128)(2,1)S(1)} %get-tuple-element.79), channel_id=1, source_target_pairs={{0,4},{4,0},{8,12},{12,8},{1,5},{5,1},{9,13},{13,9},{2,6},{6,2},{1... | collective-permute-start | bytes 442376 | tf_op jit(solution)/shard_map/ppermute | solution.py:45
  72.3 8.0 %collective-permute-start = (bf16[512,1024]{1,0:T(8,128)(2,1)S(1)}, bf16[512,1024]{1,0:T(8,128)(2,1)S(1)}, u32[]{:S(2)}, u32[]{:S(2)}) collective-permute-start(bf16[512,1024]{1,0:T(8,128)(2,1)S(1)} %bitcast.130), channel_id=1, source_target_pairs={{0,4},{4,0},{1,5},{5,1},{2,6},{6,2},{3,7},{7,3},{8,12},{12,8},{9,1... | collective-permute-start | bytes 3145736 | tf_op jit(solution)/shard_map/ppermute | solution.py:33
  72.9 5.5 %collective-permute-start.10 = (bf16[512,1024]{1,0:T(8,128)(2,1)}, bf16[512,1024]{1,0:T(8,128)(2,1)}, u32[]{:S(2)}, u32[]{:S(2)}) collective-permute-start(bf16[512,1024]{1,0:T(8,128)(2,1)} %collective-permute-done.9.refs_6_), channel_id=1, source_target_pairs={{0,4},{4,0},{1,5},{5,1},{2,6},{6,2},{3,7},{7,3},{8,12},{12,8},{9,1... | collective-permute-start | bytes 3145736 | tf_op jit(solution)/shard_map/ppermute | solution.py:33
  73.0 7.4 %collective-permute-start.2 = (bf16[512,1024]{1,0:T(8,128)(2,1)}, bf16[512,1024]{1,0:T(8,128)(2,1)S(1)}, u32[]{:S(2)}, u32[]{:S(2)}) collective-permute-start(bf16[512,1024]{1,0:T(8,128)(2,1)} %collective-permute-done.1), channel_id=1, source_target_pairs={{0,4},{4,0},{1,5},{5,1},{2,6},{6,2},{3,7},{7,3},{8,12},{12,8},{9,1... | collective-permute-start | bytes 3145736 | tf_op jit(solution)/shard_map/ppermute | solution.py:33
  76.7 133.9 %all-gather.6.cloned.1.call-start = ((), (), s32[]{:S(2)}) async-start(), calls=%async_computation.3 | async-start | bytes 2654208 | tf_op jit(solution)/shard_map/all_gather | solution.py:273
  90.8 12.4 %copy-start.22 = (bf16[8,32,1024]{2,1,0:T(8,128)(2,1)}, bf16[8,32,1024]{2,1,0:T(8,128)(2,1)S(1)}, u32[]{:S(2)}) copy-start(bf16[8,32,1024]{2,1,0:T(8,128)(2,1)S(1)} %pad_maximum_fusion.12) | copy-start | bytes 1572868
  104.8 4.2 collective-permute-start.14
  111.5 25.3 %collective-permute-start.15 = (bf16[512,1024]{1,0:T(8,128)(2,1)S(1)}, bf16[512,1024]{1,0:T(8,128)(2,1)}, u32[]{:S(2)}, u32[]{:S(2)}) collective-permute-start(bf16[512,1024]{1,0:T(8,128)(2,1)S(1)} %fusion.22), channel_id=1, source_target_pairs={{0,8},{8,0},{1,9},{9,1},{2,10},{10,2},{3,11},{11,3},{4,12},{12,4},... | collective-permute-start | bytes 3145736 | tf_op jit(solution)/shard_map/ppermute | solution.py:37
  140.0 24.6 %collective-permute-start.17 = (bf16[512,1024]{1,0:T(8,128)(2,1)S(1)}, bf16[512,1024]{1,0:T(8,128)(2,1)}, u32[]{:S(2)}, u32[]{:S(2)}) collective-permute-start(bf16[512,1024]{1,0:T(8,128)(2,1)S(1)} %multiply_convert_fusion.4.refs_0_), channel_id=1, source_target_pairs={{0,8},{8,0},{1,9},{9,1},{2,10},{10,2},{3,11},{11,3},{4,12},{12,4},... | collective-permute-start | bytes 3145736 | tf_op jit(solution)/shard_map/ppermute | solution.py:37
  141.7 254.3 %reduce-scatter.8.cloned.1.call-start = ((), (), s32[]{:S(2)}) async-start(), calls=%async_computation.6 | async-start | bytes 2654208 | tf_op jit(solution)/shard_map/reduce_scatter | solution.py:101
  141.9 27.6 %collective-permute-start.19 = (bf16[512,1024]{1,0:T(8,128)(2,1)}, bf16[512,1024]{1,0:T(8,128)(2,1)}, u32[]{:S(2)}, u32[]{:S(2)}) collective-permute-start(bf16[512,1024]{1,0:T(8,128)(2,1)} %fusion.6.refs_4_), channel_id=1, source_target_pairs={{0,4},{4,0},{1,5},{5,1},{2,6},{6,2},{3,7},{7,3},{8,12},{12,8},{9,1... | collective-permute-start | bytes 3145736 | tf_op jit(solution)/shard_map/ppermute | solution.py:33
  142.0 27.6 %collective-permute-start.16 = (bf16[512,1024]{1,0:T(8,128)(2,1)S(1)}, bf16[512,1024]{1,0:T(8,128)(2,1)}, u32[]{:S(2)}, u32[]{:S(2)}) collective-permute-start(bf16[512,1024]{1,0:T(8,128)(2,1)S(1)} %multiply_convert_fusion.4.refs_0_), channel_id=1, source_target_pairs={{0,4},{4,0},{1,5},{5,1},{2,6},{6,2},{3,7},{7,3},{8,12},{12,8},{9,1... | collective-permute-start | bytes 3145736 | tf_op jit(solution)/shard_map/ppermute | solution.py:33
  164.5 5.1 collective-permute-start.18
  240.5 10.4 %copy-start.43 = (bf16[2048,1024]{1,0:T(8,128)(2,1)S(1)}, bf16[2048,1024]{1,0:T(8,128)(2,1)}, u32[]{:S(2)}) copy-start(bf16[2048,1024]{1,0:T(8,128)(2,1)} %get-tuple-element.24) | copy-start | bytes 12582916
  240.7 4.2 collective-permute-start.23
  244.9 6.0 %copy-start.42 = (bf16[2048,2304]{1,0:T(8,128)(2,1)S(1)}, bf16[2048,2304]{1,0:T(8,128)(2,1)}, u32[]{:S(2)}) copy-start(bf16[2048,2304]{1,0:T(8,128)(2,1)} %get-tuple-element.25) | copy-start | bytes 28311556
  249.4 25.4 %collective-permute-start.24 = (bf16[512,1024]{1,0:T(8,128)(2,1)}, bf16[512,1024]{1,0:T(8,128)(2,1)S(1)}, u32[]{:S(2)}, u32[]{:S(2)}) collective-permute-start(bf16[512,1024]{1,0:T(8,128)(2,1)} %fusion.19), channel_id=1, source_target_pairs={{0,8},{8,0},{1,9},{9,1},{2,10},{10,2},{3,11},{11,3},{4,12},{12,4},... | collective-permute-start | bytes 3145736 | tf_op jit(solution)/shard_map/ppermute | solution.py:37
  266.0 11.3 %copy-start.5 = (f32[1024,1024]{1,0:T(8,128)S(1)}, f32[1024,1024]{1,0:T(8,128)}, u32[]{:S(2)}) copy-start(f32[1024,1024]{1,0:T(8,128)} %copy-done.4) | copy-start | bytes 12582916
  266.0 11.3 %copy-start.20 = (bf16[2,256,1024]{2,1,0:T(8,128)(2,1)S(1)}, bf16[2,256,1024]{2,1,0:T(8,128)(2,1)}, u32[]{:S(2)}) copy-start(bf16[2,256,1024]{2,1,0:T(8,128)(2,1)} %param.13) | copy-start | bytes 3145732
  281.1 27.7 %copy-start.23 = (bf16[8,32,1024]{2,1,0:T(8,128)(2,1)S(1)}, bf16[8,32,1024]{2,1,0:T(8,128)(2,1)}, u32[]{:S(2)}) copy-start(bf16[8,32,1024]{2,1,0:T(8,128)(2,1)} %copy-done.22) | copy-start | bytes 1572868
  281.1 24.7 %collective-permute-start.25 = (bf16[512,1024]{1,0:T(8,128)(2,1)}, bf16[512,1024]{1,0:T(8,128)(2,1)}, u32[]{:S(2)}, u32[]{:S(2)}) collective-permute-start(bf16[512,1024]{1,0:T(8,128)(2,1)} %get-tuple-element.44), channel_id=1, source_target_pairs={{0,8},{8,0},{1,9},{9,1},{2,10},{10,2},{3,11},{11,3},{4,12},{12,4},... | collective-permute-start | bytes 3145736 | tf_op jit(solution)/shard_map/ppermute | solution.py:37
  282.6 23.4 %collective-permute-start.29 = (bf16[512,1024]{1,0:T(8,128)(2,1)}, bf16[512,1024]{1,0:T(8,128)(2,1)}, u32[]{:S(2)}, u32[]{:S(2)}) collective-permute-start(bf16[512,1024]{1,0:T(8,128)(2,1)} %get-tuple-element.44), channel_id=1, source_target_pairs={{0,4},{4,0},{1,5},{5,1},{2,6},{6,2},{3,7},{7,3},{8,12},{12,8},{9,1... | collective-permute-start | bytes 3145736 | tf_op jit(solution)/shard_map/ppermute | solution.py:33
  305.8 3.0 collective-permute-start.26
  306.0 139.4 %reduce-scatter.4.cloned.1.call-start = ((), (), s32[]{:S(2)}) async-start(), calls=%async_computation.4 | async-start | bytes 1474560 | tf_op jit(solution)/shard_map/reduce_scatter | solution.py:94
  318.3 5.6 %copy-start.41 = (bf16[2048,256]{1,0:T(8,128)(2,1)}, bf16[2048,256]{1,0:T(8,128)(2,1)S(1)}, u32[]{:S(2)}) copy-start(bf16[2048,256]{1,0:T(8,128)(2,1)S(1)} %get-tuple-element.65) | copy-start | bytes 3145732
  323.9 5.7 %copy-start.31 = (bf16[2048,256]{1,0:T(8,128)(2,1)}, bf16[2048,256]{1,0:T(8,128)(2,1)S(1)}, u32[]{:S(2)}) copy-start(bf16[2048,256]{1,0:T(8,128)(2,1)S(1)} %multiply_convert_fusion) | copy-start | bytes 3145732
  338.1 35.1 %collective-permute-start.32 = (bf16[4,144,1024]{2,1,0:T(8,128)(2,1)}, bf16[4,144,1024]{2,1,0:T(8,128)(2,1)}, u32[]{:S(2)}, u32[]{:S(2)}) collective-permute-start(bf16[4,144,1024]{2,1,0:T(8,128)(2,1)} %dynamic-slice_bitcast_fusion), channel_id=1, source_target_pairs={{0,16},{16,0},{1,17},{17,1},{2,18},{18,2},{3,19},{19,3},{4,20},{20... | collective-permute-start | bytes 3538952 | tf_op jit(solution)/shard_map/ppermute | solution.py:41
  376.4 130.9 %reduce-scatter.6.cloned.1.call-start = ((), (), s32[]{:S(2)}) async-start(), calls=%async_computation.5 | async-start | bytes 5308416 | tf_op jit(solution)/shard_map/reduce_scatter | solution.py:101
  383.2 4.6 collective-permute-start.30
  386.9 6.0 %copy-start.11 = (bf16[2048,1024]{1,0:T(8,128)(2,1)}, bf16[2048,1024]{1,0:T(8,128)(2,1)S(1)}, u32[]{:S(2)}) copy-start(bf16[2048,1024]{1,0:T(8,128)(2,1)S(1)} %broadcast_add_fusion) | copy-start | bytes 12582916
  387.2 5.2 collective-permute-start.27
  390.6 26.3 %collective-permute-start.31 = (bf16[512,1024]{1,0:T(8,128)(2,1)}, bf16[512,1024]{1,0:T(8,128)(2,1)}, u32[]{:S(2)}, u32[]{:S(2)}) collective-permute-start(bf16[512,1024]{1,0:T(8,128)(2,1)} %fusion.11), channel_id=1, source_target_pairs={{0,8},{8,0},{1,9},{9,1},{2,10},{10,2},{3,11},{11,3},{4,12},{12,4},... | collective-permute-start | bytes 3145736 | tf_op jit(solution)/shard_map/ppermute | solution.py:37
  395.2 43.6 %collective-permute-start.28 = (bf16[512,1024]{1,0:T(8,128)(2,1)}, bf16[512,1024]{1,0:T(8,128)(2,1)}, u32[]{:S(2)}, u32[]{:S(2)}) collective-permute-start(bf16[512,1024]{1,0:T(8,128)(2,1)} %fusion.14), channel_id=1, source_target_pairs={{0,8},{8,0},{1,9},{9,1},{2,10},{10,2},{3,11},{11,3},{4,12},{12,4},... | collective-permute-start | bytes 3145736 | tf_op jit(solution)/shard_map/ppermute | solution.py:37
  397.8 41.0 %copy-start.13 = (f32[1024,1024]{1,0:T(8,128)S(1)}, f32[1024,1024]{1,0:T(8,128)}, u32[]{:S(2)}) copy-start(f32[1024,1024]{1,0:T(8,128)} %copy-done.12) | copy-start | bytes 12582916
  419.7 22.2 %copy-start.3 = (f32[1024,1024]{1,0:T(8,128)S(1)}, f32[1024,1024]{1,0:T(8,128)}, u32[]{:S(2)}) copy-start(f32[1024,1024]{1,0:T(8,128)} %copy-done.2) | copy-start | bytes 12582916
  419.8 22.2 %copy-start.15 = (f32[512,1024]{1,0:T(8,128)S(1)}, f32[512,1024]{1,0:T(8,128)}, u32[]{:S(2)}) copy-start(f32[512,1024]{1,0:T(8,128)} %get-tuple-element.45) | copy-start | bytes 6291460
  445.4 6.7 %copy-start.36 = (bf16[32,3072]{1,0:T(8,128)(2,1)S(1)}, bf16[32,3072]{1,0:T(8,128)(2,1)}, u32[]{:S(2)}) copy-start(bf16[32,3072]{1,0:T(8,128)(2,1)} %param.15) | copy-start | bytes 589828
  446.3 4.7 collective-permute-start.33
  446.9 4.5 collective-permute-start.34
  448.0 3.5 collective-permute-start.35
  451.6 58.8 %copy-start.39 = (bf16[32]{0:T(256)(128)(2,1)S(1)}, bf16[32]{0:T(256)(128)(2,1)}, u32[]{:S(2)}) copy-start(bf16[32]{0:T(256)(128)(2,1)} %param.14) | copy-start | bytes 196
  452.1 66.2 %copy-start.25 = (f32[32,3072]{1,0:T(8,128)}, f32[32,3072]{1,0:T(8,128)S(1)}, u32[]{:S(2)}) copy-start(f32[32,3072]{1,0:T(8,128)S(1)} %reshape.427) | copy-start | bytes 1179652
  508.4 6.2 %collective-permute-start.36 = (bf16[32,2304]{1,0:T(8,128)(2,1)S(1)}, bf16[32,2304]{1,0:T(8,128)(2,1)S(1)}, u32[]{:S(2)}, u32[]{:S(2)}) collective-permute-start(bf16[32,2304]{1,0:T(8,128)(2,1)S(1)} %get-tuple-element.75), channel_id=1, source_target_pairs={{0,12},{4,8},{8,4},{12,0},{1,13},{5,9},{9,5},{13,1},{2,14},{6,10},... | collective-permute-start | bytes 442376 | tf_op jit(solution)/shard_map/ppermute | solution.py:45
  509.4 8.5 %collective-permute-start.37 = (bf16[32,2304]{1,0:T(8,128)(2,1)S(1)}, bf16[32,2304]{1,0:T(8,128)(2,1)S(1)}, u32[]{:S(2)}, u32[]{:S(2)}) collective-permute-start(bf16[32,2304]{1,0:T(8,128)(2,1)S(1)} %get-tuple-element.76), channel_id=1, source_target_pairs={{0,8},{4,12},{8,0},{12,4},{1,9},{5,13},{9,1},{13,5},{2,10},{6,14},... | collective-permute-start | bytes 442376 | tf_op jit(solution)/shard_map/ppermute | solution.py:45
  510.0 7.8 %collective-permute-start.38 = (bf16[32,2304]{1,0:T(8,128)(2,1)S(1)}, bf16[32,2304]{1,0:T(8,128)(2,1)S(1)}, u32[]{:S(2)}, u32[]{:S(2)}) collective-permute-start(bf16[32,2304]{1,0:T(8,128)(2,1)S(1)} %get-tuple-element.74), channel_id=1, source_target_pairs={{0,4},{4,0},{8,12},{12,8},{1,5},{5,1},{9,13},{13,9},{2,6},{6,2},{1... | collective-permute-start | bytes 442376 | tf_op jit(solution)/shard_map/ppermute | solution.py:45
  (25 other events, 73.6 us)
Sparse Core Ops, SparseCore 0:
  19.7 52.3 all-gather.7
  76.8 81.3 all-gather.9
  160.4 50.2 all-gather.5
  306.1 73.5 reduce-scatter.7
  381.9 27.8 reduce-scatter.3
  413.3 93.9 reduce-scatter.5

commit v6 on v5

--- a/solution.py
+++ b/solution.py
@@ -85,20 +85,17 @@
     return lax.dynamic_index_in_dim(blocks, index, axis=0, keepdims=False)
 
 
-def scatter_first(part):
+def scatter(part, token=None):
     groups, slots = part.shape[:2]
     if groups == 2:
         row = lax.axis_index("y")
-        came = swap_row(take(part, 1 - row))
-        summed = (take(part, row).astype(f32) + came.astype(f32)).astype(bf16)
+        came = swap_row(take(part, 1 - row)).astype(f32)
+        if token is not None:
+            came = after(came, token)
+        summed = (take(part, row).astype(f32) + came).astype(bf16)
         return lax.psum_scatter(summed, "s", scatter_dimension=0, tiled=False)
     flat = part.reshape((groups * slots,) + part.shape[2:]).astype(f32)
     return lax.psum_scatter(flat, ("g", "y", "s"), scatter_dimension=0, tiled=False)
-
-
-def scatter_rest(part):
-    wide = part if part.shape[0] <= 8 else part.astype(f32)
-    return lax.psum_scatter(wide, ("g", "y", "s"), scatter_dimension=0, tiled=False)
 
 
 def forward_kernel(*refs):
@@ -322,9 +319,8 @@
         2 * unit,
         team_count * hid,
     )
-    owners = groups * slots
     down_part = rows_dot(hidden, ffn_grad).astype(bf16)
-    grad_down = scatter_rest(down_part.reshape(owners, hidden_share, features))
+    grad_down = scatter(down_part.reshape(groups, slots, hidden_share, features))
     pair_grad, normed_part, out_part = by_rows(
         backward_kernel,
         ROW_TILE,
@@ -344,9 +340,9 @@
         return jnp.transpose(split, (0, 2, 1, 3, 4)).reshape(count, slots, team * share, width)
 
     pair_part = by_owner(rows_dot(second_normed, pair_grad), TEAM)
-    pair_sum = scatter_rest(pair_part.reshape(owners, tall, 2 * hid))
+    pair_sum = scatter(pair_part)
     normed_sum = team_sum(normed_part, pair_part[0, 0, :1])
-    second_weighted = ffn_full * normed_sum
+    second_weighted = after(ffn_full, grad_down[:1]) * normed_sum
     middle_grad = upstream + norm_back(middle, second_scale, second_weighted)
 
     mixer_grad = team_rows((live * middle_grad).astype(bf16))
@@ -378,10 +374,11 @@
         conv_rows.astype(bf16),
         ((0, 0), (0, 0), (0, EXTRA_ROWS - 1), (0, features - taps * share)),
     )
-    first_sum = scatter_first(
+    first_sum = scatter(
         jnp.concatenate(
             [jnp.concatenate([in_part, out_grad_part], axis=3), conv_rows], axis=2
-        )
+        ),
+        pair_sum[:1],
     )
 
     first_weighted = norm_full * team_sum(back_dot(projected_grad, in_full).astype(bf16))

time: 535 us -> 496 us (0.927)
  waiting for transfers between devices: 287 us -> 215 us
  other arithmetic: 59.8 us -> 76.7 us
  local copies, waits for them, and re-layouts: 38.7 us -> 53.8 us
    reduce_scatter x3, waiting for transfers between devices: 55 us -> 4.11 us  [scatter(): return lax.psum_scatter(summed, 's', scatter_dimension=0, tiled=False)]
    ppermute x10, waiting for transfers between devices: 116 us -> 93.7 us  [swap_chip(): return lax.ppermute(values, 'x', [(0, 1), (1, 0)])]
    ppermute x1 -> x3, waiting for transfers between devices: 34.6 us -> 48.1 us  [swap_row(): return lax.ppermute(values, 'y', [(0, 1), (1, 0)])]
    convert_element_type x1 -> x3, other arithmetic: 3.14 us -> 10.6 us  [scatter(): summed = (take(part, row).astype(f32) + came).astype(bf16)]
    ppermute x16, waiting for transfers between devices: 13.2 us -> 6.17 us  [swap_core(): return lax.ppermute(values, 'c', [(0, 1), (1, 0)])]
    ppermute x12, waiting for transfers between devices: 54.4 us -> 48.1 us  [swap_far(): lax.ppermute(values, ('x', 'c'), [(i, i ^ distance) for i in range(TEAM)])]
    unnamed x92 -> x96, local copies, waits for them, and re-layouts: 9.99 us -> 11.7 us
  transfers between devices with their start and end apart: 45 -> 47, of which waited for: 19 -> 19; matrix products, arithmetic and copies ran while one was open for 23% -> 34% of each run, Pallas kernels for 3% -> 4%
where the time goes in v6:
time: 496 us; the launch traced here: 491 us
  waiting for transfers between devices  215 us (43%)
  other arithmetic  76.7 us (15%)
  local copies, waits for them, and re-layouts  53.8 us (11%)
  matrix products  53.8 us (11%)
  Pallas kernels  45.8 us (9%)
  starting transfers between devices  27.4 us (6%)
  between operations  18.8 us (4%)
    ppermute x10, waiting for transfers between devices, swap_chip(): return lax.ppermute(values, 'x', [(0, 1), (1, 0)])  93.7 us
    ppermute x12, waiting for transfers between devices, swap_far(): lax.ppermute(values, ('x', 'c'), [(i, i ^ distance) for i in range(TEAM)])  48.1 us
    ppermute x3, waiting for transfers between devices, swap_row(): return lax.ppermute(values, 'y', [(0, 1), (1, 0)])  48.1 us
    pallas_call x2, Pallas kernels, by_rows(): pl.pallas_call(kernel, grid=(steps,), in_specs=[row_block(value.shape[1])...  45.8 us
    dot_general x4, matrix products, rows_dot(): lax.dot_general(left_side, right_side, (((0,), (0,)), ((), ())), preferre...  31.2 us
    all_gather x1, waiting for transfers between devices, per_device(): down_full = lax.all_gather(down_weight, ('g', 'y', 's'), axis=0, tiled=True)  14.3 us
    ppermute x10, starting transfers between devices, swap_chip(): return lax.ppermute(values, 'x', [(0, 1), (1, 0)])  13.6 us
    dot_general x2, matrix products, back_dot(): lax.dot_general(left_side, right_side, (((1,), (1,)), ((), ())), preferre...  13.4 us
  transfers between devices with their start and end apart: 47, of which 19 were waited for; matrix products, arithmetic and copies ran while one was open for 34% of the time, Pallas kernels for 4%

profile of v6, /device:TPU:0, one launch (start us, length us, event | category | flops | bytes accessed | tf_op | source)
XLA Modules:
  0.0 491.0 jit_solution(13099089892680231379)
XLA Ops:
  8.1 2.9 collective-permute-start.6
  12.8 2.0 collective-permute-start.4
  21.3 1.7 collective-permute-start.9
  25.3 1.8 collective-permute-start.20
  27.5 44.8 %collective-permute-done.20 = bf16[32,2304]{1,0:T(8,128)(2,1)S(1)} collective-permute-done((bf16[32,2304]{1,0:T(8,128)(2,1)S(1)}, bf16[32,2304]{1,0:T(8,128)(2,1)S(1)}, u32[]{:S(2)}, u32[]{:S(2)}) %collective-permute-start.20) | collective-permute-done | bytes 147488 | tf_op jit(solution)/shard_map/ppermute | solution.py:45
  73.5 2.3 collective-permute-done.21
  80.3 3.5 fusion
  83.9 1.5 slice.371
  90.1 7.9 %fusion.28 = f32[2048,768]{1,0:T(8,128)S(1)} fusion(bf16[1024,768]{1,0:T(8,128)(2,1)} %bitcast.167, f32[1024]{0:T(1024)S(1)} %mul.316, f32[2048]{0:T(1024)S(1)} %add_rsqrt_fusion, bf16[512,1024]{1,0:T(8,128)(2,1)} %copy-done.36, bf16[512,1024]{1,0:T(8,128)(2,1)} %collective-permute-done.1, bf16[512,1024]{1,0:T(8,128)(2,1)} %copy-done.34, ...), kind=kOutput, calls=%fused_computation.81 | convolution fusion | flops 3244294144 | bytes 12070912 | tf_op jit(solution)/shard_map/dot_general | solution.py:17
  98.2 2.3 copy-done
  100.5 2.3 multiply_convert_fusion.5
  104.7 4.0 collective-permute-done.14
  109.6 1.6 copy-done.10
  111.2 1.6 collective-permute-start.15
  112.9 23.6 %collective-permute-done.15 = bf16[512,1024]{1,0:T(8,128)(2,1)} collective-permute-done((bf16[512,1024]{1,0:T(8,128)(2,1)S(1)}, bf16[512,1024]{1,0:T(8,128)(2,1)}, u32[]{:S(2)}, u32[]{:S(2)}) %collective-permute-start.15) | collective-permute-done | bytes 1048608 | tf_op jit(solution)/shard_map/ppermute | solution.py:37
  136.5 2.9 multiply_reduce_fusion.5
  139.7 1.7 collective-permute-start.17
  142.6 21.7 %collective-permute-done.17.refs_2_ = bf16[512,1024]{1,0:T(8,128)(2,1)} collective-permute-done((bf16[512,1024]{1,0:T(8,128)(2,1)S(1)}, bf16[512,1024]{1,0:T(8,128)(2,1)}, u32[]{:S(2)}, u32[]{:S(2)}) %collective-permute-start.17) | collective-permute-done | bytes 1048608 | tf_op jit(solution)/shard_map/ppermute | solution.py:37
  164.3 5.0 %copy.70 = bf16[2,4,4,32,2304]{4,3,1,2,0:T(8,128)(2,1)} copy(bf16[2,4,4,32,2304]{4,3,2,1,0:T(8,128)(2,1)} %bitcast.155) | data formatting | bytes 9437184 | tf_op jit(solution)/shard_map/reshape | solution.py:278
  169.3 17.7 %shard_map.186 = (bf16[2048,1152]{1,0:T(8,128)(2,1)}, bf16[2048,1152]{1,0:T(8,128)(2,1)}, bf16[2048,1152]{1,0:T(8,128)(2,1)}, bf16[2048,1024]{1,0:T(8,128)(2,1)}, bf16[2048,1024]{1,0:T(8,128)(2,1)}) custom-call(bf16[512,1024]{1,0:T(8,128)(2,1)S(1)} %multiply_convert_fusion.4.refs_0_, bf16[512,1024]{1,0:T(8,128)(2,1)} %collective-permute-done.16.refs_1_, ...), custom_call_target="tpu_custom_call" | custom-call | flops 9663676416 | bytes 35651584 | tf_op jit(solution)/shard_map/pallas_call | solution.py:149
  187.0 9.4 %convolution_convert_fusion.1.token_ref = bf16[1152,1024]{1,0:T(8,128)(2,1)} fusion(bf16[2048,1152]{1,0:T(8,128)(2,1)} %get-tuple-element.19.hidden_ref, bf16[2048,1024]{1,0:T(8,128)(2,1)} %get-tuple-element.18.grad_ref), kind=kOutput, calls=%fused_computation.12 | convolution fusion | flops 4833017856 | bytes 11272192 | tf_op jit(solution)/shard_map/dot_general | solution.py:21
  196.3 14.3 %all-gather.6.cloned.1.call-done.down_ref = bf16[1152,1024]{1,0:T(8,128)(2,1)} async-done(((bf16[144,1024]{1,0:T(8,128)(2,1)}), bf16[1152,1024]{1,0:T(8,128)(2,1)}) %all-gather.6.cloned.1.call-update) | async-done | bytes 2359312 | tf_op jit(solution)/shard_map/all_gather | solution.py:270
  210.6 28.1 %shard_map.187 = (bf16[2048,2304]{1,0:T(8,128)(2,1)}, bf16[2048,1024]{1,0:T(8,128)(2,1)}, bf16[2048,1024]{1,0:T(8,128)(2,1)}) custom-call(bf16[2048,1024]{1,0:T(8,128)(2,1)} %get-tuple-element.18.grad_ref, bf16[2048,1152]{1,0:T(8,128)(2,1)} %get-tuple-element.19.hidden_ref, bf16[2048,1152]{1,0:T(8,128)(2,1)} %get-tuple-element.20.silu_ref, ...), custom_call_target="tpu_custom_call" | custom-call | flops 19327352832 | bytes 43253760 | tf_op jit(solution)/shard_map/pallas_call | solution.py:149
  238.8 1.7 fusion.47
  240.5 1.5 pad_maximum_fusion.4
  243.9 27.9 %collective-permute-done.23 = bf16[4,144,1024]{2,1,0:T(8,128)(2,1)} collective-permute-done((bf16[4,144,1024]{2,1,0:T(8,128)(2,1)S(1)}, bf16[4,144,1024]{2,1,0:T(8,128)(2,1)}, u32[]{:S(2)}, u32[]{:S(2)}) %collective-permute-start.23) | collective-permute-done | bytes 1179680 | tf_op jit(solution)/shard_map/ppermute | solution.py:41
  271.9 3.1 fusion.7
  275.2 2.0 convert_element_type.315
  277.3 1.9 copy-done.4
  279.2 2.8 fusion.21
  282.0 1.5 collective-permute-start.25
  283.6 12.9 %convolution_convert_fusion = bf16[1024,2304]{1,0:T(8,128)(2,1)S(1)} fusion(bf16[2048,1024]{1,0:T(8,128)(2,1)S(1)} %copy-done.45, bf16[2048,2304]{1,0:T(8,128)(2,1)} %get-tuple-element.25), kind=kOutput, calls=%fused_computation.5 | convolution fusion | flops 9666035712 | bytes 18350080 | tf_op jit(solution)/shard_map/dot_general | solution.py:21
  297.4 1.9 dynamic-slice_bitcast_fusion
  300.8 2.1 reduce-scatter.4.cloned.1.call-done
  304.8 2.3 collective-permute-done.25
  307.1 2.8 multiply_reduce_fusion.4
  310.0 4.2 multiply_convert_fusion.3
  316.2 22.5 %collective-permute-done.26 = bf16[512,1024]{1,0:T(8,128)(2,1)} collective-permute-done((bf16[512,1024]{1,0:T(8,128)(2,1)}, bf16[512,1024]{1,0:T(8,128)(2,1)}, u32[]{:S(2)}, u32[]{:S(2)}) %collective-permute-start.26) | collective-permute-done | bytes 1048608 | tf_op jit(solution)/shard_map/ppermute | solution.py:37
  338.7 13.8 %collective-permute-done.34 = bf16[4,128,2304]{2,1,0:T(8,128)(2,1)} collective-permute-done((bf16[4,128,2304]{2,1,0:T(8,128)(2,1)}, bf16[4,128,2304]{2,1,0:T(8,128)(2,1)}, u32[]{:S(2)}, u32[]{:S(2)}) %collective-permute-start.34) | collective-permute-done | bytes 2359328 | tf_op jit(solution)/shard_map/ppermute | solution.py:41
  352.6 4.3 fusion.3
  358.8 9.5 %multiply_reduce_fusion.2 = (bf16[256]{0:T(256)(128)(2,1)S(1)}, bf16[256]{0:T(256)(128)(2,1)S(1)}, bf16[256]{0:T(256)(128)(2,1)S(1)}, f32[2048,256]{1,0:T(8,128)S(1)}, bf16[2048,256]{1,0:T(8,128)(2,1)S(1)}) fusion(f32[2048,256]{1,0:T(8,128)} %copy-done.9, f32[2046,256]{1,0:T(8,128)} %bitcast.151, f32[2048]{0:T(1024)S(1)} %get-tuple-element.114, ...), kind=kOutput, calls=%fused_computation.62 | convolution fusion | flops 1096285440 | bytes 18364928 | tf_op jit(solution)/shard_map/dot_general | solution.py:27
  369.0 2.5 multiply_convert_fusion.2
  371.5 2.3 multiply_convert_fusion
  374.1 5.1 %convolution_convert_fusion.4 = bf16[1024,768]{1,0:T(8,128)(2,1)S(1)} fusion(bf16[2048,256]{1,0:T(8,128)(2,1)S(1)} %multiply_convert_fusion, bf16[2048,256]{1,0:T(8,128)(2,1)S(1)} %get-tuple-element.65, bf16[2048,256]{1,0:T(8,128)(2,1)S(1)} %get-tuple-element.42, f32[1024]{0:T(1024)S(1)} %mul.316, f32[2048]{0:T(1024)S(1)} %add_rsqrt_fusion, ...), kind=kOutput, calls=%fused_computation.79 | convolution fusion | flops 3254517760 | bytes 8925184 | tf_op jit(solution)/shard_map/dot_general | solution.py:21
  380.9 3.9 convolution_convert_fusion.5
  388.5 3.9 convolution_convert_fusion.3
  392.6 1.5 pad_maximum_fusion.6
  395.5 1.6 slice.400
  398.3 1.8 pad_maximum_fusion.5
  400.8 2.0 reduce-scatter.6.cloned.1.call-done
  402.8 1.9 select_bitcast_fusion
  408.1 6.3 %collective-permute-done.33 = bf16[4,144,1024]{2,1,0:T(8,128)(2,1)} collective-permute-done((bf16[4,144,1024]{2,1,0:T(8,128)(2,1)}, bf16[4,144,1024]{2,1,0:T(8,128)(2,1)}, u32[]{:S(2)}, u32[]{:S(2)}) %collective-permute-start.33) | collective-permute-done | bytes 1179680 | tf_op jit(solution)/shard_map/ppermute | solution.py:41
  414.4 3.2 fusion.6
  417.6 2.0 convert_element_type.332
  419.7 3.4 fusion.13
  423.9 1.9 broadcast_select_fusion.17
  432.8 1.9 copy.84
  434.7 3.5 reshape.458
  438.2 2.2 convert_element_type.324
  442.7 2.6 add_reduce_fusion
  445.8 3.5 collective-permute-done.32
  449.3 1.9 fusion.9
  451.2 20.1 %collective-permute-done.29 = bf16[512,1024]{1,0:T(8,128)(2,1)S(1)} collective-permute-done((bf16[512,1024]{1,0:T(8,128)(2,1)S(1)}, bf16[512,1024]{1,0:T(8,128)(2,1)S(1)}, u32[]{:S(2)}, u32[]{:S(2)}) %collective-permute-start.29) | collective-permute-done | bytes 1048608 | tf_op jit(solution)/shard_map/ppermute | solution.py:37
  472.7 3.0 fusion.12
  (286 shorter events, 66.3 us)
Async XLA Ops:
  7.2 12.4 %copy-start.40 = (s32[2,256]{1,0:T(2,128)S(1)}, s32[2,256]{1,0:T(2,128)}, u32[]{:S(2)}) copy-start(s32[2,256]{1,0:T(2,128)} %param.12) | copy-start | bytes 6148
  7.2 12.9 %copy-start.19 = (bf16[2,256,1024]{2,1,0:T(8,128)(2,1)S(1)}, bf16[2,256,1024]{2,1,0:T(8,128)(2,1)}, u32[]{:S(2)}) copy-start(bf16[2,256,1024]{2,1,0:T(8,128)(2,1)} %param.13) | copy-start | bytes 3145732
  7.2 76.7 %all-gather.8.cloned.1.call-start = ((), (), s32[]{:S(2)}) async-start(), calls=%async_computation.7 | async-start | bytes 2654208 | tf_op jit(solution)/shard_map/all_gather | solution.py:264
  8.1 8.4 %collective-permute-start.6 = (bf16[1,64]{1,0:T(2,128)(2,1)S(1)}, bf16[1,64]{1,0:T(2,128)(2,1)S(1)}, u32[]{:S(2)}, u32[]{:S(2)}) collective-permute-start(bf16[1,64]{1,0:T(2,128)(2,1)S(1)} %maximum_bitcast_fusion.1), channel_id=1, source_target_pairs={{0,8},{8,0},{1,9},{9,1},{2,10},{10,2},{3,11},{11,3},{4,12},{12,4},... | collective-permute-start | bytes 392 | tf_op jit(solution)/shard_map/ppermute | solution.py:37
  11.0 6.0 %collective-permute-start.8 = (bf16[1,64]{1,0:T(2,128)(2,1)S(1)}, bf16[1,64]{1,0:T(2,128)(2,1)S(1)}, u32[]{:S(2)}, u32[]{:S(2)}) collective-permute-start(bf16[1,64]{1,0:T(2,128)(2,1)S(1)} %maximum_bitcast_fusion.1), channel_id=1, source_target_pairs={{0,4},{4,0},{1,5},{5,1},{2,6},{6,2},{3,7},{7,3},{8,12},{12,8},{9,1... | collective-permute-start | bytes 392 | tf_op jit(solution)/shard_map/ppermute | solution.py:33
  12.1 10.9 %copy-start.6 = (bf16[2,256,1024]{2,1,0:T(8,128)(2,1)S(1)}, bf16[2,256,1024]{2,1,0:T(8,128)(2,1)}, u32[]{:S(2)}) copy-start(bf16[2,256,1024]{2,1,0:T(8,128)(2,1)} %param.11) | copy-start | bytes 3145732
  12.1 11.3 %copy-start.26 = (bf16[32,4608]{1,0:T(8,128)(2,1)S(1)}, bf16[32,4608]{1,0:T(8,128)(2,1)}, u32[]{:S(2)}) copy-start(bf16[32,4608]{1,0:T(8,128)(2,1)} %param.19) | copy-start | bytes 884740
  12.5 6.1 %collective-permute-start.3 = (bf16[32,768]{1,0:T(8,128)(2,1)S(1)}, bf16[32,768]{1,0:T(8,128)(2,1)S(1)}, u32[]{:S(2)}, u32[]{:S(2)}) collective-permute-start(bf16[32,768]{1,0:T(8,128)(2,1)S(1)} %select_n.381), channel_id=1, source_target_pairs={{0,12},{4,8},{8,4},{12,0},{1,13},{5,9},{9,5},{13,1},{2,14},{6,10},... | collective-permute-start | bytes 147464 | tf_op jit(solution)/shard_map/ppermute | solution.py:45
  12.8 5.9 %collective-permute-start.4 = (bf16[32,768]{1,0:T(8,128)(2,1)S(1)}, bf16[32,768]{1,0:T(8,128)(2,1)S(1)}, u32[]{:S(2)}, u32[]{:S(2)}) collective-permute-start(bf16[32,768]{1,0:T(8,128)(2,1)S(1)} %select_n.385), channel_id=1, source_target_pairs={{0,8},{4,12},{8,0},{12,4},{1,9},{5,13},{9,1},{13,5},{2,10},{6,14},... | collective-permute-start | bytes 147464 | tf_op jit(solution)/shard_map/ppermute | solution.py:45
  14.8 3.8 collective-permute-start.5
  16.5 1.3 collective-permute-start.7
  18.7 5.5 %copy-start.28 = (bf16[32,4608]{1,0:T(8,128)(2,1)S(1)}, bf16[32,4608]{1,0:T(8,128)(2,1)}, u32[]{:S(2)}) copy-start(bf16[32,4608]{1,0:T(8,128)(2,1)} %param.20) | copy-start | bytes 884740
  19.5 144.7 %all-gather.10.cloned.1.call-start = ((), (), s32[]{:S(2)}) async-start(), calls=%async_computation.8 | async-start | bytes 5308416 | tf_op jit(solution)/shard_map/all_gather | solution.py:269
  19.6 5.5 %collective-permute-start.12 = (s32[512,1]{0,1:T(1,128)S(1)}, s32[512,1]{0,1:T(1,128)S(1)}, u32[]{:S(2)}, u32[]{:S(2)}) collective-permute-start(s32[512,1]{0,1:T(1,128)S(1)} %bitcast.191), channel_id=1, source_target_pairs={{0,8},{8,0},{1,9},{9,1},{2,10},{10,2},{3,11},{11,3},{4,12},{12,4},... | collective-permute-start | bytes 6152 | tf_op jit(solution)/shard_map/ppermute | solution.py:37
  19.9 7.2 %collective-permute-start.11 = (s32[512,1]{0,1:T(1,128)S(1)}, s32[512,1]{0,1:T(1,128)S(1)}, u32[]{:S(2)}, u32[]{:S(2)}) collective-permute-start(s32[512,1]{0,1:T(1,128)S(1)} %bitcast.192), channel_id=1, source_target_pairs={{0,4},{4,0},{1,5},{5,1},{2,6},{6,2},{3,7},{7,3},{8,12},{12,8},{9,1... | collective-permute-start | bytes 6152 | tf_op jit(solution)/shard_map/ppermute | solution.py:33
  21.3 51.7 %collective-permute-start.9 = (bf16[512,1024]{1,0:T(8,128)(2,1)}, bf16[512,1024]{1,0:T(8,128)(2,1)}, u32[]{:S(2)}, u32[]{:S(2)}) collective-permute-start(bf16[512,1024]{1,0:T(8,128)(2,1)} %fusion.8.refs_4_), channel_id=1, source_target_pairs={{0,8},{8,0},{1,9},{9,1},{2,10},{10,2},{3,11},{11,3},{4,12},{12,4},... | collective-permute-start | bytes 3145736 | tf_op jit(solution)/shard_map/ppermute | solution.py:37
  23.0 50.0 %collective-permute-start.1 = (bf16[512,1024]{1,0:T(8,128)(2,1)S(1)}, bf16[512,1024]{1,0:T(8,128)(2,1)}, u32[]{:S(2)}, u32[]{:S(2)}) collective-permute-start(bf16[512,1024]{1,0:T(8,128)(2,1)S(1)} %bitcast.141), channel_id=1, source_target_pairs={{0,8},{8,0},{1,9},{9,1},{2,10},{10,2},{3,11},{11,3},{4,12},{12,4},... | collective-permute-start | bytes 3145736 | tf_op jit(solution)/shard_map/ppermute | solution.py:37
  25.2 2.3 collective-permute-start.13
  25.3 47.0 %collective-permute-start.20 = (bf16[32,2304]{1,0:T(8,128)(2,1)S(1)}, bf16[32,2304]{1,0:T(8,128)(2,1)S(1)}, u32[]{:S(2)}, u32[]{:S(2)}) collective-permute-start(bf16[32,2304]{1,0:T(8,128)(2,1)S(1)} %get-tuple-element.80), channel_id=1, source_target_pairs={{0,12},{4,8},{8,4},{12,0},{1,13},{5,9},{9,5},{13,1},{2,14},{6,10},... | collective-permute-start | bytes 442376 | tf_op jit(solution)/shard_map/ppermute | solution.py:45
  27.1 48.7 %collective-permute-start.21 = (bf16[32,2304]{1,0:T(8,128)(2,1)S(1)}, bf16[32,2304]{1,0:T(8,128)(2,1)S(1)}, u32[]{:S(2)}, u32[]{:S(2)}) collective-permute-start(bf16[32,2304]{1,0:T(8,128)(2,1)S(1)} %get-tuple-element.46), channel_id=1, source_target_pairs={{0,8},{4,12},{8,0},{12,4},{1,9},{5,13},{9,1},{13,5},{2,10},{6,14},... | collective-permute-start | bytes 442376 | tf_op jit(solution)/shard_map/ppermute | solution.py:45
  27.5 48.3 %collective-permute-start.22 = (bf16[32,2304]{1,0:T(8,128)(2,1)S(1)}, bf16[32,2304]{1,0:T(8,128)(2,1)S(1)}, u32[]{:S(2)}, u32[]{:S(2)}) collective-permute-start(bf16[32,2304]{1,0:T(8,128)(2,1)S(1)} %get-tuple-element.79), channel_id=1, source_target_pairs={{0,4},{4,0},{8,12},{12,8},{1,5},{5,1},{9,13},{13,9},{2,6},{6,2},{1... | collective-permute-start | bytes 442376 | tf_op jit(solution)/shard_map/ppermute | solution.py:45
  72.3 8.0 %collective-permute-start = (bf16[512,1024]{1,0:T(8,128)(2,1)S(1)}, bf16[512,1024]{1,0:T(8,128)(2,1)S(1)}, u32[]{:S(2)}, u32[]{:S(2)}) collective-permute-start(bf16[512,1024]{1,0:T(8,128)(2,1)S(1)} %bitcast.142), channel_id=1, source_target_pairs={{0,4},{4,0},{1,5},{5,1},{2,6},{6,2},{3,7},{7,3},{8,12},{12,8},{9,1... | collective-permute-start | bytes 3145736 | tf_op jit(solution)/shard_map/ppermute | solution.py:33
  73.0 5.5 %collective-permute-start.10 = (bf16[512,1024]{1,0:T(8,128)(2,1)}, bf16[512,1024]{1,0:T(8,128)(2,1)}, u32[]{:S(2)}, u32[]{:S(2)}) collective-permute-start(bf16[512,1024]{1,0:T(8,128)(2,1)} %collective-permute-done.9.refs_6_), channel_id=1, source_target_pairs={{0,4},{4,0},{1,5},{5,1},{2,6},{6,2},{3,7},{7,3},{8,12},{12,8},{9,1... | collective-permute-start | bytes 3145736 | tf_op jit(solution)/shard_map/ppermute | solution.py:33
  73.0 7.3 %collective-permute-start.2 = (bf16[512,1024]{1,0:T(8,128)(2,1)}, bf16[512,1024]{1,0:T(8,128)(2,1)S(1)}, u32[]{:S(2)}, u32[]{:S(2)}) collective-permute-start(bf16[512,1024]{1,0:T(8,128)(2,1)} %collective-permute-done.1), channel_id=1, source_target_pairs={{0,4},{4,0},{1,5},{5,1},{2,6},{6,2},{3,7},{7,3},{8,12},{12,8},{9,1... | collective-permute-start | bytes 3145736 | tf_op jit(solution)/shard_map/ppermute | solution.py:33
  76.7 133.9 %all-gather.6.cloned.1.call-start = ((), (), s32[]{:S(2)}) async-start(), calls=%async_computation.3 | async-start | bytes 2654208 | tf_op jit(solution)/shard_map/all_gather | solution.py:270
  90.1 12.8 %copy-start.23 = (bf16[8,32,1024]{2,1,0:T(8,128)(2,1)}, bf16[8,32,1024]{2,1,0:T(8,128)(2,1)S(1)}, u32[]{:S(2)}) copy-start(bf16[8,32,1024]{2,1,0:T(8,128)(2,1)S(1)} %pad_maximum_fusion.12) | copy-start | bytes 1572868
  104.5 4.2 collective-permute-start.14
  111.2 25.3 %collective-permute-start.15 = (bf16[512,1024]{1,0:T(8,128)(2,1)S(1)}, bf16[512,1024]{1,0:T(8,128)(2,1)}, u32[]{:S(2)}, u32[]{:S(2)}) collective-permute-start(bf16[512,1024]{1,0:T(8,128)(2,1)S(1)} %fusion.24), channel_id=1, source_target_pairs={{0,8},{8,0},{1,9},{9,1},{2,10},{10,2},{3,11},{11,3},{4,12},{12,4},... | collective-permute-start | bytes 3145736 | tf_op jit(solution)/shard_map/ppermute | solution.py:37
  139.7 24.6 %collective-permute-start.17 = (bf16[512,1024]{1,0:T(8,128)(2,1)S(1)}, bf16[512,1024]{1,0:T(8,128)(2,1)}, u32[]{:S(2)}, u32[]{:S(2)}) collective-permute-start(bf16[512,1024]{1,0:T(8,128)(2,1)S(1)} %multiply_convert_fusion.4.refs_0_), channel_id=1, source_target_pairs={{0,8},{8,0},{1,9},{9,1},{2,10},{10,2},{3,11},{11,3},{4,12},{12,4},... | collective-permute-start | bytes 3145736 | tf_op jit(solution)/shard_map/ppermute | solution.py:37
  141.4 161.5 %reduce-scatter.4.cloned.1.call-start = ((), (), s32[]{:S(2)}) async-start(), calls=%async_computation.4 | async-start | bytes 1474560 | tf_op jit(solution)/shard_map/reduce_scatter | solution.py:96
  142.0 27.3 %collective-permute-start.19 = (bf16[512,1024]{1,0:T(8,128)(2,1)}, bf16[512,1024]{1,0:T(8,128)(2,1)}, u32[]{:S(2)}, u32[]{:S(2)}) collective-permute-start(bf16[512,1024]{1,0:T(8,128)(2,1)} %fusion.8.refs_4_), channel_id=1, source_target_pairs={{0,4},{4,0},{1,5},{5,1},{2,6},{6,2},{3,7},{7,3},{8,12},{12,8},{9,1... | collective-permute-start | bytes 3145736 | tf_op jit(solution)/shard_map/ppermute | solution.py:33
  142.1 27.2 %collective-permute-start.16 = (bf16[512,1024]{1,0:T(8,128)(2,1)S(1)}, bf16[512,1024]{1,0:T(8,128)(2,1)}, u32[]{:S(2)}, u32[]{:S(2)}) collective-permute-start(bf16[512,1024]{1,0:T(8,128)(2,1)S(1)} %multiply_convert_fusion.4.refs_0_), channel_id=1, source_target_pairs={{0,4},{4,0},{1,5},{5,1},{2,6},{6,2},{3,7},{7,3},{8,12},{12,8},{9,1... | collective-permute-start | bytes 3145736 | tf_op jit(solution)/shard_map/ppermute | solution.py:33
  164.2 5.0 %collective-permute-start.18 = (bf16[512,1024]{1,0:T(8,128)(2,1)}, bf16[512,1024]{1,0:T(8,128)(2,1)}, u32[]{:S(2)}, u32[]{:S(2)}) collective-permute-start(bf16[512,1024]{1,0:T(8,128)(2,1)} %collective-permute-done.17.refs_2_), channel_id=1, source_target_pairs={{0,4},{4,0},{1,5},{5,1},{2,6},{6,2},{3,7},{7,3},{8,12},{12,8},{9,1... | collective-permute-start | bytes 3145736 | tf_op jit(solution)/shard_map/ppermute | solution.py:33
  241.9 33.3 %collective-permute-start.24 = (bf16[1024,1024]{1,0:T(8,128)(2,1)}, bf16[1024,1024]{1,0:T(8,128)(2,1)}, u32[]{:S(2)}, u32[]{:S(2)}) collective-permute-start(bf16[1024,1024]{1,0:T(8,128)(2,1)} %pad_maximum_fusion.4), channel_id=1, source_target_pairs={{0,4},{4,0},{1,5},{5,1},{2,6},{6,2},{3,7},{7,3},{8,12},{12,8},{9,1... | collective-permute-start | bytes 6291464 | tf_op jit(solution)/shard_map/ppermute | solution.py:33
  243.3 28.6 %collective-permute-start.23 = (bf16[4,144,1024]{2,1,0:T(8,128)(2,1)S(1)}, bf16[4,144,1024]{2,1,0:T(8,128)(2,1)}, u32[]{:S(2)}, u32[]{:S(2)}) collective-permute-start(bf16[4,144,1024]{2,1,0:T(8,128)(2,1)S(1)} %dynamic-slice_bitcast_fusion.2), channel_id=1, source_target_pairs={{0,16},{16,0},{1,17},{17,1},{2,18},{18,2},{3,19},{19,3},{4,20},{20... | collective-permute-start | bytes 3538952 | tf_op jit(solution)/shard_map/ppermute | solution.py:41
  275.0 127.8 %reduce-scatter.6.cloned.1.call-start = ((), (), s32[]{:S(2)}) async-start(), calls=%async_computation.5 | async-start | bytes 2949120 | tf_op jit(solution)/shard_map/reduce_scatter | solution.py:96
  282.0 25.1 %collective-permute-start.25 = (bf16[512,1024]{1,0:T(8,128)(2,1)}, bf16[512,1024]{1,0:T(8,128)(2,1)S(1)}, u32[]{:S(2)}, u32[]{:S(2)}) collective-permute-start(bf16[512,1024]{1,0:T(8,128)(2,1)} %fusion.21), channel_id=1, source_target_pairs={{0,8},{8,0},{1,9},{9,1},{2,10},{10,2},{3,11},{11,3},{4,12},{12,4},... | collective-permute-start | bytes 3145736 | tf_op jit(solution)/shard_map/ppermute | solution.py:37
  299.7 52.9 %collective-permute-start.34 = (bf16[4,128,2304]{2,1,0:T(8,128)(2,1)}, bf16[4,128,2304]{2,1,0:T(8,128)(2,1)}, u32[]{:S(2)}, u32[]{:S(2)}) collective-permute-start(bf16[4,128,2304]{2,1,0:T(8,128)(2,1)} %dynamic-slice_bitcast_fusion), channel_id=1, source_target_pairs={{0,16},{16,0},{1,17},{17,1},{2,18},{18,2},{3,19},{19,3},{4,20},{20... | collective-permute-start | bytes 7077896 | tf_op jit(solution)/shard_map/ppermute | solution.py:41
  304.8 5.2 %copy-start.20 = (bf16[2,256,1024]{2,1,0:T(8,128)(2,1)S(1)}, bf16[2,256,1024]{2,1,0:T(8,128)(2,1)}, u32[]{:S(2)}) copy-start(bf16[2,256,1024]{2,1,0:T(8,128)(2,1)} %param.13) | copy-start | bytes 3145732
  310.0 5.6 %copy-start.7 = (bf16[2,256,1024]{2,1,0:T(8,128)(2,1)S(1)}, bf16[2,256,1024]{2,1,0:T(8,128)(2,1)}, u32[]{:S(2)}) copy-start(bf16[2,256,1024]{2,1,0:T(8,128)(2,1)} %param.11) | copy-start | bytes 3145732
  314.2 24.5 %collective-permute-start.26 = (bf16[512,1024]{1,0:T(8,128)(2,1)}, bf16[512,1024]{1,0:T(8,128)(2,1)}, u32[]{:S(2)}, u32[]{:S(2)}) collective-permute-start(bf16[512,1024]{1,0:T(8,128)(2,1)} %get-tuple-element.44), channel_id=1, source_target_pairs={{0,8},{8,0},{1,9},{9,1},{2,10},{10,2},{3,11},{11,3},{4,12},{12,4},... | collective-permute-start | bytes 3145736 | tf_op jit(solution)/shard_map/ppermute | solution.py:37
  316.2 42.6 %collective-permute-start.30 = (bf16[512,1024]{1,0:T(8,128)(2,1)}, bf16[512,1024]{1,0:T(8,128)(2,1)}, u32[]{:S(2)}, u32[]{:S(2)}) collective-permute-start(bf16[512,1024]{1,0:T(8,128)(2,1)} %get-tuple-element.44), channel_id=1, source_target_pairs={{0,4},{4,0},{1,5},{5,1},{2,6},{6,2},{3,7},{7,3},{8,12},{12,8},{9,1... | collective-permute-start | bytes 3145736 | tf_op jit(solution)/shard_map/ppermute | solution.py:33
  338.7 20.0 %collective-permute-start.27 = (bf16[512,1024]{1,0:T(8,128)(2,1)}, bf16[512,1024]{1,0:T(8,128)(2,1)}, u32[]{:S(2)}, u32[]{:S(2)}) collective-permute-start(bf16[512,1024]{1,0:T(8,128)(2,1)} %collective-permute-done.26), channel_id=1, source_target_pairs={{0,4},{4,0},{1,5},{5,1},{2,6},{6,2},{3,7},{7,3},{8,12},{12,8},{9,1... | collective-permute-start | bytes 3145736 | tf_op jit(solution)/shard_map/ppermute | solution.py:33
  356.9 118.8 %reduce-scatter.8.cloned.1.call-start = ((), (), s32[]{:S(2)}) async-start(), calls=%async_computation.6 | async-start | bytes 1474560 | tf_op jit(solution)/shard_map/reduce_scatter | solution.py:96
  368.3 5.5 %copy-start.43 = (bf16[2048,256]{1,0:T(8,128)(2,1)}, bf16[2048,256]{1,0:T(8,128)(2,1)S(1)}, u32[]{:S(2)}) copy-start(bf16[2048,256]{1,0:T(8,128)(2,1)S(1)} %get-tuple-element.65) | copy-start | bytes 3145732
  373.8 5.4 %copy-start.32 = (bf16[2048,256]{1,0:T(8,128)(2,1)}, bf16[2048,256]{1,0:T(8,128)(2,1)S(1)}, u32[]{:S(2)}) copy-start(bf16[2048,256]{1,0:T(8,128)(2,1)S(1)} %multiply_convert_fusion) | copy-start | bytes 3145732
  387.7 26.7 %collective-permute-start.33 = (bf16[4,144,1024]{2,1,0:T(8,128)(2,1)}, bf16[4,144,1024]{2,1,0:T(8,128)(2,1)}, u32[]{:S(2)}, u32[]{:S(2)}) collective-permute-start(bf16[4,144,1024]{2,1,0:T(8,128)(2,1)} %dynamic-slice_bitcast_fusion.1), channel_id=1, source_target_pairs={{0,16},{16,0},{1,17},{17,1},{2,18},{18,2},{3,19},{19,3},{4,20},{20... | collective-permute-start | bytes 3538952 | tf_op jit(solution)/shard_map/ppermute | solution.py:41
  392.6 5.2 %copy-start.21 = (bf16[2048,1024]{1,0:T(8,128)(2,1)S(1)}, bf16[2048,1024]{1,0:T(8,128)(2,1)}, u32[]{:S(2)}) copy-start(bf16[2048,1024]{1,0:T(8,128)(2,1)} %get-tuple-element.22) | copy-start | bytes 12582916
  395.5 22.1 %collective-permute-start.31 = (bf16[1024,1024]{1,0:T(8,128)(2,1)}, bf16[1024,1024]{1,0:T(8,128)(2,1)}, u32[]{:S(2)}, u32[]{:S(2)}) collective-permute-start(bf16[1024,1024]{1,0:T(8,128)(2,1)} %pad_maximum_fusion.6), channel_id=1, source_target_pairs={{0,4},{4,0},{1,5},{5,1},{2,6},{6,2},{3,7},{7,3},{8,12},{12,8},{9,1... | collective-permute-start | bytes 6291464 | tf_op jit(solution)/shard_map/ppermute | solution.py:33
  400.7 37.5 %collective-permute-start.28 = (bf16[1024,1024]{1,0:T(8,128)(2,1)}, bf16[1024,1024]{1,0:T(8,128)(2,1)}, u32[]{:S(2)}, u32[]{:S(2)}) collective-permute-start(bf16[1024,1024]{1,0:T(8,128)(2,1)} %pad_maximum_fusion.5), channel_id=1, source_target_pairs={{0,4},{4,0},{1,5},{5,1},{2,6},{6,2},{3,7},{7,3},{8,12},{12,8},{9,1... | collective-permute-start | bytes 6291464 | tf_op jit(solution)/shard_map/ppermute | solution.py:33
  404.7 19.1 %collective-permute-start.38 = (bf16[32,2304]{1,0:T(8,128)(2,1)}, bf16[32,2304]{1,0:T(8,128)(2,1)}, u32[]{:S(2)}, u32[]{:S(2)}) collective-permute-start(bf16[32,2304]{1,0:T(8,128)(2,1)} %get-tuple-element.75), channel_id=1, source_target_pairs={{0,12},{4,8},{8,4},{12,0},{1,13},{5,9},{9,5},{13,1},{2,14},{6,10},... | collective-permute-start | bytes 442376 | tf_op jit(solution)/shard_map/ppermute | solution.py:45
  405.5 18.4 %collective-permute-start.39 = (bf16[32,2304]{1,0:T(8,128)(2,1)}, bf16[32,2304]{1,0:T(8,128)(2,1)}, u32[]{:S(2)}, u32[]{:S(2)}) collective-permute-start(bf16[32,2304]{1,0:T(8,128)(2,1)} %get-tuple-element.76), channel_id=1, source_target_pairs={{0,8},{4,12},{8,0},{12,4},{1,9},{5,13},{9,1},{13,5},{2,10},{6,14},... | collective-permute-start | bytes 442376 | tf_op jit(solution)/shard_map/ppermute | solution.py:45
  414.4 9.5 %collective-permute-start.40 = (bf16[32,2304]{1,0:T(8,128)(2,1)}, bf16[32,2304]{1,0:T(8,128)(2,1)}, u32[]{:S(2)}, u32[]{:S(2)}) collective-permute-start(bf16[32,2304]{1,0:T(8,128)(2,1)} %get-tuple-element.74), channel_id=1, source_target_pairs={{0,4},{4,0},{8,12},{12,8},{1,5},{5,1},{9,13},{13,9},{2,6},{6,2},{1... | collective-permute-start | bytes 442376 | tf_op jit(solution)/shard_map/ppermute | solution.py:45
  419.6 6.2 %copy-start.2 = (f32[1024,1024]{1,0:T(8,128)}, f32[1024,1024]{1,0:T(8,128)S(1)}, u32[]{:S(2)}) copy-start(f32[1024,1024]{1,0:T(8,128)S(1)} %convert_element_type.332) | copy-start | bytes 12582916
  423.0 26.3 %collective-permute-start.32 = (bf16[512,1024]{1,0:T(8,128)(2,1)}, bf16[512,1024]{1,0:T(8,128)(2,1)}, u32[]{:S(2)}, u32[]{:S(2)}) collective-permute-start(bf16[512,1024]{1,0:T(8,128)(2,1)} %fusion.13), channel_id=1, source_target_pairs={{0,8},{8,0},{1,9},{9,1},{2,10},{10,2},{3,11},{11,3},{4,12},{12,4},... | collective-permute-start | bytes 3145736 | tf_op jit(solution)/shard_map/ppermute | solution.py:37
  438.2 11.1 %copy-start.17 = (bf16[2048,1024]{1,0:T(8,128)(2,1)S(1)}, bf16[2048,1024]{1,0:T(8,128)(2,1)}, u32[]{:S(2)}) copy-start(bf16[2048,1024]{1,0:T(8,128)(2,1)} %copy-done.16) | copy-start | bytes 12582916
  441.0 8.2 %copy-start.3 = (f32[1024,1024]{1,0:T(8,128)S(1)}, f32[1024,1024]{1,0:T(8,128)}, u32[]{:S(2)}) copy-start(f32[1024,1024]{1,0:T(8,128)} %copy-done.2) | copy-start | bytes 12582916
  441.4 29.8 %collective-permute-start.29 = (bf16[512,1024]{1,0:T(8,128)(2,1)S(1)}, bf16[512,1024]{1,0:T(8,128)(2,1)S(1)}, u32[]{:S(2)}, u32[]{:S(2)}) collective-permute-start(bf16[512,1024]{1,0:T(8,128)(2,1)S(1)} %fusion.16), channel_id=1, source_target_pairs={{0,8},{8,0},{1,9},{9,1},{2,10},{10,2},{3,11},{11,3},{4,12},{12,4},... | collective-permute-start | bytes 3145736 | tf_op jit(solution)/shard_map/ppermute | solution.py:37
  451.2 21.5 %copy-start.14 = (f32[512,1024]{1,0:T(8,128)S(1)}, f32[512,1024]{1,0:T(8,128)}, u32[]{:S(2)}) copy-start(f32[512,1024]{1,0:T(8,128)} %get-tuple-element.45) | copy-start | bytes 6291460
  475.8 7.4 %copy-start.38 = (bf16[32,3072]{1,0:T(8,128)(2,1)S(1)}, bf16[32,3072]{1,0:T(8,128)(2,1)}, u32[]{:S(2)}) copy-start(bf16[32,3072]{1,0:T(8,128)(2,1)} %param.15) | copy-start | bytes 589828
  475.8 7.5 %copy-start.42 = (bf16[32]{0:T(256)(128)(2,1)S(1)}, bf16[32]{0:T(256)(128)(2,1)}, u32[]{:S(2)}) copy-start(bf16[32]{0:T(256)(128)(2,1)} %param.14) | copy-start | bytes 196
  477.5 4.1 collective-permute-start.35
  477.7 4.7 collective-permute-start.36
  478.9 3.6 collective-permute-start.37
  (29 other events, 89.2 us)
Sparse Core Ops, SparseCore 0:
  19.7 52.3 all-gather.7
  76.8 81.3 all-gather.9
  160.4 50.2 all-gather.5
  275.1 27.7 reduce-scatter.3
  357.1 45.7 reduce-scatter.5
  417.7 27.1 reduce-scatter.7

commit v7 on v6

--- a/solution.py
+++ b/solution.py
@@ -77,20 +77,21 @@
     came = swap_core(sent).astype(f32)
     own = terms[:count].astype(f32) + came[:count]
     other = terms[2 * count : 3 * count].astype(f32) + came[count:]
-    came = swap_chip(other.astype(bf16)).astype(f32)
-    return own + (came if token is None else after(came, token))
+    other = other.astype(bf16)
+    came = swap_chip(other).astype(f32)
+    return own + (came if token is None else after(came, token)), other[:1, :1]
 
 
 def take(blocks, index):
     return lax.dynamic_index_in_dim(blocks, index, axis=0, keepdims=False)
 
 
-def scatter(part, token=None):
+def scatter(part, *tokens):
     groups, slots = part.shape[:2]
     if groups == 2:
         row = lax.axis_index("y")
         came = swap_row(take(part, 1 - row)).astype(f32)
-        if token is not None:
+        for token in tokens:
             came = after(came, token)
         summed = (take(part, row).astype(f32) + came).astype(bf16)
         return lax.psum_scatter(summed, "s", scatter_dimension=0, tiled=False)
@@ -302,7 +303,7 @@
     convolved = conv_full[0] * mixed + conv_full[1] * mixed_one + conv_full[2] * mixed_two
     mixer_in = (c_part * convolved).astype(bf16)
     mixer_out = team_sum(forward_dot(mixer_in, out_full).astype(bf16))
-    middle = inputs + live * mixer_out
+    middle = inputs + live * mixer_out[0]
     second_scale = inverse_rms(middle)
     second_pieces = team_pieces((middle * second_scale * ffn_full).astype(bf16))
 
@@ -340,19 +341,19 @@
         return jnp.transpose(split, (0, 2, 1, 3, 4)).reshape(count, slots, team * share, width)
 
     pair_part = by_owner(rows_dot(second_normed, pair_grad), TEAM)
-    pair_sum = scatter(pair_part)
-    normed_sum = team_sum(normed_part, pair_part[0, 0, :1])
-    second_weighted = after(ffn_full, grad_down[:1]) * normed_sum
+    normed_sum, _ = team_sum(normed_part, pair_part[0, 0, :1])
+    second_weighted = ffn_full * normed_sum
     middle_grad = upstream + norm_back(middle, second_scale, second_weighted)
 
     mixer_grad = team_rows((live * middle_grad).astype(bf16))
     mixer_in_grad = back_dot(mixer_grad, out_full)
     c_grad = mixer_in_grad * convolved
     conv_grad = mixer_in_grad * c_part
+    conv_back = after(conv_full, grad_down[:1])
     mixed_grad = (
-        conv_full[0] * conv_grad
-        + conv_full[1] * shifted_up(mask_one * conv_grad, 1)
-        + conv_full[2] * shifted_up(mask_two * conv_grad, 2)
+        conv_back[0] * conv_grad
+        + conv_back[1] * shifted_up(mask_one * conv_grad, 1)
+        + conv_back[2] * shifted_up(mask_two * conv_grad, 2)
     )
     projected_grad = jnp.concatenate(
         [mixed_grad * x_part, c_grad, mixed_grad * b_part], axis=1
@@ -374,18 +375,20 @@
         conv_rows.astype(bf16),
         ((0, 0), (0, 0), (0, EXTRA_ROWS - 1), (0, features - taps * share)),
     )
+    pair_sum = scatter(pair_part, projected_grad[-1:])
+    first_weighted, first_sent = team_sum(back_dot(projected_grad, in_full).astype(bf16))
+    input_grad = middle_grad + norm_back(inputs, inverse_rms(inputs), norm_full * first_weighted)
+    input_grad = input_grad.astype(bf16)
+    out_sum, _ = team_sum(after(out_part, mixer_grad[-1:]))
+    block_out = (middle + live * out_sum).astype(bf16)
     first_sum = scatter(
         jnp.concatenate(
             [jnp.concatenate([in_part, out_grad_part], axis=3), conv_rows], axis=2
         ),
         pair_sum[:1],
-    )
-
-    first_weighted = norm_full * team_sum(back_dot(projected_grad, in_full).astype(bf16))
-    input_grad = middle_grad + norm_back(inputs, inverse_rms(inputs), first_weighted)
-    input_grad = input_grad.astype(bf16)
-    out_sum = team_sum(after(out_part, mixer_grad[-1:]))
-    block_out = (middle + live * out_sum).astype(bf16)
+        first_sent,
+        block_out[:1],
+    )
 
     def own_rows(summed, parts, team, run):
         blocks = [summed[j * share : (j + 1) * share].astype(bf16) for j in range(team)]

time: 496 us -> 495 us (level)
    ppermute x3, waiting for transfers between devices: 48.1 us -> 24.5 us  [swap_row(): return lax.ppermute(values, 'y', [(0, 1), (1, 0)])]
    reduce_scatter x3, waiting for transfers between devices: 4.11 us -> 12.7 us  [scatter(): return lax.psum_scatter(summed, 's', scatter_dimension=0, tiled=False)]
    ppermute x10, waiting for transfers between devices: 93.7 us -> 101 us  [swap_chip(): return lax.ppermute(values, 'x', [(0, 1), (1, 0)])]
    reshape x16, local copies, waits for them, and re-layouts: 5.9 us -> 0.94 us  [own_rows(): block.reshape(share, parts, -1, 1, run)]
    unnamed x96 -> x94, local copies, waits for them, and re-layouts: 11.7 us -> 15.8 us
  transfers between devices with their start and end apart: 47 -> 47, of which waited for: 19 -> 20; matrix products, arithmetic and copies ran while one was open for 34% -> 31% of each run, Pallas kernels for 4% -> 4%
where the time goes in v7:
time: 495 us; the launch traced here: 490 us
  waiting for transfers between devices  213 us (43%)
  other arithmetic  77.9 us (16%)
  local copies, waits for them, and re-layouts  51.6 us (10%)
  matrix products  51.3 us (10%)
  Pallas kernels  45.8 us (9%)
  starting transfers between devices  28.8 us (6%)
  between operations  21 us (4%)
    ppermute x10, waiting for transfers between devices, swap_chip(): return lax.ppermute(values, 'x', [(0, 1), (1, 0)])  101 us
    ppermute x12, waiting for transfers between devices, swap_far(): lax.ppermute(values, ('x', 'c'), [(i, i ^ distance) for i in range(TEAM)])  51.8 us
    pallas_call x2, Pallas kernels, by_rows(): pl.pallas_call(kernel, grid=(steps,), in_specs=[row_block(value.shape[1])...  45.8 us
    dot_general x4, matrix products, rows_dot(): lax.dot_general(left_side, right_side, (((0,), (0,)), ((), ())), preferre...  32.1 us
    ppermute x3, waiting for transfers between devices, swap_row(): return lax.ppermute(values, 'y', [(0, 1), (1, 0)])  24.5 us
    all_gather x1, waiting for transfers between devices, per_device(): down_full = lax.all_gather(down_weight, ('g', 'y', 's'), axis=0, tiled=True)  15.8 us
    unnamed x94, local copies, waits for them, and re-layouts  15.8 us
    ppermute x10, starting transfers between devices, swap_chip(): return lax.ppermute(values, 'x', [(0, 1), (1, 0)])  13.6 us
  transfers between devices with their start and end apart: 47, of which 20 were waited for; matrix products, arithmetic and copies ran while one was open for 31% of the time, Pallas kernels for 4%

profile of v7, /device:TPU:0, one launch (start us, length us, event | category | flops | bytes accessed | tf_op | source)
XLA Modules:
  0.0 489.8 jit_solution(7441357356905577460)
XLA Ops:
  8.1 2.9 collective-permute-start.6
  12.8 2.0 collective-permute-start.4
  21.4 1.7 collective-permute-start.9
  25.4 1.8 collective-permute-start.20
  27.6 44.8 %collective-permute-done.20 = bf16[32,2304]{1,0:T(8,128)(2,1)S(1)} collective-permute-done((bf16[32,2304]{1,0:T(8,128)(2,1)S(1)}, bf16[32,2304]{1,0:T(8,128)(2,1)S(1)}, u32[]{:S(2)}, u32[]{:S(2)}) %collective-permute-start.20) | collective-permute-done | bytes 147488 | tf_op jit(solution)/shard_map/ppermute | solution.py:45
  73.5 2.3 collective-permute-done.21
  80.4 3.5 fusion
  83.9 1.5 slice.402
  89.0 7.4 %fusion.28 = f32[2048,768]{1,0:T(8,128)S(1)} fusion(bf16[1024,768]{1,0:T(8,128)(2,1)S(1)} %bitcast.176, f32[1024]{0:T(1024)S(1)} %mul.336, f32[2048]{0:T(1024)S(1)} %add_rsqrt_fusion, bf16[512,1024]{1,0:T(8,128)(2,1)} %copy-done.34, bf16[512,1024]{1,0:T(8,128)(2,1)} %collective-permute-done.1, bf16[512,1024]{1,0:T(8,128)(2,1)} %copy-done.33, ...), kind=kOutput, calls=%fused_computation.81 | convolution fusion | flops 3244294144 | bytes 12070912 | tf_op jit(solution)/shard_map/dot_general | solution.py:17
  96.7 2.3 copy-done
  99.0 2.3 multiply_convert_fusion.5
  103.2 4.0 collective-permute-done.14
  108.0 1.6 copy-done.10
  109.7 1.7 collective-permute-start.15
  111.4 23.5 %collective-permute-done.15 = bf16[512,1024]{1,0:T(8,128)(2,1)} collective-permute-done((bf16[512,1024]{1,0:T(8,128)(2,1)S(1)}, bf16[512,1024]{1,0:T(8,128)(2,1)}, u32[]{:S(2)}, u32[]{:S(2)}) %collective-permute-start.15) | collective-permute-done | bytes 1048608 | tf_op jit(solution)/shard_map/ppermute | solution.py:37
  135.0 2.9 multiply_reduce_fusion.5
  138.2 1.8 collective-permute-start.17
  141.1 21.6 %collective-permute-done.17.refs_2_ = bf16[512,1024]{1,0:T(8,128)(2,1)} collective-permute-done((bf16[512,1024]{1,0:T(8,128)(2,1)S(1)}, bf16[512,1024]{1,0:T(8,128)(2,1)}, u32[]{:S(2)}, u32[]{:S(2)}) %collective-permute-start.17) | collective-permute-done | bytes 1048608 | tf_op jit(solution)/shard_map/ppermute | solution.py:37
  162.7 4.9 copy.69
  167.6 17.7 %shard_map.186 = (bf16[2048,1152]{1,0:T(8,128)(2,1)}, bf16[2048,1152]{1,0:T(8,128)(2,1)}, bf16[2048,1152]{1,0:T(8,128)(2,1)}, bf16[2048,1024]{1,0:T(8,128)(2,1)}, bf16[2048,1024]{1,0:T(8,128)(2,1)}) custom-call(bf16[512,1024]{1,0:T(8,128)(2,1)S(1)} %multiply_convert_fusion.4.refs_0_, bf16[512,1024]{1,0:T(8,128)(2,1)} %collective-permute-done.16.refs_1_, ...), custom_call_target="tpu_custom_call" | custom-call | flops 9663676416 | bytes 35651584 | tf_op jit(solution)/shard_map/pallas_call | solution.py:150
  185.3 9.6 %convolution_convert_fusion.1.token_ref = bf16[1152,1024]{1,0:T(8,128)(2,1)} fusion(bf16[2048,1152]{1,0:T(8,128)(2,1)} %get-tuple-element.19.hidden_ref, bf16[2048,1024]{1,0:T(8,128)(2,1)} %get-tuple-element.18.grad_ref), kind=kOutput, calls=%fused_computation.12 | convolution fusion | flops 4833017856 | bytes 11272192 | tf_op jit(solution)/shard_map/dot_general | solution.py:21
  194.9 15.8 %all-gather.6.cloned.1.call-done.down_ref = bf16[1152,1024]{1,0:T(8,128)(2,1)} async-done(((bf16[144,1024]{1,0:T(8,128)(2,1)}), bf16[1152,1024]{1,0:T(8,128)(2,1)}) %all-gather.6.cloned.1.call-update) | async-done | bytes 2359312 | tf_op jit(solution)/shard_map/all_gather | solution.py:271
  210.7 28.1 %shard_map.187 = (bf16[2048,2304]{1,0:T(8,128)(2,1)}, bf16[2048,1024]{1,0:T(8,128)(2,1)}, bf16[2048,1024]{1,0:T(8,128)(2,1)}) custom-call(bf16[2048,1024]{1,0:T(8,128)(2,1)} %get-tuple-element.18.grad_ref, bf16[2048,1152]{1,0:T(8,128)(2,1)} %get-tuple-element.19.hidden_ref, bf16[2048,1152]{1,0:T(8,128)(2,1)} %get-tuple-element.20.silu_ref, ...), custom_call_target="tpu_custom_call" | custom-call | flops 19327352832 | bytes 43253760 | tf_op jit(solution)/shard_map/pallas_call | solution.py:150
  238.8 1.7 fusion.47
  240.5 1.5 pad_maximum_fusion.4
  242.0 2.4 dynamic-slice_bitcast_fusion.2
  244.9 1.6 collective-permute-done.23
  246.5 2.2 convert_element_type.327
  248.7 2.1 copy-done.3
  250.8 3.1 fusion.21
  253.9 1.5 collective-permute-start.24
  255.4 12.4 %convolution_convert_fusion = bf16[1024,2304]{1,0:T(8,128)(2,1)S(1)} fusion(bf16[2048,1024]{1,0:T(8,128)(2,1)} %get-tuple-element.24, bf16[2048,2304]{1,0:T(8,128)(2,1)S(1)} %copy-done.42), kind=kOutput, calls=%fused_computation.5 | convolution fusion | flops 9666035712 | bytes 18350080 | tf_op jit(solution)/shard_map/dot_general | solution.py:21
  268.2 2.2 copy-done.7
  271.5 1.5 collective-permute-done.29
  273.1 3.1 fusion.7
  276.3 3.1 collective-permute-done.24
  279.3 3.0 multiply_reduce_fusion.4
  282.4 4.2 multiply_convert_fusion.3
  286.6 1.5 collective-permute-start.25
  288.1 23.0 %collective-permute-done.25 = bf16[512,1024]{1,0:T(8,128)(2,1)} collective-permute-done((bf16[512,1024]{1,0:T(8,128)(2,1)}, bf16[512,1024]{1,0:T(8,128)(2,1)}, u32[]{:S(2)}, u32[]{:S(2)}) %collective-permute-start.25) | collective-permute-done | bytes 1048608 | tf_op jit(solution)/shard_map/ppermute | solution.py:37
  311.7 3.3 dynamic-slice_bitcast_fusion
  319.9 2.6 broadcast_add_fusion
  322.8 1.6 pad_maximum_fusion.5
  327.7 6.9 %multiply_reduce_fusion.2 = (bf16[256]{0:T(256)(128)(2,1)S(1)}, bf16[256]{0:T(256)(128)(2,1)S(1)}, bf16[256]{0:T(256)(128)(2,1)S(1)}, f32[2048,256]{1,0:T(8,128)S(1)}, bf16[2048,256]{1,0:T(8,128)(2,1)S(1)}) fusion(f32[2048,256]{1,0:T(8,128)S(1)} %copy-done.9, f32[2046,256]{1,0:T(8,128)S(1)} %bitcast.160, f32[2048]{0:T(1024)S(1)} %get-tuple-element.117, ...), kind=kOutput, calls=%fused_computation.62 | convolution fusion | flops 1096285440 | bytes 18364928 | tf_op jit(solution)/shard_map/dot_general | solution.py:27
  338.3 3.7 convolution_convert_fusion.3
  342.2 1.8 pad_maximum_fusion.6
  346.0 23.0 %collective-permute-done.34 = bf16[4,128,2304]{2,1,0:T(8,128)(2,1)} collective-permute-done((bf16[4,128,2304]{2,1,0:T(8,128)(2,1)}, bf16[4,128,2304]{2,1,0:T(8,128)(2,1)}, u32[]{:S(2)}, u32[]{:S(2)}) %collective-permute-start.34) | collective-permute-done | bytes 2359328 | tf_op jit(solution)/shard_map/ppermute | solution.py:41
  369.0 4.5 fusion.3
  373.7 6.6 %convolution_convert_fusion.4 = bf16[1024,768]{1,0:T(8,128)(2,1)S(1)} fusion(bf16[2048,256]{1,0:T(8,128)(2,1)} %copy-done.32, bf16[2048,256]{1,0:T(8,128)(2,1)} %copy-done.41, bf16[2048,256]{1,0:T(8,128)(2,1)} %copy-done.31, f32[1024]{0:T(1024)S(1)} %mul.336, f32[2048]{0:T(1024)S(1)} %add_rsqrt_fusion, bf16[512,1024]{1,0:T(8,128)(2,1)} %copy-done.34, ...), kind=kOutput, calls=%fused_computation.79 | convolution fusion | flops 3254517760 | bytes 8925184 | tf_op jit(solution)/shard_map/dot_general | solution.py:21
  381.6 3.4 convolution_convert_fusion.5
  385.1 2.0 convert_element_type.336
  387.2 3.4 fusion.16
  390.5 1.5 collective-permute-start.28
  392.0 2.0 convert_element_type.350
  394.1 3.4 fusion.13
  403.8 13.0 %collective-permute-done.28 = bf16[512,1024]{1,0:T(8,128)(2,1)} collective-permute-done((bf16[512,1024]{1,0:T(8,128)(2,1)}, bf16[512,1024]{1,0:T(8,128)(2,1)}, u32[]{:S(2)}, u32[]{:S(2)}) %collective-permute-start.28) | collective-permute-done | bytes 1048608 | tf_op jit(solution)/shard_map/ppermute | solution.py:37
  416.9 2.6 fusion.20
  421.7 16.4 %collective-permute-done.32 = bf16[512,1024]{1,0:T(8,128)(2,1)} collective-permute-done((bf16[512,1024]{1,0:T(8,128)(2,1)}, bf16[512,1024]{1,0:T(8,128)(2,1)}, u32[]{:S(2)}, u32[]{:S(2)}) %collective-permute-start.32) | collective-permute-done | bytes 1048608 | tf_op jit(solution)/shard_map/ppermute | solution.py:37
  438.1 2.8 fusion.9
  442.8 3.4 fusion.6
  447.5 1.5 collective-permute-start.39
  449.3 4.1 fusion.12
  453.6 3.2 collective-permute-done.39
  461.6 12.7 %reduce-scatter.8.cloned.1.call-done = bf16[1,144,1024]{2,1,0:T(8,128)(2,1)} async-done(((bf16[4,144,1024]{2,1,0:T(8,128)(2,1)}), bf16[1,144,1024]{2,1,0:T(8,128)(2,1)}) %reduce-scatter.8.cloned.1.call-update) | async-done | bytes 294928 | tf_op jit(solution)/shard_map/reduce_scatter | solution.py:97
  (291 shorter events, 63.7 us)
Async XLA Ops:
  7.2 12.5 %copy-start.38 = (s32[2,256]{1,0:T(2,128)S(1)}, s32[2,256]{1,0:T(2,128)}, u32[]{:S(2)}) copy-start(s32[2,256]{1,0:T(2,128)} %param.12) | copy-start | bytes 6148
  7.2 13.0 %copy-start.18 = (bf16[2,256,1024]{2,1,0:T(8,128)(2,1)S(1)}, bf16[2,256,1024]{2,1,0:T(8,128)(2,1)}, u32[]{:S(2)}) copy-start(bf16[2,256,1024]{2,1,0:T(8,128)(2,1)} %param.13) | copy-start | bytes 3145732
  7.2 76.7 %all-gather.8.cloned.1.call-start = ((), (), s32[]{:S(2)}) async-start(), calls=%async_computation.7 | async-start | bytes 2654208 | tf_op jit(solution)/shard_map/all_gather | solution.py:265
  8.1 8.4 %collective-permute-start.6 = (bf16[1,64]{1,0:T(2,128)(2,1)S(1)}, bf16[1,64]{1,0:T(2,128)(2,1)S(1)}, u32[]{:S(2)}, u32[]{:S(2)}) collective-permute-start(bf16[1,64]{1,0:T(2,128)(2,1)S(1)} %maximum_bitcast_fusion.1), channel_id=1, source_target_pairs={{0,8},{8,0},{1,9},{9,1},{2,10},{10,2},{3,11},{11,3},{4,12},{12,4},... | collective-permute-start | bytes 392 | tf_op jit(solution)/shard_map/ppermute | solution.py:37
  11.0 6.1 %collective-permute-start.8 = (bf16[1,64]{1,0:T(2,128)(2,1)S(1)}, bf16[1,64]{1,0:T(2,128)(2,1)S(1)}, u32[]{:S(2)}, u32[]{:S(2)}) collective-permute-start(bf16[1,64]{1,0:T(2,128)(2,1)S(1)} %maximum_bitcast_fusion.1), channel_id=1, source_target_pairs={{0,4},{4,0},{1,5},{5,1},{2,6},{6,2},{3,7},{7,3},{8,12},{12,8},{9,1... | collective-permute-start | bytes 392 | tf_op jit(solution)/shard_map/ppermute | solution.py:33
  12.1 11.0 %copy-start.5 = (bf16[2,256,1024]{2,1,0:T(8,128)(2,1)S(1)}, bf16[2,256,1024]{2,1,0:T(8,128)(2,1)}, u32[]{:S(2)}) copy-start(bf16[2,256,1024]{2,1,0:T(8,128)(2,1)} %param.11) | copy-start | bytes 3145732
  12.1 11.3 %copy-start.27 = (bf16[32,4608]{1,0:T(8,128)(2,1)S(1)}, bf16[32,4608]{1,0:T(8,128)(2,1)}, u32[]{:S(2)}) copy-start(bf16[32,4608]{1,0:T(8,128)(2,1)} %param.19) | copy-start | bytes 884740
  12.5 6.2 %collective-permute-start.3 = (bf16[32,768]{1,0:T(8,128)(2,1)S(1)}, bf16[32,768]{1,0:T(8,128)(2,1)S(1)}, u32[]{:S(2)}, u32[]{:S(2)}) collective-permute-start(bf16[32,768]{1,0:T(8,128)(2,1)S(1)} %select_n.381), channel_id=1, source_target_pairs={{0,12},{4,8},{8,4},{12,0},{1,13},{5,9},{9,5},{13,1},{2,14},{6,10},... | collective-permute-start | bytes 147464 | tf_op jit(solution)/shard_map/ppermute | solution.py:45
  12.8 5.9 %collective-permute-start.4 = (bf16[32,768]{1,0:T(8,128)(2,1)S(1)}, bf16[32,768]{1,0:T(8,128)(2,1)S(1)}, u32[]{:S(2)}, u32[]{:S(2)}) collective-permute-start(bf16[32,768]{1,0:T(8,128)(2,1)S(1)} %select_n.385), channel_id=1, source_target_pairs={{0,8},{4,12},{8,0},{12,4},{1,9},{5,13},{9,1},{13,5},{2,10},{6,14},... | collective-permute-start | bytes 147464 | tf_op jit(solution)/shard_map/ppermute | solution.py:45
  14.8 3.9 collective-permute-start.5
  16.5 1.4 collective-permute-start.7
  18.7 5.5 %copy-start.29 = (bf16[32,4608]{1,0:T(8,128)(2,1)S(1)}, bf16[32,4608]{1,0:T(8,128)(2,1)}, u32[]{:S(2)}) copy-start(bf16[32,4608]{1,0:T(8,128)(2,1)} %param.20) | copy-start | bytes 884740
  19.6 143.1 %all-gather.10.cloned.1.call-start = ((), (), s32[]{:S(2)}) async-start(), calls=%async_computation.8 | async-start | bytes 5308416 | tf_op jit(solution)/shard_map/all_gather | solution.py:270
  19.7 5.5 %collective-permute-start.12 = (s32[512,1]{0,1:T(1,128)S(1)}, s32[512,1]{0,1:T(1,128)S(1)}, u32[]{:S(2)}, u32[]{:S(2)}) collective-permute-start(s32[512,1]{0,1:T(1,128)S(1)} %bitcast.199), channel_id=1, source_target_pairs={{0,8},{8,0},{1,9},{9,1},{2,10},{10,2},{3,11},{11,3},{4,12},{12,4},... | collective-permute-start | bytes 6152 | tf_op jit(solution)/shard_map/ppermute | solution.py:37
  19.9 7.3 %collective-permute-start.11 = (s32[512,1]{0,1:T(1,128)S(1)}, s32[512,1]{0,1:T(1,128)S(1)}, u32[]{:S(2)}, u32[]{:S(2)}) collective-permute-start(s32[512,1]{0,1:T(1,128)S(1)} %bitcast.200), channel_id=1, source_target_pairs={{0,4},{4,0},{1,5},{5,1},{2,6},{6,2},{3,7},{7,3},{8,12},{12,8},{9,1... | collective-permute-start | bytes 6152 | tf_op jit(solution)/shard_map/ppermute | solution.py:33
  21.4 51.6 %collective-permute-start.9 = (bf16[512,1024]{1,0:T(8,128)(2,1)}, bf16[512,1024]{1,0:T(8,128)(2,1)}, u32[]{:S(2)}, u32[]{:S(2)}) collective-permute-start(bf16[512,1024]{1,0:T(8,128)(2,1)} %fusion.8.refs_4_), channel_id=1, source_target_pairs={{0,8},{8,0},{1,9},{9,1},{2,10},{10,2},{3,11},{11,3},{4,12},{12,4},... | collective-permute-start | bytes 3145736 | tf_op jit(solution)/shard_map/ppermute | solution.py:37
  23.0 50.0 %collective-permute-start.1 = (bf16[512,1024]{1,0:T(8,128)(2,1)S(1)}, bf16[512,1024]{1,0:T(8,128)(2,1)}, u32[]{:S(2)}, u32[]{:S(2)}) collective-permute-start(bf16[512,1024]{1,0:T(8,128)(2,1)S(1)} %bitcast.150), channel_id=1, source_target_pairs={{0,8},{8,0},{1,9},{9,1},{2,10},{10,2},{3,11},{11,3},{4,12},{12,4},... | collective-permute-start | bytes 3145736 | tf_op jit(solution)/shard_map/ppermute | solution.py:37
  25.2 2.3 collective-permute-start.13
  25.4 47.0 %collective-permute-start.20 = (bf16[32,2304]{1,0:T(8,128)(2,1)S(1)}, bf16[32,2304]{1,0:T(8,128)(2,1)S(1)}, u32[]{:S(2)}, u32[]{:S(2)}) collective-permute-start(bf16[32,2304]{1,0:T(8,128)(2,1)S(1)} %get-tuple-element.83), channel_id=1, source_target_pairs={{0,12},{4,8},{8,4},{12,0},{1,13},{5,9},{9,5},{13,1},{2,14},{6,10},... | collective-permute-start | bytes 442376 | tf_op jit(solution)/shard_map/ppermute | solution.py:45
  27.2 48.7 %collective-permute-start.21 = (bf16[32,2304]{1,0:T(8,128)(2,1)S(1)}, bf16[32,2304]{1,0:T(8,128)(2,1)S(1)}, u32[]{:S(2)}, u32[]{:S(2)}) collective-permute-start(bf16[32,2304]{1,0:T(8,128)(2,1)S(1)} %get-tuple-element.49), channel_id=1, source_target_pairs={{0,8},{4,12},{8,0},{12,4},{1,9},{5,13},{9,1},{13,5},{2,10},{6,14},... | collective-permute-start | bytes 442376 | tf_op jit(solution)/shard_map/ppermute | solution.py:45
  27.6 48.3 %collective-permute-start.22 = (bf16[32,2304]{1,0:T(8,128)(2,1)S(1)}, bf16[32,2304]{1,0:T(8,128)(2,1)S(1)}, u32[]{:S(2)}, u32[]{:S(2)}) collective-permute-start(bf16[32,2304]{1,0:T(8,128)(2,1)S(1)} %get-tuple-element.82), channel_id=1, source_target_pairs={{0,4},{4,0},{8,12},{12,8},{1,5},{5,1},{9,13},{13,9},{2,6},{6,2},{1... | collective-permute-start | bytes 442376 | tf_op jit(solution)/shard_map/ppermute | solution.py:45
  72.3 8.0 %collective-permute-start = (bf16[512,1024]{1,0:T(8,128)(2,1)S(1)}, bf16[512,1024]{1,0:T(8,128)(2,1)S(1)}, u32[]{:S(2)}, u32[]{:S(2)}) collective-permute-start(bf16[512,1024]{1,0:T(8,128)(2,1)S(1)} %bitcast.151), channel_id=1, source_target_pairs={{0,4},{4,0},{1,5},{5,1},{2,6},{6,2},{3,7},{7,3},{8,12},{12,8},{9,1... | collective-permute-start | bytes 3145736 | tf_op jit(solution)/shard_map/ppermute | solution.py:33
  73.0 5.5 %collective-permute-start.10 = (bf16[512,1024]{1,0:T(8,128)(2,1)}, bf16[512,1024]{1,0:T(8,128)(2,1)}, u32[]{:S(2)}, u32[]{:S(2)}) collective-permute-start(bf16[512,1024]{1,0:T(8,128)(2,1)} %collective-permute-done.9.refs_6_), channel_id=1, source_target_pairs={{0,4},{4,0},{1,5},{5,1},{2,6},{6,2},{3,7},{7,3},{8,12},{12,8},{9,1... | collective-permute-start | bytes 3145736 | tf_op jit(solution)/shard_map/ppermute | solution.py:33
  73.0 7.4 %collective-permute-start.2 = (bf16[512,1024]{1,0:T(8,128)(2,1)}, bf16[512,1024]{1,0:T(8,128)(2,1)S(1)}, u32[]{:S(2)}, u32[]{:S(2)}) collective-permute-start(bf16[512,1024]{1,0:T(8,128)(2,1)} %collective-permute-done.1), channel_id=1, source_target_pairs={{0,4},{4,0},{1,5},{5,1},{2,6},{6,2},{3,7},{7,3},{8,12},{12,8},{9,1... | collective-permute-start | bytes 3145736 | tf_op jit(solution)/shard_map/ppermute | solution.py:33
  76.8 133.9 %all-gather.6.cloned.1.call-start = ((), (), s32[]{:S(2)}) async-start(), calls=%async_computation.3 | async-start | bytes 2654208 | tf_op jit(solution)/shard_map/all_gather | solution.py:271
  80.4 5.1 %copy-start.33 = (bf16[512,1024]{1,0:T(8,128)(2,1)}, bf16[512,1024]{1,0:T(8,128)(2,1)S(1)}, u32[]{:S(2)}) copy-start(bf16[512,1024]{1,0:T(8,128)(2,1)S(1)} %collective-permute-done) | copy-start | bytes 3145732
  80.4 5.1 %copy-start.34 = (bf16[512,1024]{1,0:T(8,128)(2,1)}, bf16[512,1024]{1,0:T(8,128)(2,1)S(1)}, u32[]{:S(2)}) copy-start(bf16[512,1024]{1,0:T(8,128)(2,1)S(1)} %collective-permute-done.2) | copy-start | bytes 3145732
  85.6 10.8 %copy-start.24 = (bf16[2,4,4,32,768]{4,3,2,1,0:T(8,128)(2,1)}, bf16[2,4,4,32,768]{4,3,2,1,0:T(8,128)(2,1)S(1)}, u32[]{:S(2)}) copy-start(bf16[2,4,4,32,768]{4,3,2,1,0:T(8,128)(2,1)S(1)} %copy.66) | copy-start | bytes 4718596
  89.0 12.3 %copy-start.21 = (bf16[8,32,1024]{2,1,0:T(8,128)(2,1)}, bf16[8,32,1024]{2,1,0:T(8,128)(2,1)S(1)}, u32[]{:S(2)}) copy-start(bf16[8,32,1024]{2,1,0:T(8,128)(2,1)S(1)} %pad_maximum_fusion.12) | copy-start | bytes 1572868
  103.0 4.2 collective-permute-start.14
  109.7 25.3 %collective-permute-start.15 = (bf16[512,1024]{1,0:T(8,128)(2,1)S(1)}, bf16[512,1024]{1,0:T(8,128)(2,1)}, u32[]{:S(2)}, u32[]{:S(2)}) collective-permute-start(bf16[512,1024]{1,0:T(8,128)(2,1)S(1)} %fusion.24), channel_id=1, source_target_pairs={{0,8},{8,0},{1,9},{9,1},{2,10},{10,2},{3,11},{11,3},{4,12},{12,4},... | collective-permute-start | bytes 3145736 | tf_op jit(solution)/shard_map/ppermute | solution.py:37
  138.2 24.5 %collective-permute-start.17 = (bf16[512,1024]{1,0:T(8,128)(2,1)S(1)}, bf16[512,1024]{1,0:T(8,128)(2,1)}, u32[]{:S(2)}, u32[]{:S(2)}) collective-permute-start(bf16[512,1024]{1,0:T(8,128)(2,1)S(1)} %multiply_convert_fusion.4.refs_0_), channel_id=1, source_target_pairs={{0,8},{8,0},{1,9},{9,1},{2,10},{10,2},{3,11},{11,3},{4,12},{12,4},... | collective-permute-start | bytes 3145736 | tf_op jit(solution)/shard_map/ppermute | solution.py:37
  139.9 175.9 %reduce-scatter.4.cloned.1.call-start = ((), (), s32[]{:S(2)}) async-start(), calls=%async_computation.4 | async-start | bytes 1474560 | tf_op jit(solution)/shard_map/reduce_scatter | solution.py:97
  140.5 27.0 %collective-permute-start.19 = (bf16[512,1024]{1,0:T(8,128)(2,1)}, bf16[512,1024]{1,0:T(8,128)(2,1)}, u32[]{:S(2)}, u32[]{:S(2)}) collective-permute-start(bf16[512,1024]{1,0:T(8,128)(2,1)} %fusion.8.refs_4_), channel_id=1, source_target_pairs={{0,4},{4,0},{1,5},{5,1},{2,6},{6,2},{3,7},{7,3},{8,12},{12,8},{9,1... | collective-permute-start | bytes 3145736 | tf_op jit(solution)/shard_map/ppermute | solution.py:33
  140.6 27.0 %collective-permute-start.16 = (bf16[512,1024]{1,0:T(8,128)(2,1)S(1)}, bf16[512,1024]{1,0:T(8,128)(2,1)}, u32[]{:S(2)}, u32[]{:S(2)}) collective-permute-start(bf16[512,1024]{1,0:T(8,128)(2,1)S(1)} %multiply_convert_fusion.4.refs_0_), channel_id=1, source_target_pairs={{0,4},{4,0},{1,5},{5,1},{2,6},{6,2},{3,7},{7,3},{8,12},{12,8},{9,1... | collective-permute-start | bytes 3145736 | tf_op jit(solution)/shard_map/ppermute | solution.py:33
  162.7 4.9 collective-permute-start.18
  242.0 4.5 collective-permute-start.23
  244.4 28.7 %collective-permute-start.29 = (bf16[4,144,1024]{2,1,0:T(8,128)(2,1)}, bf16[4,144,1024]{2,1,0:T(8,128)(2,1)}, u32[]{:S(2)}, u32[]{:S(2)}) collective-permute-start(bf16[4,144,1024]{2,1,0:T(8,128)(2,1)} %dynamic-slice_bitcast_fusion.2), channel_id=1, source_target_pairs={{0,16},{16,0},{1,17},{17,1},{2,18},{18,2},{3,19},{19,3},{4,20},{20... | collective-permute-start | bytes 3538952 | tf_op jit(solution)/shard_map/ppermute | solution.py:41
  246.5 8.9 %copy-start.42 = (bf16[2048,2304]{1,0:T(8,128)(2,1)S(1)}, bf16[2048,2304]{1,0:T(8,128)(2,1)}, u32[]{:S(2)}) copy-start(bf16[2048,2304]{1,0:T(8,128)(2,1)} %get-tuple-element.25) | copy-start | bytes 28311556
  253.9 25.4 %collective-permute-start.24 = (bf16[512,1024]{1,0:T(8,128)(2,1)}, bf16[512,1024]{1,0:T(8,128)(2,1)S(1)}, u32[]{:S(2)}, u32[]{:S(2)}) collective-permute-start(bf16[512,1024]{1,0:T(8,128)(2,1)} %fusion.21), channel_id=1, source_target_pairs={{0,8},{8,0},{1,9},{9,1},{2,10},{10,2},{3,11},{11,3},{4,12},{12,4},... | collective-permute-start | bytes 3145736 | tf_op jit(solution)/shard_map/ppermute | solution.py:37
  276.2 164.7 %reduce-scatter.6.cloned.1.call-start = ((), (), s32[]{:S(2)}) async-start(), calls=%async_computation.5 | async-start | bytes 2949120 | tf_op jit(solution)/shard_map/reduce_scatter | solution.py:97
  276.3 6.2 %copy-start.4 = (f32[1024,1024]{1,0:T(8,128)S(1)}, f32[1024,1024]{1,0:T(8,128)}, u32[]{:S(2)}) copy-start(f32[1024,1024]{1,0:T(8,128)} %copy-done.3) | copy-start | bytes 12582916
  276.3 6.2 %copy-start.19 = (bf16[2,256,1024]{2,1,0:T(8,128)(2,1)S(1)}, bf16[2,256,1024]{2,1,0:T(8,128)(2,1)}, u32[]{:S(2)}) copy-start(bf16[2,256,1024]{2,1,0:T(8,128)(2,1)} %param.13) | copy-start | bytes 3145732
  282.4 28.7 %copy-start.6 = (bf16[2,256,1024]{2,1,0:T(8,128)(2,1)S(1)}, bf16[2,256,1024]{2,1,0:T(8,128)(2,1)}, u32[]{:S(2)}) copy-start(bf16[2,256,1024]{2,1,0:T(8,128)(2,1)} %param.11) | copy-start | bytes 3145732
  286.6 24.5 %collective-permute-start.25 = (bf16[512,1024]{1,0:T(8,128)(2,1)}, bf16[512,1024]{1,0:T(8,128)(2,1)}, u32[]{:S(2)}, u32[]{:S(2)}) collective-permute-start(bf16[512,1024]{1,0:T(8,128)(2,1)} %get-tuple-element.47), channel_id=1, source_target_pairs={{0,8},{8,0},{1,9},{9,1},{2,10},{10,2},{3,11},{11,3},{4,12},{12,4},... | collective-permute-start | bytes 3145736 | tf_op jit(solution)/shard_map/ppermute | solution.py:37
  311.1 6.9 %collective-permute-start.26 = (bf16[512,1024]{1,0:T(8,128)(2,1)}, bf16[512,1024]{1,0:T(8,128)(2,1)}, u32[]{:S(2)}, u32[]{:S(2)}) collective-permute-start(bf16[512,1024]{1,0:T(8,128)(2,1)} %collective-permute-done.25), channel_id=1, source_target_pairs={{0,4},{4,0},{1,5},{5,1},{2,6},{6,2},{3,7},{7,3},{8,12},{12,8},{9,1... | collective-permute-start | bytes 3145736 | tf_op jit(solution)/shard_map/ppermute | solution.py:33
  315.0 54.0 %collective-permute-start.34 = (bf16[4,128,2304]{2,1,0:T(8,128)(2,1)}, bf16[4,128,2304]{2,1,0:T(8,128)(2,1)}, u32[]{:S(2)}, u32[]{:S(2)}) collective-permute-start(bf16[4,128,2304]{2,1,0:T(8,128)(2,1)} %dynamic-slice_bitcast_fusion), channel_id=1, source_target_pairs={{0,16},{16,0},{1,17},{17,1},{2,18},{18,2},{3,19},{19,3},{4,20},{20... | collective-permute-start | bytes 7077896 | tf_op jit(solution)/shard_map/ppermute | solution.py:41
  315.7 10.3 %collective-permute-start.30 = (bf16[512,1024]{1,0:T(8,128)(2,1)}, bf16[512,1024]{1,0:T(8,128)(2,1)}, u32[]{:S(2)}, u32[]{:S(2)}) collective-permute-start(bf16[512,1024]{1,0:T(8,128)(2,1)} %get-tuple-element.47), channel_id=1, source_target_pairs={{0,4},{4,0},{1,5},{5,1},{2,6},{6,2},{3,7},{7,3},{8,12},{12,8},{9,1... | collective-permute-start | bytes 3145736 | tf_op jit(solution)/shard_map/ppermute | solution.py:33
  319.9 6.1 %slice-start = ((s8[6291456]{0:T(1024)(128)(4,1)}), s8[4194304]{0:T(1024)(128)(4,1)S(1)}, s32[]{:S(2)}) async-start(s8[6291456]{0:T(1024)(128)(4,1)} %bitcast.148), calls=%async_computation.9 | async-start | bytes 8388608
  325.7 59.4 %collective-permute-start.27 = (bf16[1024,1024]{1,0:T(8,128)(2,1)}, bf16[1024,1024]{1,0:T(8,128)(2,1)}, u32[]{:S(2)}, u32[]{:S(2)}) collective-permute-start(bf16[1024,1024]{1,0:T(8,128)(2,1)} %pad_maximum_fusion.5), channel_id=1, source_target_pairs={{0,4},{4,0},{1,5},{5,1},{2,6},{6,2},{3,7},{7,3},{8,12},{12,8},{9,1... | collective-permute-start | bytes 6291464 | tf_op jit(solution)/shard_map/ppermute | solution.py:33
  344.7 47.4 %collective-permute-start.31 = (bf16[1024,1024]{1,0:T(8,128)(2,1)}, bf16[1024,1024]{1,0:T(8,128)(2,1)}, u32[]{:S(2)}, u32[]{:S(2)}) collective-permute-start(bf16[1024,1024]{1,0:T(8,128)(2,1)} %pad_maximum_fusion.6), channel_id=1, source_target_pairs={{0,4},{4,0},{1,5},{5,1},{2,6},{6,2},{3,7},{7,3},{8,12},{12,8},{9,1... | collective-permute-start | bytes 6291464 | tf_op jit(solution)/shard_map/ppermute | solution.py:33
  373.4 100.9 %reduce-scatter.8.cloned.1.call-start = ((), (), s32[]{:S(2)}) async-start(), calls=%async_computation.6 | async-start | bytes 1474560 | tf_op jit(solution)/shard_map/reduce_scatter | solution.py:97
  390.5 26.4 %collective-permute-start.28 = (bf16[512,1024]{1,0:T(8,128)(2,1)}, bf16[512,1024]{1,0:T(8,128)(2,1)}, u32[]{:S(2)}, u32[]{:S(2)}) collective-permute-start(bf16[512,1024]{1,0:T(8,128)(2,1)} %fusion.16), channel_id=1, source_target_pairs={{0,8},{8,0},{1,9},{9,1},{2,10},{10,2},{3,11},{11,3},{4,12},{12,4},... | collective-permute-start | bytes 3145736 | tf_op jit(solution)/shard_map/ppermute | solution.py:37
  397.5 40.7 %collective-permute-start.32 = (bf16[512,1024]{1,0:T(8,128)(2,1)}, bf16[512,1024]{1,0:T(8,128)(2,1)}, u32[]{:S(2)}, u32[]{:S(2)}) collective-permute-start(bf16[512,1024]{1,0:T(8,128)(2,1)} %fusion.13), channel_id=1, source_target_pairs={{0,8},{8,0},{1,9},{9,1},{2,10},{10,2},{3,11},{11,3},{4,12},{12,4},... | collective-permute-start | bytes 3145736 | tf_op jit(solution)/shard_map/ppermute | solution.py:37
  400.5 42.4 %collective-permute-start.33 = (bf16[4,144,1024]{2,1,0:T(8,128)(2,1)}, bf16[4,144,1024]{2,1,0:T(8,128)(2,1)}, u32[]{:S(2)}, u32[]{:S(2)}) collective-permute-start(bf16[4,144,1024]{2,1,0:T(8,128)(2,1)} %dynamic-slice_bitcast_fusion.1), channel_id=1, source_target_pairs={{0,16},{16,0},{1,17},{17,1},{2,18},{18,2},{3,19},{19,3},{4,20},{20... | collective-permute-start | bytes 3538952 | tf_op jit(solution)/shard_map/ppermute | solution.py:41
  442.8 6.5 %copy-start.14 = (f32[512,1024]{1,0:T(8,128)S(1)}, f32[512,1024]{1,0:T(8,128)}, u32[]{:S(2)}) copy-start(f32[512,1024]{1,0:T(8,128)} %get-tuple-element.48) | copy-start | bytes 6291460
  447.4 6.2 %collective-permute-start.38 = (bf16[32,2304]{1,0:T(8,128)(2,1)S(1)}, bf16[32,2304]{1,0:T(8,128)(2,1)S(1)}, u32[]{:S(2)}, u32[]{:S(2)}) collective-permute-start(bf16[32,2304]{1,0:T(8,128)(2,1)S(1)} %get-tuple-element.78), channel_id=1, source_target_pairs={{0,12},{4,8},{8,4},{12,0},{1,13},{5,9},{9,5},{13,1},{2,14},{6,10},... | collective-permute-start | bytes 442376 | tf_op jit(solution)/shard_map/ppermute | solution.py:45
  447.5 9.3 %collective-permute-start.39 = (bf16[32,2304]{1,0:T(8,128)(2,1)S(1)}, bf16[32,2304]{1,0:T(8,128)(2,1)S(1)}, u32[]{:S(2)}, u32[]{:S(2)}) collective-permute-start(bf16[32,2304]{1,0:T(8,128)(2,1)S(1)} %get-tuple-element.79), channel_id=1, source_target_pairs={{0,8},{4,12},{8,0},{12,4},{1,9},{5,13},{9,1},{13,5},{2,10},{6,14},... | collective-permute-start | bytes 442376 | tf_op jit(solution)/shard_map/ppermute | solution.py:45
  449.0 7.8 %collective-permute-start.40 = (bf16[32,2304]{1,0:T(8,128)(2,1)S(1)}, bf16[32,2304]{1,0:T(8,128)(2,1)S(1)}, u32[]{:S(2)}, u32[]{:S(2)}) collective-permute-start(bf16[32,2304]{1,0:T(8,128)(2,1)S(1)} %get-tuple-element.77), channel_id=1, source_target_pairs={{0,4},{4,0},{8,12},{12,8},{1,5},{5,1},{9,13},{13,9},{2,6},{6,2},{1... | collective-permute-start | bytes 442376 | tf_op jit(solution)/shard_map/ppermute | solution.py:45
  461.1 20.8 %copy-start.36 = (bf16[32,3072]{1,0:T(8,128)(2,1)S(1)}, bf16[32,3072]{1,0:T(8,128)(2,1)}, u32[]{:S(2)}) copy-start(bf16[32,3072]{1,0:T(8,128)(2,1)} %param.15) | copy-start | bytes 589828
  474.3 7.8 %copy-start.40 = (bf16[32]{0:T(256)(128)(2,1)S(1)}, bf16[32]{0:T(256)(128)(2,1)}, u32[]{:S(2)}) copy-start(bf16[32]{0:T(256)(128)(2,1)} %param.14) | copy-start | bytes 196
  476.0 4.0 collective-permute-start.35
  476.7 4.5 collective-permute-start.36
  477.5 3.7 collective-permute-start.37
  (28 other events, 80.2 us)
Sparse Core Ops, SparseCore 0:
  19.7 52.3 all-gather.7
  76.9 81.3 all-gather.9
  160.4 50.2 all-gather.5
  276.3 27.7 reduce-scatter.3
  373.6 46.7 reduce-scatter.5
  446.3 27.9 reduce-scatter.7

commit v8 on v7

--- a/solution.py
+++ b/solution.py
@@ -96,6 +96,14 @@
         summed = (take(part, row).astype(f32) + came).astype(bf16)
         return lax.psum_scatter(summed, "s", scatter_dimension=0, tiled=False)
     flat = part.reshape((groups * slots,) + part.shape[2:]).astype(f32)
+    return lax.psum_scatter(flat, ("g", "y", "s"), scatter_dimension=0, tiled=False)
+
+
+def scatter_plain(part):
+    groups, slots = part.shape[:2]
+    flat = part.reshape((groups * slots,) + part.shape[2:])
+    if groups > 2:
+        flat = flat.astype(f32)
     return lax.psum_scatter(flat, ("g", "y", "s"), scatter_dimension=0, tiled=False)
 
 
@@ -321,7 +329,6 @@
         team_count * hid,
     )
     down_part = rows_dot(hidden, ffn_grad).astype(bf16)
-    grad_down = scatter(down_part.reshape(groups, slots, hidden_share, features))
     pair_grad, normed_part, out_part = by_rows(
         backward_kernel,
         ROW_TILE,
@@ -349,11 +356,10 @@
     mixer_in_grad = back_dot(mixer_grad, out_full)
     c_grad = mixer_in_grad * convolved
     conv_grad = mixer_in_grad * c_part
-    conv_back = after(conv_full, grad_down[:1])
     mixed_grad = (
-        conv_back[0] * conv_grad
-        + conv_back[1] * shifted_up(mask_one * conv_grad, 1)
-        + conv_back[2] * shifted_up(mask_two * conv_grad, 2)
+        conv_full[0] * conv_grad
+        + conv_full[1] * shifted_up(mask_one * conv_grad, 1)
+        + conv_full[2] * shifted_up(mask_two * conv_grad, 2)
     )
     projected_grad = jnp.concatenate(
         [mixed_grad * x_part, c_grad, mixed_grad * b_part], axis=1
@@ -375,7 +381,10 @@
         conv_rows.astype(bf16),
         ((0, 0), (0, 0), (0, EXTRA_ROWS - 1), (0, features - taps * share)),
     )
-    pair_sum = scatter(pair_part, projected_grad[-1:])
+    pair_sum = scatter_plain(pair_part)
+    grad_down = scatter(
+        down_part.reshape(groups, slots, hidden_share, features), pair_sum[:1]
+    )
     first_weighted, first_sent = team_sum(back_dot(projected_grad, in_full).astype(bf16))
     input_grad = middle_grad + norm_back(inputs, inverse_rms(inputs), norm_full * first_weighted)
     input_grad = input_grad.astype(bf16)
@@ -387,7 +396,6 @@
         ),
         pair_sum[:1],
         first_sent,
-        block_out[:1],
     )
 
     def own_rows(summed, parts, team, run):

time: 495 us -> 495 us (level)
  waiting for transfers between devices: 213 us -> 232 us
  local copies, waits for them, and re-layouts: 51.6 us -> 42 us
  other arithmetic: 77.9 us -> 69 us
    reduce_scatter x0 -> x1, waiting for transfers between devices: none -> 51.3 us  [scatter_plain(): lax.psum_scatter(flat, ('g', 'y', 's'), scatter_dimension=0, tiled=False)]
    ppermute x10, waiting for transfers between devices: 101 us -> 78.5 us  [swap_chip(): return lax.ppermute(values, 'x', [(0, 1), (1, 0)])]
    ppermute x3 -> x2, waiting for transfers between devices: 24.5 us -> 13.8 us  [swap_row(): return lax.ppermute(values, 'y', [(0, 1), (1, 0)])]
    convert_element_type x3 -> x2, other arithmetic: 10.9 us -> 4.77 us  [scatter(): summed = (take(part, row).astype(f32) + came).astype(bf16)]
    ppermute x16, waiting for transfers between devices: 7.72 us -> 13.1 us  [swap_core(): return lax.ppermute(values, 'c', [(0, 1), (1, 0)])]
    unnamed x94 -> x96, local copies, waits for them, and re-layouts: 15.8 us -> 10.6 us
    transpose x0 -> x1, local copies, waits for them, and re-layouts: none -> 4.96 us  [per_device(): jnp.transpose(pair_all.reshape(groups, slots, TEAM, share, 2 * hid), (0,...]
    reduce_scatter x3 -> x2, waiting for transfers between devices: 12.7 us -> 10.8 us  [scatter(): return lax.psum_scatter(summed, 's', scatter_dimension=0, tiled=False)]
  transfers between devices with their start and end apart: 47 -> 46, of which waited for: 20 -> 17; matrix products, arithmetic and copies ran while one was open for 31% -> 28% of each run, Pallas kernels for 4% -> 4%
where the time goes in v8:
time: 495 us; the launch traced here: 490 us
  waiting for transfers between devices  232 us (47%)
  other arithmetic  69 us (14%)
  matrix products  53.2 us (11%)
  Pallas kernels  45.8 us (9%)
  local copies, waits for them, and re-layouts  42 us (8%)
  starting transfers between devices  29.3 us (6%)
  between operations  18.9 us (4%)
    ppermute x10, waiting for transfers between devices, swap_chip(): return lax.ppermute(values, 'x', [(0, 1), (1, 0)])  78.5 us
    reduce_scatter x1, waiting for transfers between devices, scatter_plain(): lax.psum_scatter(flat, ('g', 'y', 's'), scatter_dimension=0, tiled=False)  51.3 us
    ppermute x12, waiting for transfers between devices, swap_far(): lax.ppermute(values, ('x', 'c'), [(i, i ^ distance) for i in range(TEAM)])  50 us
    pallas_call x2, Pallas kernels, by_rows(): pl.pallas_call(kernel, grid=(steps,), in_specs=[row_block(value.shape[1])...  45.8 us
    dot_general x4, matrix products, rows_dot(): lax.dot_general(left_side, right_side, (((0,), (0,)), ((), ())), preferre...  29.1 us
    dot_general x2, matrix products, back_dot(): lax.dot_general(left_side, right_side, (((1,), (1,)), ((), ())), preferre...  15.5 us
    all_gather x1, waiting for transfers between devices, per_device(): down_full = lax.all_gather(down_weight, ('g', 'y', 's'), axis=0, tiled=True)  14.6 us
    ppermute x10, starting transfers between devices, swap_chip(): return lax.ppermute(values, 'x', [(0, 1), (1, 0)])  14.5 us
  transfers between devices with their start and end apart: 46, of which 17 were waited for; matrix products, arithmetic and copies ran while one was open for 28% of the time, Pallas kernels for 4%

profile of v8, /device:TPU:0, one launch (start us, length us, event | category | flops | bytes accessed | tf_op | source)
XLA Modules:
  0.0 490.4 jit_solution(3244673633015694932)
XLA Ops:
  8.1 2.9 collective-permute-start.6
  12.8 2.0 collective-permute-start.4
  21.3 1.7 collective-permute-start.9
  25.3 1.8 collective-permute-start.20
  27.5 44.8 %collective-permute-done.20 = bf16[32,2304]{1,0:T(8,128)(2,1)S(1)} collective-permute-done((bf16[32,2304]{1,0:T(8,128)(2,1)S(1)}, bf16[32,2304]{1,0:T(8,128)(2,1)S(1)}, u32[]{:S(2)}, u32[]{:S(2)}) %collective-permute-start.20) | collective-permute-done | bytes 147488 | tf_op jit(solution)/shard_map/ppermute | solution.py:45
  73.5 2.3 collective-permute-done.21
  80.3 3.5 fusion
  83.9 1.5 slice.369
  90.2 7.4 %fusion.27 = f32[2048,768]{1,0:T(8,128)S(1)} fusion(bf16[1024,768]{1,0:T(8,128)(2,1)S(1)} %bitcast.164, f32[1024]{0:T(1024)S(1)} %mul.313, f32[2048]{0:T(1024)S(1)} %add_rsqrt_fusion, bf16[512,1024]{1,0:T(8,128)(2,1)} %copy-done.36, bf16[512,1024]{1,0:T(8,128)(2,1)} %collective-permute-done.1, bf16[512,1024]{1,0:T(8,128)(2,1)} %copy-done.34, ...), kind=kOutput, calls=%fused_computation.78 | convolution fusion | flops 3244294144 | bytes 12070912 | tf_op jit(solution)/shard_map/dot_general | solution.py:17
  97.9 2.3 copy-done
  100.2 2.3 multiply_convert_fusion.5
  104.4 4.0 collective-permute-done.14
  109.3 1.6 copy-done.10
  110.9 1.6 collective-permute-start.15
  112.6 23.6 %collective-permute-done.15 = bf16[512,1024]{1,0:T(8,128)(2,1)} collective-permute-done((bf16[512,1024]{1,0:T(8,128)(2,1)S(1)}, bf16[512,1024]{1,0:T(8,128)(2,1)}, u32[]{:S(2)}, u32[]{:S(2)}) %collective-permute-start.15) | collective-permute-done | bytes 1048608 | tf_op jit(solution)/shard_map/ppermute | solution.py:37
  136.2 2.9 multiply_reduce_fusion.5
  139.4 1.7 collective-permute-start.17
  142.2 21.7 %collective-permute-done.17.refs_2_ = bf16[512,1024]{1,0:T(8,128)(2,1)} collective-permute-done((bf16[512,1024]{1,0:T(8,128)(2,1)S(1)}, bf16[512,1024]{1,0:T(8,128)(2,1)}, u32[]{:S(2)}, u32[]{:S(2)}) %collective-permute-start.17) | collective-permute-done | bytes 1048608 | tf_op jit(solution)/shard_map/ppermute | solution.py:37
  163.9 5.0 %copy.68 = bf16[2,4,4,32,2304]{4,3,2,1,0:T(8,128)(2,1)} copy(bf16[2,4,4,32,2304]{4,3,1,2,0:T(8,128)(2,1)} %bitcast.151) | data formatting | bytes 9437184 | tf_op jit(solution)/shard_map/transpose | solution.py:286
  168.9 17.7 %shard_map.186 = (bf16[2048,1152]{1,0:T(8,128)(2,1)}, bf16[2048,1152]{1,0:T(8,128)(2,1)}, bf16[2048,1152]{1,0:T(8,128)(2,1)}, bf16[2048,1024]{1,0:T(8,128)(2,1)}, bf16[2048,1024]{1,0:T(8,128)(2,1)}) custom-call(bf16[512,1024]{1,0:T(8,128)(2,1)S(1)} %multiply_convert_fusion.4.refs_0_, bf16[512,1024]{1,0:T(8,128)(2,1)} %collective-permute-done.16.refs_1_, ...), custom_call_target="tpu_custom_call" | custom-call | flops 9663676416 | bytes 35651584 | tf_op jit(solution)/shard_map/pallas_call | solution.py:158
  186.6 9.4 %convolution_convert_fusion.1.token_ref = bf16[1152,1024]{1,0:T(8,128)(2,1)} fusion(bf16[2048,1152]{1,0:T(8,128)(2,1)} %get-tuple-element.19.hidden_ref, bf16[2048,1024]{1,0:T(8,128)(2,1)} %get-tuple-element.18.grad_ref), kind=kOutput, calls=%fused_computation.10 | convolution fusion | flops 4833017856 | bytes 11272192 | tf_op jit(solution)/shard_map/dot_general | solution.py:21
  196.0 14.6 %all-gather.6.cloned.1.call-done.down_ref = bf16[1152,1024]{1,0:T(8,128)(2,1)} async-done(((bf16[144,1024]{1,0:T(8,128)(2,1)}), bf16[1152,1024]{1,0:T(8,128)(2,1)}) %all-gather.6.cloned.1.call-update) | async-done | bytes 2359312 | tf_op jit(solution)/shard_map/all_gather | solution.py:279
  210.6 28.1 %shard_map.187 = (bf16[2048,2304]{1,0:T(8,128)(2,1)}, bf16[2048,1024]{1,0:T(8,128)(2,1)}, bf16[2048,1024]{1,0:T(8,128)(2,1)}) custom-call(bf16[2048,1024]{1,0:T(8,128)(2,1)} %get-tuple-element.18.grad_ref, bf16[2048,1152]{1,0:T(8,128)(2,1)} %get-tuple-element.19.hidden_ref, bf16[2048,1152]{1,0:T(8,128)(2,1)} %get-tuple-element.20.silu_ref, ...), custom_call_target="tpu_custom_call" | custom-call | flops 19327352832 | bytes 43253760 | tf_op jit(solution)/shard_map/pallas_call | solution.py:158
  238.7 1.7 fusion.46
  240.7 4.1 collective-permute-done.23
  245.3 4.1 fusion.20
  249.4 1.5 collective-permute-start.24
  250.9 11.1 %convolution_convert_fusion = bf16[1024,2304]{1,0:T(8,128)(2,1)S(1)} fusion(bf16[2048,1024]{1,0:T(8,128)(2,1)S(1)} %copy-done.45, bf16[2048,2304]{1,0:T(8,128)(2,1)S(1)} %copy-done.44), kind=kOutput, calls=%fused_computation.5 | convolution fusion | flops 9666035712 | bytes 18350080 | tf_op jit(solution)/shard_map/dot_general | solution.py:21
  262.4 2.2 copy-done.8
  265.8 9.1 %collective-permute-done.24 = bf16[512,1024]{1,0:T(8,128)(2,1)S(1)} collective-permute-done((bf16[512,1024]{1,0:T(8,128)(2,1)}, bf16[512,1024]{1,0:T(8,128)(2,1)S(1)}, u32[]{:S(2)}, u32[]{:S(2)}) %collective-permute-start.24) | collective-permute-done | bytes 1048608 | tf_op jit(solution)/shard_map/ppermute | solution.py:37
  274.8 2.5 multiply_reduce_fusion.4
  277.3 3.8 multiply_convert_fusion.3
  281.1 1.5 collective-permute-start.25
  282.6 23.2 %collective-permute-done.25 = bf16[512,1024]{1,0:T(8,128)(2,1)} collective-permute-done((bf16[512,1024]{1,0:T(8,128)(2,1)}, bf16[512,1024]{1,0:T(8,128)(2,1)}, u32[]{:S(2)}, u32[]{:S(2)}) %collective-permute-start.25) | collective-permute-done | bytes 1048608 | tf_op jit(solution)/shard_map/ppermute | solution.py:37
  306.0 2.8 collective-permute-done.26
  308.8 9.5 %multiply_reduce_fusion.2 = (bf16[256]{0:T(256)(128)(2,1)S(1)}, bf16[256]{0:T(256)(128)(2,1)S(1)}, bf16[256]{0:T(256)(128)(2,1)S(1)}, f32[2048,256]{1,0:T(8,128)S(1)}, bf16[2048,256]{1,0:T(8,128)(2,1)S(1)}) fusion(f32[2048,256]{1,0:T(8,128)} %copy-done.9, f32[2046,256]{1,0:T(8,128)} %bitcast.147, f32[2048]{0:T(1024)S(1)} %get-tuple-element.114, ...), kind=kOutput, calls=%fused_computation.59 | convolution fusion | flops 1096285440 | bytes 18364928 | tf_op jit(solution)/shard_map/dot_general | solution.py:27
  319.0 2.5 multiply_convert_fusion.2
  321.6 2.3 multiply_convert_fusion
  324.5 5.0 %convolution_convert_fusion.4 = bf16[1024,768]{1,0:T(8,128)(2,1)S(1)} fusion(bf16[2048,256]{1,0:T(8,128)(2,1)S(1)} %multiply_convert_fusion, bf16[2048,256]{1,0:T(8,128)(2,1)S(1)} %get-tuple-element.65, bf16[2048,256]{1,0:T(8,128)(2,1)S(1)} %get-tuple-element.42, f32[1024]{0:T(1024)S(1)} %mul.313, f32[2048]{0:T(1024)S(1)} %add_rsqrt_fusion, ...), kind=kOutput, calls=%fused_computation.76 | convolution fusion | flops 3254517760 | bytes 8925184 | tf_op jit(solution)/shard_map/dot_general | solution.py:21
  331.2 6.0 %convolution_convert_fusion.3 = bf16[2048,1024]{1,0:T(8,128)(2,1)S(1)} fusion(bf16[1024,768]{1,0:T(8,128)(2,1)} %bitcast.163, bf16[2048,256]{1,0:T(8,128)(2,1)} %copy-done.33, bf16[2048,256]{1,0:T(8,128)(2,1)} %copy-done.43, bf16[2048,256]{1,0:T(8,128)(2,1)} %copy-done.32), kind=kOutput, calls=%fused_computation.12 | convolution fusion | flops 3232759808 | bytes 8912896 | tf_op jit(solution)/shard_map/dot_general | solution.py:27
  337.3 1.8 copy-done.17
  339.2 1.5 pad_maximum_fusion.6
  340.8 3.6 convolution_convert_fusion.5
  346.7 1.4 slice.397
  349.3 1.9 copy-done.11
  351.2 1.5 pad_maximum_fusion.5
  353.1 2.1 convert_element_type.315
  355.2 3.4 fusion.12
  359.7 1.5 collective-permute-start.31
  361.8 51.3 %reduce-scatter.4.cloned.1.call-done = bf16[1,128,2304]{2,1,0:T(8,128)(2,1)} async-done(((bf16[8,128,2304]{2,1,0:T(8,128)(2,1)}), bf16[1,128,2304]{2,1,0:T(8,128)(2,1)}) %reduce-scatter.4.cloned.1.call-update) | async-done | bytes 589840 | tf_op jit(solution)/shard_map/reduce_scatter | solution.py:107
  414.9 3.2 fusion.6
  420.0 1.5 collective-permute-start.39
  421.5 2.2 convert_element_type.307
  423.7 3.6 fusion.15
  427.3 1.5 collective-permute-start.28
  428.8 1.9 fusion.8
  430.7 3.2 fusion.11
  433.9 13.8 %collective-permute-done.39 = bf16[4,144,1024]{2,1,0:T(8,128)(2,1)S(1)} collective-permute-done((bf16[4,144,1024]{2,1,0:T(8,128)(2,1)S(1)}, bf16[4,144,1024]{2,1,0:T(8,128)(2,1)S(1)}, u32[]{:S(2)}, u32[]{:S(2)}) %collective-permute-start.39) | collective-permute-done | bytes 1179680 | tf_op jit(solution)/shard_map/ppermute | solution.py:41
  447.7 1.6 fusion.5
  449.5 1.4 collective-permute-start.37
  452.2 3.6 fusion.19
  455.8 2.9 collective-permute-done.37
  467.9 10.8 %reduce-scatter.8.cloned.1.call-done = bf16[1,144,1024]{2,1,0:T(8,128)(2,1)} async-done(((bf16[4,144,1024]{2,1,0:T(8,128)(2,1)}), bf16[1,144,1024]{2,1,0:T(8,128)(2,1)}) %reduce-scatter.8.cloned.1.call-update) | async-done | bytes 294928 | tf_op jit(solution)/shard_map/reduce_scatter | solution.py:97
  478.6 1.8 bitcast_convert_fusion
  (280 shorter events, 51.4 us)
Async XLA Ops:
  7.2 12.4 %copy-start.40 = (s32[2,256]{1,0:T(2,128)S(1)}, s32[2,256]{1,0:T(2,128)}, u32[]{:S(2)}) copy-start(s32[2,256]{1,0:T(2,128)} %param.12) | copy-start | bytes 6148
  7.2 12.9 %copy-start.20 = (bf16[2,256,1024]{2,1,0:T(8,128)(2,1)S(1)}, bf16[2,256,1024]{2,1,0:T(8,128)(2,1)}, u32[]{:S(2)}) copy-start(bf16[2,256,1024]{2,1,0:T(8,128)(2,1)} %param.13) | copy-start | bytes 3145732
  7.2 76.7 %all-gather.8.cloned.1.call-start = ((), (), s32[]{:S(2)}) async-start(), calls=%async_computation.7 | async-start | bytes 2654208 | tf_op jit(solution)/shard_map/all_gather | solution.py:273
  8.1 8.4 %collective-permute-start.6 = (bf16[1,64]{1,0:T(2,128)(2,1)S(1)}, bf16[1,64]{1,0:T(2,128)(2,1)S(1)}, u32[]{:S(2)}, u32[]{:S(2)}) collective-permute-start(bf16[1,64]{1,0:T(2,128)(2,1)S(1)} %maximum_bitcast_fusion.1), channel_id=1, source_target_pairs={{0,8},{8,0},{1,9},{9,1},{2,10},{10,2},{3,11},{11,3},{4,12},{12,4},... | collective-permute-start | bytes 392 | tf_op jit(solution)/shard_map/ppermute | solution.py:37
  11.0 6.0 %collective-permute-start.8 = (bf16[1,64]{1,0:T(2,128)(2,1)S(1)}, bf16[1,64]{1,0:T(2,128)(2,1)S(1)}, u32[]{:S(2)}, u32[]{:S(2)}) collective-permute-start(bf16[1,64]{1,0:T(2,128)(2,1)S(1)} %maximum_bitcast_fusion.1), channel_id=1, source_target_pairs={{0,4},{4,0},{1,5},{5,1},{2,6},{6,2},{3,7},{7,3},{8,12},{12,8},{9,1... | collective-permute-start | bytes 392 | tf_op jit(solution)/shard_map/ppermute | solution.py:33
  12.2 10.7 %copy-start.6 = (bf16[2,256,1024]{2,1,0:T(8,128)(2,1)S(1)}, bf16[2,256,1024]{2,1,0:T(8,128)(2,1)}, u32[]{:S(2)}) copy-start(bf16[2,256,1024]{2,1,0:T(8,128)(2,1)} %param.11) | copy-start | bytes 3145732
  12.2 11.1 %copy-start.28 = (bf16[32,4608]{1,0:T(8,128)(2,1)S(1)}, bf16[32,4608]{1,0:T(8,128)(2,1)}, u32[]{:S(2)}) copy-start(bf16[32,4608]{1,0:T(8,128)(2,1)} %param.19) | copy-start | bytes 884740
  12.5 6.1 %collective-permute-start.3 = (bf16[32,768]{1,0:T(8,128)(2,1)S(1)}, bf16[32,768]{1,0:T(8,128)(2,1)S(1)}, u32[]{:S(2)}, u32[]{:S(2)}) collective-permute-start(bf16[32,768]{1,0:T(8,128)(2,1)S(1)} %select_n.378), channel_id=1, source_target_pairs={{0,12},{4,8},{8,4},{12,0},{1,13},{5,9},{9,5},{13,1},{2,14},{6,10},... | collective-permute-start | bytes 147464 | tf_op jit(solution)/shard_map/ppermute | solution.py:45
  12.8 5.9 %collective-permute-start.4 = (bf16[32,768]{1,0:T(8,128)(2,1)S(1)}, bf16[32,768]{1,0:T(8,128)(2,1)S(1)}, u32[]{:S(2)}, u32[]{:S(2)}) collective-permute-start(bf16[32,768]{1,0:T(8,128)(2,1)S(1)} %select_n.382), channel_id=1, source_target_pairs={{0,8},{4,12},{8,0},{12,4},{1,9},{5,13},{9,1},{13,5},{2,10},{6,14},... | collective-permute-start | bytes 147464 | tf_op jit(solution)/shard_map/ppermute | solution.py:45
  14.8 3.8 collective-permute-start.5
  16.5 1.3 collective-permute-start.7
  19.5 4.7 copy-start.30
  19.5 144.4 %all-gather.10.cloned.1.call-start = ((), (), s32[]{:S(2)}) async-start(), calls=%async_computation.8 | async-start | bytes 5308416 | tf_op jit(solution)/shard_map/all_gather | solution.py:278
  19.6 5.5 %collective-permute-start.12 = (s32[512,1]{0,1:T(1,128)S(1)}, s32[512,1]{0,1:T(1,128)S(1)}, u32[]{:S(2)}, u32[]{:S(2)}) collective-permute-start(s32[512,1]{0,1:T(1,128)S(1)} %bitcast.186), channel_id=1, source_target_pairs={{0,8},{8,0},{1,9},{9,1},{2,10},{10,2},{3,11},{11,3},{4,12},{12,4},... | collective-permute-start | bytes 6152 | tf_op jit(solution)/shard_map/ppermute | solution.py:37
  19.9 7.2 %collective-permute-start.11 = (s32[512,1]{0,1:T(1,128)S(1)}, s32[512,1]{0,1:T(1,128)S(1)}, u32[]{:S(2)}, u32[]{:S(2)}) collective-permute-start(s32[512,1]{0,1:T(1,128)S(1)} %bitcast.187), channel_id=1, source_target_pairs={{0,4},{4,0},{1,5},{5,1},{2,6},{6,2},{3,7},{7,3},{8,12},{12,8},{9,1... | collective-permute-start | bytes 6152 | tf_op jit(solution)/shard_map/ppermute | solution.py:33
  21.3 51.7 %collective-permute-start.9 = (bf16[512,1024]{1,0:T(8,128)(2,1)}, bf16[512,1024]{1,0:T(8,128)(2,1)}, u32[]{:S(2)}, u32[]{:S(2)}) collective-permute-start(bf16[512,1024]{1,0:T(8,128)(2,1)} %fusion.7.refs_4_), channel_id=1, source_target_pairs={{0,8},{8,0},{1,9},{9,1},{2,10},{10,2},{3,11},{11,3},{4,12},{12,4},... | collective-permute-start | bytes 3145736 | tf_op jit(solution)/shard_map/ppermute | solution.py:37
  23.0 50.0 %collective-permute-start.1 = (bf16[512,1024]{1,0:T(8,128)(2,1)S(1)}, bf16[512,1024]{1,0:T(8,128)(2,1)}, u32[]{:S(2)}, u32[]{:S(2)}) collective-permute-start(bf16[512,1024]{1,0:T(8,128)(2,1)S(1)} %bitcast.138), channel_id=1, source_target_pairs={{0,8},{8,0},{1,9},{9,1},{2,10},{10,2},{3,11},{11,3},{4,12},{12,4},... | collective-permute-start | bytes 3145736 | tf_op jit(solution)/shard_map/ppermute | solution.py:37
  25.2 2.3 collective-permute-start.13
  25.3 47.0 %collective-permute-start.20 = (bf16[32,2304]{1,0:T(8,128)(2,1)S(1)}, bf16[32,2304]{1,0:T(8,128)(2,1)S(1)}, u32[]{:S(2)}, u32[]{:S(2)}) collective-permute-start(bf16[32,2304]{1,0:T(8,128)(2,1)S(1)} %get-tuple-element.80), channel_id=1, source_target_pairs={{0,12},{4,8},{8,4},{12,0},{1,13},{5,9},{9,5},{13,1},{2,14},{6,10},... | collective-permute-start | bytes 442376 | tf_op jit(solution)/shard_map/ppermute | solution.py:45
  27.1 48.7 %collective-permute-start.21 = (bf16[32,2304]{1,0:T(8,128)(2,1)S(1)}, bf16[32,2304]{1,0:T(8,128)(2,1)S(1)}, u32[]{:S(2)}, u32[]{:S(2)}) collective-permute-start(bf16[32,2304]{1,0:T(8,128)(2,1)S(1)} %get-tuple-element.46), channel_id=1, source_target_pairs={{0,8},{4,12},{8,0},{12,4},{1,9},{5,13},{9,1},{13,5},{2,10},{6,14},... | collective-permute-start | bytes 442376 | tf_op jit(solution)/shard_map/ppermute | solution.py:45
  27.5 48.3 %collective-permute-start.22 = (bf16[32,2304]{1,0:T(8,128)(2,1)S(1)}, bf16[32,2304]{1,0:T(8,128)(2,1)S(1)}, u32[]{:S(2)}, u32[]{:S(2)}) collective-permute-start(bf16[32,2304]{1,0:T(8,128)(2,1)S(1)} %get-tuple-element.79), channel_id=1, source_target_pairs={{0,4},{4,0},{8,12},{12,8},{1,5},{5,1},{9,13},{13,9},{2,6},{6,2},{1... | collective-permute-start | bytes 442376 | tf_op jit(solution)/shard_map/ppermute | solution.py:45
  72.3 8.0 %collective-permute-start = (bf16[512,1024]{1,0:T(8,128)(2,1)S(1)}, bf16[512,1024]{1,0:T(8,128)(2,1)S(1)}, u32[]{:S(2)}, u32[]{:S(2)}) collective-permute-start(bf16[512,1024]{1,0:T(8,128)(2,1)S(1)} %bitcast.139), channel_id=1, source_target_pairs={{0,4},{4,0},{1,5},{5,1},{2,6},{6,2},{3,7},{7,3},{8,12},{12,8},{9,1... | collective-permute-start | bytes 3145736 | tf_op jit(solution)/shard_map/ppermute | solution.py:33
  72.9 5.5 %collective-permute-start.10 = (bf16[512,1024]{1,0:T(8,128)(2,1)}, bf16[512,1024]{1,0:T(8,128)(2,1)}, u32[]{:S(2)}, u32[]{:S(2)}) collective-permute-start(bf16[512,1024]{1,0:T(8,128)(2,1)} %collective-permute-done.9.refs_6_), channel_id=1, source_target_pairs={{0,4},{4,0},{1,5},{5,1},{2,6},{6,2},{3,7},{7,3},{8,12},{12,8},{9,1... | collective-permute-start | bytes 3145736 | tf_op jit(solution)/shard_map/ppermute | solution.py:33
  73.0 7.4 %collective-permute-start.2 = (bf16[512,1024]{1,0:T(8,128)(2,1)}, bf16[512,1024]{1,0:T(8,128)(2,1)S(1)}, u32[]{:S(2)}, u32[]{:S(2)}) collective-permute-start(bf16[512,1024]{1,0:T(8,128)(2,1)} %collective-permute-done.1), channel_id=1, source_target_pairs={{0,4},{4,0},{1,5},{5,1},{2,6},{6,2},{3,7},{7,3},{8,12},{12,8},{9,1... | collective-permute-start | bytes 3145736 | tf_op jit(solution)/shard_map/ppermute | solution.py:33
  76.7 133.9 %all-gather.6.cloned.1.call-start = ((), (), s32[]{:S(2)}) async-start(), calls=%async_computation.3 | async-start | bytes 2654208 | tf_op jit(solution)/shard_map/all_gather | solution.py:279
  90.2 12.3 %copy-start.24 = (bf16[8,32,1024]{2,1,0:T(8,128)(2,1)}, bf16[8,32,1024]{2,1,0:T(8,128)(2,1)S(1)}, u32[]{:S(2)}) copy-start(bf16[8,32,1024]{2,1,0:T(8,128)(2,1)S(1)} %pad_maximum_fusion.12) | copy-start | bytes 1572868
  103.8 5.1 %copy-start.1 = (bf16[2048,1024]{1,0:T(8,128)(2,1)}, bf16[2048,1024]{1,0:T(8,128)(2,1)S(1)}, u32[]{:S(2)}) copy-start(bf16[2048,1024]{1,0:T(8,128)(2,1)S(1)} %convolution_convert_fusion.2) | copy-start | bytes 12582916
  104.2 4.2 collective-permute-start.14
  110.9 25.3 %collective-permute-start.15 = (bf16[512,1024]{1,0:T(8,128)(2,1)S(1)}, bf16[512,1024]{1,0:T(8,128)(2,1)}, u32[]{:S(2)}, u32[]{:S(2)}) collective-permute-start(bf16[512,1024]{1,0:T(8,128)(2,1)S(1)} %fusion.23), channel_id=1, source_target_pairs={{0,8},{8,0},{1,9},{9,1},{2,10},{10,2},{3,11},{11,3},{4,12},{12,4},... | collective-permute-start | bytes 3145736 | tf_op jit(solution)/shard_map/ppermute | solution.py:37
  139.4 24.6 %collective-permute-start.17 = (bf16[512,1024]{1,0:T(8,128)(2,1)S(1)}, bf16[512,1024]{1,0:T(8,128)(2,1)}, u32[]{:S(2)}, u32[]{:S(2)}) collective-permute-start(bf16[512,1024]{1,0:T(8,128)(2,1)S(1)} %multiply_convert_fusion.4.refs_0_), channel_id=1, source_target_pairs={{0,8},{8,0},{1,9},{9,1},{2,10},{10,2},{3,11},{11,3},{4,12},{12,4},... | collective-permute-start | bytes 3145736 | tf_op jit(solution)/shard_map/ppermute | solution.py:37
  141.1 272.0 %reduce-scatter.4.cloned.1.call-start = ((), (), s32[]{:S(2)}) async-start(), calls=%async_computation.4 | async-start | bytes 5308416 | tf_op jit(solution)/shard_map/reduce_scatter | solution.py:107
  141.7 27.3 %collective-permute-start.19 = (bf16[512,1024]{1,0:T(8,128)(2,1)}, bf16[512,1024]{1,0:T(8,128)(2,1)}, u32[]{:S(2)}, u32[]{:S(2)}) collective-permute-start(bf16[512,1024]{1,0:T(8,128)(2,1)} %fusion.7.refs_4_), channel_id=1, source_target_pairs={{0,4},{4,0},{1,5},{5,1},{2,6},{6,2},{3,7},{7,3},{8,12},{12,8},{9,1... | collective-permute-start | bytes 3145736 | tf_op jit(solution)/shard_map/ppermute | solution.py:33
  141.7 27.2 %collective-permute-start.16 = (bf16[512,1024]{1,0:T(8,128)(2,1)S(1)}, bf16[512,1024]{1,0:T(8,128)(2,1)}, u32[]{:S(2)}, u32[]{:S(2)}) collective-permute-start(bf16[512,1024]{1,0:T(8,128)(2,1)S(1)} %multiply_convert_fusion.4.refs_0_), channel_id=1, source_target_pairs={{0,4},{4,0},{1,5},{5,1},{2,6},{6,2},{3,7},{7,3},{8,12},{12,8},{9,1... | collective-permute-start | bytes 3145736 | tf_op jit(solution)/shard_map/ppermute | solution.py:33
  163.9 5.0 %collective-permute-start.18 = (bf16[512,1024]{1,0:T(8,128)(2,1)}, bf16[512,1024]{1,0:T(8,128)(2,1)}, u32[]{:S(2)}, u32[]{:S(2)}) collective-permute-start(bf16[512,1024]{1,0:T(8,128)(2,1)} %collective-permute-done.17.refs_2_), channel_id=1, source_target_pairs={{0,4},{4,0},{1,5},{5,1},{2,6},{6,2},{3,7},{7,3},{8,12},{12,8},{9,1... | collective-permute-start | bytes 3145736 | tf_op jit(solution)/shard_map/ppermute | solution.py:33
  240.5 10.4 %copy-start.45 = (bf16[2048,1024]{1,0:T(8,128)(2,1)S(1)}, bf16[2048,1024]{1,0:T(8,128)(2,1)}, u32[]{:S(2)}) copy-start(bf16[2048,1024]{1,0:T(8,128)(2,1)} %get-tuple-element.24) | copy-start | bytes 12582916
  240.6 4.2 collective-permute-start.23
  244.9 6.0 %copy-start.44 = (bf16[2048,2304]{1,0:T(8,128)(2,1)S(1)}, bf16[2048,2304]{1,0:T(8,128)(2,1)}, u32[]{:S(2)}) copy-start(bf16[2048,2304]{1,0:T(8,128)(2,1)} %get-tuple-element.25) | copy-start | bytes 28311556
  249.4 25.4 %collective-permute-start.24 = (bf16[512,1024]{1,0:T(8,128)(2,1)}, bf16[512,1024]{1,0:T(8,128)(2,1)S(1)}, u32[]{:S(2)}, u32[]{:S(2)}) collective-permute-start(bf16[512,1024]{1,0:T(8,128)(2,1)} %fusion.20), channel_id=1, source_target_pairs={{0,8},{8,0},{1,9},{9,1},{2,10},{10,2},{3,11},{11,3},{4,12},{12,4},... | collective-permute-start | bytes 3145736 | tf_op jit(solution)/shard_map/ppermute | solution.py:37
  265.7 11.6 %copy-start.5 = (f32[1024,1024]{1,0:T(8,128)S(1)}, f32[1024,1024]{1,0:T(8,128)}, u32[]{:S(2)}) copy-start(f32[1024,1024]{1,0:T(8,128)} %copy-done.4) | copy-start | bytes 12582916
  265.7 11.6 %copy-start.21 = (bf16[2,256,1024]{2,1,0:T(8,128)(2,1)S(1)}, bf16[2,256,1024]{2,1,0:T(8,128)(2,1)}, u32[]{:S(2)}) copy-start(bf16[2,256,1024]{2,1,0:T(8,128)(2,1)} %param.13) | copy-start | bytes 3145732
  281.1 24.7 %collective-permute-start.25 = (bf16[512,1024]{1,0:T(8,128)(2,1)}, bf16[512,1024]{1,0:T(8,128)(2,1)}, u32[]{:S(2)}, u32[]{:S(2)}) collective-permute-start(bf16[512,1024]{1,0:T(8,128)(2,1)} %get-tuple-element.44), channel_id=1, source_target_pairs={{0,8},{8,0},{1,9},{9,1},{2,10},{10,2},{3,11},{11,3},{4,12},{12,4},... | collective-permute-start | bytes 3145736 | tf_op jit(solution)/shard_map/ppermute | solution.py:37
  282.6 23.4 %collective-permute-start.29 = (bf16[512,1024]{1,0:T(8,128)(2,1)}, bf16[512,1024]{1,0:T(8,128)(2,1)}, u32[]{:S(2)}, u32[]{:S(2)}) collective-permute-start(bf16[512,1024]{1,0:T(8,128)(2,1)} %get-tuple-element.44), channel_id=1, source_target_pairs={{0,4},{4,0},{1,5},{5,1},{2,6},{6,2},{3,7},{7,3},{8,12},{12,8},{9,1... | collective-permute-start | bytes 3145736 | tf_op jit(solution)/shard_map/ppermute | solution.py:33
  305.8 3.0 collective-permute-start.26
  306.0 157.6 %reduce-scatter.6.cloned.1.call-start = ((), (), s32[]{:S(2)}) async-start(), calls=%async_computation.5 | async-start | bytes 1474560 | tf_op jit(solution)/shard_map/reduce_scatter | solution.py:97
  318.3 5.6 %copy-start.43 = (bf16[2048,256]{1,0:T(8,128)(2,1)}, bf16[2048,256]{1,0:T(8,128)(2,1)S(1)}, u32[]{:S(2)}) copy-start(bf16[2048,256]{1,0:T(8,128)(2,1)S(1)} %get-tuple-element.65) | copy-start | bytes 3145732
  323.9 5.7 %copy-start.33 = (bf16[2048,256]{1,0:T(8,128)(2,1)}, bf16[2048,256]{1,0:T(8,128)(2,1)S(1)}, u32[]{:S(2)}) copy-start(bf16[2048,256]{1,0:T(8,128)(2,1)S(1)} %multiply_convert_fusion) | copy-start | bytes 3145732
  340.6 12.4 %collective-permute-start.30 = (bf16[1024,1024]{1,0:T(8,128)(2,1)}, bf16[1024,1024]{1,0:T(8,128)(2,1)}, u32[]{:S(2)}, u32[]{:S(2)}) collective-permute-start(bf16[1024,1024]{1,0:T(8,128)(2,1)} %pad_maximum_fusion.6), channel_id=1, source_target_pairs={{0,4},{4,0},{1,5},{5,1},{2,6},{6,2},{3,7},{7,3},{8,12},{12,8},{9,1... | collective-permute-start | bytes 6291464 | tf_op jit(solution)/shard_map/ppermute | solution.py:33
  346.2 68.7 %collective-permute-start.32 = (bf16[4,144,1024]{2,1,0:T(8,128)(2,1)}, bf16[4,144,1024]{2,1,0:T(8,128)(2,1)}, u32[]{:S(2)}, u32[]{:S(2)}) collective-permute-start(bf16[4,144,1024]{2,1,0:T(8,128)(2,1)} %dynamic-slice_bitcast_fusion.1), channel_id=1, source_target_pairs={{0,16},{16,0},{1,17},{17,1},{2,18},{18,2},{3,19},{19,3},{4,20},{20... | collective-permute-start | bytes 3538952 | tf_op jit(solution)/shard_map/ppermute | solution.py:41
  352.7 68.8 %collective-permute-start.27 = (bf16[1024,1024]{1,0:T(8,128)(2,1)}, bf16[1024,1024]{1,0:T(8,128)(2,1)}, u32[]{:S(2)}, u32[]{:S(2)}) collective-permute-start(bf16[1024,1024]{1,0:T(8,128)(2,1)} %pad_maximum_fusion.5), channel_id=1, source_target_pairs={{0,4},{4,0},{1,5},{5,1},{2,6},{6,2},{3,7},{7,3},{8,12},{12,8},{9,1... | collective-permute-start | bytes 6291464 | tf_op jit(solution)/shard_map/ppermute | solution.py:33
  359.7 69.1 %collective-permute-start.31 = (bf16[512,1024]{1,0:T(8,128)(2,1)}, bf16[512,1024]{1,0:T(8,128)(2,1)}, u32[]{:S(2)}, u32[]{:S(2)}) collective-permute-start(bf16[512,1024]{1,0:T(8,128)(2,1)} %fusion.12), channel_id=1, source_target_pairs={{0,8},{8,0},{1,9},{9,1},{2,10},{10,2},{3,11},{11,3},{4,12},{12,4},... | collective-permute-start | bytes 3145736 | tf_op jit(solution)/shard_map/ppermute | solution.py:37
  418.2 60.5 %reduce-scatter.8.cloned.1.call-start = ((), (), s32[]{:S(2)}) async-start(), calls=%async_computation.6 | async-start | bytes 1474560 | tf_op jit(solution)/shard_map/reduce_scatter | solution.py:97
  420.0 27.7 %collective-permute-start.39 = (bf16[4,144,1024]{2,1,0:T(8,128)(2,1)S(1)}, bf16[4,144,1024]{2,1,0:T(8,128)(2,1)S(1)}, u32[]{:S(2)}, u32[]{:S(2)}) collective-permute-start(bf16[4,144,1024]{2,1,0:T(8,128)(2,1)S(1)} %dynamic-slice_bitcast_fusion), channel_id=1, source_target_pairs={{0,16},{16,0},{1,17},{17,1},{2,18},{18,2},{3,19},{19,3},{4,20},{20... | collective-permute-start | bytes 3538952 | tf_op jit(solution)/shard_map/ppermute | solution.py:41
  421.5 7.3 %copy-start.18 = (bf16[2048,1024]{1,0:T(8,128)(2,1)S(1)}, bf16[2048,1024]{1,0:T(8,128)(2,1)}, u32[]{:S(2)}) copy-start(bf16[2048,1024]{1,0:T(8,128)(2,1)} %copy-done.17) | copy-start | bytes 12582916
  423.7 5.1 %copy-start.3 = (f32[1024,1024]{1,0:T(8,128)S(1)}, f32[1024,1024]{1,0:T(8,128)}, u32[]{:S(2)}) copy-start(f32[1024,1024]{1,0:T(8,128)} %copy-done.2) | copy-start | bytes 12582916
  427.3 24.9 %collective-permute-start.28 = (bf16[512,1024]{1,0:T(8,128)(2,1)}, bf16[512,1024]{1,0:T(8,128)(2,1)}, u32[]{:S(2)}, u32[]{:S(2)}) collective-permute-start(bf16[512,1024]{1,0:T(8,128)(2,1)} %fusion.15), channel_id=1, source_target_pairs={{0,8},{8,0},{1,9},{9,1},{2,10},{10,2},{3,11},{11,3},{4,12},{12,4},... | collective-permute-start | bytes 3145736 | tf_op jit(solution)/shard_map/ppermute | solution.py:37
  430.7 17.0 %copy-start.23 = (bf16[1152,1024]{1,0:T(8,128)(2,1)S(1)}, bf16[1152,1024]{1,0:T(8,128)(2,1)}, u32[]{:S(2)}) copy-start(bf16[1152,1024]{1,0:T(8,128)(2,1)} %convolution_convert_fusion.1.token_ref) | copy-start | bytes 7077892
  433.9 15.4 %copy-start.39 = (bf16[1,128,2304]{2,1,0:T(8,128)(2,1)S(1)}, bf16[1,128,2304]{2,1,0:T(8,128)(2,1)}, u32[]{:S(2)}) copy-start(bf16[1,128,2304]{2,1,0:T(8,128)(2,1)} %reduce-scatter.4.cloned.1.call-done) | copy-start | bytes 1769476
  449.4 6.5 %collective-permute-start.36 = (bf16[32,2304]{1,0:T(8,128)(2,1)S(1)}, bf16[32,2304]{1,0:T(8,128)(2,1)S(1)}, u32[]{:S(2)}, u32[]{:S(2)}) collective-permute-start(bf16[32,2304]{1,0:T(8,128)(2,1)S(1)} %get-tuple-element.75), channel_id=1, source_target_pairs={{0,12},{4,8},{8,4},{12,0},{1,13},{5,9},{9,5},{13,1},{2,14},{6,10},... | collective-permute-start | bytes 442376 | tf_op jit(solution)/shard_map/ppermute | solution.py:45
  449.5 9.2 %collective-permute-start.37 = (bf16[32,2304]{1,0:T(8,128)(2,1)S(1)}, bf16[32,2304]{1,0:T(8,128)(2,1)S(1)}, u32[]{:S(2)}, u32[]{:S(2)}) collective-permute-start(bf16[32,2304]{1,0:T(8,128)(2,1)S(1)} %get-tuple-element.76), channel_id=1, source_target_pairs={{0,8},{4,12},{8,0},{12,4},{1,9},{5,13},{9,1},{13,5},{2,10},{6,14},... | collective-permute-start | bytes 442376 | tf_op jit(solution)/shard_map/ppermute | solution.py:45
  451.0 7.8 %collective-permute-start.38 = (bf16[32,2304]{1,0:T(8,128)(2,1)S(1)}, bf16[32,2304]{1,0:T(8,128)(2,1)S(1)}, u32[]{:S(2)}, u32[]{:S(2)}) collective-permute-start(bf16[32,2304]{1,0:T(8,128)(2,1)S(1)} %get-tuple-element.74), channel_id=1, source_target_pairs={{0,4},{4,0},{8,12},{12,8},{1,5},{5,1},{9,13},{13,9},{2,6},{6,2},{1... | collective-permute-start | bytes 442376 | tf_op jit(solution)/shard_map/ppermute | solution.py:45
  464.5 17.3 %collective-permute-start.33 = (bf16[32,768]{1,0:T(8,128)(2,1)S(1)}, bf16[32,768]{1,0:T(8,128)(2,1)S(1)}, u32[]{:S(2)}, u32[]{:S(2)}) collective-permute-start(bf16[32,768]{1,0:T(8,128)(2,1)S(1)} %get-tuple-element.90), channel_id=1, source_target_pairs={{0,12},{4,8},{8,4},{12,0},{1,13},{5,9},{9,5},{13,1},{2,14},{6,10},... | collective-permute-start | bytes 147464 | tf_op jit(solution)/shard_map/ppermute | solution.py:45
  465.5 16.3 %collective-permute-start.34 = (bf16[32,768]{1,0:T(8,128)(2,1)S(1)}, bf16[32,768]{1,0:T(8,128)(2,1)S(1)}, u32[]{:S(2)}, u32[]{:S(2)}) collective-permute-start(bf16[32,768]{1,0:T(8,128)(2,1)S(1)} %get-tuple-element.91), channel_id=1, source_target_pairs={{0,8},{4,12},{8,0},{12,4},{1,9},{5,13},{9,1},{13,5},{2,10},{6,14},... | collective-permute-start | bytes 147464 | tf_op jit(solution)/shard_map/ppermute | solution.py:45
  466.4 15.5 %collective-permute-start.35 = (bf16[32,768]{1,0:T(8,128)(2,1)S(1)}, bf16[32,768]{1,0:T(8,128)(2,1)S(1)}, u32[]{:S(2)}, u32[]{:S(2)}) collective-permute-start(bf16[32,768]{1,0:T(8,128)(2,1)S(1)} %get-tuple-element.89), channel_id=1, source_target_pairs={{0,4},{4,0},{8,12},{12,8},{1,5},{5,1},{9,13},{13,9},{2,6},{6,2},{1... | collective-permute-start | bytes 147464 | tf_op jit(solution)/shard_map/ppermute | solution.py:45
  467.9 14.7 %copy-start.38 = (bf16[32,3072]{1,0:T(8,128)(2,1)S(1)}, bf16[32,3072]{1,0:T(8,128)(2,1)}, u32[]{:S(2)}) copy-start(bf16[32,3072]{1,0:T(8,128)(2,1)} %param.15) | copy-start | bytes 589828
  (28 other events, 75.4 us)
Sparse Core Ops, SparseCore 0:
  19.7 52.3 all-gather.7
  76.8 81.3 all-gather.9
  160.4 50.2 all-gather.5
  306.1 106.9 reduce-scatter.3
  418.3 28.9 reduce-scatter.5
  449.4 29.1 reduce-scatter.7

commit v9 on v7

--- a/solution.py
+++ b/solution.py
@@ -96,6 +96,14 @@
         summed = (take(part, row).astype(f32) + came).astype(bf16)
         return lax.psum_scatter(summed, "s", scatter_dimension=0, tiled=False)
     flat = part.reshape((groups * slots,) + part.shape[2:]).astype(f32)
+    return lax.psum_scatter(flat, ("g", "y", "s"), scatter_dimension=0, tiled=False)
+
+
+def scatter_plain(part):
+    groups, slots = part.shape[:2]
+    flat = part.reshape((groups * slots,) + part.shape[2:])
+    if groups > 2:
+        flat = flat.astype(f32)
     return lax.psum_scatter(flat, ("g", "y", "s"), scatter_dimension=0, tiled=False)
 
 
@@ -375,7 +383,7 @@
         conv_rows.astype(bf16),
         ((0, 0), (0, 0), (0, EXTRA_ROWS - 1), (0, features - taps * share)),
     )
-    pair_sum = scatter(pair_part, projected_grad[-1:])
+    pair_sum = scatter_plain(pair_part)
     first_weighted, first_sent = team_sum(back_dot(projected_grad, in_full).astype(bf16))
     input_grad = middle_grad + norm_back(inputs, inverse_rms(inputs), norm_full * first_weighted)
     input_grad = input_grad.astype(bf16)
@@ -387,7 +395,6 @@
         ),
         pair_sum[:1],
         first_sent,
-        block_out[:1],
     )
 
     def own_rows(summed, parts, team, run):

time: 495 us -> 470 us (0.949)
  waiting for transfers between devices: 213 us -> 198 us
  local copies, waits for them, and re-layouts: 51.6 us -> 44.4 us
    reduce_scatter x0 -> x1, waiting for transfers between devices: none -> 23 us  [scatter_plain(): lax.psum_scatter(flat, ('g', 'y', 's'), scatter_dimension=0, tiled=False)]
    ppermute x3 -> x2, waiting for transfers between devices: 24.5 us -> 2.24 us  [swap_row(): return lax.ppermute(values, 'y', [(0, 1), (1, 0)])]
    ppermute x10, waiting for transfers between devices: 101 us -> 85.2 us  [swap_chip(): return lax.ppermute(values, 'x', [(0, 1), (1, 0)])]
    unnamed x94 -> x82, local copies, waits for them, and re-layouts: 15.8 us -> 10.5 us
    convert_element_type x3 -> x2, other arithmetic: 10.9 us -> 6.39 us  [scatter(): summed = (take(part, row).astype(f32) + came).astype(bf16)]
    reduce_scatter x3 -> x2, waiting for transfers between devices: 12.7 us -> 13.1 us  [scatter(): return lax.psum_scatter(summed, 's', scatter_dimension=0, tiled=False)]
  transfers between devices with their start and end apart: 47 -> 46, of which waited for: 20 -> 19; matrix products, arithmetic and copies ran while one was open for 31% -> 33% of each run, Pallas kernels for 4% -> 4%
where the time goes in v9:
time: 470 us; the launch traced here: 465 us
  waiting for transfers between devices  198 us (42%)
  other arithmetic  76.3 us (16%)
  matrix products  52.3 us (11%)
  Pallas kernels  45.8 us (10%)
  local copies, waits for them, and re-layouts  44.4 us (9%)
  starting transfers between devices  27.9 us (6%)
  between operations  19.5 us (4%)
    ppermute x10, waiting for transfers between devices, swap_chip(): return lax.ppermute(values, 'x', [(0, 1), (1, 0)])  85.2 us
    ppermute x12, waiting for transfers between devices, swap_far(): lax.ppermute(values, ('x', 'c'), [(i, i ^ distance) for i in range(TEAM)])  52.3 us
    pallas_call x2, Pallas kernels, by_rows(): pl.pallas_call(kernel, grid=(steps,), in_specs=[row_block(value.shape[1])...  45.8 us
    dot_general x4, matrix products, rows_dot(): lax.dot_general(left_side, right_side, (((0,), (0,)), ((), ())), preferre...  30.6 us
    reduce_scatter x1, waiting for transfers between devices, scatter_plain(): lax.psum_scatter(flat, ('g', 'y', 's'), scatter_dimension=0, tiled=False)  23 us
    all_gather x1, waiting for transfers between devices, per_device(): down_full = lax.all_gather(down_weight, ('g', 'y', 's'), axis=0, tiled=True)  14.6 us
    ppermute x10, starting transfers between devices, swap_chip(): return lax.ppermute(values, 'x', [(0, 1), (1, 0)])  13.6 us
    reduce_scatter x2, waiting for transfers between devices, scatter(): return lax.psum_scatter(summed, 's', scatter_dimension=0, tiled=False)  13.1 us
  transfers between devices with their start and end apart: 46, of which 19 were waited for; matrix products, arithmetic and copies ran while one was open for 33% of the time, Pallas kernels for 4%

profile of v9, /device:TPU:0, one launch (start us, length us, event | category | flops | bytes accessed | tf_op | source)
XLA Modules:
  0.0 464.6 jit_solution(17712575177415977781)
XLA Ops:
  8.1 2.9 collective-permute-start.6
  12.8 2.0 collective-permute-start.4
  21.3 1.7 collective-permute-start.9
  25.3 1.8 collective-permute-start.20
  27.5 44.8 %collective-permute-done.20 = bf16[32,2304]{1,0:T(8,128)(2,1)S(1)} collective-permute-done((bf16[32,2304]{1,0:T(8,128)(2,1)S(1)}, bf16[32,2304]{1,0:T(8,128)(2,1)S(1)}, u32[]{:S(2)}, u32[]{:S(2)}) %collective-permute-start.20) | collective-permute-done | bytes 147488 | tf_op jit(solution)/shard_map/ppermute | solution.py:45
  73.5 2.3 collective-permute-done.21
  77.1 1.4 collective-permute-done.10.refs_7_
  80.3 3.5 fusion
  83.9 1.5 slice.387
  90.2 7.4 %fusion.27 = f32[2048,768]{1,0:T(8,128)S(1)} fusion(bf16[1024,768]{1,0:T(8,128)(2,1)S(1)} %bitcast.166, f32[1024]{0:T(1024)S(1)} %mul.328, f32[2048]{0:T(1024)S(1)} %add_rsqrt_fusion, bf16[512,1024]{1,0:T(8,128)(2,1)} %copy-done.31, bf16[512,1024]{1,0:T(8,128)(2,1)} %collective-permute-done.1, bf16[512,1024]{1,0:T(8,128)(2,1)} %copy-done.29, ...), kind=kOutput, calls=%fused_computation.78 | convolution fusion | flops 3244294144 | bytes 12070912 | tf_op jit(solution)/shard_map/dot_general | solution.py:17
  97.9 2.3 copy-done
  100.2 2.4 multiply_convert_fusion.5
  104.4 4.0 collective-permute-done.14
  109.3 1.6 copy-done.10
  110.9 1.6 collective-permute-start.15
  112.6 23.6 %collective-permute-done.15 = bf16[512,1024]{1,0:T(8,128)(2,1)} collective-permute-done((bf16[512,1024]{1,0:T(8,128)(2,1)S(1)}, bf16[512,1024]{1,0:T(8,128)(2,1)}, u32[]{:S(2)}, u32[]{:S(2)}) %collective-permute-start.15) | collective-permute-done | bytes 1048608 | tf_op jit(solution)/shard_map/ppermute | solution.py:37
  136.3 2.9 multiply_reduce_fusion.5
  139.4 1.7 collective-permute-start.17
  142.3 21.7 %collective-permute-done.17.refs_2_ = bf16[512,1024]{1,0:T(8,128)(2,1)} collective-permute-done((bf16[512,1024]{1,0:T(8,128)(2,1)S(1)}, bf16[512,1024]{1,0:T(8,128)(2,1)}, u32[]{:S(2)}, u32[]{:S(2)}) %collective-permute-start.17) | collective-permute-done | bytes 1048608 | tf_op jit(solution)/shard_map/ppermute | solution.py:37
  164.0 4.9 %copy.69 = bf16[2,4,4,32,2304]{4,3,1,2,0:T(8,128)(2,1)} copy(bf16[2,4,4,32,2304]{4,3,2,1,0:T(8,128)(2,1)} %bitcast.154) | data formatting | bytes 9437184 | tf_op jit(solution)/shard_map/reshape | solution.py:287
  169.0 17.7 %shard_map.186 = (bf16[2048,1152]{1,0:T(8,128)(2,1)}, bf16[2048,1152]{1,0:T(8,128)(2,1)}, bf16[2048,1152]{1,0:T(8,128)(2,1)}, bf16[2048,1024]{1,0:T(8,128)(2,1)}, bf16[2048,1024]{1,0:T(8,128)(2,1)}) custom-call(bf16[512,1024]{1,0:T(8,128)(2,1)S(1)} %multiply_convert_fusion.4.refs_0_, bf16[512,1024]{1,0:T(8,128)(2,1)} %collective-permute-done.16.refs_1_, ...), custom_call_target="tpu_custom_call" | custom-call | flops 9663676416 | bytes 35651584 | tf_op jit(solution)/shard_map/pallas_call | solution.py:158
  186.7 9.4 %convolution_convert_fusion.1.token_ref = bf16[1152,1024]{1,0:T(8,128)(2,1)} fusion(bf16[2048,1152]{1,0:T(8,128)(2,1)} %get-tuple-element.19.hidden_ref, bf16[2048,1024]{1,0:T(8,128)(2,1)} %get-tuple-element.18.grad_ref), kind=kOutput, calls=%fused_computation.10 | convolution fusion | flops 4833017856 | bytes 11272192 | tf_op jit(solution)/shard_map/dot_general | solution.py:21
  196.0 14.6 %all-gather.6.cloned.1.call-done.down_ref = bf16[1152,1024]{1,0:T(8,128)(2,1)} async-done(((bf16[144,1024]{1,0:T(8,128)(2,1)}), bf16[1152,1024]{1,0:T(8,128)(2,1)}) %all-gather.6.cloned.1.call-update) | async-done | bytes 2359312 | tf_op jit(solution)/shard_map/all_gather | solution.py:279
  210.6 28.1 %shard_map.187 = (bf16[2048,2304]{1,0:T(8,128)(2,1)}, bf16[2048,1024]{1,0:T(8,128)(2,1)}, bf16[2048,1024]{1,0:T(8,128)(2,1)}) custom-call(bf16[2048,1024]{1,0:T(8,128)(2,1)} %get-tuple-element.18.grad_ref, bf16[2048,1152]{1,0:T(8,128)(2,1)} %get-tuple-element.19.hidden_ref, bf16[2048,1152]{1,0:T(8,128)(2,1)} %get-tuple-element.20.silu_ref, ...), custom_call_target="tpu_custom_call" | custom-call | flops 19327352832 | bytes 43253760 | tf_op jit(solution)/shard_map/pallas_call | solution.py:158
  238.8 1.7 fusion.46
  240.5 1.5 pad_maximum_fusion.4
  241.9 2.4 dynamic-slice_bitcast_fusion.1
  244.9 1.6 collective-permute-done.23
  246.4 2.2 convert_element_type.303
  248.7 4.5 fusion.20
  253.2 1.5 collective-permute-start.24
  254.7 12.4 %convolution_convert_fusion = bf16[1024,2304]{1,0:T(8,128)(2,1)S(1)} fusion(bf16[2048,1024]{1,0:T(8,128)(2,1)} %get-tuple-element.24, bf16[2048,2304]{1,0:T(8,128)(2,1)S(1)} %copy-done.38), kind=kOutput, calls=%fused_computation.5 | convolution fusion | flops 9666035712 | bytes 18350080 | tf_op jit(solution)/shard_map/dot_general | solution.py:21
  267.4 2.2 copy-done.8
  270.8 2.2 collective-permute-done.29
  273.0 3.1 fusion.6
  276.2 2.4 collective-permute-done.24
  278.6 2.9 multiply_reduce_fusion.4
  281.6 4.2 multiply_convert_fusion.3
  285.8 1.4 collective-permute-start.25
  287.2 23.2 %collective-permute-done.25 = bf16[512,1024]{1,0:T(8,128)(2,1)} collective-permute-done((bf16[512,1024]{1,0:T(8,128)(2,1)}, bf16[512,1024]{1,0:T(8,128)(2,1)}, u32[]{:S(2)}, u32[]{:S(2)}) %collective-permute-start.25) | collective-permute-done | bytes 1048608 | tf_op jit(solution)/shard_map/ppermute | solution.py:37
  313.2 1.8 bitcast_convert_fusion
  315.1 9.5 %multiply_reduce_fusion.2 = (bf16[256]{0:T(256)(128)(2,1)S(1)}, bf16[256]{0:T(256)(128)(2,1)S(1)}, bf16[256]{0:T(256)(128)(2,1)S(1)}, f32[2048,256]{1,0:T(8,128)S(1)}, bf16[2048,256]{1,0:T(8,128)(2,1)S(1)}) fusion(f32[2048,256]{1,0:T(8,128)} %copy-done.9, f32[2046,256]{1,0:T(8,128)} %bitcast.150, f32[2048]{0:T(1024)S(1)} %get-tuple-element.117, ...), kind=kOutput, calls=%fused_computation.59 | convolution fusion | flops 1096285440 | bytes 18364928 | tf_op jit(solution)/shard_map/dot_general | solution.py:27
  325.2 2.5 multiply_convert_fusion.2
  327.8 2.0 multiply_convert_fusion
  329.9 3.7 convolution_convert_fusion.3
  333.8 1.9 copy-done.15
  335.7 1.5 pad_maximum_fusion.6
  340.1 1.8 copy-done.11
  341.9 1.5 pad_maximum_fusion.5
  344.2 5.0 %convolution_convert_fusion.4 = bf16[1024,768]{1,0:T(8,128)(2,1)S(1)} fusion(bf16[2048,256]{1,0:T(8,128)(2,1)S(1)} %multiply_convert_fusion, bf16[2048,256]{1,0:T(8,128)(2,1)S(1)} %get-tuple-element.68, bf16[2048,256]{1,0:T(8,128)(2,1)S(1)} %get-tuple-element.45, f32[1024]{0:T(1024)S(1)} %mul.328, f32[2048]{0:T(1024)S(1)} %add_rsqrt_fusion, ...), kind=kOutput, calls=%fused_computation.76 | convolution fusion | flops 3254517760 | bytes 8925184 | tf_op jit(solution)/shard_map/dot_general | solution.py:21
  350.9 3.8 convolution_convert_fusion.5
  354.8 2.0 convert_element_type.326
  356.9 3.6 fusion.12
  360.4 1.5 collective-permute-start.32
  364.5 2.1 convert_element_type.312
  366.6 3.4 fusion.15
  372.5 14.2 %collective-permute-done.32 = bf16[512,1024]{1,0:T(8,128)(2,1)} collective-permute-done((bf16[512,1024]{1,0:T(8,128)(2,1)}, bf16[512,1024]{1,0:T(8,128)(2,1)}, u32[]{:S(2)}, u32[]{:S(2)}) %collective-permute-start.32) | collective-permute-done | bytes 1048608 | tf_op jit(solution)/shard_map/ppermute | solution.py:37
  386.7 2.8 fusion.8
  389.5 4.0 fusion.11
  393.5 23.0 %reduce-scatter.6.cloned.1.call-done = bf16[1,128,2304]{2,1,0:T(8,128)(2,1)} async-done(((bf16[8,128,2304]{2,1,0:T(8,128)(2,1)}), bf16[1,128,2304]{2,1,0:T(8,128)(2,1)}) %reduce-scatter.6.cloned.1.call-update) | async-done | bytes 589840 | tf_op jit(solution)/shard_map/reduce_scatter | solution.py:107
  418.4 3.3 fusion.5
  423.7 3.6 fusion.19
  427.9 3.3 collective-permute-done.38
  436.0 13.1 %reduce-scatter.8.cloned.1.call-done = bf16[1,144,1024]{2,1,0:T(8,128)(2,1)} async-done(((bf16[4,144,1024]{2,1,0:T(8,128)(2,1)}), bf16[1,144,1024]{2,1,0:T(8,128)(2,1)}) %reduce-scatter.8.cloned.1.call-update) | async-done | bytes 294928 | tf_op jit(solution)/shard_map/reduce_scatter | solution.py:97
  (272 shorter events, 54.9 us)
Async XLA Ops:
  7.2 12.4 %copy-start.35 = (s32[2,256]{1,0:T(2,128)S(1)}, s32[2,256]{1,0:T(2,128)}, u32[]{:S(2)}) copy-start(s32[2,256]{1,0:T(2,128)} %param.12) | copy-start | bytes 6148
  7.2 12.9 %copy-start.17 = (bf16[2,256,1024]{2,1,0:T(8,128)(2,1)S(1)}, bf16[2,256,1024]{2,1,0:T(8,128)(2,1)}, u32[]{:S(2)}) copy-start(bf16[2,256,1024]{2,1,0:T(8,128)(2,1)} %param.13) | copy-start | bytes 3145732
  7.2 76.7 %all-gather.8.cloned.1.call-start = ((), (), s32[]{:S(2)}) async-start(), calls=%async_computation.7 | async-start | bytes 2654208 | tf_op jit(solution)/shard_map/all_gather | solution.py:273
  8.1 8.4 %collective-permute-start.6 = (bf16[1,64]{1,0:T(2,128)(2,1)S(1)}, bf16[1,64]{1,0:T(2,128)(2,1)S(1)}, u32[]{:S(2)}, u32[]{:S(2)}) collective-permute-start(bf16[1,64]{1,0:T(2,128)(2,1)S(1)} %maximum_bitcast_fusion.1), channel_id=1, source_target_pairs={{0,8},{8,0},{1,9},{9,1},{2,10},{10,2},{3,11},{11,3},{4,12},{12,4},... | collective-permute-start | bytes 392 | tf_op jit(solution)/shard_map/ppermute | solution.py:37
  11.0 6.0 %collective-permute-start.8 = (bf16[1,64]{1,0:T(2,128)(2,1)S(1)}, bf16[1,64]{1,0:T(2,128)(2,1)S(1)}, u32[]{:S(2)}, u32[]{:S(2)}) collective-permute-start(bf16[1,64]{1,0:T(2,128)(2,1)S(1)} %maximum_bitcast_fusion.1), channel_id=1, source_target_pairs={{0,4},{4,0},{1,5},{5,1},{2,6},{6,2},{3,7},{7,3},{8,12},{12,8},{9,1... | collective-permute-start | bytes 392 | tf_op jit(solution)/shard_map/ppermute | solution.py:33
  12.2 10.7 %copy-start.6 = (bf16[2,256,1024]{2,1,0:T(8,128)(2,1)S(1)}, bf16[2,256,1024]{2,1,0:T(8,128)(2,1)}, u32[]{:S(2)}) copy-start(bf16[2,256,1024]{2,1,0:T(8,128)(2,1)} %param.11) | copy-start | bytes 3145732
  12.2 11.1 %copy-start.25 = (bf16[32,4608]{1,0:T(8,128)(2,1)S(1)}, bf16[32,4608]{1,0:T(8,128)(2,1)}, u32[]{:S(2)}) copy-start(bf16[32,4608]{1,0:T(8,128)(2,1)} %param.19) | copy-start | bytes 884740
  12.5 6.1 %collective-permute-start.3 = (bf16[32,768]{1,0:T(8,128)(2,1)S(1)}, bf16[32,768]{1,0:T(8,128)(2,1)S(1)}, u32[]{:S(2)}, u32[]{:S(2)}) collective-permute-start(bf16[32,768]{1,0:T(8,128)(2,1)S(1)} %select_n.378), channel_id=1, source_target_pairs={{0,12},{4,8},{8,4},{12,0},{1,13},{5,9},{9,5},{13,1},{2,14},{6,10},... | collective-permute-start | bytes 147464 | tf_op jit(solution)/shard_map/ppermute | solution.py:45
  12.8 5.9 %collective-permute-start.4 = (bf16[32,768]{1,0:T(8,128)(2,1)S(1)}, bf16[32,768]{1,0:T(8,128)(2,1)S(1)}, u32[]{:S(2)}, u32[]{:S(2)}) collective-permute-start(bf16[32,768]{1,0:T(8,128)(2,1)S(1)} %select_n.382), channel_id=1, source_target_pairs={{0,8},{4,12},{8,0},{12,4},{1,9},{5,13},{9,1},{13,5},{2,10},{6,14},... | collective-permute-start | bytes 147464 | tf_op jit(solution)/shard_map/ppermute | solution.py:45
  14.8 3.8 collective-permute-start.5
  16.5 1.3 collective-permute-start.7
  19.5 4.7 %copy-start.27 = (bf16[32,4608]{1,0:T(8,128)(2,1)S(1)}, bf16[32,4608]{1,0:T(8,128)(2,1)}, u32[]{:S(2)}) copy-start(bf16[32,4608]{1,0:T(8,128)(2,1)} %param.20) | copy-start | bytes 884740
  19.5 144.5 %all-gather.10.cloned.1.call-start = ((), (), s32[]{:S(2)}) async-start(), calls=%async_computation.8 | async-start | bytes 5308416 | tf_op jit(solution)/shard_map/all_gather | solution.py:278
  19.6 5.5 %collective-permute-start.12 = (s32[512,1]{0,1:T(1,128)S(1)}, s32[512,1]{0,1:T(1,128)S(1)}, u32[]{:S(2)}, u32[]{:S(2)}) collective-permute-start(s32[512,1]{0,1:T(1,128)S(1)} %bitcast.189), channel_id=1, source_target_pairs={{0,8},{8,0},{1,9},{9,1},{2,10},{10,2},{3,11},{11,3},{4,12},{12,4},... | collective-permute-start | bytes 6152 | tf_op jit(solution)/shard_map/ppermute | solution.py:37
  19.9 7.2 %collective-permute-start.11 = (s32[512,1]{0,1:T(1,128)S(1)}, s32[512,1]{0,1:T(1,128)S(1)}, u32[]{:S(2)}, u32[]{:S(2)}) collective-permute-start(s32[512,1]{0,1:T(1,128)S(1)} %bitcast.190), channel_id=1, source_target_pairs={{0,4},{4,0},{1,5},{5,1},{2,6},{6,2},{3,7},{7,3},{8,12},{12,8},{9,1... | collective-permute-start | bytes 6152 | tf_op jit(solution)/shard_map/ppermute | solution.py:33
  21.3 51.7 %collective-permute-start.9 = (bf16[512,1024]{1,0:T(8,128)(2,1)}, bf16[512,1024]{1,0:T(8,128)(2,1)}, u32[]{:S(2)}, u32[]{:S(2)}) collective-permute-start(bf16[512,1024]{1,0:T(8,128)(2,1)} %fusion.7.refs_4_), channel_id=1, source_target_pairs={{0,8},{8,0},{1,9},{9,1},{2,10},{10,2},{3,11},{11,3},{4,12},{12,4},... | collective-permute-start | bytes 3145736 | tf_op jit(solution)/shard_map/ppermute | solution.py:37
  23.0 50.0 %collective-permute-start.1 = (bf16[512,1024]{1,0:T(8,128)(2,1)S(1)}, bf16[512,1024]{1,0:T(8,128)(2,1)}, u32[]{:S(2)}, u32[]{:S(2)}) collective-permute-start(bf16[512,1024]{1,0:T(8,128)(2,1)S(1)} %bitcast.141), channel_id=1, source_target_pairs={{0,8},{8,0},{1,9},{9,1},{2,10},{10,2},{3,11},{11,3},{4,12},{12,4},... | collective-permute-start | bytes 3145736 | tf_op jit(solution)/shard_map/ppermute | solution.py:37
  25.2 2.3 collective-permute-start.13
  25.3 47.0 %collective-permute-start.20 = (bf16[32,2304]{1,0:T(8,128)(2,1)S(1)}, bf16[32,2304]{1,0:T(8,128)(2,1)S(1)}, u32[]{:S(2)}, u32[]{:S(2)}) collective-permute-start(bf16[32,2304]{1,0:T(8,128)(2,1)S(1)} %get-tuple-element.83), channel_id=1, source_target_pairs={{0,12},{4,8},{8,4},{12,0},{1,13},{5,9},{9,5},{13,1},{2,14},{6,10},... | collective-permute-start | bytes 442376 | tf_op jit(solution)/shard_map/ppermute | solution.py:45
  27.1 48.7 %collective-permute-start.21 = (bf16[32,2304]{1,0:T(8,128)(2,1)S(1)}, bf16[32,2304]{1,0:T(8,128)(2,1)S(1)}, u32[]{:S(2)}, u32[]{:S(2)}) collective-permute-start(bf16[32,2304]{1,0:T(8,128)(2,1)S(1)} %get-tuple-element.49), channel_id=1, source_target_pairs={{0,8},{4,12},{8,0},{12,4},{1,9},{5,13},{9,1},{13,5},{2,10},{6,14},... | collective-permute-start | bytes 442376 | tf_op jit(solution)/shard_map/ppermute | solution.py:45
  27.5 48.3 %collective-permute-start.22 = (bf16[32,2304]{1,0:T(8,128)(2,1)S(1)}, bf16[32,2304]{1,0:T(8,128)(2,1)S(1)}, u32[]{:S(2)}, u32[]{:S(2)}) collective-permute-start(bf16[32,2304]{1,0:T(8,128)(2,1)S(1)} %get-tuple-element.82), channel_id=1, source_target_pairs={{0,4},{4,0},{8,12},{12,8},{1,5},{5,1},{9,13},{13,9},{2,6},{6,2},{1... | collective-permute-start | bytes 442376 | tf_op jit(solution)/shard_map/ppermute | solution.py:45
  72.3 8.0 %collective-permute-start = (bf16[512,1024]{1,0:T(8,128)(2,1)S(1)}, bf16[512,1024]{1,0:T(8,128)(2,1)S(1)}, u32[]{:S(2)}, u32[]{:S(2)}) collective-permute-start(bf16[512,1024]{1,0:T(8,128)(2,1)S(1)} %bitcast.142), channel_id=1, source_target_pairs={{0,4},{4,0},{1,5},{5,1},{2,6},{6,2},{3,7},{7,3},{8,12},{12,8},{9,1... | collective-permute-start | bytes 3145736 | tf_op jit(solution)/shard_map/ppermute | solution.py:33
  72.9 5.5 %collective-permute-start.10 = (bf16[512,1024]{1,0:T(8,128)(2,1)}, bf16[512,1024]{1,0:T(8,128)(2,1)}, u32[]{:S(2)}, u32[]{:S(2)}) collective-permute-start(bf16[512,1024]{1,0:T(8,128)(2,1)} %collective-permute-done.9.refs_6_), channel_id=1, source_target_pairs={{0,4},{4,0},{1,5},{5,1},{2,6},{6,2},{3,7},{7,3},{8,12},{12,8},{9,1... | collective-permute-start | bytes 3145736 | tf_op jit(solution)/shard_map/ppermute | solution.py:33
  73.0 7.4 %collective-permute-start.2 = (bf16[512,1024]{1,0:T(8,128)(2,1)}, bf16[512,1024]{1,0:T(8,128)(2,1)S(1)}, u32[]{:S(2)}, u32[]{:S(2)}) collective-permute-start(bf16[512,1024]{1,0:T(8,128)(2,1)} %collective-permute-done.1), channel_id=1, source_target_pairs={{0,4},{4,0},{1,5},{5,1},{2,6},{6,2},{3,7},{7,3},{8,12},{12,8},{9,1... | collective-permute-start | bytes 3145736 | tf_op jit(solution)/shard_map/ppermute | solution.py:33
  76.7 133.9 %all-gather.6.cloned.1.call-start = ((), (), s32[]{:S(2)}) async-start(), calls=%async_computation.3 | async-start | bytes 2654208 | tf_op jit(solution)/shard_map/all_gather | solution.py:279
  90.2 12.4 %copy-start.21 = (bf16[8,32,1024]{2,1,0:T(8,128)(2,1)}, bf16[8,32,1024]{2,1,0:T(8,128)(2,1)S(1)}, u32[]{:S(2)}) copy-start(bf16[8,32,1024]{2,1,0:T(8,128)(2,1)S(1)} %pad_maximum_fusion.12) | copy-start | bytes 1572868
  97.9 4.7 %copy-start.9 = (f32[2048,256]{1,0:T(8,128)}, f32[2048,256]{1,0:T(8,128)S(1)}, u32[]{:S(2)}) copy-start(f32[2048,256]{1,0:T(8,128)S(1)} %slice_multiply_fusion.2) | copy-start | bytes 6291460
  103.8 5.1 %copy-start.1 = (bf16[2048,1024]{1,0:T(8,128)(2,1)}, bf16[2048,1024]{1,0:T(8,128)(2,1)S(1)}, u32[]{:S(2)}) copy-start(bf16[2048,1024]{1,0:T(8,128)(2,1)S(1)} %convolution_convert_fusion.2) | copy-start | bytes 12582916
  104.2 4.2 collective-permute-start.14
  110.9 25.3 %collective-permute-start.15 = (bf16[512,1024]{1,0:T(8,128)(2,1)S(1)}, bf16[512,1024]{1,0:T(8,128)(2,1)}, u32[]{:S(2)}, u32[]{:S(2)}) collective-permute-start(bf16[512,1024]{1,0:T(8,128)(2,1)S(1)} %fusion.23), channel_id=1, source_target_pairs={{0,8},{8,0},{1,9},{9,1},{2,10},{10,2},{3,11},{11,3},{4,12},{12,4},... | collective-permute-start | bytes 3145736 | tf_op jit(solution)/shard_map/ppermute | solution.py:37
  139.4 24.6 %collective-permute-start.17 = (bf16[512,1024]{1,0:T(8,128)(2,1)S(1)}, bf16[512,1024]{1,0:T(8,128)(2,1)}, u32[]{:S(2)}, u32[]{:S(2)}) collective-permute-start(bf16[512,1024]{1,0:T(8,128)(2,1)S(1)} %multiply_convert_fusion.4.refs_0_), channel_id=1, source_target_pairs={{0,8},{8,0},{1,9},{9,1},{2,10},{10,2},{3,11},{11,3},{4,12},{12,4},... | collective-permute-start | bytes 3145736 | tf_op jit(solution)/shard_map/ppermute | solution.py:37
  141.1 169.9 %reduce-scatter.4.cloned.1.call-start = ((), (), s32[]{:S(2)}) async-start(), calls=%async_computation.4 | async-start | bytes 1474560 | tf_op jit(solution)/shard_map/reduce_scatter | solution.py:97
  141.7 27.2 %collective-permute-start.19 = (bf16[512,1024]{1,0:T(8,128)(2,1)}, bf16[512,1024]{1,0:T(8,128)(2,1)}, u32[]{:S(2)}, u32[]{:S(2)}) collective-permute-start(bf16[512,1024]{1,0:T(8,128)(2,1)} %fusion.7.refs_4_), channel_id=1, source_target_pairs={{0,4},{4,0},{1,5},{5,1},{2,6},{6,2},{3,7},{7,3},{8,12},{12,8},{9,1... | collective-permute-start | bytes 3145736 | tf_op jit(solution)/shard_map/ppermute | solution.py:33
  141.8 27.2 %collective-permute-start.16 = (bf16[512,1024]{1,0:T(8,128)(2,1)S(1)}, bf16[512,1024]{1,0:T(8,128)(2,1)}, u32[]{:S(2)}, u32[]{:S(2)}) collective-permute-start(bf16[512,1024]{1,0:T(8,128)(2,1)S(1)} %multiply_convert_fusion.4.refs_0_), channel_id=1, source_target_pairs={{0,4},{4,0},{1,5},{5,1},{2,6},{6,2},{3,7},{7,3},{8,12},{12,8},{9,1... | collective-permute-start | bytes 3145736 | tf_op jit(solution)/shard_map/ppermute | solution.py:33
  164.0 5.0 %collective-permute-start.18 = (bf16[512,1024]{1,0:T(8,128)(2,1)}, bf16[512,1024]{1,0:T(8,128)(2,1)}, u32[]{:S(2)}, u32[]{:S(2)}) collective-permute-start(bf16[512,1024]{1,0:T(8,128)(2,1)} %collective-permute-done.17.refs_2_), channel_id=1, source_target_pairs={{0,4},{4,0},{1,5},{5,1},{2,6},{6,2},{3,7},{7,3},{8,12},{12,8},{9,1... | collective-permute-start | bytes 3145736 | tf_op jit(solution)/shard_map/ppermute | solution.py:33
  241.9 4.5 collective-permute-start.23
  244.3 28.7 %collective-permute-start.29 = (bf16[4,144,1024]{2,1,0:T(8,128)(2,1)}, bf16[4,144,1024]{2,1,0:T(8,128)(2,1)}, u32[]{:S(2)}, u32[]{:S(2)}) collective-permute-start(bf16[4,144,1024]{2,1,0:T(8,128)(2,1)} %dynamic-slice_bitcast_fusion.1), channel_id=1, source_target_pairs={{0,16},{16,0},{1,17},{17,1},{2,18},{18,2},{3,19},{19,3},{4,20},{20... | collective-permute-start | bytes 3538952 | tf_op jit(solution)/shard_map/ppermute | solution.py:41
  246.4 8.2 %copy-start.38 = (bf16[2048,2304]{1,0:T(8,128)(2,1)S(1)}, bf16[2048,2304]{1,0:T(8,128)(2,1)}, u32[]{:S(2)}) copy-start(bf16[2048,2304]{1,0:T(8,128)(2,1)} %get-tuple-element.25) | copy-start | bytes 28311556
  248.6 4.6 copy-start.4
  253.2 25.4 %collective-permute-start.24 = (bf16[512,1024]{1,0:T(8,128)(2,1)}, bf16[512,1024]{1,0:T(8,128)(2,1)S(1)}, u32[]{:S(2)}, u32[]{:S(2)}) collective-permute-start(bf16[512,1024]{1,0:T(8,128)(2,1)} %fusion.20), channel_id=1, source_target_pairs={{0,8},{8,0},{1,9},{9,1},{2,10},{10,2},{3,11},{11,3},{4,12},{12,4},... | collective-permute-start | bytes 3145736 | tf_op jit(solution)/shard_map/ppermute | solution.py:37
  276.2 140.4 %reduce-scatter.6.cloned.1.call-start = ((), (), s32[]{:S(2)}) async-start(), calls=%async_computation.5 | async-start | bytes 5308416 | tf_op jit(solution)/shard_map/reduce_scatter | solution.py:107
  276.2 5.3 %copy-start.5 = (f32[1024,1024]{1,0:T(8,128)S(1)}, f32[1024,1024]{1,0:T(8,128)}, u32[]{:S(2)}) copy-start(f32[1024,1024]{1,0:T(8,128)} %copy-done.4) | copy-start | bytes 12582916
  276.2 5.3 %copy-start.18 = (bf16[2,256,1024]{2,1,0:T(8,128)(2,1)S(1)}, bf16[2,256,1024]{2,1,0:T(8,128)(2,1)}, u32[]{:S(2)}) copy-start(bf16[2,256,1024]{2,1,0:T(8,128)(2,1)} %param.13) | copy-start | bytes 3145732
  281.5 28.9 %copy-start.7 = (bf16[2,256,1024]{2,1,0:T(8,128)(2,1)S(1)}, bf16[2,256,1024]{2,1,0:T(8,128)(2,1)}, u32[]{:S(2)}) copy-start(bf16[2,256,1024]{2,1,0:T(8,128)(2,1)} %param.11) | copy-start | bytes 3145732
  285.8 24.7 %collective-permute-start.25 = (bf16[512,1024]{1,0:T(8,128)(2,1)}, bf16[512,1024]{1,0:T(8,128)(2,1)}, u32[]{:S(2)}, u32[]{:S(2)}) collective-permute-start(bf16[512,1024]{1,0:T(8,128)(2,1)} %get-tuple-element.47), channel_id=1, source_target_pairs={{0,8},{8,0},{1,9},{9,1},{2,10},{10,2},{3,11},{11,3},{4,12},{12,4},... | collective-permute-start | bytes 3145736 | tf_op jit(solution)/shard_map/ppermute | solution.py:37
  287.2 27.9 %collective-permute-start.30 = (bf16[512,1024]{1,0:T(8,128)(2,1)}, bf16[512,1024]{1,0:T(8,128)(2,1)}, u32[]{:S(2)}, u32[]{:S(2)}) collective-permute-start(bf16[512,1024]{1,0:T(8,128)(2,1)} %get-tuple-element.47), channel_id=1, source_target_pairs={{0,4},{4,0},{1,5},{5,1},{2,6},{6,2},{3,7},{7,3},{8,12},{12,8},{9,1... | collective-permute-start | bytes 3145736 | tf_op jit(solution)/shard_map/ppermute | solution.py:33
  310.4 4.7 %collective-permute-start.26 = (bf16[512,1024]{1,0:T(8,128)(2,1)}, bf16[512,1024]{1,0:T(8,128)(2,1)}, u32[]{:S(2)}, u32[]{:S(2)}) collective-permute-start(bf16[512,1024]{1,0:T(8,128)(2,1)} %collective-permute-done.25), channel_id=1, source_target_pairs={{0,4},{4,0},{1,5},{5,1},{2,6},{6,2},{3,7},{7,3},{8,12},{12,8},{9,1... | collective-permute-start | bytes 3145736 | tf_op jit(solution)/shard_map/ppermute | solution.py:33
  311.0 138.1 %reduce-scatter.8.cloned.1.call-start = ((), (), s32[]{:S(2)}) async-start(), calls=%async_computation.6 | async-start | bytes 1474560 | tf_op jit(solution)/shard_map/reduce_scatter | solution.py:97
  335.7 3.9 copy-start.19
  337.1 17.6 %collective-permute-start.31 = (bf16[1024,1024]{1,0:T(8,128)(2,1)}, bf16[1024,1024]{1,0:T(8,128)(2,1)}, u32[]{:S(2)}, u32[]{:S(2)}) collective-permute-start(bf16[1024,1024]{1,0:T(8,128)(2,1)} %pad_maximum_fusion.6), channel_id=1, source_target_pairs={{0,4},{4,0},{1,5},{5,1},{2,6},{6,2},{3,7},{7,3},{8,12},{12,8},{9,1... | collective-permute-start | bytes 6291464 | tf_op jit(solution)/shard_map/ppermute | solution.py:33
  343.4 21.0 %collective-permute-start.27 = (bf16[1024,1024]{1,0:T(8,128)(2,1)}, bf16[1024,1024]{1,0:T(8,128)(2,1)}, u32[]{:S(2)}, u32[]{:S(2)}) collective-permute-start(bf16[1024,1024]{1,0:T(8,128)(2,1)} %pad_maximum_fusion.5), channel_id=1, source_target_pairs={{0,4},{4,0},{1,5},{5,1},{2,6},{6,2},{3,7},{7,3},{8,12},{12,8},{9,1... | collective-permute-start | bytes 6291464 | tf_op jit(solution)/shard_map/ppermute | solution.py:33
  356.8 5.1 %copy-start.16 = (bf16[2,4,4,32,768]{4,3,2,1,0:T(8,128)(2,1)S(1)}, bf16[2,4,4,32,768]{4,3,2,1,0:T(8,128)(2,1)}, u32[]{:S(2)}) copy-start(bf16[2,4,4,32,768]{4,3,2,1,0:T(8,128)(2,1)} %copy.71) | copy-start | bytes 4718596
  360.4 26.3 %collective-permute-start.32 = (bf16[512,1024]{1,0:T(8,128)(2,1)}, bf16[512,1024]{1,0:T(8,128)(2,1)}, u32[]{:S(2)}, u32[]{:S(2)}) collective-permute-start(bf16[512,1024]{1,0:T(8,128)(2,1)} %fusion.12), channel_id=1, source_target_pairs={{0,8},{8,0},{1,9},{9,1},{2,10},{10,2},{3,11},{11,3},{4,12},{12,4},... | collective-permute-start | bytes 3145736 | tf_op jit(solution)/shard_map/ppermute | solution.py:37
  363.8 54.5 %collective-permute-start.33 = (bf16[4,144,1024]{2,1,0:T(8,128)(2,1)}, bf16[4,144,1024]{2,1,0:T(8,128)(2,1)}, u32[]{:S(2)}, u32[]{:S(2)}) collective-permute-start(bf16[4,144,1024]{2,1,0:T(8,128)(2,1)} %dynamic-slice_bitcast_fusion), channel_id=1, source_target_pairs={{0,16},{16,0},{1,17},{17,1},{2,18},{18,2},{3,19},{19,3},{4,20},{20... | collective-permute-start | bytes 3538952 | tf_op jit(solution)/shard_map/ppermute | solution.py:41
  371.8 17.7 %copy-start.3 = (f32[1024,1024]{1,0:T(8,128)S(1)}, f32[1024,1024]{1,0:T(8,128)}, u32[]{:S(2)}) copy-start(f32[1024,1024]{1,0:T(8,128)} %copy-done.2) | copy-start | bytes 12582916
  371.8 51.8 %collective-permute-start.28 = (bf16[512,1024]{1,0:T(8,128)(2,1)}, bf16[512,1024]{1,0:T(8,128)(2,1)}, u32[]{:S(2)}, u32[]{:S(2)}) collective-permute-start(bf16[512,1024]{1,0:T(8,128)(2,1)} %fusion.15), channel_id=1, source_target_pairs={{0,8},{8,0},{1,9},{9,1},{2,10},{10,2},{3,11},{11,3},{4,12},{12,4},... | collective-permute-start | bytes 3145736 | tf_op jit(solution)/shard_map/ppermute | solution.py:37
  421.7 6.1 %collective-permute-start.37 = (bf16[32,2304]{1,0:T(8,128)(2,1)S(1)}, bf16[32,2304]{1,0:T(8,128)(2,1)S(1)}, u32[]{:S(2)}, u32[]{:S(2)}) collective-permute-start(bf16[32,2304]{1,0:T(8,128)(2,1)S(1)} %get-tuple-element.78), channel_id=1, source_target_pairs={{0,12},{4,8},{8,4},{12,0},{1,13},{5,9},{9,5},{13,1},{2,14},{6,10},... | collective-permute-start | bytes 442376 | tf_op jit(solution)/shard_map/ppermute | solution.py:45
  422.3 8.8 %collective-permute-start.38 = (bf16[32,2304]{1,0:T(8,128)(2,1)S(1)}, bf16[32,2304]{1,0:T(8,128)(2,1)S(1)}, u32[]{:S(2)}, u32[]{:S(2)}) collective-permute-start(bf16[32,2304]{1,0:T(8,128)(2,1)S(1)} %get-tuple-element.79), channel_id=1, source_target_pairs={{0,8},{4,12},{8,0},{12,4},{1,9},{5,13},{9,1},{13,5},{2,10},{6,14},... | collective-permute-start | bytes 442376 | tf_op jit(solution)/shard_map/ppermute | solution.py:45
  423.3 7.8 %collective-permute-start.39 = (bf16[32,2304]{1,0:T(8,128)(2,1)S(1)}, bf16[32,2304]{1,0:T(8,128)(2,1)S(1)}, u32[]{:S(2)}, u32[]{:S(2)}) collective-permute-start(bf16[32,2304]{1,0:T(8,128)(2,1)S(1)} %get-tuple-element.77), channel_id=1, source_target_pairs={{0,4},{4,0},{8,12},{12,8},{1,5},{5,1},{9,13},{13,9},{2,6},{6,2},{1... | collective-permute-start | bytes 442376 | tf_op jit(solution)/shard_map/ppermute | solution.py:45
  436.0 20.8 %copy-start.33 = (bf16[32,3072]{1,0:T(8,128)(2,1)S(1)}, bf16[32,3072]{1,0:T(8,128)(2,1)}, u32[]{:S(2)}) copy-start(bf16[32,3072]{1,0:T(8,128)(2,1)} %param.15) | copy-start | bytes 589828
  450.8 4.1 collective-permute-start.34
  451.6 4.5 collective-permute-start.35
  452.4 3.7 collective-permute-start.36
  452.7 4.2 copy-start.37
  (21 other events, 49.2 us)
Sparse Core Ops, SparseCore 0:
  19.7 52.3 all-gather.7
  76.8 81.3 all-gather.9
  160.4 50.2 all-gather.5
  276.3 27.7 reduce-scatter.3
  311.1 105.3 reduce-scatter.5
  421.8 27.2 reduce-scatter.7

commit v10 on v7

--- a/solution.py
+++ b/solution.py
@@ -120,24 +120,14 @@
 
 
 def backward_kernel(
-    grad_ref,
-    hidden_ref,
-    silu_ref,
-    slope_ref,
-    pair_ref,
-    down_ref,
-    token_ref,
-    pair_grad_ref,
-    normed_ref,
-    out_ref,
+    grad_ref, silu_ref, slope_ref, pair_ref, down_ref, token_ref, pair_grad_ref, normed_ref
 ):
     del token_ref
-    width = hidden_ref.shape[1]
+    width = silu_ref.shape[1]
     hidden_grad = back_dot(grad_ref[...], down_ref[...])
     pair_grad_ref[:, :width] = (hidden_grad * slope_ref[...].astype(f32)).astype(bf16)
     pair_grad_ref[:, width:] = (hidden_grad * silu_ref[...].astype(f32)).astype(bf16)
     normed_ref[...] = back_dot(pair_grad_ref[...], pair_ref[...]).astype(bf16)
-    out_ref[...] = forward_dot(hidden_ref[...], down_ref[...]).astype(bf16)
 
 
 def by_rows(kernel, tile, steps, rowed, whole, tokens, columns, flops, transcendentals):
@@ -322,15 +312,15 @@
     )
     down_part = rows_dot(hidden, ffn_grad).astype(bf16)
     grad_down = scatter(down_part.reshape(groups, slots, hidden_share, features))
-    pair_grad, normed_part, out_part = by_rows(
+    pair_grad, normed_part = by_rows(
         backward_kernel,
         ROW_TILE,
         team_count // ROW_TILE,
-        [ffn_grad, hidden, silu, slope],
+        [ffn_grad, silu, slope],
         [pair_full, down_full],
         [down_part],
-        [2 * hid, features, features],
-        4 * unit,
+        [2 * hid, features],
+        3 * unit,
         0,
     )
 
@@ -375,10 +365,11 @@
         conv_rows.astype(bf16),
         ((0, 0), (0, 0), (0, EXTRA_ROWS - 1), (0, features - taps * share)),
     )
-    pair_sum = scatter(pair_part, projected_grad[-1:])
+    pair_sum = scatter(pair_part)
     first_weighted, first_sent = team_sum(back_dot(projected_grad, in_full).astype(bf16))
     input_grad = middle_grad + norm_back(inputs, inverse_rms(inputs), norm_full * first_weighted)
     input_grad = input_grad.astype(bf16)
+    out_part = forward_dot(hidden, down_full).astype(bf16)
     out_sum, _ = team_sum(after(out_part, mixer_grad[-1:]))
     block_out = (middle + live * out_sum).astype(bf16)
     first_sum = scatter(
@@ -387,7 +378,6 @@
         ),
         pair_sum[:1],
         first_sent,
-        block_out[:1],
     )
 
     def own_rows(summed, parts, team, run):

time: 495 us -> 476 us (0.962)
  waiting for transfers between devices: 213 us -> 185 us
  local copies, waits for them, and re-layouts: 51.6 us -> 62.7 us
  matrix products: 51.3 us -> 59.9 us
  Pallas kernels: 45.8 us -> 39.2 us
    reduce_scatter x3, waiting for transfers between devices: 12.7 us -> 0.02 us  [scatter(): return lax.psum_scatter(summed, 's', scatter_dimension=0, tiled=False)]
    ppermute x10, waiting for transfers between devices: 101 us -> 91.3 us  [swap_chip(): return lax.ppermute(values, 'x', [(0, 1), (1, 0)])]
    dot_general x2 -> x3, matrix products: 8.63 us -> 17 us  [forward_dot(): return jnp.dot(left_side, right_side, preferred_element_type=f32)]
    pallas_call x2, Pallas kernels: 45.8 us -> 39.2 us  [by_rows(): pl.pallas_call(kernel, grid=(steps,), in_specs=[row_block(value.shape[1])...]
    reshape x16, local copies, waits for them, and re-layouts: 0.94 us -> 6.56 us  [own_rows(): block.reshape(share, parts, -1, 1, run)]
    unnamed x94 -> x102, local copies, waits for them, and re-layouts: 15.8 us -> 17 us
  transfers between devices with their start and end apart: 47 -> 47, of which waited for: 20 -> 17; matrix products, arithmetic and copies ran while one was open for 31% -> 37% of each run, Pallas kernels for 4% -> 4%
where the time goes in v10:
time: 476 us; the launch traced here: 471 us
  waiting for transfers between devices  185 us (39%)
  other arithmetic  76 us (16%)
  local copies, waits for them, and re-layouts  62.7 us (13%)
  matrix products  59.9 us (13%)
  Pallas kernels  39.2 us (8%)
  starting transfers between devices  28.6 us (6%)
  between operations  19.5 us (4%)
    ppermute x10, waiting for transfers between devices, swap_chip(): return lax.ppermute(values, 'x', [(0, 1), (1, 0)])  91.3 us
    ppermute x12, waiting for transfers between devices, swap_far(): lax.ppermute(values, ('x', 'c'), [(i, i ^ distance) for i in range(TEAM)])  50 us
    pallas_call x2, Pallas kernels, by_rows(): pl.pallas_call(kernel, grid=(steps,), in_specs=[row_block(value.shape[1])...  39.2 us
    dot_general x4, matrix products, rows_dot(): lax.dot_general(left_side, right_side, (((0,), (0,)), ((), ())), preferre...  32.1 us
    ppermute x3, waiting for transfers between devices, swap_row(): return lax.ppermute(values, 'y', [(0, 1), (1, 0)])  20 us
    dot_general x3, matrix products, forward_dot(): return jnp.dot(left_side, right_side, preferred_element_type=f32)  17 us
    unnamed x102, local copies, waits for them, and re-layouts  17 us
    all_gather x1, waiting for transfers between devices, per_device(): down_full = lax.all_gather(down_weight, ('g', 'y', 's'), axis=0, tiled=True)  15.9 us
  transfers between devices with their start and end apart: 47, of which 17 were waited for; matrix products, arithmetic and copies ran while one was open for 37% of the time, Pallas kernels for 4%

profile of v10, /device:TPU:0, one launch (start us, length us, event | category | flops | bytes accessed | tf_op | source)
XLA Modules:
  0.0 470.7 jit_solution(11245798714561953234)
XLA Ops:
  8.1 2.9 collective-permute-start.6
  12.8 2.0 collective-permute-start.4
  21.4 1.7 collective-permute-start.9
  25.4 1.8 collective-permute-start.20
  27.6 44.8 %collective-permute-done.20 = bf16[32,2304]{1,0:T(8,128)(2,1)S(1)} collective-permute-done((bf16[32,2304]{1,0:T(8,128)(2,1)S(1)}, bf16[32,2304]{1,0:T(8,128)(2,1)S(1)}, u32[]{:S(2)}, u32[]{:S(2)}) %collective-permute-start.20) | collective-permute-done | bytes 147488 | tf_op jit(solution)/shard_map/ppermute | solution.py:45
  73.5 2.3 collective-permute-done.21
  80.4 3.5 fusion
  83.9 1.5 slice.387
  89.0 7.4 %fusion.28 = f32[2048,768]{1,0:T(8,128)S(1)} fusion(bf16[1024,768]{1,0:T(8,128)(2,1)S(1)} %bitcast.174, f32[1024]{0:T(1024)S(1)} %mul.328, f32[2048]{0:T(1024)S(1)} %add_rsqrt_fusion, bf16[512,1024]{1,0:T(8,128)(2,1)} %copy-done.37, bf16[512,1024]{1,0:T(8,128)(2,1)} %collective-permute-done.1, bf16[512,1024]{1,0:T(8,128)(2,1)} %copy-done.36, ...), kind=kOutput, calls=%fused_computation.81 | convolution fusion | flops 3244294144 | bytes 12070912 | tf_op jit(solution)/shard_map/dot_general | solution.py:17
  96.7 2.3 copy-done
  99.0 2.3 multiply_convert_fusion.5
  103.2 4.0 collective-permute-done.14
  108.1 1.6 copy-done.11
  109.7 1.7 collective-permute-start.15
  111.4 23.6 %collective-permute-done.15 = bf16[512,1024]{1,0:T(8,128)(2,1)} collective-permute-done((bf16[512,1024]{1,0:T(8,128)(2,1)S(1)}, bf16[512,1024]{1,0:T(8,128)(2,1)}, u32[]{:S(2)}, u32[]{:S(2)}) %collective-permute-start.15) | collective-permute-done | bytes 1048608 | tf_op jit(solution)/shard_map/ppermute | solution.py:37
  135.0 2.9 multiply_reduce_fusion.5
  138.2 1.7 collective-permute-start.17
  140.7 22.0 %collective-permute-done.17.refs_2_ = bf16[512,1024]{1,0:T(8,128)(2,1)} collective-permute-done((bf16[512,1024]{1,0:T(8,128)(2,1)S(1)}, bf16[512,1024]{1,0:T(8,128)(2,1)}, u32[]{:S(2)}, u32[]{:S(2)}) %collective-permute-start.17) | collective-permute-done | bytes 1048608 | tf_op jit(solution)/shard_map/ppermute | solution.py:37
  162.7 4.9 %copy.69 = bf16[2,4,4,32,2304]{4,3,1,2,0:T(8,128)(2,1)} copy(bf16[2,4,4,32,2304]{4,3,2,1,0:T(8,128)(2,1)} %bitcast.162) | data formatting | bytes 9437184 | tf_op jit(solution)/shard_map/reshape | solution.py:269
  167.6 17.6 %shard_map.186 = (bf16[2048,1152]{1,0:T(8,128)(2,1)}, bf16[2048,1152]{1,0:T(8,128)(2,1)}, bf16[2048,1152]{1,0:T(8,128)(2,1)}, bf16[2048,1024]{1,0:T(8,128)(2,1)}, bf16[2048,1024]{1,0:T(8,128)(2,1)}) custom-call(bf16[512,1024]{1,0:T(8,128)(2,1)S(1)} %multiply_convert_fusion.4.refs_0_, bf16[512,1024]{1,0:T(8,128)(2,1)} %collective-permute-done.16.refs_1_, ...), custom_call_target="tpu_custom_call" | custom-call | flops 9663676416 | bytes 35651584 | tf_op jit(solution)/shard_map/pallas_call | solution.py:140
  185.2 9.6 %convolution_convert_fusion.1.token_ref = bf16[1152,1024]{1,0:T(8,128)(2,1)} fusion(bf16[2048,1152]{1,0:T(8,128)(2,1)} %get-tuple-element.17, bf16[2048,1024]{1,0:T(8,128)(2,1)} %get-tuple-element.18.grad_ref), kind=kOutput, calls=%fused_computation.13 | convolution fusion | flops 4833017856 | bytes 11272192 | tf_op jit(solution)/shard_map/dot_general | solution.py:21
  194.9 15.9 %all-gather.6.cloned.1.call-done.down_ref = bf16[1152,1024]{1,0:T(8,128)(2,1)} async-done(((bf16[144,1024]{1,0:T(8,128)(2,1)}), bf16[1152,1024]{1,0:T(8,128)(2,1)}) %all-gather.6.cloned.1.call-update) | async-done | bytes 2359312 | tf_op jit(solution)/shard_map/all_gather | solution.py:261
  210.7 21.7 %shard_map.187 = (bf16[2048,2304]{1,0:T(8,128)(2,1)}, bf16[2048,1024]{1,0:T(8,128)(2,1)}) custom-call(bf16[2048,1024]{1,0:T(8,128)(2,1)} %get-tuple-element.18.grad_ref, bf16[2048,1152]{1,0:T(8,128)(2,1)} %get-tuple-element.19.silu_ref, bf16[2048,1152]{1,0:T(8,128)(2,1)} %get-tuple-element.20.slope_ref, bf16[1024,2304]{1,0:T(8,128)(2,1)} %bitcast.164, ...), custom_call_target="tpu_custom_call" | custom-call | flops 14495514624 | bytes 34340864 | tf_op jit(solution)/shard_map/pallas_call | solution.py:140
  232.4 1.7 fusion.47
  234.1 1.5 pad_maximum_fusion.4
  235.6 2.4 dynamic-slice_bitcast_fusion.2
  238.5 1.6 collective-permute-done.23
  240.1 2.2 convert_element_type.319
  242.3 2.1 copy-done.4
  244.4 3.1 fusion.21
  249.0 12.4 %convolution_convert_fusion = bf16[1024,2304]{1,0:T(8,128)(2,1)S(1)} fusion(bf16[2048,1024]{1,0:T(8,128)(2,1)} %get-tuple-element.22, bf16[2048,2304]{1,0:T(8,128)(2,1)S(1)} %copy-done.46), kind=kOutput, calls=%fused_computation.5 | convolution fusion | flops 9666035712 | bytes 18350080 | tf_op jit(solution)/shard_map/dot_general | solution.py:21
  261.8 2.1 copy-done.8
  265.1 3.4 dynamic-slice_bitcast_fusion
  269.1 2.8 fusion.7
  272.9 3.3 multiply_reduce_fusion.4
  276.3 4.2 multiply_convert_fusion.3
  282.2 23.0 %collective-permute-done.25 = bf16[512,1024]{1,0:T(8,128)(2,1)} collective-permute-done((bf16[512,1024]{1,0:T(8,128)(2,1)}, bf16[512,1024]{1,0:T(8,128)(2,1)}, u32[]{:S(2)}, u32[]{:S(2)}) %collective-permute-start.25) | collective-permute-done | bytes 1048608 | tf_op jit(solution)/shard_map/ppermute | solution.py:37
  305.2 16.7 %collective-permute-done.34 = bf16[4,128,2304]{2,1,0:T(8,128)(2,1)} collective-permute-done((bf16[4,128,2304]{2,1,0:T(8,128)(2,1)}, bf16[4,128,2304]{2,1,0:T(8,128)(2,1)}, u32[]{:S(2)}, u32[]{:S(2)}) %collective-permute-start.34) | collective-permute-done | bytes 2359328 | tf_op jit(solution)/shard_map/ppermute | solution.py:41
  321.9 4.3 fusion.3
  330.4 8.4 %convert_add_fusion.1 = bf16[2048,1024]{1,0:T(8,128)(2,1)S(1)} fusion(bf16[]{:T(256)} %bitcast.30, bf16[2048,1152]{1,0:T(8,128)(2,1)} %get-tuple-element.17, bf16[1152,1024]{1,0:T(8,128)(2,1)} %all-gather.6.cloned.1.call-done.down_ref), kind=kOutput, calls=%fused_computation.12 | convolution fusion | flops 4833935360 | bytes 11272194 | tf_op jit(solution)/shard_map/dot_general | solution.py:17
  339.1 1.5 pad_maximum_fusion.5
  343.4 6.6 %multiply_reduce_fusion.2 = (bf16[256]{0:T(256)(128)(2,1)S(1)}, bf16[256]{0:T(256)(128)(2,1)S(1)}, bf16[256]{0:T(256)(128)(2,1)S(1)}, f32[2048,256]{1,0:T(8,128)S(1)}, bf16[2048,256]{1,0:T(8,128)(2,1)S(1)}) fusion(f32[2048,256]{1,0:T(8,128)S(1)} %copy-done.10, f32[2046,256]{1,0:T(8,128)S(1)} %bitcast.158, f32[2048]{0:T(1024)S(1)} %get-tuple-element.115, ...), kind=kOutput, calls=%fused_computation.63 | convolution fusion | flops 1096285440 | bytes 18364928 | tf_op jit(solution)/shard_map/dot_general | solution.py:27
  353.9 4.1 convolution_convert_fusion.3
  358.2 1.8 pad_maximum_fusion.6
  361.5 6.7 %convolution_convert_fusion.4 = bf16[1024,768]{1,0:T(8,128)(2,1)S(1)} fusion(bf16[2048,256]{1,0:T(8,128)(2,1)} %copy-done.35, bf16[2048,256]{1,0:T(8,128)(2,1)} %copy-done.45, bf16[2048,256]{1,0:T(8,128)(2,1)} %copy-done.34, f32[1024]{0:T(1024)S(1)} %mul.328, f32[2048]{0:T(1024)S(1)} %add_rsqrt_fusion, bf16[512,1024]{1,0:T(8,128)(2,1)} %copy-done.37, ...), kind=kOutput, calls=%fused_computation.79 | convolution fusion | flops 3254517760 | bytes 8925184 | tf_op jit(solution)/shard_map/dot_general | solution.py:21
  369.8 3.4 convolution_convert_fusion.5
  374.1 1.9 select_bitcast_fusion
  376.5 2.0 fusion.5
  385.7 2.1 collective-permute-done.39
  387.9 1.9 broadcast_select_fusion.17
  396.3 2.0 convert_element_type.342
  398.3 2.1 copy-done.2
  400.4 2.6 fusion.13
  406.1 3.4 collective-permute-done.33
  409.5 3.2 fusion.6
  413.8 1.9 copy.83
  415.7 3.5 reshape.468
  419.2 2.2 convert_element_type.328
  421.4 1.8 fusion.16
  426.4 3.0 collective-permute-done.32
  429.4 1.9 fusion.9
  431.4 18.8 %collective-permute-done.28 = bf16[512,1024]{1,0:T(8,128)(2,1)S(1)} collective-permute-done((bf16[512,1024]{1,0:T(8,128)(2,1)S(1)}, bf16[512,1024]{1,0:T(8,128)(2,1)S(1)}, u32[]{:S(2)}, u32[]{:S(2)}) %collective-permute-start.28) | collective-permute-done | bytes 1048608 | tf_op jit(solution)/shard_map/ppermute | solution.py:37
  450.2 2.7 fusion.20
  452.9 3.0 fusion.12
  (297 shorter events, 72.1 us)
Async XLA Ops:
  7.2 12.5 %copy-start.42 = (s32[2,256]{1,0:T(2,128)S(1)}, s32[2,256]{1,0:T(2,128)}, u32[]{:S(2)}) copy-start(s32[2,256]{1,0:T(2,128)} %param.12) | copy-start | bytes 6148
  7.2 13.0 %copy-start.19 = (bf16[2,256,1024]{2,1,0:T(8,128)(2,1)S(1)}, bf16[2,256,1024]{2,1,0:T(8,128)(2,1)}, u32[]{:S(2)}) copy-start(bf16[2,256,1024]{2,1,0:T(8,128)(2,1)} %param.13) | copy-start | bytes 3145732
  7.2 76.7 %all-gather.8.cloned.1.call-start = ((), (), s32[]{:S(2)}) async-start(), calls=%async_computation.7 | async-start | bytes 2654208 | tf_op jit(solution)/shard_map/all_gather | solution.py:255
  8.1 8.4 %collective-permute-start.6 = (bf16[1,64]{1,0:T(2,128)(2,1)S(1)}, bf16[1,64]{1,0:T(2,128)(2,1)S(1)}, u32[]{:S(2)}, u32[]{:S(2)}) collective-permute-start(bf16[1,64]{1,0:T(2,128)(2,1)S(1)} %maximum_bitcast_fusion.1), channel_id=1, source_target_pairs={{0,8},{8,0},{1,9},{9,1},{2,10},{10,2},{3,11},{11,3},{4,12},{12,4},... | collective-permute-start | bytes 392 | tf_op jit(solution)/shard_map/ppermute | solution.py:37
  11.0 6.1 %collective-permute-start.8 = (bf16[1,64]{1,0:T(2,128)(2,1)S(1)}, bf16[1,64]{1,0:T(2,128)(2,1)S(1)}, u32[]{:S(2)}, u32[]{:S(2)}) collective-permute-start(bf16[1,64]{1,0:T(2,128)(2,1)S(1)} %maximum_bitcast_fusion.1), channel_id=1, source_target_pairs={{0,4},{4,0},{1,5},{5,1},{2,6},{6,2},{3,7},{7,3},{8,12},{12,8},{9,1... | collective-permute-start | bytes 392 | tf_op jit(solution)/shard_map/ppermute | solution.py:33
  12.1 11.0 %copy-start.6 = (bf16[2,256,1024]{2,1,0:T(8,128)(2,1)S(1)}, bf16[2,256,1024]{2,1,0:T(8,128)(2,1)}, u32[]{:S(2)}) copy-start(bf16[2,256,1024]{2,1,0:T(8,128)(2,1)} %param.11) | copy-start | bytes 3145732
  12.1 11.3 %copy-start.30 = (bf16[32,4608]{1,0:T(8,128)(2,1)S(1)}, bf16[32,4608]{1,0:T(8,128)(2,1)}, u32[]{:S(2)}) copy-start(bf16[32,4608]{1,0:T(8,128)(2,1)} %param.19) | copy-start | bytes 884740
  12.5 6.2 %collective-permute-start.3 = (bf16[32,768]{1,0:T(8,128)(2,1)S(1)}, bf16[32,768]{1,0:T(8,128)(2,1)S(1)}, u32[]{:S(2)}, u32[]{:S(2)}) collective-permute-start(bf16[32,768]{1,0:T(8,128)(2,1)S(1)} %select_n.381), channel_id=1, source_target_pairs={{0,12},{4,8},{8,4},{12,0},{1,13},{5,9},{9,5},{13,1},{2,14},{6,10},... | collective-permute-start | bytes 147464 | tf_op jit(solution)/shard_map/ppermute | solution.py:45
  12.8 5.9 %collective-permute-start.4 = (bf16[32,768]{1,0:T(8,128)(2,1)S(1)}, bf16[32,768]{1,0:T(8,128)(2,1)S(1)}, u32[]{:S(2)}, u32[]{:S(2)}) collective-permute-start(bf16[32,768]{1,0:T(8,128)(2,1)S(1)} %select_n.385), channel_id=1, source_target_pairs={{0,8},{4,12},{8,0},{12,4},{1,9},{5,13},{9,1},{13,5},{2,10},{6,14},... | collective-permute-start | bytes 147464 | tf_op jit(solution)/shard_map/ppermute | solution.py:45
  14.8 3.9 collective-permute-start.5
  16.5 1.4 collective-permute-start.7
  19.6 143.1 %all-gather.10.cloned.1.call-start = ((), (), s32[]{:S(2)}) async-start(), calls=%async_computation.8 | async-start | bytes 5308416 | tf_op jit(solution)/shard_map/all_gather | solution.py:260
  19.7 5.5 %collective-permute-start.12 = (s32[512,1]{0,1:T(1,128)S(1)}, s32[512,1]{0,1:T(1,128)S(1)}, u32[]{:S(2)}, u32[]{:S(2)}) collective-permute-start(s32[512,1]{0,1:T(1,128)S(1)} %bitcast.197), channel_id=1, source_target_pairs={{0,8},{8,0},{1,9},{9,1},{2,10},{10,2},{3,11},{11,3},{4,12},{12,4},... | collective-permute-start | bytes 6152 | tf_op jit(solution)/shard_map/ppermute | solution.py:37
  19.9 7.3 %collective-permute-start.11 = (s32[512,1]{0,1:T(1,128)S(1)}, s32[512,1]{0,1:T(1,128)S(1)}, u32[]{:S(2)}, u32[]{:S(2)}) collective-permute-start(s32[512,1]{0,1:T(1,128)S(1)} %bitcast.198), channel_id=1, source_target_pairs={{0,4},{4,0},{1,5},{5,1},{2,6},{6,2},{3,7},{7,3},{8,12},{12,8},{9,1... | collective-permute-start | bytes 6152 | tf_op jit(solution)/shard_map/ppermute | solution.py:33
  21.4 51.6 %collective-permute-start.9 = (bf16[512,1024]{1,0:T(8,128)(2,1)}, bf16[512,1024]{1,0:T(8,128)(2,1)}, u32[]{:S(2)}, u32[]{:S(2)}) collective-permute-start(bf16[512,1024]{1,0:T(8,128)(2,1)} %fusion.8.refs_4_), channel_id=1, source_target_pairs={{0,8},{8,0},{1,9},{9,1},{2,10},{10,2},{3,11},{11,3},{4,12},{12,4},... | collective-permute-start | bytes 3145736 | tf_op jit(solution)/shard_map/ppermute | solution.py:37
  23.0 50.0 %collective-permute-start.1 = (bf16[512,1024]{1,0:T(8,128)(2,1)S(1)}, bf16[512,1024]{1,0:T(8,128)(2,1)}, u32[]{:S(2)}, u32[]{:S(2)}) collective-permute-start(bf16[512,1024]{1,0:T(8,128)(2,1)S(1)} %bitcast.148), channel_id=1, source_target_pairs={{0,8},{8,0},{1,9},{9,1},{2,10},{10,2},{3,11},{11,3},{4,12},{12,4},... | collective-permute-start | bytes 3145736 | tf_op jit(solution)/shard_map/ppermute | solution.py:37
  25.2 2.3 collective-permute-start.13
  25.4 47.0 %collective-permute-start.20 = (bf16[32,2304]{1,0:T(8,128)(2,1)S(1)}, bf16[32,2304]{1,0:T(8,128)(2,1)S(1)}, u32[]{:S(2)}, u32[]{:S(2)}) collective-permute-start(bf16[32,2304]{1,0:T(8,128)(2,1)S(1)} %get-tuple-element.81), channel_id=1, source_target_pairs={{0,12},{4,8},{8,4},{12,0},{1,13},{5,9},{9,5},{13,1},{2,14},{6,10},... | collective-permute-start | bytes 442376 | tf_op jit(solution)/shard_map/ppermute | solution.py:45
  27.2 48.7 %collective-permute-start.21 = (bf16[32,2304]{1,0:T(8,128)(2,1)S(1)}, bf16[32,2304]{1,0:T(8,128)(2,1)S(1)}, u32[]{:S(2)}, u32[]{:S(2)}) collective-permute-start(bf16[32,2304]{1,0:T(8,128)(2,1)S(1)} %get-tuple-element.47), channel_id=1, source_target_pairs={{0,8},{4,12},{8,0},{12,4},{1,9},{5,13},{9,1},{13,5},{2,10},{6,14},... | collective-permute-start | bytes 442376 | tf_op jit(solution)/shard_map/ppermute | solution.py:45
  27.6 48.3 %collective-permute-start.22 = (bf16[32,2304]{1,0:T(8,128)(2,1)S(1)}, bf16[32,2304]{1,0:T(8,128)(2,1)S(1)}, u32[]{:S(2)}, u32[]{:S(2)}) collective-permute-start(bf16[32,2304]{1,0:T(8,128)(2,1)S(1)} %get-tuple-element.80), channel_id=1, source_target_pairs={{0,4},{4,0},{8,12},{12,8},{1,5},{5,1},{9,13},{13,9},{2,6},{6,2},{1... | collective-permute-start | bytes 442376 | tf_op jit(solution)/shard_map/ppermute | solution.py:45
  72.3 8.0 %collective-permute-start = (bf16[512,1024]{1,0:T(8,128)(2,1)S(1)}, bf16[512,1024]{1,0:T(8,128)(2,1)S(1)}, u32[]{:S(2)}, u32[]{:S(2)}) collective-permute-start(bf16[512,1024]{1,0:T(8,128)(2,1)S(1)} %bitcast.149), channel_id=1, source_target_pairs={{0,4},{4,0},{1,5},{5,1},{2,6},{6,2},{3,7},{7,3},{8,12},{12,8},{9,1... | collective-permute-start | bytes 3145736 | tf_op jit(solution)/shard_map/ppermute | solution.py:33
  73.0 5.5 %collective-permute-start.10 = (bf16[512,1024]{1,0:T(8,128)(2,1)}, bf16[512,1024]{1,0:T(8,128)(2,1)}, u32[]{:S(2)}, u32[]{:S(2)}) collective-permute-start(bf16[512,1024]{1,0:T(8,128)(2,1)} %collective-permute-done.9.refs_6_), channel_id=1, source_target_pairs={{0,4},{4,0},{1,5},{5,1},{2,6},{6,2},{3,7},{7,3},{8,12},{12,8},{9,1... | collective-permute-start | bytes 3145736 | tf_op jit(solution)/shard_map/ppermute | solution.py:33
  73.0 7.4 %collective-permute-start.2 = (bf16[512,1024]{1,0:T(8,128)(2,1)}, bf16[512,1024]{1,0:T(8,128)(2,1)S(1)}, u32[]{:S(2)}, u32[]{:S(2)}) collective-permute-start(bf16[512,1024]{1,0:T(8,128)(2,1)} %collective-permute-done.1), channel_id=1, source_target_pairs={{0,4},{4,0},{1,5},{5,1},{2,6},{6,2},{3,7},{7,3},{8,12},{12,8},{9,1... | collective-permute-start | bytes 3145736 | tf_op jit(solution)/shard_map/ppermute | solution.py:33
  76.8 133.9 %all-gather.6.cloned.1.call-start = ((), (), s32[]{:S(2)}) async-start(), calls=%async_computation.3 | async-start | bytes 2654208 | tf_op jit(solution)/shard_map/all_gather | solution.py:261
  85.6 10.8 %copy-start.27 = (bf16[2,4,4,32,768]{4,3,2,1,0:T(8,128)(2,1)}, bf16[2,4,4,32,768]{4,3,2,1,0:T(8,128)(2,1)S(1)}, u32[]{:S(2)}) copy-start(bf16[2,4,4,32,768]{4,3,2,1,0:T(8,128)(2,1)S(1)} %copy.66) | copy-start | bytes 4718596
  89.0 12.3 %copy-start.24 = (bf16[8,32,1024]{2,1,0:T(8,128)(2,1)}, bf16[8,32,1024]{2,1,0:T(8,128)(2,1)S(1)}, u32[]{:S(2)}) copy-start(bf16[8,32,1024]{2,1,0:T(8,128)(2,1)S(1)} %pad_maximum_fusion.12) | copy-start | bytes 1572868
  103.0 4.2 collective-permute-start.14
  109.7 25.3 %collective-permute-start.15 = (bf16[512,1024]{1,0:T(8,128)(2,1)S(1)}, bf16[512,1024]{1,0:T(8,128)(2,1)}, u32[]{:S(2)}, u32[]{:S(2)}) collective-permute-start(bf16[512,1024]{1,0:T(8,128)(2,1)S(1)} %fusion.24), channel_id=1, source_target_pairs={{0,8},{8,0},{1,9},{9,1},{2,10},{10,2},{3,11},{11,3},{4,12},{12,4},... | collective-permute-start | bytes 3145736 | tf_op jit(solution)/shard_map/ppermute | solution.py:37
  138.2 24.5 %collective-permute-start.17 = (bf16[512,1024]{1,0:T(8,128)(2,1)S(1)}, bf16[512,1024]{1,0:T(8,128)(2,1)}, u32[]{:S(2)}, u32[]{:S(2)}) collective-permute-start(bf16[512,1024]{1,0:T(8,128)(2,1)S(1)} %multiply_convert_fusion.4.refs_0_), channel_id=1, source_target_pairs={{0,8},{8,0},{1,9},{9,1},{2,10},{10,2},{3,11},{11,3},{4,12},{12,4},... | collective-permute-start | bytes 3145736 | tf_op jit(solution)/shard_map/ppermute | solution.py:37
  139.9 186.5 %reduce-scatter.4.cloned.1.call-start = ((), (), s32[]{:S(2)}) async-start(), calls=%async_computation.4 | async-start | bytes 1474560 | tf_op jit(solution)/shard_map/reduce_scatter | solution.py:97
  140.2 27.5 %collective-permute-start.19 = (bf16[512,1024]{1,0:T(8,128)(2,1)}, bf16[512,1024]{1,0:T(8,128)(2,1)}, u32[]{:S(2)}, u32[]{:S(2)}) collective-permute-start(bf16[512,1024]{1,0:T(8,128)(2,1)} %fusion.8.refs_4_), channel_id=1, source_target_pairs={{0,4},{4,0},{1,5},{5,1},{2,6},{6,2},{3,7},{7,3},{8,12},{12,8},{9,1... | collective-permute-start | bytes 3145736 | tf_op jit(solution)/shard_map/ppermute | solution.py:33
  140.2 27.4 %collective-permute-start.16 = (bf16[512,1024]{1,0:T(8,128)(2,1)S(1)}, bf16[512,1024]{1,0:T(8,128)(2,1)}, u32[]{:S(2)}, u32[]{:S(2)}) collective-permute-start(bf16[512,1024]{1,0:T(8,128)(2,1)S(1)} %multiply_convert_fusion.4.refs_0_), channel_id=1, source_target_pairs={{0,4},{4,0},{1,5},{5,1},{2,6},{6,2},{3,7},{7,3},{8,12},{12,8},{9,1... | collective-permute-start | bytes 3145736 | tf_op jit(solution)/shard_map/ppermute | solution.py:33
  162.7 4.9 %collective-permute-start.18 = (bf16[512,1024]{1,0:T(8,128)(2,1)}, bf16[512,1024]{1,0:T(8,128)(2,1)}, u32[]{:S(2)}, u32[]{:S(2)}) collective-permute-start(bf16[512,1024]{1,0:T(8,128)(2,1)} %collective-permute-done.17.refs_2_), channel_id=1, source_target_pairs={{0,4},{4,0},{1,5},{5,1},{2,6},{6,2},{3,7},{7,3},{8,12},{12,8},{9,1... | collective-permute-start | bytes 3145736 | tf_op jit(solution)/shard_map/ppermute | solution.py:33
  235.6 4.5 collective-permute-start.23
  237.9 31.2 %collective-permute-start.29 = (bf16[4,144,1024]{2,1,0:T(8,128)(2,1)}, bf16[4,144,1024]{2,1,0:T(8,128)(2,1)}, u32[]{:S(2)}, u32[]{:S(2)}) collective-permute-start(bf16[4,144,1024]{2,1,0:T(8,128)(2,1)} %dynamic-slice_bitcast_fusion.2), channel_id=1, source_target_pairs={{0,16},{16,0},{1,17},{17,1},{2,18},{18,2},{3,19},{19,3},{4,20},{20... | collective-permute-start | bytes 3538952 | tf_op jit(solution)/shard_map/ppermute | solution.py:41
  240.1 8.9 %copy-start.46 = (bf16[2048,2304]{1,0:T(8,128)(2,1)S(1)}, bf16[2048,2304]{1,0:T(8,128)(2,1)}, u32[]{:S(2)}) copy-start(bf16[2048,2304]{1,0:T(8,128)(2,1)} %get-tuple-element.23) | copy-start | bytes 28311556
  247.5 25.4 %collective-permute-start.24 = (bf16[512,1024]{1,0:T(8,128)(2,1)}, bf16[512,1024]{1,0:T(8,128)(2,1)S(1)}, u32[]{:S(2)}, u32[]{:S(2)}) collective-permute-start(bf16[512,1024]{1,0:T(8,128)(2,1)} %fusion.21), channel_id=1, source_target_pairs={{0,8},{8,0},{1,9},{9,1},{2,10},{10,2},{3,11},{11,3},{4,12},{12,4},... | collective-permute-start | bytes 3145736 | tf_op jit(solution)/shard_map/ppermute | solution.py:37
  268.5 53.3 %collective-permute-start.34 = (bf16[4,128,2304]{2,1,0:T(8,128)(2,1)}, bf16[4,128,2304]{2,1,0:T(8,128)(2,1)}, u32[]{:S(2)}, u32[]{:S(2)}) collective-permute-start(bf16[4,128,2304]{2,1,0:T(8,128)(2,1)} %dynamic-slice_bitcast_fusion), channel_id=1, source_target_pairs={{0,16},{16,0},{1,17},{17,1},{2,18},{18,2},{3,19},{19,3},{4,20},{20... | collective-permute-start | bytes 7077896 | tf_op jit(solution)/shard_map/ppermute | solution.py:41
  271.9 102.2 %reduce-scatter.6.cloned.1.call-start = ((), (), s32[]{:S(2)}) async-start(), calls=%async_computation.5 | async-start | bytes 2949120 | tf_op jit(solution)/shard_map/reduce_scatter | solution.py:97
  280.5 24.7 %collective-permute-start.25 = (bf16[512,1024]{1,0:T(8,128)(2,1)}, bf16[512,1024]{1,0:T(8,128)(2,1)}, u32[]{:S(2)}, u32[]{:S(2)}) collective-permute-start(bf16[512,1024]{1,0:T(8,128)(2,1)} %get-tuple-element.45), channel_id=1, source_target_pairs={{0,8},{8,0},{1,9},{9,1},{2,10},{10,2},{3,11},{11,3},{4,12},{12,4},... | collective-permute-start | bytes 3145736 | tf_op jit(solution)/shard_map/ppermute | solution.py:37
  305.2 23.4 %collective-permute-start.26 = (bf16[512,1024]{1,0:T(8,128)(2,1)}, bf16[512,1024]{1,0:T(8,128)(2,1)}, u32[]{:S(2)}, u32[]{:S(2)}) collective-permute-start(bf16[512,1024]{1,0:T(8,128)(2,1)} %collective-permute-done.25), channel_id=1, source_target_pairs={{0,4},{4,0},{1,5},{5,1},{2,6},{6,2},{3,7},{7,3},{8,12},{12,8},{9,1... | collective-permute-start | bytes 3145736 | tf_op jit(solution)/shard_map/ppermute | solution.py:33
  326.2 129.7 %reduce-scatter.8.cloned.1.call-start = ((), (), s32[]{:S(2)}) async-start(), calls=%async_computation.6 | async-start | bytes 1474560 | tf_op jit(solution)/shard_map/reduce_scatter | solution.py:97
  326.3 16.2 %collective-permute-start.30 = (bf16[512,1024]{1,0:T(8,128)(2,1)}, bf16[512,1024]{1,0:T(8,128)(2,1)}, u32[]{:S(2)}, u32[]{:S(2)}) collective-permute-start(bf16[512,1024]{1,0:T(8,128)(2,1)} %get-tuple-element.45), channel_id=1, source_target_pairs={{0,4},{4,0},{1,5},{5,1},{2,6},{6,2},{3,7},{7,3},{8,12},{12,8},{9,1... | collective-permute-start | bytes 3145736 | tf_op jit(solution)/shard_map/ppermute | solution.py:33
  339.1 11.6 %slice-start = ((s8[6291456]{0:T(1024)(128)(4,1)}), s8[4194304]{0:T(1024)(128)(4,1)S(1)}, s32[]{:S(2)}) async-start(s8[6291456]{0:T(1024)(128)(4,1)} %bitcast.146), calls=%async_computation.9 | async-start | bytes 8388608
  342.0 77.2 %collective-permute-start.27 = (bf16[1024,1024]{1,0:T(8,128)(2,1)}, bf16[1024,1024]{1,0:T(8,128)(2,1)}, u32[]{:S(2)}, u32[]{:S(2)}) collective-permute-start(bf16[1024,1024]{1,0:T(8,128)(2,1)} %pad_maximum_fusion.5), channel_id=1, source_target_pairs={{0,4},{4,0},{1,5},{5,1},{2,6},{6,2},{3,7},{7,3},{8,12},{12,8},{9,1... | collective-permute-start | bytes 6291464 | tf_op jit(solution)/shard_map/ppermute | solution.py:33
  343.4 7.3 %slice-start.1 = ((s8[6291456]{0:T(1024)(128)(4,1)}), s8[2097152]{0:T(1024)(128)(4,1)S(1)}, s32[]{:S(2)}) async-start(s8[6291456]{0:T(1024)(128)(4,1)} %bitcast.146), calls=%async_computation.10 | async-start | bytes 4194304
  352.2 5.8 %copy-start.35 = (bf16[2048,256]{1,0:T(8,128)(2,1)}, bf16[2048,256]{1,0:T(8,128)(2,1)S(1)}, u32[]{:S(2)}) copy-start(bf16[2048,256]{1,0:T(8,128)(2,1)S(1)} %multiply_convert_fusion) | copy-start | bytes 3145732
  360.7 35.6 %collective-permute-start.31 = (bf16[1024,1024]{1,0:T(8,128)(2,1)}, bf16[1024,1024]{1,0:T(8,128)(2,1)}, u32[]{:S(2)}, u32[]{:S(2)}) collective-permute-start(bf16[1024,1024]{1,0:T(8,128)(2,1)} %pad_maximum_fusion.6), channel_id=1, source_target_pairs={{0,4},{4,0},{1,5},{5,1},{2,6},{6,2},{3,7},{7,3},{8,12},{12,8},{9,1... | collective-permute-start | bytes 6291464 | tf_op jit(solution)/shard_map/ppermute | solution.py:33
  376.0 7.0 %collective-permute-start.38 = (bf16[32,2304]{1,0:T(8,128)(2,1)S(1)}, bf16[32,2304]{1,0:T(8,128)(2,1)S(1)}, u32[]{:S(2)}, u32[]{:S(2)}) collective-permute-start(bf16[32,2304]{1,0:T(8,128)(2,1)S(1)} %get-tuple-element.76), channel_id=1, source_target_pairs={{0,12},{4,8},{8,4},{12,0},{1,13},{5,9},{9,5},{13,1},{2,14},{6,10},... | collective-permute-start | bytes 442376 | tf_op jit(solution)/shard_map/ppermute | solution.py:45
  376.5 6.5 %copy-start.40 = (bf16[1,144,1024]{2,1,0:T(8,128)(2,1)S(1)}, bf16[1,144,1024]{2,1,0:T(8,128)(2,1)}, u32[]{:S(2)}) copy-start(bf16[1,144,1024]{2,1,0:T(8,128)(2,1)} %reduce-scatter.4.cloned.1.call-done) | copy-start | bytes 884740
  381.0 28.5 %collective-permute-start.33 = (bf16[4,144,1024]{2,1,0:T(8,128)(2,1)}, bf16[4,144,1024]{2,1,0:T(8,128)(2,1)}, u32[]{:S(2)}, u32[]{:S(2)}) collective-permute-start(bf16[4,144,1024]{2,1,0:T(8,128)(2,1)} %dynamic-slice_bitcast_fusion.1), channel_id=1, source_target_pairs={{0,16},{16,0},{1,17},{17,1},{2,18},{18,2},{3,19},{19,3},{4,20},{20... | collective-permute-start | bytes 3538952 | tf_op jit(solution)/shard_map/ppermute | solution.py:41
  381.6 6.3 %collective-permute-start.39 = (bf16[32,2304]{1,0:T(8,128)(2,1)}, bf16[32,2304]{1,0:T(8,128)(2,1)}, u32[]{:S(2)}, u32[]{:S(2)}) collective-permute-start(bf16[32,2304]{1,0:T(8,128)(2,1)} %get-tuple-element.77), channel_id=1, source_target_pairs={{0,8},{4,12},{8,0},{12,4},{1,9},{5,13},{9,1},{13,5},{2,10},{6,14},... | collective-permute-start | bytes 442376 | tf_op jit(solution)/shard_map/ppermute | solution.py:45
  383.0 4.9 %collective-permute-start.40 = (bf16[32,2304]{1,0:T(8,128)(2,1)}, bf16[32,2304]{1,0:T(8,128)(2,1)}, u32[]{:S(2)}, u32[]{:S(2)}) collective-permute-start(bf16[32,2304]{1,0:T(8,128)(2,1)} %get-tuple-element.75), channel_id=1, source_target_pairs={{0,4},{4,0},{8,12},{12,8},{1,5},{5,1},{9,13},{13,9},{2,6},{6,2},{1... | collective-permute-start | bytes 442376 | tf_op jit(solution)/shard_map/ppermute | solution.py:45
  403.0 26.4 %collective-permute-start.32 = (bf16[512,1024]{1,0:T(8,128)(2,1)}, bf16[512,1024]{1,0:T(8,128)(2,1)}, u32[]{:S(2)}, u32[]{:S(2)}) collective-permute-start(bf16[512,1024]{1,0:T(8,128)(2,1)} %fusion.13), channel_id=1, source_target_pairs={{0,8},{8,0},{1,9},{9,1},{2,10},{10,2},{3,11},{11,3},{4,12},{12,4},... | collective-permute-start | bytes 3145736 | tf_op jit(solution)/shard_map/ppermute | solution.py:37
  406.1 6.6 %copy-start.39 = (bf16[32,2,2,1,576]{4,0,3,2,1:T(8,128)(2,1)S(1)}, bf16[32,2,2,1,576]{4,0,3,2,1:T(8,128)(2,1)}, u32[]{:S(2)}) copy-start(bf16[32,2,2,1,576]{4,0,3,2,1:T(8,128)(2,1)} %copy.81) | copy-start | bytes 442372
  419.2 10.2 %copy-start.17 = (bf16[2048,1024]{1,0:T(8,128)(2,1)S(1)}, bf16[2048,1024]{1,0:T(8,128)(2,1)}, u32[]{:S(2)}) copy-start(bf16[2048,1024]{1,0:T(8,128)(2,1)} %copy-done.16) | copy-start | bytes 12582916
  421.4 8.0 %copy-start.3 = (f32[1024,1024]{1,0:T(8,128)S(1)}, f32[1024,1024]{1,0:T(8,128)}, u32[]{:S(2)}) copy-start(f32[1024,1024]{1,0:T(8,128)} %copy-done.2) | copy-start | bytes 12582916
  423.2 26.9 %collective-permute-start.28 = (bf16[512,1024]{1,0:T(8,128)(2,1)S(1)}, bf16[512,1024]{1,0:T(8,128)(2,1)S(1)}, u32[]{:S(2)}, u32[]{:S(2)}) collective-permute-start(bf16[512,1024]{1,0:T(8,128)(2,1)S(1)} %fusion.16), channel_id=1, source_target_pairs={{0,8},{8,0},{1,9},{9,1},{2,10},{10,2},{3,11},{11,3},{4,12},{12,4},... | collective-permute-start | bytes 3145736 | tf_op jit(solution)/shard_map/ppermute | solution.py:37
  431.3 21.5 %copy-start.13 = (f32[512,1024]{1,0:T(8,128)S(1)}, f32[512,1024]{1,0:T(8,128)}, u32[]{:S(2)}) copy-start(f32[512,1024]{1,0:T(8,128)} %get-tuple-element.46) | copy-start | bytes 6291460
  455.9 7.0 %copy-start.38 = (bf16[32,3072]{1,0:T(8,128)(2,1)S(1)}, bf16[32,3072]{1,0:T(8,128)(2,1)}, u32[]{:S(2)}) copy-start(bf16[32,3072]{1,0:T(8,128)(2,1)} %param.15) | copy-start | bytes 589828
  455.9 7.2 %copy-start.44 = (bf16[32]{0:T(256)(128)(2,1)S(1)}, bf16[32]{0:T(256)(128)(2,1)}, u32[]{:S(2)}) copy-start(bf16[32]{0:T(256)(128)(2,1)} %param.14) | copy-start | bytes 196
  457.6 3.9 collective-permute-start.35
  457.6 4.6 collective-permute-start.36
  458.7 3.6 collective-permute-start.37
  (32 other events, 106.0 us)
Sparse Core Ops, SparseCore 0:
  19.7 52.3 all-gather.7
  76.9 81.3 all-gather.9
  160.4 50.2 all-gather.5
  272.0 27.7 reduce-scatter.3
  326.4 45.6 reduce-scatter.5
  412.8 27.9 reduce-scatter.7

commit v11 on v10

--- a/solution.py
+++ b/solution.py
@@ -355,6 +355,8 @@
             jnp.sum(conv_grad * mixed_two, axis=0),
         ]
     )
+    out_sum, _ = team_sum(forward_dot(hidden, down_full).astype(bf16))
+    block_out = (middle + live * out_sum).astype(bf16)
     in_part = by_owner(rows_dot(first_normed, projected_grad), TEAM)
     out_grad_part = rows_dot(mixer_in, mixer_grad).astype(bf16)
     out_grad_part = stacked(out_grad_part.reshape(groups, slots, share, features), chan)
@@ -362,16 +364,13 @@
         grad_conv_part.reshape(taps, groups, slots, share), (1, 2, 0, 3)
     ).reshape(groups, slots, 1, taps * share)
     conv_rows = jnp.pad(
-        conv_rows.astype(bf16),
+        after(conv_rows, block_out[:1]).astype(bf16),
         ((0, 0), (0, 0), (0, EXTRA_ROWS - 1), (0, features - taps * share)),
     )
     pair_sum = scatter(pair_part)
     first_weighted, first_sent = team_sum(back_dot(projected_grad, in_full).astype(bf16))
     input_grad = middle_grad + norm_back(inputs, inverse_rms(inputs), norm_full * first_weighted)
     input_grad = input_grad.astype(bf16)
-    out_part = forward_dot(hidden, down_full).astype(bf16)
-    out_sum, _ = team_sum(after(out_part, mixer_grad[-1:]))
-    block_out = (middle + live * out_sum).astype(bf16)
     first_sum = scatter(
         jnp.concatenate(
             [jnp.concatenate([in_part, out_grad_part], axis=3), conv_rows], axis=2

time: 476 us -> 459 us (0.964)
  local copies, waits for them, and re-layouts: 62.7 us -> 51.1 us
  other arithmetic: 76 us -> 67.6 us
    reduce_scatter x3, waiting for transfers between devices: 0.02 us -> 15.6 us  [scatter(): return lax.psum_scatter(summed, 's', scatter_dimension=0, tiled=False)]
    ppermute x3, waiting for transfers between devices: 20 us -> 6.6 us  [swap_row(): return lax.ppermute(values, 'y', [(0, 1), (1, 0)])]
    reshape x16, local copies, waits for them, and re-layouts: 6.56 us -> 0.94 us  [own_rows(): block.reshape(share, parts, -1, 1, run)]
    unnamed x102 -> x90, local copies, waits for them, and re-layouts: 17 us -> 16.9 us
  transfers between devices with their start and end apart: 47 -> 47, of which waited for: 17 -> 16; matrix products, arithmetic and copies ran while one was open for 37% -> 35% of each run, Pallas kernels for 4% -> 4%
where the time goes in v11:
time: 459 us; the launch traced here: 454 us
  waiting for transfers between devices  183 us (40%)
  other arithmetic  67.6 us (15%)
  matrix products  63.1 us (14%)
  local copies, waits for them, and re-layouts  51.1 us (11%)
  Pallas kernels  39.3 us (9%)
  starting transfers between devices  30.3 us (7%)
  between operations  19.5 us (4%)
    ppermute x10, waiting for transfers between devices, swap_chip(): return lax.ppermute(values, 'x', [(0, 1), (1, 0)])  90 us
    ppermute x12, waiting for transfers between devices, swap_far(): lax.ppermute(values, ('x', 'c'), [(i, i ^ distance) for i in range(TEAM)])  48.5 us
    pallas_call x2, Pallas kernels, by_rows(): pl.pallas_call(kernel, grid=(steps,), in_specs=[row_block(value.shape[1])...  39.3 us
    dot_general x4, matrix products, rows_dot(): lax.dot_general(left_side, right_side, (((0,), (0,)), ((), ())), preferre...  33.3 us
    unnamed x90, local copies, waits for them, and re-layouts  16.9 us
    dot_general x3, matrix products, forward_dot(): return jnp.dot(left_side, right_side, preferred_element_type=f32)  16.8 us
    all_gather x1, waiting for transfers between devices, per_device(): down_full = lax.all_gather(down_weight, ('g', 'y', 's'), axis=0, tiled=True)  15.9 us
    reduce_scatter x3, waiting for transfers between devices, scatter(): return lax.psum_scatter(summed, 's', scatter_dimension=0, tiled=False)  15.6 us
  transfers between devices with their start and end apart: 47, of which 16 were waited for; matrix products, arithmetic and copies ran while one was open for 35% of the time, Pallas kernels for 4%

profile of v11, /device:TPU:0, one launch (start us, length us, event | category | flops | bytes accessed | tf_op | source)
XLA Modules:
  0.0 453.7 jit_solution(12112321657949350198)
XLA Ops:
  8.1 2.9 collective-permute-start.6
  12.8 2.0 collective-permute-start.4
  21.4 1.7 collective-permute-start.9
  25.4 1.8 collective-permute-start.20
  27.6 44.8 %collective-permute-done.20 = bf16[32,2304]{1,0:T(8,128)(2,1)S(1)} collective-permute-done((bf16[32,2304]{1,0:T(8,128)(2,1)S(1)}, bf16[32,2304]{1,0:T(8,128)(2,1)S(1)}, u32[]{:S(2)}, u32[]{:S(2)}) %collective-permute-start.20) | collective-permute-done | bytes 147488 | tf_op jit(solution)/shard_map/ppermute | solution.py:45
  73.5 2.3 collective-permute-done.21
  80.4 3.5 fusion
  83.9 1.5 slice.387
  89.0 7.4 %fusion.28 = f32[2048,768]{1,0:T(8,128)S(1)} fusion(bf16[1024,768]{1,0:T(8,128)(2,1)S(1)} %bitcast.175, f32[1024]{0:T(1024)S(1)} %mul.326, f32[2048]{0:T(1024)S(1)} %add_rsqrt_fusion, bf16[512,1024]{1,0:T(8,128)(2,1)} %copy-done.32, bf16[512,1024]{1,0:T(8,128)(2,1)} %collective-permute-done.1, bf16[512,1024]{1,0:T(8,128)(2,1)} %copy-done.30, ...), kind=kOutput, calls=%fused_computation.81 | convolution fusion | flops 3244294144 | bytes 12070912 | tf_op jit(solution)/shard_map/dot_general | solution.py:17
  96.7 2.3 copy-done
  99.0 2.3 multiply_convert_fusion.5
  103.2 4.0 collective-permute-done.14
  108.0 1.6 copy-done.11
  109.7 1.7 collective-permute-start.15
  111.4 23.6 %collective-permute-done.15 = bf16[512,1024]{1,0:T(8,128)(2,1)} collective-permute-done((bf16[512,1024]{1,0:T(8,128)(2,1)S(1)}, bf16[512,1024]{1,0:T(8,128)(2,1)}, u32[]{:S(2)}, u32[]{:S(2)}) %collective-permute-start.15) | collective-permute-done | bytes 1048608 | tf_op jit(solution)/shard_map/ppermute | solution.py:37
  135.0 2.9 multiply_reduce_fusion.5
  138.2 1.7 collective-permute-start.17
  141.1 21.6 %collective-permute-done.17.refs_2_ = bf16[512,1024]{1,0:T(8,128)(2,1)} collective-permute-done((bf16[512,1024]{1,0:T(8,128)(2,1)S(1)}, bf16[512,1024]{1,0:T(8,128)(2,1)}, u32[]{:S(2)}, u32[]{:S(2)}) %collective-permute-start.17) | collective-permute-done | bytes 1048608 | tf_op jit(solution)/shard_map/ppermute | solution.py:37
  162.7 4.9 %copy.66 = bf16[2,4,4,32,2304]{4,3,1,2,0:T(8,128)(2,1)} copy(bf16[2,4,4,32,2304]{4,3,2,1,0:T(8,128)(2,1)} %bitcast.163) | data formatting | bytes 9437184 | tf_op jit(solution)/shard_map/reshape | solution.py:269
  167.6 17.6 %shard_map.186 = (bf16[2048,1152]{1,0:T(8,128)(2,1)}, bf16[2048,1152]{1,0:T(8,128)(2,1)}, bf16[2048,1152]{1,0:T(8,128)(2,1)}, bf16[2048,1024]{1,0:T(8,128)(2,1)}, bf16[2048,1024]{1,0:T(8,128)(2,1)}) custom-call(bf16[512,1024]{1,0:T(8,128)(2,1)S(1)} %multiply_convert_fusion.4.refs_0_, bf16[512,1024]{1,0:T(8,128)(2,1)} %collective-permute-done.16.refs_1_, ...), custom_call_target="tpu_custom_call" | custom-call | flops 9663676416 | bytes 35651584 | tf_op jit(solution)/shard_map/pallas_call | solution.py:140
  185.3 9.7 %convolution_convert_fusion.1.token_ref = bf16[1152,1024]{1,0:T(8,128)(2,1)} fusion(bf16[2048,1152]{1,0:T(8,128)(2,1)} %get-tuple-element.17, bf16[2048,1024]{1,0:T(8,128)(2,1)} %get-tuple-element.18.grad_ref), kind=kOutput, calls=%fused_computation.12 | convolution fusion | flops 4833017856 | bytes 11272192 | tf_op jit(solution)/shard_map/dot_general | solution.py:21
  194.9 15.9 %all-gather.6.cloned.1.call-done.down_ref = bf16[1152,1024]{1,0:T(8,128)(2,1)} async-done(((bf16[144,1024]{1,0:T(8,128)(2,1)}), bf16[1152,1024]{1,0:T(8,128)(2,1)}) %all-gather.6.cloned.1.call-update) | async-done | bytes 2359312 | tf_op jit(solution)/shard_map/all_gather | solution.py:261
  210.8 21.7 %shard_map.187 = (bf16[2048,2304]{1,0:T(8,128)(2,1)}, bf16[2048,1024]{1,0:T(8,128)(2,1)}) custom-call(bf16[2048,1024]{1,0:T(8,128)(2,1)} %get-tuple-element.18.grad_ref, bf16[2048,1152]{1,0:T(8,128)(2,1)} %get-tuple-element.19.silu_ref, bf16[2048,1152]{1,0:T(8,128)(2,1)} %get-tuple-element.20.slope_ref, bf16[1024,2304]{1,0:T(8,128)(2,1)} %bitcast.165, ...), custom_call_target="tpu_custom_call" | custom-call | flops 14495514624 | bytes 34340864 | tf_op jit(solution)/shard_map/pallas_call | solution.py:140
  232.4 1.7 fusion.48
  234.1 1.5 pad_maximum_fusion.5
  235.6 8.1 %convolution_convert_fusion.2 = bf16[2048,1024]{1,0:T(8,128)(2,1)S(1)} fusion(bf16[2048,1152]{1,0:T(8,128)(2,1)} %get-tuple-element.17, bf16[1152,1024]{1,0:T(8,128)(2,1)} %all-gather.6.cloned.1.call-done.down_ref), kind=kOutput, calls=%fused_computation.13 | convolution fusion | flops 4833935360 | bytes 11272192 | tf_op jit(solution)/shard_map/dot_general | solution.py:17
  244.7 2.2 copy-done.21
  248.7 2.0 convert_element_type.333
  250.7 2.0 copy-done.4
  252.7 2.7 fusion.16
  255.4 1.5 collective-permute-start.26
  256.9 13.0 %convolution_convert_fusion = bf16[1024,2304]{1,0:T(8,128)(2,1)S(1)} fusion(bf16[2048,1024]{1,0:T(8,128)(2,1)S(1)} %copy-done.40, bf16[2048,2304]{1,0:T(8,128)(2,1)} %get-tuple-element.23), kind=kOutput, calls=%fused_computation.5 | convolution fusion | flops 9666035712 | bytes 18350080 | tf_op jit(solution)/shard_map/dot_general | solution.py:21
  270.8 2.3 copy-done.10
  275.0 1.6 dynamic-slice_bitcast_fusion
  277.8 1.5 collective-permute-start.34
  279.4 3.1 fusion.7
  282.6 2.9 multiply_reduce_fusion.4
  285.5 18.0 %collective-permute-done.24 = bf16[512,1024]{1,0:T(8,128)(2,1)} collective-permute-done((bf16[512,1024]{1,0:T(8,128)(2,1)}, bf16[512,1024]{1,0:T(8,128)(2,1)}, u32[]{:S(2)}, u32[]{:S(2)}) %collective-permute-start.24) | collective-permute-done | bytes 1048608 | tf_op jit(solution)/shard_map/ppermute | solution.py:37
  303.5 4.9 %multiply_convert_fusion.3 = (bf16[512,1024]{1,0:T(8,128)(2,1)}, f32[512,1024]{1,0:T(8,128)}, bf16[512,1024]{1,0:T(8,128)(2,1)}) fusion(f32[512]{0:T(512)S(1)} %compare_convert_fusion.2, f32[512,1024]{1,0:T(8,128)S(1)} %get-tuple-element.51, f32[512]{0:T(512)S(1)} %fusion.40, f32[]{:T(128)S(6)} %convert.32, bf16[512,1024]{1,0:T(8,128)(2,1)} %copy-done.20, ...), kind=kLoop, calls=%fused_computation.68 | loop fusion | flops 10485760 | bytes 15738884 | tf_op jit(solution)/shard_map/convert_element_type | solution.py:338
  308.4 1.5 collective-permute-start.29
  310.4 22.8 %collective-permute-done.29 = bf16[512,1024]{1,0:T(8,128)(2,1)} collective-permute-done((bf16[512,1024]{1,0:T(8,128)(2,1)}, bf16[512,1024]{1,0:T(8,128)(2,1)}, u32[]{:S(2)}, u32[]{:S(2)}) %collective-permute-start.29) | collective-permute-done | bytes 1048608 | tf_op jit(solution)/shard_map/ppermute | solution.py:37
  333.2 4.5 fusion.3
  341.8 9.4 %multiply_reduce_fusion.2 = (f32[256]{0:T(256)S(1)}, f32[256]{0:T(256)S(1)}, f32[256]{0:T(256)S(1)}, f32[2048,256]{1,0:T(8,128)S(1)}, bf16[2048,256]{1,0:T(8,128)(2,1)S(1)}) fusion(f32[2048,256]{1,0:T(8,128)} %copy-done.9, f32[2046,256]{1,0:T(8,128)} %bitcast.159, f32[2048]{0:T(1024)S(1)} %get-tuple-element.116, f32[2047,256]{1,0:T(8,128)} %bitcast.160, ...), kind=kOutput, calls=%fused_computation.63 | convolution fusion | flops 1096285440 | bytes 18366464 | tf_op jit(solution)/shard_map/dot_general | solution.py:27
  354.3 3.7 convolution_convert_fusion.4
  358.2 1.8 copy-done.16
  360.0 1.6 pad_maximum_fusion.6
  362.1 6.3 %convolution_convert_fusion.5 = bf16[1024,768]{1,0:T(8,128)(2,1)} fusion(bf16[2048,256]{1,0:T(8,128)(2,1)S(1)} %multiply_convert_fusion, bf16[2048,256]{1,0:T(8,128)(2,1)S(1)} %get-tuple-element.67, bf16[2048,256]{1,0:T(8,128)(2,1)S(1)} %get-tuple-element.43, f32[1024]{0:T(1024)S(1)} %mul.326, f32[2048]{0:T(1024)S(1)} %add_rsqrt_fusion, ...), kind=kOutput, calls=%fused_computation.79 | convolution fusion | flops 3254517760 | bytes 8925184 | tf_op jit(solution)/shard_map/dot_general | solution.py:21
  368.4 4.3 convolution_convert_fusion.6
  373.1 1.6 copy.68
  375.4 1.4 copy-done.12
  377.9 1.5 collective-permute-start.33
  380.2 5.3 %reduce-scatter.6.cloned.1.call-done = bf16[1,128,2304]{2,1,0:T(8,128)(2,1)} async-done(((bf16[4,128,2304]{2,1,0:T(8,128)(2,1)}), bf16[1,128,2304]{2,1,0:T(8,128)(2,1)}) %reduce-scatter.6.cloned.1.call-update) | async-done | bytes 589840 | tf_op jit(solution)/shard_map/reduce_scatter | solution.py:97
  387.3 1.9 select_bitcast_fusion
  391.6 2.0 copy-done.2
  393.6 2.6 fusion.13
  396.2 1.5 collective-permute-start.32
  399.6 6.6 %collective-permute-done.33 = bf16[4,144,1024]{2,1,0:T(8,128)(2,1)} collective-permute-done((bf16[4,144,1024]{2,1,0:T(8,128)(2,1)}, bf16[4,144,1024]{2,1,0:T(8,128)(2,1)}, u32[]{:S(2)}, u32[]{:S(2)}) %collective-permute-start.33) | collective-permute-done | bytes 1179680 | tf_op jit(solution)/shard_map/ppermute | solution.py:41
  406.2 3.2 fusion.6
  412.5 2.1 reshape.474
  414.6 2.6 add_reduce_fusion
  417.8 4.0 collective-permute-done.32
  421.7 2.8 fusion.9
  424.6 3.4 fusion.12
  428.0 10.3 %reduce-scatter.8.cloned.1.call-done = bf16[1,144,1024]{2,1,0:T(8,128)(2,1)} async-done(((bf16[4,144,1024]{2,1,0:T(8,128)(2,1)}), bf16[1,144,1024]{2,1,0:T(8,128)(2,1)}) %reduce-scatter.8.cloned.1.call-update) | async-done | bytes 294928 | tf_op jit(solution)/shard_map/reduce_scatter | solution.py:97
  (283 shorter events, 57.1 us)
Async XLA Ops:
  7.2 12.5 %copy-start.37 = (s32[2,256]{1,0:T(2,128)S(1)}, s32[2,256]{1,0:T(2,128)}, u32[]{:S(2)}) copy-start(s32[2,256]{1,0:T(2,128)} %param.12) | copy-start | bytes 6148
  7.2 13.0 %copy-start.17 = (bf16[2,256,1024]{2,1,0:T(8,128)(2,1)S(1)}, bf16[2,256,1024]{2,1,0:T(8,128)(2,1)}, u32[]{:S(2)}) copy-start(bf16[2,256,1024]{2,1,0:T(8,128)(2,1)} %param.13) | copy-start | bytes 3145732
  7.2 76.7 %all-gather.8.cloned.1.call-start = ((), (), s32[]{:S(2)}) async-start(), calls=%async_computation.7 | async-start | bytes 2654208 | tf_op jit(solution)/shard_map/all_gather | solution.py:255
  8.1 8.4 %collective-permute-start.6 = (bf16[1,64]{1,0:T(2,128)(2,1)S(1)}, bf16[1,64]{1,0:T(2,128)(2,1)S(1)}, u32[]{:S(2)}, u32[]{:S(2)}) collective-permute-start(bf16[1,64]{1,0:T(2,128)(2,1)S(1)} %maximum_bitcast_fusion), channel_id=1, source_target_pairs={{0,8},{8,0},{1,9},{9,1},{2,10},{10,2},{3,11},{11,3},{4,12},{12,4},... | collective-permute-start | bytes 392 | tf_op jit(solution)/shard_map/ppermute | solution.py:37
  11.0 6.1 %collective-permute-start.8 = (bf16[1,64]{1,0:T(2,128)(2,1)S(1)}, bf16[1,64]{1,0:T(2,128)(2,1)S(1)}, u32[]{:S(2)}, u32[]{:S(2)}) collective-permute-start(bf16[1,64]{1,0:T(2,128)(2,1)S(1)} %maximum_bitcast_fusion), channel_id=1, source_target_pairs={{0,4},{4,0},{1,5},{5,1},{2,6},{6,2},{3,7},{7,3},{8,12},{12,8},{9,1... | collective-permute-start | bytes 392 | tf_op jit(solution)/shard_map/ppermute | solution.py:33
  12.1 11.0 %copy-start.6 = (bf16[2,256,1024]{2,1,0:T(8,128)(2,1)S(1)}, bf16[2,256,1024]{2,1,0:T(8,128)(2,1)}, u32[]{:S(2)}) copy-start(bf16[2,256,1024]{2,1,0:T(8,128)(2,1)} %param.11) | copy-start | bytes 3145732
  12.1 11.3 %copy-start.26 = (bf16[32,4608]{1,0:T(8,128)(2,1)S(1)}, bf16[32,4608]{1,0:T(8,128)(2,1)}, u32[]{:S(2)}) copy-start(bf16[32,4608]{1,0:T(8,128)(2,1)} %param.19) | copy-start | bytes 884740
  12.5 6.2 %collective-permute-start.3 = (bf16[32,768]{1,0:T(8,128)(2,1)S(1)}, bf16[32,768]{1,0:T(8,128)(2,1)S(1)}, u32[]{:S(2)}, u32[]{:S(2)}) collective-permute-start(bf16[32,768]{1,0:T(8,128)(2,1)S(1)} %select_n.381), channel_id=1, source_target_pairs={{0,12},{4,8},{8,4},{12,0},{1,13},{5,9},{9,5},{13,1},{2,14},{6,10},... | collective-permute-start | bytes 147464 | tf_op jit(solution)/shard_map/ppermute | solution.py:45
  12.8 5.9 %collective-permute-start.4 = (bf16[32,768]{1,0:T(8,128)(2,1)S(1)}, bf16[32,768]{1,0:T(8,128)(2,1)S(1)}, u32[]{:S(2)}, u32[]{:S(2)}) collective-permute-start(bf16[32,768]{1,0:T(8,128)(2,1)S(1)} %select_n.385), channel_id=1, source_target_pairs={{0,8},{4,12},{8,0},{12,4},{1,9},{5,13},{9,1},{13,5},{2,10},{6,14},... | collective-permute-start | bytes 147464 | tf_op jit(solution)/shard_map/ppermute | solution.py:45
  14.8 3.9 collective-permute-start.5
  16.5 1.4 collective-permute-start.7
  19.6 143.1 %all-gather.10.cloned.1.call-start = ((), (), s32[]{:S(2)}) async-start(), calls=%async_computation.8 | async-start | bytes 5308416 | tf_op jit(solution)/shard_map/all_gather | solution.py:260
  19.7 5.5 %collective-permute-start.12 = (s32[512,1]{0,1:T(1,128)S(1)}, s32[512,1]{0,1:T(1,128)S(1)}, u32[]{:S(2)}, u32[]{:S(2)}) collective-permute-start(s32[512,1]{0,1:T(1,128)S(1)} %bitcast.198), channel_id=1, source_target_pairs={{0,8},{8,0},{1,9},{9,1},{2,10},{10,2},{3,11},{11,3},{4,12},{12,4},... | collective-permute-start | bytes 6152 | tf_op jit(solution)/shard_map/ppermute | solution.py:37
  19.9 7.3 %collective-permute-start.11 = (s32[512,1]{0,1:T(1,128)S(1)}, s32[512,1]{0,1:T(1,128)S(1)}, u32[]{:S(2)}, u32[]{:S(2)}) collective-permute-start(s32[512,1]{0,1:T(1,128)S(1)} %bitcast.199), channel_id=1, source_target_pairs={{0,4},{4,0},{1,5},{5,1},{2,6},{6,2},{3,7},{7,3},{8,12},{12,8},{9,1... | collective-permute-start | bytes 6152 | tf_op jit(solution)/shard_map/ppermute | solution.py:33
  21.4 51.6 %collective-permute-start.9 = (bf16[512,1024]{1,0:T(8,128)(2,1)}, bf16[512,1024]{1,0:T(8,128)(2,1)}, u32[]{:S(2)}, u32[]{:S(2)}) collective-permute-start(bf16[512,1024]{1,0:T(8,128)(2,1)} %fusion.8.refs_4_), channel_id=1, source_target_pairs={{0,8},{8,0},{1,9},{9,1},{2,10},{10,2},{3,11},{11,3},{4,12},{12,4},... | collective-permute-start | bytes 3145736 | tf_op jit(solution)/shard_map/ppermute | solution.py:37
  23.0 50.0 %collective-permute-start.1 = (bf16[512,1024]{1,0:T(8,128)(2,1)S(1)}, bf16[512,1024]{1,0:T(8,128)(2,1)}, u32[]{:S(2)}, u32[]{:S(2)}) collective-permute-start(bf16[512,1024]{1,0:T(8,128)(2,1)S(1)} %bitcast.149), channel_id=1, source_target_pairs={{0,8},{8,0},{1,9},{9,1},{2,10},{10,2},{3,11},{11,3},{4,12},{12,4},... | collective-permute-start | bytes 3145736 | tf_op jit(solution)/shard_map/ppermute | solution.py:37
  25.2 2.3 collective-permute-start.13
  25.4 47.0 %collective-permute-start.20 = (bf16[32,2304]{1,0:T(8,128)(2,1)S(1)}, bf16[32,2304]{1,0:T(8,128)(2,1)S(1)}, u32[]{:S(2)}, u32[]{:S(2)}) collective-permute-start(bf16[32,2304]{1,0:T(8,128)(2,1)S(1)} %get-tuple-element.82), channel_id=1, source_target_pairs={{0,12},{4,8},{8,4},{12,0},{1,13},{5,9},{9,5},{13,1},{2,14},{6,10},... | collective-permute-start | bytes 442376 | tf_op jit(solution)/shard_map/ppermute | solution.py:45
  27.2 48.7 %collective-permute-start.21 = (bf16[32,2304]{1,0:T(8,128)(2,1)S(1)}, bf16[32,2304]{1,0:T(8,128)(2,1)S(1)}, u32[]{:S(2)}, u32[]{:S(2)}) collective-permute-start(bf16[32,2304]{1,0:T(8,128)(2,1)S(1)} %get-tuple-element.47), channel_id=1, source_target_pairs={{0,8},{4,12},{8,0},{12,4},{1,9},{5,13},{9,1},{13,5},{2,10},{6,14},... | collective-permute-start | bytes 442376 | tf_op jit(solution)/shard_map/ppermute | solution.py:45
  27.6 48.3 %collective-permute-start.22 = (bf16[32,2304]{1,0:T(8,128)(2,1)S(1)}, bf16[32,2304]{1,0:T(8,128)(2,1)S(1)}, u32[]{:S(2)}, u32[]{:S(2)}) collective-permute-start(bf16[32,2304]{1,0:T(8,128)(2,1)S(1)} %get-tuple-element.81), channel_id=1, source_target_pairs={{0,4},{4,0},{8,12},{12,8},{1,5},{5,1},{9,13},{13,9},{2,6},{6,2},{1... | collective-permute-start | bytes 442376 | tf_op jit(solution)/shard_map/ppermute | solution.py:45
  72.3 8.0 %collective-permute-start = (bf16[512,1024]{1,0:T(8,128)(2,1)S(1)}, bf16[512,1024]{1,0:T(8,128)(2,1)S(1)}, u32[]{:S(2)}, u32[]{:S(2)}) collective-permute-start(bf16[512,1024]{1,0:T(8,128)(2,1)S(1)} %bitcast.150), channel_id=1, source_target_pairs={{0,4},{4,0},{1,5},{5,1},{2,6},{6,2},{3,7},{7,3},{8,12},{12,8},{9,1... | collective-permute-start | bytes 3145736 | tf_op jit(solution)/shard_map/ppermute | solution.py:33
  73.0 5.5 %collective-permute-start.10 = (bf16[512,1024]{1,0:T(8,128)(2,1)}, bf16[512,1024]{1,0:T(8,128)(2,1)}, u32[]{:S(2)}, u32[]{:S(2)}) collective-permute-start(bf16[512,1024]{1,0:T(8,128)(2,1)} %collective-permute-done.9.refs_6_), channel_id=1, source_target_pairs={{0,4},{4,0},{1,5},{5,1},{2,6},{6,2},{3,7},{7,3},{8,12},{12,8},{9,1... | collective-permute-start | bytes 3145736 | tf_op jit(solution)/shard_map/ppermute | solution.py:33
  73.0 7.4 %collective-permute-start.2 = (bf16[512,1024]{1,0:T(8,128)(2,1)}, bf16[512,1024]{1,0:T(8,128)(2,1)S(1)}, u32[]{:S(2)}, u32[]{:S(2)}) collective-permute-start(bf16[512,1024]{1,0:T(8,128)(2,1)} %collective-permute-done.1), channel_id=1, source_target_pairs={{0,4},{4,0},{1,5},{5,1},{2,6},{6,2},{3,7},{7,3},{8,12},{12,8},{9,1... | collective-permute-start | bytes 3145736 | tf_op jit(solution)/shard_map/ppermute | solution.py:33
  76.8 134.0 %all-gather.6.cloned.1.call-start = ((), (), s32[]{:S(2)}) async-start(), calls=%async_computation.3 | async-start | bytes 2654208 | tf_op jit(solution)/shard_map/all_gather | solution.py:261
  85.6 10.8 %copy-start.23 = (bf16[2,4,4,32,768]{4,3,2,1,0:T(8,128)(2,1)}, bf16[2,4,4,32,768]{4,3,2,1,0:T(8,128)(2,1)S(1)}, u32[]{:S(2)}) copy-start(bf16[2,4,4,32,768]{4,3,2,1,0:T(8,128)(2,1)S(1)} %copy.63) | copy-start | bytes 4718596
  89.0 12.3 %copy-start.22 = (bf16[8,32,1024]{2,1,0:T(8,128)(2,1)}, bf16[8,32,1024]{2,1,0:T(8,128)(2,1)S(1)}, u32[]{:S(2)}) copy-start(bf16[8,32,1024]{2,1,0:T(8,128)(2,1)S(1)} %pad_maximum_fusion.12) | copy-start | bytes 1572868
  102.9 4.2 collective-permute-start.14
  109.7 25.3 %collective-permute-start.15 = (bf16[512,1024]{1,0:T(8,128)(2,1)S(1)}, bf16[512,1024]{1,0:T(8,128)(2,1)}, u32[]{:S(2)}, u32[]{:S(2)}) collective-permute-start(bf16[512,1024]{1,0:T(8,128)(2,1)S(1)} %fusion.24), channel_id=1, source_target_pairs={{0,8},{8,0},{1,9},{9,1},{2,10},{10,2},{3,11},{11,3},{4,12},{12,4},... | collective-permute-start | bytes 3145736 | tf_op jit(solution)/shard_map/ppermute | solution.py:37
  138.2 24.6 %collective-permute-start.17 = (bf16[512,1024]{1,0:T(8,128)(2,1)S(1)}, bf16[512,1024]{1,0:T(8,128)(2,1)}, u32[]{:S(2)}, u32[]{:S(2)}) collective-permute-start(bf16[512,1024]{1,0:T(8,128)(2,1)S(1)} %multiply_convert_fusion.4.refs_0_), channel_id=1, source_target_pairs={{0,8},{8,0},{1,9},{9,1},{2,10},{10,2},{3,11},{11,3},{4,12},{12,4},... | collective-permute-start | bytes 3145736 | tf_op jit(solution)/shard_map/ppermute | solution.py:37
  139.9 199.7 %reduce-scatter.4.cloned.1.call-start = ((), (), s32[]{:S(2)}) async-start(), calls=%async_computation.4 | async-start | bytes 1474560 | tf_op jit(solution)/shard_map/reduce_scatter | solution.py:97
  140.5 27.1 %collective-permute-start.19 = (bf16[512,1024]{1,0:T(8,128)(2,1)}, bf16[512,1024]{1,0:T(8,128)(2,1)}, u32[]{:S(2)}, u32[]{:S(2)}) collective-permute-start(bf16[512,1024]{1,0:T(8,128)(2,1)} %fusion.8.refs_4_), channel_id=1, source_target_pairs={{0,4},{4,0},{1,5},{5,1},{2,6},{6,2},{3,7},{7,3},{8,12},{12,8},{9,1... | collective-permute-start | bytes 3145736 | tf_op jit(solution)/shard_map/ppermute | solution.py:33
  140.6 27.0 %collective-permute-start.16 = (bf16[512,1024]{1,0:T(8,128)(2,1)S(1)}, bf16[512,1024]{1,0:T(8,128)(2,1)}, u32[]{:S(2)}, u32[]{:S(2)}) collective-permute-start(bf16[512,1024]{1,0:T(8,128)(2,1)S(1)} %multiply_convert_fusion.4.refs_0_), channel_id=1, source_target_pairs={{0,4},{4,0},{1,5},{5,1},{2,6},{6,2},{3,7},{7,3},{8,12},{12,8},{9,1... | collective-permute-start | bytes 3145736 | tf_op jit(solution)/shard_map/ppermute | solution.py:33
  162.7 4.9 %collective-permute-start.18 = (bf16[512,1024]{1,0:T(8,128)(2,1)}, bf16[512,1024]{1,0:T(8,128)(2,1)}, u32[]{:S(2)}, u32[]{:S(2)}) collective-permute-start(bf16[512,1024]{1,0:T(8,128)(2,1)} %collective-permute-done.17.refs_2_), channel_id=1, source_target_pairs={{0,4},{4,0},{1,5},{5,1},{2,6},{6,2},{3,7},{7,3},{8,12},{12,8},{9,1... | collective-permute-start | bytes 3145736 | tf_op jit(solution)/shard_map/ppermute | solution.py:33
  235.6 13.1 %collective-permute-start.25 = (bf16[1024,1024]{1,0:T(8,128)(2,1)}, bf16[1024,1024]{1,0:T(8,128)(2,1)}, u32[]{:S(2)}, u32[]{:S(2)}) collective-permute-start(bf16[1024,1024]{1,0:T(8,128)(2,1)} %pad_maximum_fusion.5), channel_id=1, source_target_pairs={{0,4},{4,0},{1,5},{5,1},{2,6},{6,2},{3,7},{7,3},{8,12},{12,8},{9,1... | collective-permute-start | bytes 6291464 | tf_op jit(solution)/shard_map/ppermute | solution.py:33
  243.8 27.0 %copy-start.19 = (bf16[2048,1024]{1,0:T(8,128)(2,1)}, bf16[2048,1024]{1,0:T(8,128)(2,1)S(1)}, u32[]{:S(2)}) copy-start(bf16[2048,1024]{1,0:T(8,128)(2,1)S(1)} %convolution_convert_fusion.2) | copy-start | bytes 12582916
  244.2 26.2 %collective-permute-start.23 = (bf16[1024,1024]{1,0:T(8,128)(2,1)S(1)}, bf16[1024,1024]{1,0:T(8,128)(2,1)S(1)}, u32[]{:S(2)}, u32[]{:S(2)}) collective-permute-start(bf16[1024,1024]{1,0:T(8,128)(2,1)S(1)} %pad_maximum_fusion.4), channel_id=1, source_target_pairs={{0,4},{4,0},{1,5},{5,1},{2,6},{6,2},{3,7},{7,3},{8,12},{12,8},{9,1... | collective-permute-start | bytes 6291464 | tf_op jit(solution)/shard_map/ppermute | solution.py:33
  248.1 31.2 %collective-permute-start.27 = (bf16[4,144,1024]{2,1,0:T(8,128)(2,1)}, bf16[4,144,1024]{2,1,0:T(8,128)(2,1)}, u32[]{:S(2)}, u32[]{:S(2)}) collective-permute-start(bf16[4,144,1024]{2,1,0:T(8,128)(2,1)} %dynamic-slice_bitcast_fusion.2), channel_id=1, source_target_pairs={{0,16},{16,0},{1,17},{17,1},{2,18},{18,2},{3,19},{19,3},{4,20},{20... | collective-permute-start | bytes 3538952 | tf_op jit(solution)/shard_map/ppermute | solution.py:41
  255.4 27.1 %collective-permute-start.26 = (bf16[512,1024]{1,0:T(8,128)(2,1)}, bf16[512,1024]{1,0:T(8,128)(2,1)S(1)}, u32[]{:S(2)}, u32[]{:S(2)}) collective-permute-start(bf16[512,1024]{1,0:T(8,128)(2,1)} %fusion.16), channel_id=1, source_target_pairs={{0,8},{8,0},{1,9},{9,1},{2,10},{10,2},{3,11},{11,3},{4,12},{12,4},... | collective-permute-start | bytes 3145736 | tf_op jit(solution)/shard_map/ppermute | solution.py:37
  274.5 29.0 %collective-permute-start.24 = (bf16[512,1024]{1,0:T(8,128)(2,1)}, bf16[512,1024]{1,0:T(8,128)(2,1)}, u32[]{:S(2)}, u32[]{:S(2)}) collective-permute-start(bf16[512,1024]{1,0:T(8,128)(2,1)} %fusion.19), channel_id=1, source_target_pairs={{0,8},{8,0},{1,9},{9,1},{2,10},{10,2},{3,11},{11,3},{4,12},{12,4},... | collective-permute-start | bytes 3145736 | tf_op jit(solution)/shard_map/ppermute | solution.py:37
  277.8 55.4 %collective-permute-start.34 = (bf16[4,128,2304]{2,1,0:T(8,128)(2,1)}, bf16[4,128,2304]{2,1,0:T(8,128)(2,1)}, u32[]{:S(2)}, u32[]{:S(2)}) collective-permute-start(bf16[4,128,2304]{2,1,0:T(8,128)(2,1)} %dynamic-slice_bitcast_fusion), channel_id=1, source_target_pairs={{0,16},{16,0},{1,17},{17,1},{2,18},{18,2},{3,19},{19,3},{4,20},{20... | collective-permute-start | bytes 7077896 | tf_op jit(solution)/shard_map/ppermute | solution.py:41
  282.5 103.0 %reduce-scatter.6.cloned.1.call-start = ((), (), s32[]{:S(2)}) async-start(), calls=%async_computation.5 | async-start | bytes 2949120 | tf_op jit(solution)/shard_map/reduce_scatter | solution.py:97
  282.6 21.0 %copy-start.5 = (f32[1024,1024]{1,0:T(8,128)S(1)}, f32[1024,1024]{1,0:T(8,128)}, u32[]{:S(2)}) copy-start(f32[1024,1024]{1,0:T(8,128)} %copy-done.4) | copy-start | bytes 12582916
  282.6 21.0 %copy-start.18 = (bf16[2,256,1024]{2,1,0:T(8,128)(2,1)S(1)}, bf16[2,256,1024]{2,1,0:T(8,128)(2,1)}, u32[]{:S(2)}) copy-start(bf16[2,256,1024]{2,1,0:T(8,128)(2,1)} %param.13) | copy-start | bytes 3145732
  285.5 24.4 %copy-start.7 = (bf16[2,256,1024]{2,1,0:T(8,128)(2,1)S(1)}, bf16[2,256,1024]{2,1,0:T(8,128)(2,1)}, u32[]{:S(2)}) copy-start(bf16[2,256,1024]{2,1,0:T(8,128)(2,1)} %param.11) | copy-start | bytes 3145732
  308.4 24.8 %collective-permute-start.29 = (bf16[512,1024]{1,0:T(8,128)(2,1)}, bf16[512,1024]{1,0:T(8,128)(2,1)}, u32[]{:S(2)}, u32[]{:S(2)}) collective-permute-start(bf16[512,1024]{1,0:T(8,128)(2,1)} %get-tuple-element.45), channel_id=1, source_target_pairs={{0,8},{8,0},{1,9},{9,1},{2,10},{10,2},{3,11},{11,3},{4,12},{12,4},... | collective-permute-start | bytes 3145736 | tf_op jit(solution)/shard_map/ppermute | solution.py:37
  310.4 31.4 %collective-permute-start.28 = (bf16[512,1024]{1,0:T(8,128)(2,1)}, bf16[512,1024]{1,0:T(8,128)(2,1)}, u32[]{:S(2)}, u32[]{:S(2)}) collective-permute-start(bf16[512,1024]{1,0:T(8,128)(2,1)} %get-tuple-element.45), channel_id=1, source_target_pairs={{0,4},{4,0},{1,5},{5,1},{2,6},{6,2},{3,7},{7,3},{8,12},{12,8},{9,1... | collective-permute-start | bytes 3145736 | tf_op jit(solution)/shard_map/ppermute | solution.py:33
  333.2 8.6 %collective-permute-start.30 = (bf16[512,1024]{1,0:T(8,128)(2,1)}, bf16[512,1024]{1,0:T(8,128)(2,1)}, u32[]{:S(2)}, u32[]{:S(2)}) collective-permute-start(bf16[512,1024]{1,0:T(8,128)(2,1)} %collective-permute-done.29), channel_id=1, source_target_pairs={{0,4},{4,0},{1,5},{5,1},{2,6},{6,2},{3,7},{7,3},{8,12},{12,8},{9,1... | collective-permute-start | bytes 3145736 | tf_op jit(solution)/shard_map/ppermute | solution.py:33
  333.2 18.7 %slice-start = ((s8[6291456]{0:T(1024)(128)(4,1)}), s8[2097152]{0:T(1024)(128)(4,1)S(1)}, s32[]{:S(2)}) async-start(s8[6291456]{0:T(1024)(128)(4,1)} %bitcast.147), calls=%async_computation.9 | async-start | bytes 4194304
  337.7 100.5 %reduce-scatter.8.cloned.1.call-start = ((), (), s32[]{:S(2)}) async-start(), calls=%async_computation.6 | async-start | bytes 1474560 | tf_op jit(solution)/shard_map/reduce_scatter | solution.py:97
  341.8 10.1 %slice-start.1 = ((s8[6291456]{0:T(1024)(128)(4,1)}), s8[4194304]{0:T(1024)(128)(4,1)S(1)}, s32[]{:S(2)}) async-start(s8[6291456]{0:T(1024)(128)(4,1)} %bitcast.147), calls=%async_computation.10 | async-start | bytes 8388608
  361.6 6.8 %copy-start.15 = (bf16[2048,256]{1,0:T(8,128)(2,1)S(1)}, bf16[2048,256]{1,0:T(8,128)(2,1)}, u32[]{:S(2)}) copy-start(bf16[2048,256]{1,0:T(8,128)(2,1)} %copy-done.14) | copy-start | bytes 3145732
  361.6 29.5 %collective-permute-start.31 = (bf16[1024,1024]{1,0:T(8,128)(2,1)}, bf16[1024,1024]{1,0:T(8,128)(2,1)S(1)}, u32[]{:S(2)}, u32[]{:S(2)}) collective-permute-start(bf16[1024,1024]{1,0:T(8,128)(2,1)} %pad_maximum_fusion.6), channel_id=1, source_target_pairs={{0,4},{4,0},{1,5},{5,1},{2,6},{6,2},{3,7},{7,3},{8,12},{12,8},{9,1... | collective-permute-start | bytes 6291464 | tf_op jit(solution)/shard_map/ppermute | solution.py:33
  377.9 28.3 %collective-permute-start.33 = (bf16[4,144,1024]{2,1,0:T(8,128)(2,1)}, bf16[4,144,1024]{2,1,0:T(8,128)(2,1)}, u32[]{:S(2)}, u32[]{:S(2)}) collective-permute-start(bf16[4,144,1024]{2,1,0:T(8,128)(2,1)} %dynamic-slice_bitcast_fusion.1), channel_id=1, source_target_pairs={{0,16},{16,0},{1,17},{17,1},{2,18},{18,2},{3,19},{19,3},{4,20},{20... | collective-permute-start | bytes 3538952 | tf_op jit(solution)/shard_map/ppermute | solution.py:41
  389.3 20.1 %collective-permute-start.38 = (bf16[32,2304]{1,0:T(8,128)(2,1)}, bf16[32,2304]{1,0:T(8,128)(2,1)}, u32[]{:S(2)}, u32[]{:S(2)}) collective-permute-start(bf16[32,2304]{1,0:T(8,128)(2,1)} %get-tuple-element.77), channel_id=1, source_target_pairs={{0,12},{4,8},{8,4},{12,0},{1,13},{5,9},{9,5},{13,1},{2,14},{6,10},... | collective-permute-start | bytes 442376 | tf_op jit(solution)/shard_map/ppermute | solution.py:45
  390.0 19.4 %collective-permute-start.39 = (bf16[32,2304]{1,0:T(8,128)(2,1)}, bf16[32,2304]{1,0:T(8,128)(2,1)}, u32[]{:S(2)}, u32[]{:S(2)}) collective-permute-start(bf16[32,2304]{1,0:T(8,128)(2,1)} %get-tuple-element.78), channel_id=1, source_target_pairs={{0,8},{4,12},{8,0},{12,4},{1,9},{5,13},{9,1},{13,5},{2,10},{6,14},... | collective-permute-start | bytes 442376 | tf_op jit(solution)/shard_map/ppermute | solution.py:45
  390.8 18.6 %collective-permute-start.40 = (bf16[32,2304]{1,0:T(8,128)(2,1)}, bf16[32,2304]{1,0:T(8,128)(2,1)}, u32[]{:S(2)}, u32[]{:S(2)}) collective-permute-start(bf16[32,2304]{1,0:T(8,128)(2,1)} %get-tuple-element.76), channel_id=1, source_target_pairs={{0,4},{4,0},{8,12},{12,8},{1,5},{5,1},{9,13},{13,9},{2,6},{6,2},{1... | collective-permute-start | bytes 442376 | tf_op jit(solution)/shard_map/ppermute | solution.py:45
  396.2 25.5 %collective-permute-start.32 = (bf16[512,1024]{1,0:T(8,128)(2,1)}, bf16[512,1024]{1,0:T(8,128)(2,1)}, u32[]{:S(2)}, u32[]{:S(2)}) collective-permute-start(bf16[512,1024]{1,0:T(8,128)(2,1)} %fusion.13), channel_id=1, source_target_pairs={{0,8},{8,0},{1,9},{9,1},{2,10},{10,2},{3,11},{11,3},{4,12},{12,4},... | collective-permute-start | bytes 3145736 | tf_op jit(solution)/shard_map/ppermute | solution.py:37
  414.6 10.0 %copy-start.13 = (f32[512,1024]{1,0:T(8,128)S(1)}, f32[512,1024]{1,0:T(8,128)}, u32[]{:S(2)}) copy-start(f32[512,1024]{1,0:T(8,128)} %get-tuple-element.46) | copy-start | bytes 6291460
  417.7 6.8 %copy-start.3 = (f32[1024,1024]{1,0:T(8,128)S(1)}, f32[1024,1024]{1,0:T(8,128)}, u32[]{:S(2)}) copy-start(f32[1024,1024]{1,0:T(8,128)} %copy-done.2) | copy-start | bytes 12582916
  428.0 17.8 %copy-start.34 = (bf16[32,3072]{1,0:T(8,128)(2,1)S(1)}, bf16[32,3072]{1,0:T(8,128)(2,1)}, u32[]{:S(2)}) copy-start(bf16[32,3072]{1,0:T(8,128)(2,1)} %param.15) | copy-start | bytes 589828
  438.2 7.8 %copy-start.39 = (bf16[32]{0:T(256)(128)(2,1)S(1)}, bf16[32]{0:T(256)(128)(2,1)}, u32[]{:S(2)}) copy-start(bf16[32]{0:T(256)(128)(2,1)} %param.14) | copy-start | bytes 196
  439.9 4.0 collective-permute-start.35
  440.6 4.5 collective-permute-start.36
  441.4 3.7 collective-permute-start.37
  (26 other events, 84.6 us)
Sparse Core Ops, SparseCore 0:
  19.7 52.3 all-gather.7
  76.9 81.4 all-gather.9
  160.5 50.2 all-gather.5
  282.6 27.7 reduce-scatter.3
  337.8 47.6 reduce-scatter.5
  409.5 28.6 reduce-scatter.7

commit v12 on v11

--- a/solution.py
+++ b/solution.py
@@ -71,13 +71,13 @@
     return jnp.concatenate(team_pieces(rows), axis=0)
 
 
-def team_sum(terms, token=None):
+def team_sum(terms, token=None, gate=None):
     count = terms.shape[0] // TEAM
     sent = jnp.concatenate([terms[count : 2 * count], terms[3 * count :]], axis=0)
     came = swap_core(sent).astype(f32)
     own = terms[:count].astype(f32) + came[:count]
     other = terms[2 * count : 3 * count].astype(f32) + came[count:]
-    other = other.astype(bf16)
+    other = (other if gate is None else after(other, gate)).astype(bf16)
     came = swap_chip(other).astype(f32)
     return own + (came if token is None else after(came, token)), other[:1, :1]
 
@@ -355,7 +355,9 @@
             jnp.sum(conv_grad * mixed_two, axis=0),
         ]
     )
-    out_sum, _ = team_sum(forward_dot(hidden, down_full).astype(bf16))
+    out_sum, _ = team_sum(
+        forward_dot(hidden, down_full).astype(bf16), gate=mixer_grad[-1:]
+    )
     block_out = (middle + live * out_sum).astype(bf16)
     in_part = by_owner(rows_dot(first_normed, projected_grad), TEAM)
     out_grad_part = rows_dot(mixer_in, mixer_grad).astype(bf16)

time: 459 us -> 509 us (1.11)
  waiting for transfers between devices: 183 us -> 212 us
  other arithmetic: 67.6 us -> 80.8 us
  local copies, waits for them, and re-layouts: 51.1 us -> 59.9 us
    ppermute x3, waiting for transfers between devices: 6.6 us -> 66.9 us  [swap_row(): return lax.ppermute(values, 'y', [(0, 1), (1, 0)])]
    ppermute x10, waiting for transfers between devices: 90 us -> 63.8 us  [swap_chip(): return lax.ppermute(values, 'x', [(0, 1), (1, 0)])]
    convert_element_type x4 -> x5, other arithmetic: 7.07 us -> 11.7 us  [the longest x4 9.05 us: team_sum(): other = (other if gate is None else after(other, gate)).astype(bf16)]
    unnamed x90 -> x94, local copies, waits for them, and re-layouts: 16.9 us -> 17.6 us
  transfers between devices with their start and end apart: 47 -> 47, of which waited for: 16 -> 15; matrix products, arithmetic and copies ran while one was open for 35% -> 36% of each run, Pallas kernels for 4% -> 4%
where the time goes in v12:
time: 509 us; the launch traced here: 504 us
  waiting for transfers between devices  212 us (42%)
  other arithmetic  80.8 us (16%)
  matrix products  62.8 us (12%)
  local copies, waits for them, and re-layouts  59.9 us (12%)
  Pallas kernels  39.3 us (8%)
  starting transfers between devices  28.6 us (6%)
  between operations  20.1 us (4%)
    ppermute x3, waiting for transfers between devices, swap_row(): return lax.ppermute(values, 'y', [(0, 1), (1, 0)])  66.9 us
    ppermute x10, waiting for transfers between devices, swap_chip(): return lax.ppermute(values, 'x', [(0, 1), (1, 0)])  63.8 us
    ppermute x12, waiting for transfers between devices, swap_far(): lax.ppermute(values, ('x', 'c'), [(i, i ^ distance) for i in range(TEAM)])  48.5 us
    pallas_call x2, Pallas kernels, by_rows(): pl.pallas_call(kernel, grid=(steps,), in_specs=[row_block(value.shape[1])...  39.3 us
    dot_general x4, matrix products, rows_dot(): lax.dot_general(left_side, right_side, (((0,), (0,)), ((), ())), preferre...  30.9 us
    unnamed x94, local copies, waits for them, and re-layouts  17.6 us
    dot_general x3, matrix products, forward_dot(): return jnp.dot(left_side, right_side, preferred_element_type=f32)  16.3 us
    dot_general x2, matrix products, back_dot(): lax.dot_general(left_side, right_side, (((1,), (1,)), ((), ())), preferre...  15.5 us
  transfers between devices with their start and end apart: 47, of which 15 were waited for; matrix products, arithmetic and copies ran while one was open for 36% of the time, Pallas kernels for 4%

profile of v12, /device:TPU:0, one launch (start us, length us, event | category | flops | bytes accessed | tf_op | source)
XLA Modules:
  0.0 503.8 jit_solution(810370690025442649)
XLA Ops:
  8.1 2.9 collective-permute-start.6
  12.8 2.0 collective-permute-start.4
  21.3 1.7 collective-permute-start.9
  25.3 1.8 collective-permute-start.20
  27.5 44.8 %collective-permute-done.20 = bf16[32,2304]{1,0:T(8,128)(2,1)S(1)} collective-permute-done((bf16[32,2304]{1,0:T(8,128)(2,1)S(1)}, bf16[32,2304]{1,0:T(8,128)(2,1)S(1)}, u32[]{:S(2)}, u32[]{:S(2)}) %collective-permute-start.20) | collective-permute-done | bytes 147488 | tf_op jit(solution)/shard_map/ppermute | solution.py:45
  73.5 2.3 collective-permute-done.21
  80.3 3.5 fusion
  83.9 1.5 slice.394
  90.1 7.9 %fusion.29 = f32[2048,768]{1,0:T(8,128)S(1)} fusion(bf16[1024,768]{1,0:T(8,128)(2,1)} %bitcast.175, f32[1024]{0:T(1024)S(1)} %mul.330, f32[2048]{0:T(1024)S(1)} %add_rsqrt_fusion, bf16[512,1024]{1,0:T(8,128)(2,1)} %copy-done.31, bf16[512,1024]{1,0:T(8,128)(2,1)} %collective-permute-done.1, bf16[512,1024]{1,0:T(8,128)(2,1)} %copy-done.29, ...), kind=kOutput, calls=%fused_computation.82 | convolution fusion | flops 3244294144 | bytes 12070912 | tf_op jit(solution)/shard_map/dot_general | solution.py:17
  98.3 2.3 copy-done
  100.6 2.2 multiply_convert_fusion.5
  104.7 4.0 collective-permute-done.14
  109.5 1.6 copy-done.10
  111.2 1.6 collective-permute-start.15
  112.9 23.6 %collective-permute-done.15 = bf16[512,1024]{1,0:T(8,128)(2,1)} collective-permute-done((bf16[512,1024]{1,0:T(8,128)(2,1)S(1)}, bf16[512,1024]{1,0:T(8,128)(2,1)}, u32[]{:S(2)}, u32[]{:S(2)}) %collective-permute-start.15) | collective-permute-done | bytes 1048608 | tf_op jit(solution)/shard_map/ppermute | solution.py:37
  136.5 2.9 multiply_reduce_fusion.5
  139.6 1.7 collective-permute-start.17
  142.5 21.7 %collective-permute-done.17.refs_2_ = bf16[512,1024]{1,0:T(8,128)(2,1)} collective-permute-done((bf16[512,1024]{1,0:T(8,128)(2,1)S(1)}, bf16[512,1024]{1,0:T(8,128)(2,1)}, u32[]{:S(2)}, u32[]{:S(2)}) %collective-permute-start.17) | collective-permute-done | bytes 1048608 | tf_op jit(solution)/shard_map/ppermute | solution.py:37
  164.2 5.0 copy.66
  169.2 17.7 %shard_map.186 = (bf16[2048,1152]{1,0:T(8,128)(2,1)}, bf16[2048,1152]{1,0:T(8,128)(2,1)}, bf16[2048,1152]{1,0:T(8,128)(2,1)}, bf16[2048,1024]{1,0:T(8,128)(2,1)}, bf16[2048,1024]{1,0:T(8,128)(2,1)}) custom-call(bf16[512,1024]{1,0:T(8,128)(2,1)S(1)} %multiply_convert_fusion.4.refs_0_, bf16[512,1024]{1,0:T(8,128)(2,1)} %collective-permute-done.16.refs_1_, ...), custom_call_target="tpu_custom_call" | custom-call | flops 9663676416 | bytes 35651584 | tf_op jit(solution)/shard_map/pallas_call | solution.py:140
  186.9 9.4 %convolution_convert_fusion.1.token_ref = bf16[1152,1024]{1,0:T(8,128)(2,1)} fusion(bf16[2048,1152]{1,0:T(8,128)(2,1)} %get-tuple-element.17, bf16[2048,1024]{1,0:T(8,128)(2,1)} %get-tuple-element.18.grad_ref), kind=kOutput, calls=%fused_computation.12 | convolution fusion | flops 4833017856 | bytes 11272192 | tf_op jit(solution)/shard_map/dot_general | solution.py:21
  196.3 14.4 %all-gather.6.cloned.1.call-done.down_ref = bf16[1152,1024]{1,0:T(8,128)(2,1)} async-done(((bf16[144,1024]{1,0:T(8,128)(2,1)}), bf16[1152,1024]{1,0:T(8,128)(2,1)}) %all-gather.6.cloned.1.call-update) | async-done | bytes 2359312 | tf_op jit(solution)/shard_map/all_gather | solution.py:261
  210.6 21.7 %shard_map.187 = (bf16[2048,2304]{1,0:T(8,128)(2,1)}, bf16[2048,1024]{1,0:T(8,128)(2,1)}) custom-call(bf16[2048,1024]{1,0:T(8,128)(2,1)} %get-tuple-element.18.grad_ref, bf16[2048,1152]{1,0:T(8,128)(2,1)} %get-tuple-element.19.silu_ref, bf16[2048,1152]{1,0:T(8,128)(2,1)} %get-tuple-element.20.slope_ref, bf16[1024,2304]{1,0:T(8,128)(2,1)} %bitcast.165, ...), custom_call_target="tpu_custom_call" | custom-call | flops 14495514624 | bytes 34340864 | tf_op jit(solution)/shard_map/pallas_call | solution.py:140
  232.3 1.7 fusion.49
  234.3 1.9 copy-done.42
  236.2 13.0 %convolution_convert_fusion = bf16[1024,2304]{1,0:T(8,128)(2,1)S(1)} fusion(bf16[2048,1024]{1,0:T(8,128)(2,1)S(1)} %copy-done.42, bf16[2048,2304]{1,0:T(8,128)(2,1)} %get-tuple-element.23), kind=kOutput, calls=%fused_computation.5 | convolution fusion | flops 9666035712 | bytes 18350080 | tf_op jit(solution)/shard_map/dot_general | solution.py:21
  249.7 1.6 dynamic-slice_bitcast_fusion
  255.2 2.0 copy-done.4
  257.2 2.7 fusion.16
  259.9 1.5 collective-permute-start.25
  261.4 7.2 %convolution_convert_fusion.2 = bf16[2048,1024]{1,0:T(8,128)(2,1)} fusion(bf16[2048,1152]{1,0:T(8,128)(2,1)S(1)} %bitcast.201, bf16[1152,1024]{1,0:T(8,128)(2,1)S(1)} %copy-done.40), kind=kOutput, calls=%fused_computation.13 | convolution fusion | flops 4833935360 | bytes 11272192 | tf_op jit(solution)/shard_map/dot_general | solution.py:17
  269.8 1.7 fusion.50
  271.5 1.5 pad_maximum_fusion.4
  273.0 55.6 %collective-permute-done.29 = bf16[4,144,1024]{2,1,0:T(8,128)(2,1)} collective-permute-done((bf16[4,144,1024]{2,1,0:T(8,128)(2,1)}, bf16[4,144,1024]{2,1,0:T(8,128)(2,1)}, u32[]{:S(2)}, u32[]{:S(2)}) %collective-permute-start.29) | collective-permute-done | bytes 1179680 | tf_op jit(solution)/shard_map/ppermute | solution.py:41
  328.6 2.8 fusion.7
  331.5 2.9 multiply_reduce_fusion.4
  335.3 4.2 multiply_convert_fusion.3
  339.5 1.5 collective-permute-start.26
  341.5 4.0 convert_element_type.332
  345.5 17.1 %collective-permute-done.26 = bf16[512,1024]{1,0:T(8,128)(2,1)} collective-permute-done((bf16[512,1024]{1,0:T(8,128)(2,1)}, bf16[512,1024]{1,0:T(8,128)(2,1)}, u32[]{:S(2)}, u32[]{:S(2)}) %collective-permute-start.26) | collective-permute-done | bytes 1048608 | tf_op jit(solution)/shard_map/ppermute | solution.py:37
  362.6 4.3 fusion.3
  369.2 10.6 %multiply_reduce_fusion.2 = (f32[256]{0:T(256)}, f32[256]{0:T(256)}, f32[256]{0:T(256)}, f32[2048,256]{1,0:T(8,128)S(1)}, bf16[2048,256]{1,0:T(8,128)(2,1)}) fusion(f32[2048,256]{1,0:T(8,128)} %copy-done.9, f32[2046,256]{1,0:T(8,128)} %bitcast.159, f32[2048]{0:T(1024)S(1)} %get-tuple-element.115, f32[2047,256]{1,0:T(8,128)} %bitcast.160, ...), kind=kOutput, calls=%fused_computation.64 | convolution fusion | flops 1096285440 | bytes 18366464 | tf_op jit(solution)/shard_map/dot_general | solution.py:27
  380.5 3.6 multiply_convert_fusion.2
  384.1 2.9 multiply_convert_fusion
  388.8 3.3 fusion.20
  392.1 1.5 collective-permute-start.28
  393.6 5.0 convolution_convert_fusion.4
  398.8 1.8 copy-done.15
  400.6 1.6 pad_maximum_fusion.6
  402.5 5.1 %convolution_convert_fusion.5 = bf16[1024,768]{1,0:T(8,128)(2,1)S(1)} fusion(bf16[2048,256]{1,0:T(8,128)(2,1)S(1)} %copy-done.28, bf16[2048,256]{1,0:T(8,128)(2,1)S(1)} %copy-done.41, bf16[2048,256]{1,0:T(8,128)(2,1)S(1)} %copy-done.27, f32[1024]{0:T(1024)S(1)} %mul.330, f32[2048]{0:T(1024)S(1)} %add_rsqrt_fusion, bf16[512,1024]{1,0:T(8,128)(2,1)S(1)} %copy-done.32, ...), kind=kOutput, calls=%fused_computation.80 | convolution fusion | flops 3254517760 | bytes 8925184 | tf_op jit(solution)/shard_map/dot_general | solution.py:21
  407.6 3.4 convolution_convert_fusion.6
  418.0 2.6 fusion.24
  423.5 1.9 fusion.5
  433.3 2.0 convert_element_type.358
  435.4 2.0 copy-done.2
  437.4 2.6 fusion.13
  443.3 11.3 %collective-permute-done.33 = bf16[4,144,1024]{2,1,0:T(8,128)(2,1)} collective-permute-done((bf16[4,144,1024]{2,1,0:T(8,128)(2,1)S(1)}, bf16[4,144,1024]{2,1,0:T(8,128)(2,1)}, u32[]{:S(2)}, u32[]{:S(2)}) %collective-permute-start.33) | collective-permute-done | bytes 1179680 | tf_op jit(solution)/shard_map/ppermute | solution.py:41
  454.6 3.2 fusion.6
  460.6 1.9 copy.79
  462.5 3.5 reshape.482
  466.0 2.7 add_reduce_fusion
  469.2 3.0 fusion.9
  472.7 3.3 fusion.12
  476.0 12.2 %reduce-scatter.8.cloned.1.call-done = bf16[1,144,1024]{2,1,0:T(8,128)(2,1)} async-done(((bf16[4,144,1024]{2,1,0:T(8,128)(2,1)}), bf16[1,144,1024]{2,1,0:T(8,128)(2,1)}) %reduce-scatter.8.cloned.1.call-update) | async-done | bytes 294928 | tf_op jit(solution)/shard_map/reduce_scatter | solution.py:97
  (289 shorter events, 67.0 us)
Async XLA Ops:
  7.2 12.4 %copy-start.37 = (s32[2,256]{1,0:T(2,128)S(1)}, s32[2,256]{1,0:T(2,128)}, u32[]{:S(2)}) copy-start(s32[2,256]{1,0:T(2,128)} %param.12) | copy-start | bytes 6148
  7.2 12.9 %copy-start.16 = (bf16[2,256,1024]{2,1,0:T(8,128)(2,1)S(1)}, bf16[2,256,1024]{2,1,0:T(8,128)(2,1)}, u32[]{:S(2)}) copy-start(bf16[2,256,1024]{2,1,0:T(8,128)(2,1)} %param.13) | copy-start | bytes 3145732
  7.2 76.7 %all-gather.8.cloned.1.call-start = ((), (), s32[]{:S(2)}) async-start(), calls=%async_computation.7 | async-start | bytes 2654208 | tf_op jit(solution)/shard_map/all_gather | solution.py:255
  8.1 8.4 %collective-permute-start.6 = (bf16[1,64]{1,0:T(2,128)(2,1)S(1)}, bf16[1,64]{1,0:T(2,128)(2,1)S(1)}, u32[]{:S(2)}, u32[]{:S(2)}) collective-permute-start(bf16[1,64]{1,0:T(2,128)(2,1)S(1)} %maximum_bitcast_fusion), channel_id=1, source_target_pairs={{0,8},{8,0},{1,9},{9,1},{2,10},{10,2},{3,11},{11,3},{4,12},{12,4},... | collective-permute-start | bytes 392 | tf_op jit(solution)/shard_map/ppermute | solution.py:37
  11.0 6.0 %collective-permute-start.8 = (bf16[1,64]{1,0:T(2,128)(2,1)S(1)}, bf16[1,64]{1,0:T(2,128)(2,1)S(1)}, u32[]{:S(2)}, u32[]{:S(2)}) collective-permute-start(bf16[1,64]{1,0:T(2,128)(2,1)S(1)} %maximum_bitcast_fusion), channel_id=1, source_target_pairs={{0,4},{4,0},{1,5},{5,1},{2,6},{6,2},{3,7},{7,3},{8,12},{12,8},{9,1... | collective-permute-start | bytes 392 | tf_op jit(solution)/shard_map/ppermute | solution.py:33
  12.1 10.9 %copy-start.6 = (bf16[2,256,1024]{2,1,0:T(8,128)(2,1)S(1)}, bf16[2,256,1024]{2,1,0:T(8,128)(2,1)}, u32[]{:S(2)}) copy-start(bf16[2,256,1024]{2,1,0:T(8,128)(2,1)} %param.11) | copy-start | bytes 3145732
  12.1 11.3 %copy-start.24 = (bf16[32,4608]{1,0:T(8,128)(2,1)S(1)}, bf16[32,4608]{1,0:T(8,128)(2,1)}, u32[]{:S(2)}) copy-start(bf16[32,4608]{1,0:T(8,128)(2,1)} %param.19) | copy-start | bytes 884740
  12.5 6.1 %collective-permute-start.3 = (bf16[32,768]{1,0:T(8,128)(2,1)S(1)}, bf16[32,768]{1,0:T(8,128)(2,1)S(1)}, u32[]{:S(2)}, u32[]{:S(2)}) collective-permute-start(bf16[32,768]{1,0:T(8,128)(2,1)S(1)} %select_n.381), channel_id=1, source_target_pairs={{0,12},{4,8},{8,4},{12,0},{1,13},{5,9},{9,5},{13,1},{2,14},{6,10},... | collective-permute-start | bytes 147464 | tf_op jit(solution)/shard_map/ppermute | solution.py:45
  12.8 5.9 %collective-permute-start.4 = (bf16[32,768]{1,0:T(8,128)(2,1)S(1)}, bf16[32,768]{1,0:T(8,128)(2,1)S(1)}, u32[]{:S(2)}, u32[]{:S(2)}) collective-permute-start(bf16[32,768]{1,0:T(8,128)(2,1)S(1)} %select_n.385), channel_id=1, source_target_pairs={{0,8},{4,12},{8,0},{12,4},{1,9},{5,13},{9,1},{13,5},{2,10},{6,14},... | collective-permute-start | bytes 147464 | tf_op jit(solution)/shard_map/ppermute | solution.py:45
  14.8 3.8 collective-permute-start.5
  16.5 1.3 collective-permute-start.7
  18.7 5.5 %copy-start.26 = (bf16[32,4608]{1,0:T(8,128)(2,1)S(1)}, bf16[32,4608]{1,0:T(8,128)(2,1)}, u32[]{:S(2)}) copy-start(bf16[32,4608]{1,0:T(8,128)(2,1)} %param.20) | copy-start | bytes 884740
  19.5 144.7 %all-gather.10.cloned.1.call-start = ((), (), s32[]{:S(2)}) async-start(), calls=%async_computation.8 | async-start | bytes 5308416 | tf_op jit(solution)/shard_map/all_gather | solution.py:260
  19.6 5.5 %collective-permute-start.12 = (s32[512,1]{0,1:T(1,128)S(1)}, s32[512,1]{0,1:T(1,128)S(1)}, u32[]{:S(2)}, u32[]{:S(2)}) collective-permute-start(s32[512,1]{0,1:T(1,128)S(1)} %bitcast.198), channel_id=1, source_target_pairs={{0,8},{8,0},{1,9},{9,1},{2,10},{10,2},{3,11},{11,3},{4,12},{12,4},... | collective-permute-start | bytes 6152 | tf_op jit(solution)/shard_map/ppermute | solution.py:37
  19.9 7.2 %collective-permute-start.11 = (s32[512,1]{0,1:T(1,128)S(1)}, s32[512,1]{0,1:T(1,128)S(1)}, u32[]{:S(2)}, u32[]{:S(2)}) collective-permute-start(s32[512,1]{0,1:T(1,128)S(1)} %bitcast.199), channel_id=1, source_target_pairs={{0,4},{4,0},{1,5},{5,1},{2,6},{6,2},{3,7},{7,3},{8,12},{12,8},{9,1... | collective-permute-start | bytes 6152 | tf_op jit(solution)/shard_map/ppermute | solution.py:33
  21.3 51.7 %collective-permute-start.9 = (bf16[512,1024]{1,0:T(8,128)(2,1)}, bf16[512,1024]{1,0:T(8,128)(2,1)}, u32[]{:S(2)}, u32[]{:S(2)}) collective-permute-start(bf16[512,1024]{1,0:T(8,128)(2,1)} %fusion.8.refs_4_), channel_id=1, source_target_pairs={{0,8},{8,0},{1,9},{9,1},{2,10},{10,2},{3,11},{11,3},{4,12},{12,4},... | collective-permute-start | bytes 3145736 | tf_op jit(solution)/shard_map/ppermute | solution.py:37
  23.0 50.0 %collective-permute-start.1 = (bf16[512,1024]{1,0:T(8,128)(2,1)S(1)}, bf16[512,1024]{1,0:T(8,128)(2,1)}, u32[]{:S(2)}, u32[]{:S(2)}) collective-permute-start(bf16[512,1024]{1,0:T(8,128)(2,1)S(1)} %bitcast.149), channel_id=1, source_target_pairs={{0,8},{8,0},{1,9},{9,1},{2,10},{10,2},{3,11},{11,3},{4,12},{12,4},... | collective-permute-start | bytes 3145736 | tf_op jit(solution)/shard_map/ppermute | solution.py:37
  25.2 2.3 collective-permute-start.13
  25.3 47.0 %collective-permute-start.20 = (bf16[32,2304]{1,0:T(8,128)(2,1)S(1)}, bf16[32,2304]{1,0:T(8,128)(2,1)S(1)}, u32[]{:S(2)}, u32[]{:S(2)}) collective-permute-start(bf16[32,2304]{1,0:T(8,128)(2,1)S(1)} %get-tuple-element.81), channel_id=1, source_target_pairs={{0,12},{4,8},{8,4},{12,0},{1,13},{5,9},{9,5},{13,1},{2,14},{6,10},... | collective-permute-start | bytes 442376 | tf_op jit(solution)/shard_map/ppermute | solution.py:45
  27.1 48.6 %collective-permute-start.21 = (bf16[32,2304]{1,0:T(8,128)(2,1)S(1)}, bf16[32,2304]{1,0:T(8,128)(2,1)S(1)}, u32[]{:S(2)}, u32[]{:S(2)}) collective-permute-start(bf16[32,2304]{1,0:T(8,128)(2,1)S(1)} %get-tuple-element.47), channel_id=1, source_target_pairs={{0,8},{4,12},{8,0},{12,4},{1,9},{5,13},{9,1},{13,5},{2,10},{6,14},... | collective-permute-start | bytes 442376 | tf_op jit(solution)/shard_map/ppermute | solution.py:45
  27.5 48.3 %collective-permute-start.22 = (bf16[32,2304]{1,0:T(8,128)(2,1)S(1)}, bf16[32,2304]{1,0:T(8,128)(2,1)S(1)}, u32[]{:S(2)}, u32[]{:S(2)}) collective-permute-start(bf16[32,2304]{1,0:T(8,128)(2,1)S(1)} %get-tuple-element.80), channel_id=1, source_target_pairs={{0,4},{4,0},{8,12},{12,8},{1,5},{5,1},{9,13},{13,9},{2,6},{6,2},{1... | collective-permute-start | bytes 442376 | tf_op jit(solution)/shard_map/ppermute | solution.py:45
  72.3 8.0 %collective-permute-start = (bf16[512,1024]{1,0:T(8,128)(2,1)S(1)}, bf16[512,1024]{1,0:T(8,128)(2,1)S(1)}, u32[]{:S(2)}, u32[]{:S(2)}) collective-permute-start(bf16[512,1024]{1,0:T(8,128)(2,1)S(1)} %bitcast.150), channel_id=1, source_target_pairs={{0,4},{4,0},{1,5},{5,1},{2,6},{6,2},{3,7},{7,3},{8,12},{12,8},{9,1... | collective-permute-start | bytes 3145736 | tf_op jit(solution)/shard_map/ppermute | solution.py:33
  73.0 5.5 %collective-permute-start.10 = (bf16[512,1024]{1,0:T(8,128)(2,1)}, bf16[512,1024]{1,0:T(8,128)(2,1)}, u32[]{:S(2)}, u32[]{:S(2)}) collective-permute-start(bf16[512,1024]{1,0:T(8,128)(2,1)} %collective-permute-done.9.refs_6_), channel_id=1, source_target_pairs={{0,4},{4,0},{1,5},{5,1},{2,6},{6,2},{3,7},{7,3},{8,12},{12,8},{9,1... | collective-permute-start | bytes 3145736 | tf_op jit(solution)/shard_map/ppermute | solution.py:33
  73.0 7.4 %collective-permute-start.2 = (bf16[512,1024]{1,0:T(8,128)(2,1)}, bf16[512,1024]{1,0:T(8,128)(2,1)S(1)}, u32[]{:S(2)}, u32[]{:S(2)}) collective-permute-start(bf16[512,1024]{1,0:T(8,128)(2,1)} %collective-permute-done.1), channel_id=1, source_target_pairs={{0,4},{4,0},{1,5},{5,1},{2,6},{6,2},{3,7},{7,3},{8,12},{12,8},{9,1... | collective-permute-start | bytes 3145736 | tf_op jit(solution)/shard_map/ppermute | solution.py:33
  76.7 133.9 %all-gather.6.cloned.1.call-start = ((), (), s32[]{:S(2)}) async-start(), calls=%async_computation.3 | async-start | bytes 2654208 | tf_op jit(solution)/shard_map/all_gather | solution.py:261
  90.1 12.7 %copy-start.21 = (bf16[8,32,1024]{2,1,0:T(8,128)(2,1)}, bf16[8,32,1024]{2,1,0:T(8,128)(2,1)S(1)}, u32[]{:S(2)}) copy-start(bf16[8,32,1024]{2,1,0:T(8,128)(2,1)S(1)} %pad_maximum_fusion.12) | copy-start | bytes 1572868
  104.5 4.2 collective-permute-start.14
  111.2 25.3 %collective-permute-start.15 = (bf16[512,1024]{1,0:T(8,128)(2,1)S(1)}, bf16[512,1024]{1,0:T(8,128)(2,1)}, u32[]{:S(2)}, u32[]{:S(2)}) collective-permute-start(bf16[512,1024]{1,0:T(8,128)(2,1)S(1)} %fusion.25), channel_id=1, source_target_pairs={{0,8},{8,0},{1,9},{9,1},{2,10},{10,2},{3,11},{11,3},{4,12},{12,4},... | collective-permute-start | bytes 3145736 | tf_op jit(solution)/shard_map/ppermute | solution.py:37
  139.6 24.6 %collective-permute-start.17 = (bf16[512,1024]{1,0:T(8,128)(2,1)S(1)}, bf16[512,1024]{1,0:T(8,128)(2,1)}, u32[]{:S(2)}, u32[]{:S(2)}) collective-permute-start(bf16[512,1024]{1,0:T(8,128)(2,1)S(1)} %multiply_convert_fusion.4.refs_0_), channel_id=1, source_target_pairs={{0,8},{8,0},{1,9},{9,1},{2,10},{10,2},{3,11},{11,3},{4,12},{12,4},... | collective-permute-start | bytes 3145736 | tf_op jit(solution)/shard_map/ppermute | solution.py:37
  141.3 225.7 %reduce-scatter.4.cloned.1.call-start = ((), (), s32[]{:S(2)}) async-start(), calls=%async_computation.4 | async-start | bytes 1474560 | tf_op jit(solution)/shard_map/reduce_scatter | solution.py:97
  141.9 27.3 %collective-permute-start.19 = (bf16[512,1024]{1,0:T(8,128)(2,1)}, bf16[512,1024]{1,0:T(8,128)(2,1)}, u32[]{:S(2)}, u32[]{:S(2)}) collective-permute-start(bf16[512,1024]{1,0:T(8,128)(2,1)} %fusion.8.refs_4_), channel_id=1, source_target_pairs={{0,4},{4,0},{1,5},{5,1},{2,6},{6,2},{3,7},{7,3},{8,12},{12,8},{9,1... | collective-permute-start | bytes 3145736 | tf_op jit(solution)/shard_map/ppermute | solution.py:33
  142.0 27.2 %collective-permute-start.16 = (bf16[512,1024]{1,0:T(8,128)(2,1)S(1)}, bf16[512,1024]{1,0:T(8,128)(2,1)}, u32[]{:S(2)}, u32[]{:S(2)}) collective-permute-start(bf16[512,1024]{1,0:T(8,128)(2,1)S(1)} %multiply_convert_fusion.4.refs_0_), channel_id=1, source_target_pairs={{0,4},{4,0},{1,5},{5,1},{2,6},{6,2},{3,7},{7,3},{8,12},{12,8},{9,1... | collective-permute-start | bytes 3145736 | tf_op jit(solution)/shard_map/ppermute | solution.py:33
  164.2 5.0 %collective-permute-start.18 = (bf16[512,1024]{1,0:T(8,128)(2,1)}, bf16[512,1024]{1,0:T(8,128)(2,1)}, u32[]{:S(2)}, u32[]{:S(2)}) collective-permute-start(bf16[512,1024]{1,0:T(8,128)(2,1)} %collective-permute-done.17.refs_2_), channel_id=1, source_target_pairs={{0,4},{4,0},{1,5},{5,1},{2,6},{6,2},{3,7},{7,3},{8,12},{12,8},{9,1... | collective-permute-start | bytes 3145736 | tf_op jit(solution)/shard_map/ppermute | solution.py:33
  234.2 20.5 %collective-permute-start.24 = (bf16[1024,1024]{1,0:T(8,128)(2,1)S(1)}, bf16[1024,1024]{1,0:T(8,128)(2,1)S(1)}, u32[]{:S(2)}, u32[]{:S(2)}) collective-permute-start(bf16[1024,1024]{1,0:T(8,128)(2,1)S(1)} %pad_maximum_fusion.5), channel_id=1, source_target_pairs={{0,4},{4,0},{1,5},{5,1},{2,6},{6,2},{3,7},{7,3},{8,12},{12,8},{9,1... | collective-permute-start | bytes 6291464 | tf_op jit(solution)/shard_map/ppermute | solution.py:33
  249.6 19.0 %copy-start.8 = (bf16[2,4,4,32,2304]{4,3,2,1,0:T(8,128)(2,1)}, bf16[2,4,4,32,2304]{4,3,2,1,0:T(8,128)(2,1)S(1)}, u32[]{:S(2)}) copy-start(bf16[2,4,4,32,2304]{4,3,2,1,0:T(8,128)(2,1)S(1)} %copy.67) | copy-start | bytes 14155780
  251.3 111.3 %collective-permute-start.34 = (bf16[4,128,2304]{2,1,0:T(8,128)(2,1)}, bf16[4,128,2304]{2,1,0:T(8,128)(2,1)}, u32[]{:S(2)}, u32[]{:S(2)}) collective-permute-start(bf16[4,128,2304]{2,1,0:T(8,128)(2,1)} %dynamic-slice_bitcast_fusion), channel_id=1, source_target_pairs={{0,16},{16,0},{1,17},{17,1},{2,18},{18,2},{3,19},{19,3},{4,20},{20... | collective-permute-start | bytes 7077896 | tf_op jit(solution)/shard_map/ppermute | solution.py:41
  253.0 8.4 %slice-start = ((s8[4718592]{0:T(1024)(128)(4,1)}), s8[4194304]{0:T(1024)(128)(4,1)S(1)}, s32[]{:S(2)}) async-start(s8[4718592]{0:T(1024)(128)(4,1)} %bitcast.200), calls=%async_computation.9 | async-start | bytes 8388608
  254.2 7.2 %slice-start.1 = ((s8[4718592]{0:T(1024)(128)(4,1)}), s8[524288]{0:T(1024)(128)(4,1)S(1)}, s32[]{:S(2)}) async-start(s8[4718592]{0:T(1024)(128)(4,1)} %bitcast.200), calls=%async_computation.10 | async-start | bytes 1048576
  254.2 74.5 %collective-permute-start.29 = (bf16[4,144,1024]{2,1,0:T(8,128)(2,1)}, bf16[4,144,1024]{2,1,0:T(8,128)(2,1)}, u32[]{:S(2)}, u32[]{:S(2)}) collective-permute-start(bf16[4,144,1024]{2,1,0:T(8,128)(2,1)} %dynamic-slice_bitcast_fusion.2), channel_id=1, source_target_pairs={{0,16},{16,0},{1,17},{17,1},{2,18},{18,2},{3,19},{19,3},{4,20},{20... | collective-permute-start | bytes 3538952 | tf_op jit(solution)/shard_map/ppermute | solution.py:41
  259.9 71.6 %collective-permute-start.25 = (bf16[512,1024]{1,0:T(8,128)(2,1)}, bf16[512,1024]{1,0:T(8,128)(2,1)S(1)}, u32[]{:S(2)}, u32[]{:S(2)}) collective-permute-start(bf16[512,1024]{1,0:T(8,128)(2,1)} %fusion.16), channel_id=1, source_target_pairs={{0,8},{8,0},{1,9},{9,1},{2,10},{10,2},{3,11},{11,3},{4,12},{12,4},... | collective-permute-start | bytes 3145736 | tf_op jit(solution)/shard_map/ppermute | solution.py:37
  271.5 57.1 %copy-start.20 = (bf16[1152,1024]{1,0:T(8,128)(2,1)S(1)}, bf16[1152,1024]{1,0:T(8,128)(2,1)}, u32[]{:S(2)}) copy-start(bf16[1152,1024]{1,0:T(8,128)(2,1)} %convolution_convert_fusion.1.token_ref) | copy-start | bytes 7077892
  273.0 68.5 %collective-permute-start.23 = (bf16[1024,1024]{1,0:T(8,128)(2,1)}, bf16[1024,1024]{1,0:T(8,128)(2,1)}, u32[]{:S(2)}, u32[]{:S(2)}) collective-permute-start(bf16[1024,1024]{1,0:T(8,128)(2,1)} %pad_maximum_fusion.4), channel_id=1, source_target_pairs={{0,4},{4,0},{1,5},{5,1},{2,6},{6,2},{3,7},{7,3},{8,12},{12,8},{9,1... | collective-permute-start | bytes 6291464 | tf_op jit(solution)/shard_map/ppermute | solution.py:33
  331.4 97.0 %reduce-scatter.6.cloned.1.call-start = ((), (), s32[]{:S(2)}) async-start(), calls=%async_computation.5 | async-start | bytes 2949120 | tf_op jit(solution)/shard_map/reduce_scatter | solution.py:97
  335.3 5.7 %copy-start.7 = (bf16[2,256,1024]{2,1,0:T(8,128)(2,1)S(1)}, bf16[2,256,1024]{2,1,0:T(8,128)(2,1)}, u32[]{:S(2)}) copy-start(bf16[2,256,1024]{2,1,0:T(8,128)(2,1)} %param.11) | copy-start | bytes 3145732
  339.5 23.1 %collective-permute-start.26 = (bf16[512,1024]{1,0:T(8,128)(2,1)}, bf16[512,1024]{1,0:T(8,128)(2,1)}, u32[]{:S(2)}, u32[]{:S(2)}) collective-permute-start(bf16[512,1024]{1,0:T(8,128)(2,1)} %get-tuple-element.45), channel_id=1, source_target_pairs={{0,8},{8,0},{1,9},{9,1},{2,10},{10,2},{3,11},{11,3},{4,12},{12,4},... | collective-permute-start | bytes 3145736 | tf_op jit(solution)/shard_map/ppermute | solution.py:37
  345.5 23.7 %collective-permute-start.30 = (bf16[512,1024]{1,0:T(8,128)(2,1)}, bf16[512,1024]{1,0:T(8,128)(2,1)}, u32[]{:S(2)}, u32[]{:S(2)}) collective-permute-start(bf16[512,1024]{1,0:T(8,128)(2,1)} %get-tuple-element.45), channel_id=1, source_target_pairs={{0,4},{4,0},{1,5},{5,1},{2,6},{6,2},{3,7},{7,3},{8,12},{12,8},{9,1... | collective-permute-start | bytes 3145736 | tf_op jit(solution)/shard_map/ppermute | solution.py:33
  362.6 6.6 %collective-permute-start.27 = (bf16[512,1024]{1,0:T(8,128)(2,1)}, bf16[512,1024]{1,0:T(8,128)(2,1)}, u32[]{:S(2)}, u32[]{:S(2)}) collective-permute-start(bf16[512,1024]{1,0:T(8,128)(2,1)} %collective-permute-done.26), channel_id=1, source_target_pairs={{0,4},{4,0},{1,5},{5,1},{2,6},{6,2},{3,7},{7,3},{8,12},{12,8},{9,1... | collective-permute-start | bytes 3145736 | tf_op jit(solution)/shard_map/ppermute | solution.py:33
  367.0 121.3 %reduce-scatter.8.cloned.1.call-start = ((), (), s32[]{:S(2)}) async-start(), calls=%async_computation.6 | async-start | bytes 1474560 | tf_op jit(solution)/shard_map/reduce_scatter | solution.py:97
  392.1 25.9 %collective-permute-start.28 = (bf16[512,1024]{1,0:T(8,128)(2,1)}, bf16[512,1024]{1,0:T(8,128)(2,1)}, u32[]{:S(2)}, u32[]{:S(2)}) collective-permute-start(bf16[512,1024]{1,0:T(8,128)(2,1)} %fusion.20), channel_id=1, source_target_pairs={{0,8},{8,0},{1,9},{9,1},{2,10},{10,2},{3,11},{11,3},{4,12},{12,4},... | collective-permute-start | bytes 3145736 | tf_op jit(solution)/shard_map/ppermute | solution.py:37
  402.2 5.4 %copy-start.14 = (bf16[2048,256]{1,0:T(8,128)(2,1)S(1)}, bf16[2048,256]{1,0:T(8,128)(2,1)}, u32[]{:S(2)}) copy-start(bf16[2048,256]{1,0:T(8,128)(2,1)} %copy-done.13) | copy-start | bytes 3145732
  402.2 31.1 %collective-permute-start.31 = (bf16[1024,1024]{1,0:T(8,128)(2,1)}, bf16[1024,1024]{1,0:T(8,128)(2,1)}, u32[]{:S(2)}, u32[]{:S(2)}) collective-permute-start(bf16[1024,1024]{1,0:T(8,128)(2,1)} %pad_maximum_fusion.6), channel_id=1, source_target_pairs={{0,4},{4,0},{1,5},{5,1},{2,6},{6,2},{3,7},{7,3},{8,12},{12,8},{9,1... | collective-permute-start | bytes 6291464 | tf_op jit(solution)/shard_map/ppermute | solution.py:33
  426.9 27.7 %collective-permute-start.33 = (bf16[4,144,1024]{2,1,0:T(8,128)(2,1)S(1)}, bf16[4,144,1024]{2,1,0:T(8,128)(2,1)}, u32[]{:S(2)}, u32[]{:S(2)}) collective-permute-start(bf16[4,144,1024]{2,1,0:T(8,128)(2,1)S(1)} %dynamic-slice_bitcast_fusion.1), channel_id=1, source_target_pairs={{0,16},{16,0},{1,17},{17,1},{2,18},{18,2},{3,19},{19,3},{4,20},{20... | collective-permute-start | bytes 3538952 | tf_op jit(solution)/shard_map/ppermute | solution.py:41
  429.6 28.3 %collective-permute-start.38 = (bf16[32,2304]{1,0:T(8,128)(2,1)S(1)}, bf16[32,2304]{1,0:T(8,128)(2,1)S(1)}, u32[]{:S(2)}, u32[]{:S(2)}) collective-permute-start(bf16[32,2304]{1,0:T(8,128)(2,1)S(1)} %get-tuple-element.76), channel_id=1, source_target_pairs={{0,12},{4,8},{8,4},{12,0},{1,13},{5,9},{9,5},{13,1},{2,14},{6,10},... | collective-permute-start | bytes 442376 | tf_op jit(solution)/shard_map/ppermute | solution.py:45
  430.2 27.7 %collective-permute-start.39 = (bf16[32,2304]{1,0:T(8,128)(2,1)S(1)}, bf16[32,2304]{1,0:T(8,128)(2,1)S(1)}, u32[]{:S(2)}, u32[]{:S(2)}) collective-permute-start(bf16[32,2304]{1,0:T(8,128)(2,1)S(1)} %get-tuple-element.77), channel_id=1, source_target_pairs={{0,8},{4,12},{8,0},{12,4},{1,9},{5,13},{9,1},{13,5},{2,10},{6,14},... | collective-permute-start | bytes 442376 | tf_op jit(solution)/shard_map/ppermute | solution.py:45
  431.2 26.7 %collective-permute-start.40 = (bf16[32,2304]{1,0:T(8,128)(2,1)S(1)}, bf16[32,2304]{1,0:T(8,128)(2,1)S(1)}, u32[]{:S(2)}, u32[]{:S(2)}) collective-permute-start(bf16[32,2304]{1,0:T(8,128)(2,1)S(1)} %get-tuple-element.75), channel_id=1, source_target_pairs={{0,4},{4,0},{8,12},{12,8},{1,5},{5,1},{9,13},{13,9},{2,6},{6,2},{1... | collective-permute-start | bytes 442376 | tf_op jit(solution)/shard_map/ppermute | solution.py:45
  441.2 28.1 %collective-permute-start.32 = (bf16[512,1024]{1,0:T(8,128)(2,1)}, bf16[512,1024]{1,0:T(8,128)(2,1)}, u32[]{:S(2)}, u32[]{:S(2)}) collective-permute-start(bf16[512,1024]{1,0:T(8,128)(2,1)} %fusion.13), channel_id=1, source_target_pairs={{0,8},{8,0},{1,9},{9,1},{2,10},{10,2},{3,11},{11,3},{4,12},{12,4},... | collective-permute-start | bytes 3145736 | tf_op jit(solution)/shard_map/ppermute | solution.py:37
  460.6 5.4 %copy-start.25 = (bf16[32,4608]{1,0:T(8,128)(2,1)S(1)}, bf16[32,4608]{1,0:T(8,128)(2,1)}, u32[]{:S(2)}) copy-start(bf16[32,4608]{1,0:T(8,128)(2,1)} %param.19) | copy-start | bytes 884740
  462.5 6.2 %copy-start.38 = (bf16[32]{0:T(256)(128)(2,1)S(1)}, bf16[32]{0:T(256)(128)(2,1)}, u32[]{:S(2)}) copy-start(bf16[32]{0:T(256)(128)(2,1)} %param.18) | copy-start | bytes 196
  466.0 6.2 %copy-start.12 = (f32[512,1024]{1,0:T(8,128)S(1)}, f32[512,1024]{1,0:T(8,128)}, u32[]{:S(2)}) copy-start(f32[512,1024]{1,0:T(8,128)} %get-tuple-element.46) | copy-start | bytes 6291460
  476.0 19.9 %copy-start.34 = (bf16[32,3072]{1,0:T(8,128)(2,1)S(1)}, bf16[32,3072]{1,0:T(8,128)(2,1)}, u32[]{:S(2)}) copy-start(bf16[32,3072]{1,0:T(8,128)(2,1)} %param.15) | copy-start | bytes 589828
  488.3 7.8 %copy-start.39 = (bf16[32]{0:T(256)(128)(2,1)S(1)}, bf16[32]{0:T(256)(128)(2,1)}, u32[]{:S(2)}) copy-start(bf16[32]{0:T(256)(128)(2,1)} %param.14) | copy-start | bytes 196
  490.0 4.1 collective-permute-start.35
  490.8 4.5 collective-permute-start.36
  491.6 3.7 collective-permute-start.37
  (28 other events, 85.6 us)
Sparse Core Ops, SparseCore 0:
  19.7 52.3 all-gather.7
  76.8 81.3 all-gather.9
  160.4 50.2 all-gather.5
  331.6 28.8 reduce-scatter.3
  367.1 49.0 reduce-scatter.5
  458.0 30.2 reduce-scatter.7
